TPU v7x, 768 devices: a whole 4x8x12 slice. The times are simulated.
768 devices in a mesh: win: 96 (over y, x, z_hi), head: 8 (over z_lo, core).
Axes of the slice: x: 4, y: 8, z: 12 (z_hi: 3, z_lo: 4; z = z_hi * 4 + z_lo), core: 2. Of those that a mesh axis runs over, the one named last changes fastest.
Arguments:
- block_input: bfloat16 [55296, 512], P('win'), may hold values from -40 to 40
- stream: bfloat16 [55296, 512], P('win'), may hold values from -6 to 6
- grad_out: bfloat16 [55296, 512], P('win'), may hold values from -6 to 6
- regions: int32 [55296], P('win'), may hold values from 0 to 2
- qkv_weight: bfloat16 [3, 512, 512], P(None, None, 'head'), may hold values from -12 to 12
- out_weight: bfloat16 [512, 512], P('head'), may hold values from -0.25 to 0.25
- up_weight: bfloat16 [512, 2048], P(None, 'head'), may hold values from -0.25 to 0.25
- down_weight: bfloat16 [2048, 512], P('head'), may hold values from -0.125 to 0.125
Outputs:
- grad_input: bfloat16 [55296, 512], P(('win', 'head'))
- weight_grads: float32 [8, 393216], P('head', 'win')
All inputs are finite; a program needn't handle non-finite values.
Results may differ from a plain program's by a relative error of at most 0.018.
The roundings to bfloat16 on the way count: a program that leaves them out, or rounds other values in their place, can miss the bound.
Values may be sent and summed in bfloat16 or wider, within the bound.
No kernel may reach another device: no remote copies, remote signals or barrier semaphores. Data moves between devices by JAX's collectives and lax.ppermute only.
A program may use at most 32 MiB of HBM per device.

v0:
```python
from functools import partial

import jax
import jax.numpy as jnp
from jax import lax
from jax.sharding import PartitionSpec as P

HS = 64
WIN = 144
HALF = 72


epsilon = 1e-05


def shifted(block, axis, distance):
    devices = range(lax.axis_size(axis))
    route = [((i - distance) % len(devices), i) for i in devices]
    return lax.ppermute(block, axis, route)


def normalize(values):
    data_f = values.astype(jnp.float32)
    centred = data_f - jnp.mean(data_f, axis=-1, keepdims=True)
    factor = lax.rsqrt(jnp.mean(centred * centred, axis=-1, keepdims=True) + epsilon)
    return (centred * factor, factor)


def norm_back(normed, factor, upper):
    inner = upper - jnp.mean(upper, axis=-1, keepdims=True)
    return factor * (inner - normed * jnp.mean(upper * normed, axis=-1, keepdims=True))


def contract_rows(left, right):
    return lax.dot_general(
        left, right, (((0,), (0,)), ((), ())), preferred_element_type=jnp.float32
    )


def contract_cols(left, right):
    return lax.dot_general(
        left, right, (((1,), (1,)), ((), ())), preferred_element_type=jnp.float32
    )


def mlp_back(stream, grad_out, up_weight, down_weight):
    normed, factor = normalize(stream)
    unit = normed.astype(jnp.bfloat16)
    pre = jnp.dot(unit, up_weight, preferred_element_type=jnp.float32)
    act, pull = jax.vjp(partial(jax.nn.gelu, approximate=True), pre)
    act_b = act.astype(jnp.bfloat16)
    upper = contract_cols(grad_out, down_weight)
    pre_grad = pull(upper)[0].astype(jnp.bfloat16)
    down_grad = contract_rows(act_b, grad_out)
    up_grad = contract_rows(unit, pre_grad)
    unit_grad = contract_cols(pre_grad, up_weight)
    return (normed, factor, up_grad, down_grad, unit_grad)


def attend_back(shifted_in, shifted_grad, regions, qkv_weight, out_weight, width, head_size):
    row_count = shifted_in.shape[0]
    windows = row_count // width
    columns = qkv_weight.shape[2]
    heads = columns // head_size
    scaling = head_size ** (-0.5)
    proj = jnp.einsum(
        "td,idc->itc", shifted_in, qkv_weight, preferred_element_type=jnp.float32
    ).astype(jnp.bfloat16)
    proj = proj.reshape(3, windows, width, heads, head_size)
    query, keys, value = (proj[0], proj[1], proj[2])
    scores = (
        jnp.einsum("wqhe,wkhe->whqk", query, keys, preferred_element_type=jnp.float32) * scaling
    )
    labels = regions.reshape(windows, width)
    same = labels[:, None, :, None] == labels[:, None, None, :]
    kept = jnp.where(same, scores, -jnp.inf)
    highest = jnp.max(kept, axis=-1, keepdims=True)
    raised = jnp.exp(kept - highest)
    probs = raised / jnp.sum(raised, axis=-1, keepdims=True)
    probs_b = probs.astype(jnp.bfloat16)
    attended = jnp.einsum(
        "whqk,wkhe->wqhe", probs_b, value, preferred_element_type=jnp.float32
    ).astype(jnp.bfloat16)
    out_grad = contract_rows(attended.reshape(row_count, columns), shifted_grad)
    attended_grad = (
        contract_cols(shifted_grad, out_weight)
        .astype(jnp.bfloat16)
        .reshape(windows, width, heads, head_size)
    )
    prob_grad = jnp.einsum(
        "wqhe,wkhe->whqk", attended_grad, value, preferred_element_type=jnp.float32
    )
    score_grad = (
        probs * (prob_grad - jnp.sum(prob_grad * probs, axis=-1, keepdims=True)) * scaling
    ).astype(jnp.bfloat16)
    value_grad = jnp.einsum(
        "whqk,wqhe->wkhe", probs_b, attended_grad, preferred_element_type=jnp.float32
    ).astype(jnp.bfloat16)
    query_grad = jnp.einsum(
        "whqk,wkhe->wqhe", score_grad, keys, preferred_element_type=jnp.float32
    ).astype(jnp.bfloat16)
    key_grad = jnp.einsum(
        "whqk,wqhe->wkhe", score_grad, query, preferred_element_type=jnp.float32
    ).astype(jnp.bfloat16)
    stacked = jnp.stack([query_grad, key_grad, value_grad]).reshape(3, row_count, columns)
    qkv_grad = jnp.einsum("td,itc->idc", shifted_in, stacked, preferred_element_type=jnp.float32)
    in_grad = jnp.einsum("itc,idc->td", stacked, qkv_weight, preferred_element_type=jnp.float32)
    return (qkv_grad, out_grad, in_grad)


def shards(block_input, stream, grad_out, regions, qkv_weight, out_weight, up_weight, down_weight):
    row_count = block_input.shape[0]
    head_count = lax.axis_size("head")
    share_rows = row_count // head_count
    share_start = lax.axis_index("head") * share_rows
    normed_in, factor_in = normalize(block_input)
    hidden = normed_in.astype(jnp.bfloat16)
    normed_mid, factor_mid, up_grad, down_grad, unit_grad = mlp_back(
        stream, grad_out, up_weight, down_weight
    )
    summed = lax.psum(unit_grad, "head")
    middle = grad_out.astype(jnp.float32) + norm_back(normed_mid, factor_mid, summed)
    grad_mid = middle.astype(jnp.bfloat16)
    mid_share = lax.dynamic_slice_in_dim(middle, share_start, share_rows, 0)
    far_hidden, far_grad = shifted((hidden[:HALF], grad_mid[:HALF]), "win", -1)
    shifted_in = jnp.concatenate([hidden[HALF:], far_hidden], 0)
    shifted_grad = jnp.concatenate([grad_mid[HALF:], far_grad], 0)
    qkv_grad, out_grad, in_grad = attend_back(
        shifted_in, shifted_grad, regions, qkv_weight, out_weight, WIN, HS
    )
    returned = shifted(in_grad[row_count - HALF :].astype(jnp.bfloat16), "win", 1).astype(
        jnp.float32
    )
    plain_grad = jnp.concatenate([returned, in_grad[: row_count - HALF]], 0)
    own_grad = lax.psum_scatter(
        plain_grad.astype(jnp.bfloat16), "head", scatter_dimension=0, tiled=True
    ).astype(jnp.float32)
    own_in = lax.dynamic_slice_in_dim(normed_in, share_start, share_rows, 0)
    own_in_factor = lax.dynamic_slice_in_dim(factor_in, share_start, share_rows, 0)
    grad_input = (mid_share + norm_back(own_in, own_in_factor, own_grad)).astype(jnp.bfloat16)
    flattened = jnp.concatenate(
        [qkv_grad.reshape(-1), out_grad.reshape(-1), up_grad.reshape(-1), down_grad.reshape(-1)]
    )
    owned = lax.psum_scatter(flattened, "win", scatter_dimension=0, tiled=True)
    return (grad_input, owned.reshape(1, -1))


def solution(mesh):
    return jax.shard_map(
        shards,
        mesh=mesh,
        in_specs=(
            P("win", None),
            P("win", None),
            P("win", None),
            P("win"),
            P(None, None, "head"),
            P("head", None),
            P(None, "head"),
            P("head", None),
        ),
        out_specs=(P(("win", "head"), None), P("head", "win")),
        check_vma=False,
    )
```

profile of v0, /device:TPU:6, one launch (start us, length us, event | category | flops | bytes accessed | tf_op | source)
XLA Modules:
  0.0 1449.5 jit_solution(15911449144945416337)
XLA Ops:
  7.2 1.4 convert_reduce_fusion.1
  8.6 1.4 fusion.22
  10.0 1.3 fusion.98
  11.4 0.7 fusion.37
  12.0 1.4 fusion.99
  14.1 1.3 fusion.7
  15.3 14.8 %collective-permute-start = (bf16[72,512]{1,0:T(8,128)(2,1)S(1)}, bf16[72,512]{1,0:T(8,128)(2,1)S(1)}, u32[]{:S(2)}, u32[]{:S(2)}) collective-permute-start(bf16[72,512]{1,0:T(8,128)(2,1)S(1)} %slice.42), channel_id=1, source_target_pairs={{8,0},{16,8},{24,16},{32,24},{40,32},{48,40},{56,48},{64,56},{72,6... | collective-permute-start | bytes 221192 | tf_op jit(solution)/shard_map/ppermute | solution.py:19
  30.7 0.6 convolution_bitcast_fusion.2
  31.3 0.9 slice.41
  32.7 3.9 collective-permute-done
  37.6 1.2 fusion.93
  38.8 67.6 %all-reduce.4.cloned.1.call-done = f32[576,512]{1,0:T(8,128)} async-done(((f32[576,512]{1,0:T(8,128)}), f32[576,512]{1,0:T(8,128)}) %all-reduce.4.cloned.1.call-update) | async-done | bytes 1179664 | tf_op jit(solution)/shard_map/psum | solution.py:121
  106.4 1.9 fusion.89
  108.3 1.5 fusion.90
  109.8 6.8 collective-permute-start.1
  117.1 4.4 collective-permute-done.1
  122.2 1.3 fusion.25
  123.8 1.6 fusion.24
  125.3 1.6 fusion.23
  128.2 0.7 copy-done.7
  129.7 6.5 collective-permute-start.2
  136.2 1.3 convolution_bitcast_fusion.4
  137.5 4.1 collective-permute-done.2
  141.6 0.9 pad_maximum_fusion.3
  142.6 1.2 pad_maximum_fusion
  143.9 0.8 dynamic-slice.3
  144.6 1.3 dynamic-slice.4
  146.6 37.6 %reduce-scatter.2.cloned.1.call-done = bf16[72,512]{1,0:T(8,128)(2,1)} async-done(((bf16[576,512]{1,0:T(8,128)(2,1)}), bf16[72,512]{1,0:T(8,128)(2,1)}) %reduce-scatter.2.cloned.1.call-update) | async-done | bytes 73744 | tf_op jit(solution)/shard_map/reduce_scatter | solution.py:135
  184.2 1.1 convert_reduce_fusion.2
  185.3 1.8 fusion.49
  187.0 1254.7 %all-reduce.6.cloned.1.call-done = f32[393216]{0:T(1024)} async-done(((f32[393216]{0:T(1024)}), f32[393216]{0:T(1024)}) %all-reduce.6.cloned.1.call-update) | async-done | bytes 1572880
  1441.7 1.3 dynamic-slice.5
  (94 shorter events, 6.1 us)
Async XLA Ops:
  7.2 4.2 copy-start
  7.2 4.2 copy-start.1
  7.2 2.8 copy-start.4
  7.2 99.2 %all-reduce.4.cloned.1.call-start = ((), (), s32[]{:S(2)}) async-start(), calls=%async_computation.1 | async-start | bytes 2359296 | tf_op jit(solution)/shard_map/psum | solution.py:121
  12.0 1.5 copy-start.2
  13.5 170.7 %reduce-scatter.2.cloned.1.call-start = ((), (), s32[]{:S(2)}) async-start(), calls=%async_computation.2 | async-start | bytes 663552 | tf_op jit(solution)/shard_map/reduce_scatter | solution.py:135
  14.1 1.3 copy-start.9
  15.3 21.2 %collective-permute-start = (bf16[72,512]{1,0:T(8,128)(2,1)S(1)}, bf16[72,512]{1,0:T(8,128)(2,1)S(1)}, u32[]{:S(2)}, u32[]{:S(2)}) collective-permute-start(bf16[72,512]{1,0:T(8,128)(2,1)S(1)} %slice.42), channel_id=1, source_target_pairs={{8,0},{16,8},{24,16},{32,24},{40,32},{48,40},{56,48},{64,56},{72,6... | collective-permute-start | bytes 221192 | tf_op jit(solution)/shard_map/ppermute | solution.py:19
  30.6 1.5 copy-start.10
  32.1 4.4 copy-start.11
  32.2 4.3 copy-start.6
  36.6 0.6 copy-start.13
  38.8 77.8 %copy-start.19 = (f32[4,144]{1,0:T(4,128)}, f32[4,144]{1,0:T(4,128)S(1)}, u32[]{:S(2)}) copy-start(f32[4,144]{1,0:T(4,128)S(1)} %get-tuple-element.15) | copy-start | bytes 6916
  106.4 1.9 copy-start.3
  108.3 8.3 copy-start.18
  109.8 11.7 collective-permute-start.1
  116.8 4.7 copy-start.17
  117.1 5.1 copy-start.20
  117.1 6.4 copy-start.8
  121.5 0.6 copy-start.15
  122.2 1.6 copy-start.21
  126.9 0.9 copy-start.12
  127.8 1.0 copy-start.7
  127.8 1.0 copy-start.14
  128.2 1.0 copy-start.5
  129.2 7.0 copy-start.16
  129.5 12.1 slice-start
  129.7 11.9 collective-permute-start.2
  142.5 1299.1 %all-reduce.6.cloned.1.call-start = ((), (), s32[]{:S(2)}) async-start(), calls=%async_computation.3 | async-start | bytes 3145728
Sparse Core Ops, SparseCore 0:
  13.6 92.7 all-reduce.3
  142.7 41.4 reduce-scatter.1
  187.4 1254.2 all-reduce.5
where the time goes:
time: 1460 us; the launch traced here: 1450 us
  waiting for transfers between devices  1370 us (94%)
  starting transfers between devices  28.2 us (2%)
  between operations  15 us (1%)
    unnamed x4, waiting for transfers between devices  1250 us
    psum x1, waiting for transfers between devices, shards(): summed = lax.psum(unit_grad, 'head')  67.6 us
    reduce_scatter x1, waiting for transfers between devices, shards(): lax.psum_scatter(plain_grad.astype(jnp.bfloat16), 'head', scatter_dimensi...  37.6 us
  transfers between devices with their start and end apart: 6, of which 6 were waited for; matrix products, arithmetic and copies ran while one was open for 1% of the time, Pallas kernels for 0%

commit v1 on v0

--- a/solution.py
+++ b/solution.py
@@ -3,7 +3,7 @@
 import jax
 import jax.numpy as jnp
 from jax import lax
-from jax.sharding import PartitionSpec as P
+from jax.sharding import Mesh, PartitionSpec as P
 
 HS = 64
 WIN = 144
@@ -13,10 +13,19 @@
 epsilon = 1e-05
 
 
+WIN_AXES = ("y", "x", "zh")
+HEAD_AXES = ("zl", "core")
+
+
 def shifted(block, axis, distance):
     devices = range(lax.axis_size(axis))
     route = [((i - distance) % len(devices), i) for i in devices]
     return lax.ppermute(block, axis, route)
+
+
+def exchange(pieces, axis):
+    received = lax.all_to_all(pieces.astype(jnp.bfloat16), axis, 0, 0)
+    return jnp.sum(received.astype(jnp.float32), axis=0)
 
 
 def normalize(values):
@@ -110,55 +119,61 @@
 
 def shards(block_input, stream, grad_out, regions, qkv_weight, out_weight, up_weight, down_weight):
     row_count = block_input.shape[0]
-    head_count = lax.axis_size("head")
+    width = block_input.shape[1]
+    y_count, x_count, z_count = [lax.axis_size(axis) for axis in WIN_AXES]
+    head_count = lax.axis_size(HEAD_AXES)
     share_rows = row_count // head_count
-    share_start = lax.axis_index("head") * share_rows
+    share_start = lax.axis_index(HEAD_AXES) * share_rows
+
+    def share(values):
+        return lax.dynamic_slice_in_dim(values, share_start, share_rows, 0)
+
     normed_in, factor_in = normalize(block_input)
     hidden = normed_in.astype(jnp.bfloat16)
+    far_hidden = shifted(hidden[:HALF], WIN_AXES, -1)
     normed_mid, factor_mid, up_grad, down_grad, unit_grad = mlp_back(
         stream, grad_out, up_weight, down_weight
     )
-    summed = lax.psum(unit_grad, "head")
-    middle = grad_out.astype(jnp.float32) + norm_back(normed_mid, factor_mid, summed)
-    grad_mid = middle.astype(jnp.bfloat16)
-    mid_share = lax.dynamic_slice_in_dim(middle, share_start, share_rows, 0)
-    far_hidden, far_grad = shifted((hidden[:HALF], grad_mid[:HALF]), "win", -1)
+    summed = exchange(unit_grad.reshape(head_count, share_rows, width), HEAD_AXES)
+    own_mid, own_mid_factor = normalize(share(stream))
+    mid_share = share(grad_out).astype(jnp.float32) + norm_back(own_mid, own_mid_factor, summed)
+    grad_mid = lax.all_gather(mid_share.astype(jnp.bfloat16), HEAD_AXES, axis=0, tiled=True)
+    far_grad = shifted(grad_mid[:HALF], WIN_AXES, -1)
     shifted_in = jnp.concatenate([hidden[HALF:], far_hidden], 0)
     shifted_grad = jnp.concatenate([grad_mid[HALF:], far_grad], 0)
     qkv_grad, out_grad, in_grad = attend_back(
         shifted_in, shifted_grad, regions, qkv_weight, out_weight, WIN, HS
     )
-    returned = shifted(in_grad[row_count - HALF :].astype(jnp.bfloat16), "win", 1).astype(
-        jnp.float32
-    )
-    plain_grad = jnp.concatenate([returned, in_grad[: row_count - HALF]], 0)
-    own_grad = lax.psum_scatter(
-        plain_grad.astype(jnp.bfloat16), "head", scatter_dimension=0, tiled=True
-    ).astype(jnp.float32)
-    own_in = lax.dynamic_slice_in_dim(normed_in, share_start, share_rows, 0)
-    own_in_factor = lax.dynamic_slice_in_dim(factor_in, share_start, share_rows, 0)
-    grad_input = (mid_share + norm_back(own_in, own_in_factor, own_grad)).astype(jnp.bfloat16)
+    in_grad = in_grad.astype(jnp.bfloat16)
+    returned = shifted(in_grad[row_count - HALF :], WIN_AXES, 1)
     flattened = jnp.concatenate(
         [qkv_grad.reshape(-1), out_grad.reshape(-1), up_grad.reshape(-1), down_grad.reshape(-1)]
-    )
-    owned = lax.psum_scatter(flattened, "win", scatter_dimension=0, tiled=True)
+    ).astype(jnp.bfloat16)
+    pieces = flattened.reshape(y_count, x_count, z_count, -1, 128).transpose(1, 0, 2, 3, 4)
+    partial_sum = exchange(pieces, "x")
+    owned = exchange(partial_sum.reshape(y_count * z_count, -1, 128), ("y", "zh"))
+    plain_grad = jnp.concatenate([returned, in_grad[: row_count - HALF]], 0)
+    own_grad = exchange(plain_grad.reshape(head_count, share_rows, width), HEAD_AXES)
+    own_in, own_in_factor = normalize(share(block_input))
+    grad_input = (mid_share + norm_back(own_in, own_in_factor, own_grad)).astype(jnp.bfloat16)
     return (grad_input, owned.reshape(1, -1))
 
 
 def solution(mesh):
+    fine = Mesh(mesh.devices.reshape(8, 4, 3, 4, 2), WIN_AXES + HEAD_AXES)
     return jax.shard_map(
         shards,
-        mesh=mesh,
+        mesh=fine,
         in_specs=(
-            P("win", None),
-            P("win", None),
-            P("win", None),
-            P("win"),
-            P(None, None, "head"),
-            P("head", None),
-            P(None, "head"),
-            P("head", None),
+            P(WIN_AXES, None),
+            P(WIN_AXES, None),
+            P(WIN_AXES, None),
+            P(WIN_AXES),
+            P(None, None, HEAD_AXES),
+            P(HEAD_AXES, None),
+            P(None, HEAD_AXES),
+            P(HEAD_AXES, None),
         ),
-        out_specs=(P(("win", "head"), None), P("head", "win")),
+        out_specs=(P(WIN_AXES + HEAD_AXES, None), P(HEAD_AXES, WIN_AXES)),
         check_vma=False,
     )

time: 1460 us -> 154 us (0.11)
  the two profiles are of different devices: /device:TPU:6 before, /device:TPU:1 now
where the time goes in v1:
time: 154 us; the launch traced here: 153 us
  starting transfers between devices  59.6 us (39%)
  blocking collectives  34.3 us (22%)
  waiting for transfers between devices  26.5 us (17%)
  matrix products  16.8 us (11%)
  other arithmetic  7.75 us (5%)
  local copies, waits for them, and re-layouts  7.18 us (5%)
    all_to_all x3, starting transfers between devices, exchange(): received = lax.all_to_all(pieces.astype(jnp.bfloat16), axis, 0, 0)  32.8 us
    ppermute x3, starting transfers between devices, shifted(): return lax.ppermute(block, axis, route)  26.8 us
    all_gather x1, blocking collectives, shards(): lax.all_gather(mid_share.astype(jnp.bfloat16), HEAD_AXES, axis=0, tiled=T...  19.1 us
    all_to_all x1, blocking collectives, exchange(): received = lax.all_to_all(pieces.astype(jnp.bfloat16), axis, 0, 0)  15.2 us
    all_to_all x3, waiting for transfers between devices, exchange(): received = lax.all_to_all(pieces.astype(jnp.bfloat16), axis, 0, 0)  14.9 us
    ppermute x3, waiting for transfers between devices, shifted(): return lax.ppermute(block, axis, route)  11.6 us
    dot_general x3, matrix products, contract_rows(): lax.dot_general(left, right, (((0,), (0,)), ((), ())), preferred_element_...  3.78 us
  transfers between devices with their start and end apart: 6, of which 3 were waited for; matrix products, arithmetic and copies ran while one was open for 10% of the time, Pallas kernels for 0%

profile of v1, /device:TPU:1, one launch (start us, length us, event | category | flops | bytes accessed | tf_op | source)
XLA Modules:
  0.0 153.3 jit_solution(5266120433541259274)
XLA Ops:
  0.7 1.3 convert_reduce_fusion.5
  2.4 1.3 fusion.109
  3.7 1.5 fusion.36
  5.2 1.1 convolution_convert_fusion
  6.3 14.1 %all-to-all-start = ((bf16[8,72,512]{2,1,0:T(8,128)(2,1)}), bf16[8,72,512]{2,1,0:T(8,128)(2,1)S(1)}, u32[]{:S(2)}, u32[]{:S(2)}) async-start(bf16[8,72,512]{2,1,0:T(8,128)(2,1)} %bitcast), calls=%async_computation | async-start | bytes 1179648 | tf_op jit(solution)/shard_map/all_to_all | solution.py:27
  21.2 0.6 slice.40
  21.8 11.5 %collective-permute-start = (bf16[72,512]{1,0:T(8,128)(2,1)}, bf16[72,512]{1,0:T(8,128)(2,1)}, u32[]{:S(2)}, u32[]{:S(2)}) collective-permute-start(bf16[72,512]{1,0:T(8,128)(2,1)} %slice.40), channel_id=1, source_target_pairs={{8,0},{16,8},{24,16},{32,24},{40,32},{48,40},{56,48},{64,56},{72,6... | collective-permute-start | bytes 221192 | tf_op jit(solution)/shard_map/ppermute | solution.py:23
  34.1 2.2 %fusion.19 = bf16[32,4,8,128]{3,2,1,0:T(8,128)(2,1)} fusion(bf16[576,512]{1,0:T(8,128)(2,1)S(1)} %copy-done.3, f32[576,256]{1,0:T(8,128)} %get-tuple-element.12), kind=kOutput, calls=%fused_computation.33 | convolution fusion | flops 152453120 | bytes 1441792 | tf_op jit(solution)/shard_map/dot_general | solution.py:44
  36.3 0.6 add_rsqrt_fusion.3
  36.9 1.3 fusion.18
  38.3 0.8 slice.39
  39.2 1.2 copy.97
  40.6 1.3 fusion.38
  41.9 0.8 reshape.190
  43.0 2.1 %fusion.104 = (f32[4,144]{1,0:T(4,128)S(1)}, f32[4,144,144]{1,2,0:T(8,128)}) fusion(s32[4,144]{1,0:T(4,128)S(1)} %eq.16, bf16[4,144,64]{1,0,2:T(4,128)(2,1)} %reshape.190, bf16[4,144,64]{1,0,2:T(4,128)(2,1)S(1)} %reshape.191), kind=kOutput, calls=%fused_computation.141 | convolution fusion | flops 11031695 | bytes 483840 | tf_op jit(solution)/shard_map/sub | solution.py:87
  45.7 19.1 %all_gather.3 = bf16[576,512]{1,0:T(8,128)(2,1)S(1)} all-gather(bf16[72,512]{1,0:T(8,128)(2,1)S(1)} %get-tuple-element.6), channel_id=1, replica_groups=mesh['y'=8,'x'=4,'zh'=3,'zl'=4,'core'=2] {'zl','core'}, dimensions={0}, use_global_device_ids=true | all-gather | bytes 663552 | tf_op jit(solution)/shard_map/all_gather | solution.py:140
  64.8 8.3 %collective-permute-start.1 = (bf16[72,512]{1,0:T(8,128)(2,1)S(1)}, bf16[72,512]{1,0:T(8,128)(2,1)S(1)}, u32[]{:S(2)}, u32[]{:S(2)}) collective-permute-start(bf16[72,512]{1,0:T(8,128)(2,1)S(1)} %slice.44), channel_id=1, source_target_pairs={{8,0},{16,8},{24,16},{32,24},{40,32},{48,40},{56,48},{64,56},{72,6... | collective-permute-start | bytes 221192 | tf_op jit(solution)/shard_map/ppermute | solution.py:23
  73.6 2.5 %collective-permute-done.1 = bf16[72,512]{1,0:T(8,128)(2,1)S(1)} collective-permute-done((bf16[72,512]{1,0:T(8,128)(2,1)S(1)}, bf16[72,512]{1,0:T(8,128)(2,1)S(1)}, u32[]{:S(2)}, u32[]{:S(2)}) %collective-permute-start.1) | collective-permute-done | bytes 73760 | tf_op jit(solution)/shard_map/ppermute | solution.py:23
  77.1 0.6 copy-done.9
  77.7 1.6 %fusion.22 = bf16[4,144,1,64]{1,3,0,2:T(8,128)(2,1)S(1)} fusion(f32[4,144,144]{1,2,0:T(8,128)S(1)} %fusion.69, bf16[4,144,64]{1,0,2:T(4,128)(2,1)S(1)} %copy-done.9, f32[4,144,144]{1,2,0:T(8,128)} %get-tuple-element.14, f32[4,144]{1,0:T(4,128)S(1)} %copy-done.20), kind=kOutput, calls=%fused_computation.40 | convolution fusion | flops 11235023 | bytes 813312 | tf_op jit(solution)/shard_map/whqk,wqhe->wkhe/dot_general | solution.py:111
  79.3 1.6 %fusion.21 = bf16[4,144,1,64]{1,3,0,2:T(8,128)(2,1)S(1)} fusion(f32[4,144,144]{1,2,0:T(8,128)S(1)} %fusion.69, bf16[4,144,64]{1,0,2:T(4,128)(2,1)S(1)} %copy-done.7, f32[4,144,144]{1,2,0:T(8,128)} %get-tuple-element.14, f32[4,144]{1,0:T(4,128)S(1)} %copy-done.20), kind=kOutput, calls=%fused_computation.39 | convolution fusion | flops 11235023 | bytes 813312 | tf_op jit(solution)/shard_map/whqk,wkhe->wqhe/dot_general | solution.py:108
  82.3 1.2 fusion.20
  84.1 15.2 %all_to_all.20 = bf16[4,8,3,32,128]{4,3,2,1,0:T(8,128)(2,1)S(1)} all-to-all(bf16[4,8,3,32,128]{4,3,2,1,0:T(8,128)(2,1)S(1)} %copy.91), channel_id=1, replica_groups=mesh['y'=8,'x'=4,'zh'=3,'zl'=4,'core'=2] {'x'}, dimensions={0} | all-to-all | bytes 1572864 | tf_op jit(solution)/shard_map/all_to_all | solution.py:27
  99.3 0.8 reduce_sum.181
  100.1 11.4 %all-to-all-start.3 = ((bf16[24,32,128]{2,1,0:T(8,128)(2,1)}), bf16[24,32,128]{2,1,0:T(8,128)(2,1)S(1)}, u32[]{:S(2)}, u32[]{:S(2)}) async-start(bf16[24,32,128]{2,1,0:T(8,128)(2,1)} %bitcast.19), calls=%async_computation.3 | async-start | bytes 393216 | tf_op jit(solution)/shard_map/all_to_all | solution.py:27
  111.9 7.1 %collective-permute-start.2 = (bf16[72,512]{1,0:T(8,128)(2,1)S(1)}, bf16[72,512]{1,0:T(8,128)(2,1)S(1)}, u32[]{:S(2)}, u32[]{:S(2)}) collective-permute-start(bf16[72,512]{1,0:T(8,128)(2,1)S(1)} %slice.46), channel_id=1, source_target_pairs={{760,0},{0,8},{8,16},{16,24},{24,32},{32,40},{40,48},{48,56},{56,6... | collective-permute-start | bytes 221192 | tf_op jit(solution)/shard_map/ppermute | solution.py:23
  119.0 9.1 %collective-permute-done.2 = bf16[72,512]{1,0:T(8,128)(2,1)S(1)} collective-permute-done((bf16[72,512]{1,0:T(8,128)(2,1)S(1)}, bf16[72,512]{1,0:T(8,128)(2,1)S(1)}, u32[]{:S(2)}, u32[]{:S(2)}) %collective-permute-start.2) | collective-permute-done | bytes 73760 | tf_op jit(solution)/shard_map/ppermute | solution.py:23
  128.1 0.8 pad_maximum_fusion.3
  128.9 7.3 %all-to-all-start.1 = ((bf16[8,72,512]{2,1,0:T(8,128)(2,1)}), bf16[8,72,512]{2,1,0:T(8,128)(2,1)S(1)}, u32[]{:S(2)}, u32[]{:S(2)}) async-start(bf16[8,72,512]{2,1,0:T(8,128)(2,1)} %bitcast.12), calls=%async_computation.1 | async-start | bytes 1179648 | tf_op jit(solution)/shard_map/all_to_all | solution.py:27
  136.6 0.6 convert_reduce_fusion.6
  137.2 14.9 %all-to-all-done.1 = bf16[8,72,512]{2,1,0:T(8,128)(2,1)S(1)} async-done(((bf16[8,72,512]{2,1,0:T(8,128)(2,1)}), bf16[8,72,512]{2,1,0:T(8,128)(2,1)S(1)}, u32[]{:S(2)}, u32[]{:S(2)}) %all-to-all-start.1) | async-done | bytes 589856 | tf_op jit(solution)/shard_map/all_to_all | solution.py:27
  152.6 0.8 fusion.61
  (100 shorter events, 7.4 us)
Async XLA Ops:
  0.6 3.1 %copy-start = (bf16[512,256]{1,0:T(8,128)(2,1)S(1)}, bf16[512,256]{1,0:T(8,128)(2,1)}, u32[]{:S(2)}) copy-start(bf16[512,256]{1,0:T(8,128)(2,1)} %param.14) | copy-start | bytes 786436
  0.6 1.4 copy-start.2
  0.7 1.7 %copy-start.3 = (bf16[576,512]{1,0:T(8,128)(2,1)S(1)}, bf16[576,512]{1,0:T(8,128)(2,1)}, u32[]{:S(2)}) copy-start(bf16[576,512]{1,0:T(8,128)(2,1)} %param.10) | copy-start | bytes 1769476
  6.3 14.1 %copy-start.1 = (bf16[576,512]{1,0:T(8,128)(2,1)S(1)}, bf16[576,512]{1,0:T(8,128)(2,1)}, u32[]{:S(2)}) copy-start(bf16[576,512]{1,0:T(8,128)(2,1)} %param.8) | copy-start | bytes 1769476
  6.3 38.8 %all-to-all-start = ((bf16[8,72,512]{2,1,0:T(8,128)(2,1)}), bf16[8,72,512]{2,1,0:T(8,128)(2,1)S(1)}, u32[]{:S(2)}, u32[]{:S(2)}) async-start(bf16[8,72,512]{2,1,0:T(8,128)(2,1)} %bitcast), calls=%async_computation | async-start | bytes 1179648 | tf_op jit(solution)/shard_map/all_to_all | solution.py:27
  21.8 18.7 %collective-permute-start = (bf16[72,512]{1,0:T(8,128)(2,1)}, bf16[72,512]{1,0:T(8,128)(2,1)}, u32[]{:S(2)}, u32[]{:S(2)}) collective-permute-start(bf16[72,512]{1,0:T(8,128)(2,1)} %slice.40), channel_id=1, source_target_pairs={{8,0},{16,8},{24,16},{32,24},{40,32},{48,40},{56,48},{64,56},{72,6... | collective-permute-start | bytes 221192 | tf_op jit(solution)/shard_map/ppermute | solution.py:23
  33.5 0.5 copy-start.10
  38.3 0.8 copy-start.12
  38.3 2.2 %copy-start.6 = (bf16[32,4,8,128]{3,2,1,0:T(8,128)(2,1)S(1)}, bf16[32,4,8,128]{3,2,1,0:T(8,128)(2,1)}, u32[]{:S(2)}) copy-start(bf16[32,4,8,128]{3,2,1,0:T(8,128)(2,1)} %fusion.19) | copy-start | bytes 786436
  39.2 1.4 copy-start.4
  39.2 1.4 copy-start.14
  42.8 2.3 %copy-start.8 = (bf16[4,144,64]{1,0,2:T(4,128)(2,1)}, bf16[4,144,64]{1,0,2:T(4,128)(2,1)S(1)}, u32[]{:S(2)}) copy-start(bf16[4,144,64]{1,0,2:T(4,128)(2,1)S(1)} %reshape.191) | copy-start | bytes 221188
  43.0 2.4 %copy-start.11 = (f32[72]{0:T(128)S(1)}, f32[72]{0:T(128)}, u32[]{:S(2)}) copy-start(f32[72]{0:T(128)} %copy-done.10) | copy-start | bytes 868
  43.0 2.4 %copy-start.13 = (f32[72]{0:T(128)S(1)}, f32[72]{0:T(128)}, u32[]{:S(2)}) copy-start(f32[72]{0:T(128)} %add_rsqrt_fusion.3) | copy-start | bytes 868
  45.1 27.9 %copy-start.19 = (f32[4,144]{1,0:T(4,128)}, f32[4,144]{1,0:T(4,128)S(1)}, u32[]{:S(2)}) copy-start(f32[4,144]{1,0:T(4,128)S(1)} %get-tuple-element.13) | copy-start | bytes 6916
  45.3 27.7 %copy-start.17 = (f32[4,144,144]{1,2,0:T(8,128)S(1)}, f32[4,144,144]{1,2,0:T(8,128)}, u32[]{:S(2)}) copy-start(f32[4,144,144]{1,2,0:T(8,128)} %get-tuple-element.14) | copy-start | bytes 995332
  64.8 11.3 %collective-permute-start.1 = (bf16[72,512]{1,0:T(8,128)(2,1)S(1)}, bf16[72,512]{1,0:T(8,128)(2,1)S(1)}, u32[]{:S(2)}, u32[]{:S(2)}) collective-permute-start(bf16[72,512]{1,0:T(8,128)(2,1)S(1)} %slice.44), channel_id=1, source_target_pairs={{8,0},{16,8},{24,16},{32,24},{40,32},{48,40},{56,48},{64,56},{72,6... | collective-permute-start | bytes 221192 | tf_op jit(solution)/shard_map/ppermute | solution.py:23
  73.3 2.8 %copy-start.16 = (bf16[64,512]{1,0:T(8,128)(2,1)S(1)}, bf16[64,512]{1,0:T(8,128)(2,1)}, u32[]{:S(2)}) copy-start(bf16[64,512]{1,0:T(8,128)(2,1)} %param.13) | copy-start | bytes 196612
  73.6 2.9 %copy-start.18 = (f32[4,144,144]{1,2,0:T(8,128)S(1)}, f32[4,144,144]{1,2,0:T(8,128)}, u32[]{:S(2)}) copy-start(f32[4,144,144]{1,2,0:T(8,128)} %get-tuple-element.14) | copy-start | bytes 995332
  73.6 2.9 %copy-start.20 = (f32[4,144]{1,0:T(4,128)S(1)}, f32[4,144]{1,0:T(4,128)}, u32[]{:S(2)}) copy-start(f32[4,144]{1,0:T(4,128)} %copy-done.19) | copy-start | bytes 6916
  76.8 0.9 copy-start.9
  77.7 1.6 %copy-start.7 = (bf16[4,144,64]{1,0,2:T(4,128)(2,1)S(1)}, bf16[4,144,64]{1,0,2:T(4,128)(2,1)}, u32[]{:S(2)}) copy-start(bf16[4,144,64]{1,0,2:T(4,128)(2,1)} %reshape.190) | copy-start | bytes 221188
  81.3 1.0 copy-start.5
  99.3 12.2 %copy-start.15 = (bf16[3,512,64]{1,2,0:T(8,128)(2,1)S(1)}, bf16[3,512,64]{1,2,0:T(8,128)(2,1)}, u32[]{:S(2)}) copy-start(bf16[3,512,64]{1,2,0:T(8,128)(2,1)} %param.12) | copy-start | bytes 589828
  100.1 28.8 %all-to-all-start.3 = ((bf16[24,32,128]{2,1,0:T(8,128)(2,1)}), bf16[24,32,128]{2,1,0:T(8,128)(2,1)S(1)}, u32[]{:S(2)}, u32[]{:S(2)}) async-start(bf16[24,32,128]{2,1,0:T(8,128)(2,1)} %bitcast.19), calls=%async_computation.3 | async-start | bytes 393216 | tf_op jit(solution)/shard_map/all_to_all | solution.py:27
  111.9 16.2 %collective-permute-start.2 = (bf16[72,512]{1,0:T(8,128)(2,1)S(1)}, bf16[72,512]{1,0:T(8,128)(2,1)S(1)}, u32[]{:S(2)}, u32[]{:S(2)}) collective-permute-start(bf16[72,512]{1,0:T(8,128)(2,1)S(1)} %slice.46), channel_id=1, source_target_pairs={{760,0},{0,8},{8,16},{16,24},{24,32},{32,40},{40,48},{48,56},{56,6... | collective-permute-start | bytes 221192 | tf_op jit(solution)/shard_map/ppermute | solution.py:23
  128.9 23.2 %all-to-all-start.1 = ((bf16[8,72,512]{2,1,0:T(8,128)(2,1)}), bf16[8,72,512]{2,1,0:T(8,128)(2,1)S(1)}, u32[]{:S(2)}, u32[]{:S(2)}) async-start(bf16[8,72,512]{2,1,0:T(8,128)(2,1)} %bitcast.12), calls=%async_computation.1 | async-start | bytes 1179648 | tf_op jit(solution)/shard_map/all_to_all | solution.py:27

commit v2 on v1

v2 whole, which is shorter than its diff:
```python
import jax
import jax.numpy as jnp
from jax import lax
from jax.experimental import pallas as pl
from jax.experimental.pallas import tpu as pltpu
from jax.sharding import Mesh, PartitionSpec as P

HS = 64
WIN = 144
HALF = 72
WIN_AXES = ("y", "x", "zh")
HEAD_AXES = ("zl", "core")
BLOCK = (32, 128)
EPSILON = 1e-05
BF = jnp.bfloat16
F32 = jnp.float32


def normalize(values):
    data_f = values.astype(F32)
    centred = data_f - jnp.mean(data_f, axis=-1, keepdims=True)
    factor = lax.rsqrt(jnp.mean(centred * centred, axis=-1, keepdims=True) + EPSILON)
    return (centred * factor, factor)


def norm_back(normed, factor, upper):
    inner = upper - jnp.mean(upper, axis=-1, keepdims=True)
    return factor * (inner - normed * jnp.mean(upper * normed, axis=-1, keepdims=True))


def dot(left, right):
    return lax.dot_general(left, right, (((1,), (0,)), ((), ())), preferred_element_type=F32)


def contract_rows(left, right):
    return lax.dot_general(left, right, (((0,), (0,)), ((), ())), preferred_element_type=F32)


def contract_cols(left, right):
    return lax.dot_general(left, right, (((1,), (1,)), ((), ())), preferred_element_type=F32)


def call(kernel, outs, args, scratch=(), flops=10**8, scalars=0):
    vmem = pl.BlockSpec(memory_space=pltpu.VMEM)
    smem = pl.BlockSpec(memory_space=pltpu.SMEM)
    size = sum(a.size * a.dtype.itemsize for a in args)
    return pl.pallas_call(
        kernel,
        out_shape=[jax.ShapeDtypeStruct(shape, dtype) for shape, dtype in outs],
        in_specs=[smem] * scalars + [vmem] * (len(args) - scalars),
        out_specs=[vmem] * len(outs),
        scratch_shapes=list(scratch),
        compiler_params=pltpu.CompilerParams(vmem_limit_bytes=40 * 2**20),
        cost_estimate=pl.CostEstimate(flops=flops, bytes_accessed=2 * size, transcendentals=0),
    )(*args)


def mlp_kernel(stream, grad_out, up_weight, down_weight, unit_grad, unit_out, act_out, pre_out):
    rows = stream.shape[0]
    for start in range(0, rows, WIN):
        part = pl.ds(start, WIN)
        unit = normalize(stream[part, :])[0].astype(BF)
        pre = dot(unit, up_weight[...])
        upper = contract_cols(grad_out[part, :], down_weight[...])
        scale = 0.7978845608028654
        square = pre * pre
        bent = jnp.tanh(scale * (pre + 0.044715 * (square * pre)))
        act = 0.5 * pre * (1.0 + bent)
        slope = 0.5 * (1.0 + bent) + 0.5 * pre * (1.0 - bent * bent) * (
            scale * (1.0 + 3 * 0.044715 * square)
        )
        pre_grad = (upper * slope).astype(BF)
        unit_out[part, :] = unit
        act_out[part, :] = act.astype(BF)
        pre_out[part, :] = pre_grad
        grad = contract_cols(pre_grad, up_weight[...])
        first = start // HALF
        unit_grad[first] = grad[:HALF].astype(BF)
        unit_grad[first + 1] = grad[HALF:].astype(BF)


def forward_kernel(
    block_input, far_input, labels_col, labels_row, qkv_weight, unit, act, pre_grad, grad_out,
    shifted_in, query_out, key_out, value_out, probs_out, attended_out, early, late, rows_f32,
):
    near = normalize(block_input[...])[0]
    far = normalize(far_input[...])[0]
    windows = block_input.shape[0] // WIN
    for index in range(windows):
        start = HALF + WIN * index
        if index < windows - 1:
            piece = near[start : start + WIN]
        else:
            piece = jnp.concatenate([near[start:], far], axis=0)
        inputs = piece.astype(BF)
        shifted_in[index] = inputs
        query, key, value = [dot(inputs, qkv_weight[i]).astype(BF) for i in range(3)]
        query_out[index] = query
        key_out[index] = key
        value_out[index] = value
        scores = contract_cols(query, key) * HS**-0.5
        kept = jnp.where(labels_col[index] == labels_row[index], scores, -jnp.inf)
        raised = jnp.exp(kept - jnp.max(kept, axis=-1, keepdims=True))
        probs = raised / jnp.sum(raised, axis=-1, keepdims=True)
        probs_out[index] = probs
        attended_out[index] = dot(probs.astype(BF), value).astype(BF)
    up_grad = contract_rows(unit[...], pre_grad[...])
    ups, wide = up_grad.shape[0], up_grad.shape[1] // 128
    for column in range(wide):
        rows_f32[pl.ds(column, ups, stride=wide), :] = up_grad[:, 128 * column : 128 * column + 128]
    down_grad = contract_rows(act[...], grad_out[...])
    downs, wide = down_grad.shape[0], down_grad.shape[1] // 128
    base = ups * up_grad.shape[1] // 128
    for column in range(wide):
        rows_f32[pl.ds(base + column, downs, stride=wide), :] = down_grad[
            :, 128 * column : 128 * column + 128
        ]
    for owner in range(32, 96):
        block = rows_f32[32 * (owner - 32) : 32 * (owner - 31), :].astype(BF)
        if owner < 36:
            early[owner - 32] = block
        else:
            late[owner % 12 // 3, owner // 12 * 3 + owner % 3 - 9] = block


def middle_kernel(parts, stream, grad_out, mid, grad_mid):
    summed = jnp.sum(parts[...].astype(F32), axis=0)
    normed, factor = normalize(stream[...])
    middle = grad_out[...].astype(F32) + norm_back(normed, factor, summed)
    mid[...] = middle
    grad_mid[...] = middle.astype(BF)


def backward_kernel(
    place, mine, theirs, shifted_in, query_in, key_in, value_in, probs_in, attended,
    qkv_weight, out_weight, early, keep, give, pieces, grads, outs,
):
    chip, core = place[0], place[1]
    windows = shifted_in.shape[0]

    def where(chunk):
        head = (chunk + 1) % 8
        return lax.rem(head // 2 - chip + 4, 4), head % 2

    def load(chunk):
        slot, owner = where(chunk)
        return jnp.where(core == owner, mine[slot].astype(F32), theirs[slot].astype(F32))

    def store(chunk, value):
        slot, owner = where(chunk)

        @pl.when(core == owner)
        def _():
            keep[slot] = value

        @pl.when(core != owner)
        def _():
            give[slot] = value

    totals = [0.0, 0.0, 0.0]
    out_grad = 0.0
    for index in range(windows):
        upper = jnp.concatenate([load(2 * index), load(2 * index + 1)], axis=0).astype(BF)
        query, key, value = query_in[index], key_in[index], value_in[index]
        probs = probs_in[index]
        attended_grad = contract_cols(upper, out_weight[...]).astype(BF)
        out_grad = out_grad + contract_rows(attended[index], upper)
        prob_grad = contract_cols(attended_grad, value)
        inner = prob_grad - jnp.sum(prob_grad * probs, axis=-1, keepdims=True)
        score_grad = (probs * inner * HS**-0.5).astype(BF)
        grads_b = [
            dot(score_grad, key).astype(BF),
            contract_rows(score_grad, query).astype(BF),
            contract_rows(probs.astype(BF), attended_grad).astype(BF),
        ]
        in_grad = sum(contract_cols(grads_b[i], qkv_weight[i]) for i in range(3)).astype(F32)
        store(2 * index, in_grad[:HALF].astype(BF))
        store(2 * index + 1, in_grad[HALF:].astype(BF))
        for i in range(3):
            totals[i] = totals[i] + contract_rows(shifted_in[index], grads_b[i])
    half = grads.shape[1] // 2
    for i in range(3):
        grads[i] = totals[i]
    for column in range(out_grad.shape[1] // 128):
        outs[pl.ds(column, HS, stride=4), :] = out_grad[:, 128 * column : 128 * column + 128]
    for owner in range(36):
        if owner < 24:
            kind, first = owner // 8, owner % 8 * 64
            even = grads[kind, pl.ds(first, 32, stride=2), :]
            odd = grads[kind, pl.ds(first + 1, 32, stride=2), :]
            block = jnp.concatenate([even, odd], axis=1).astype(BF)
        elif owner < 32:
            block = outs[32 * (owner - 24) : 32 * (owner - 23), :].astype(BF)
        else:
            block = early[owner - 32]
        pieces[owner % 12 // 3, owner // 12 * 3 + owner % 3] = block


def final_kernel(first, second, third, fourth, mid, block_input, grad_input):
    total = (first[...].astype(F32) + second[...].astype(F32)) + (
        third[...].astype(F32) + fourth[...].astype(F32)
    )
    normed, factor = normalize(block_input[...])
    grad_input[...] = (mid[...] + norm_back(normed, factor, total)).astype(BF)


def exchange(pieces, axis):
    received = lax.all_to_all(pieces, axis, 0, 0)
    return jnp.sum(received.astype(F32), axis=0)


def routes(step, back):
    pairs = []
    for win in range(96):
        for chip in range(4):
            for core in range(2):
                goal = (chip + step) % 4
                far = core == 0 and (goal if back else chip) == 0
                if step == 0 and not far:
                    continue
                other = (win + ((1 if back else -1) if far else 0)) % 96
                pairs.append((win * 8 + chip * 2 + core, other * 8 + goal * 2 + core))
    return pairs


def send(value, step, back):
    return lax.ppermute(value, WIN_AXES + HEAD_AXES, routes(step, back))


def shards(block_input, stream, grad_out, regions, qkv_weight, out_weight, up_weight, down_weight):
    rows, width = block_input.shape
    windows = rows // WIN
    head_count = lax.axis_size(HEAD_AXES)
    share_rows = rows // head_count
    share_start = lax.axis_index(HEAD_AXES) * share_rows
    chip, core = lax.axis_index("zl"), lax.axis_index("core")
    at_start = (chip == 0) & (core == 0)
    columns = qkv_weight.shape[2]
    units = up_weight.shape[1]

    def share(values):
        return lax.dynamic_slice_in_dim(values, share_start, share_rows, 0)

    count = lax.axis_size(WIN_AXES)
    far_input = lax.ppermute(
        block_input[:HALF], WIN_AXES, [((i + 1) % count, i) for i in range(count)]
    )
    unit_grad, unit, act, pre_grad = call(
        mlp_kernel,
        [((head_count, share_rows, width), BF), ((rows, width), BF)] + [((rows, units), BF)] * 2,
        (stream, grad_out, up_weight, down_weight),
    )
    parts = lax.all_to_all(unit_grad, HEAD_AXES, 0, 0)
    labels = regions.reshape(windows, WIN)
    per_window = (windows, WIN, columns)
    shifted_in, query, key, value, probs, attended, early, late = call(
        forward_kernel,
        [
            ((windows, WIN, width), BF),
            (per_window, BF),
            (per_window, BF),
            (per_window, BF),
            ((windows, WIN, WIN), F32),
            (per_window, BF),
            ((4,) + BLOCK, BF),
            ((4, 15) + BLOCK, BF),
        ],
        (
            block_input, far_input, labels[:, :, None], labels[:, None, :], qkv_weight,
            unit, act, pre_grad, grad_out,
        ),
        scratch=[pltpu.VMEM((64 * 32, 128), F32)],
    )
    mid, grad_mid = call(
        middle_kernel,
        [((share_rows, width), F32), ((share_rows, width), BF)],
        (parts, share(stream), share(grad_out)),
    )
    late_sum = exchange(late, "x")
    arrived = [send(grad_mid, step, False) for step in range(4)]
    mine = jnp.stack([jnp.where(at_start, arrived[0], grad_mid)] + arrived[:0:-1])
    theirs = lax.ppermute(mine, "core", [(0, 1), (1, 0)])
    keep, give, pieces = call(
        backward_kernel,
        [((4, HALF, width), BF), ((4, HALF, width), BF), ((4, 9) + BLOCK, BF)],
        (
            jnp.stack([chip, core]).astype(jnp.int32), mine, theirs, shifted_in, query, key, value,
            probs, attended, qkv_weight, out_weight, early,
        ),
        scratch=[pltpu.VMEM((3, width, columns), F32), pltpu.VMEM((8 * 32, 128), F32)],
        scalars=1,
    )
    early_sum = exchange(pieces, "x")
    received = lax.ppermute(give, "core", [(0, 1), (1, 0)])
    pair = [(keep[k].astype(F32) + received[k].astype(F32)).astype(BF) for k in range(4)]
    back = [send(pair[step], step, True) for step in range(4)]
    (grad_input,) = call(
        final_kernel,
        [((share_rows, width), BF)],
        (jnp.where(at_start, back[0], pair[0]), *back[1:], mid, share(block_input)),
    )
    partial_sum = jnp.concatenate([early_sum, late_sum], 0).astype(BF)
    owned = exchange(partial_sum, ("y", "zh"))
    return (grad_input, owned.reshape(1, -1))


def solution(mesh):
    fine = Mesh(mesh.devices.reshape(8, 4, 3, 4, 2), WIN_AXES + HEAD_AXES)
    return jax.shard_map(
        shards,
        mesh=fine,
        in_specs=(
            P(WIN_AXES, None),
            P(WIN_AXES, None),
            P(WIN_AXES, None),
            P(WIN_AXES),
            P(None, None, HEAD_AXES),
            P(HEAD_AXES, None),
            P(None, HEAD_AXES),
            P(HEAD_AXES, None),
        ),
        out_specs=(P(WIN_AXES + HEAD_AXES, None), P(HEAD_AXES, WIN_AXES)),
        check_vma=False,
    )
```

time: 154 us -> 138 us (0.90)
  the two profiles are of different devices: /device:TPU:1 before, /device:TPU:32 now
where the time goes in v2:
time: 138 us; the launch traced here: 137 us
  starting transfers between devices  82.5 us (60%)
  waiting for transfers between devices  23.9 us (17%)
  Pallas kernels  14.2 us (10%)
  local copies, waits for them, and re-layouts  11.9 us (9%)
  other arithmetic  3.6 us (3%)
    ppermute x8, starting transfers between devices, send(): return lax.ppermute(value, WIN_AXES + HEAD_AXES, routes(step, back))  39.5 us
    all_to_all x3, starting transfers between devices, exchange(): received = lax.all_to_all(pieces, axis, 0, 0)  17.7 us
    pallas_call x5, Pallas kernels, call(): pl.pallas_call(kernel, out_shape=[jax.ShapeDtypeStruct(shape, dtype) for...  14.2 us
    ppermute x1, starting transfers between devices, shards(): lax.ppermute(block_input[:HALF], WIN_AXES, [((i + 1) % count, i) for i in...  13.9 us
    ppermute x8, waiting for transfers between devices, send(): return lax.ppermute(value, WIN_AXES + HEAD_AXES, routes(step, back))  11.6 us
    unnamed x47, local copies, waits for them, and re-layouts  10.1 us
    all_to_all x1, starting transfers between devices, shards(): parts = lax.all_to_all(unit_grad, HEAD_AXES, 0, 0)  7.4 us
    all_to_all x1, waiting for transfers between devices, shards(): parts = lax.all_to_all(unit_grad, HEAD_AXES, 0, 0)  6.49 us
  transfers between devices with their start and end apart: 15, of which 7 were waited for; matrix products, arithmetic and copies ran while one was open for 4% of the time, Pallas kernels for 9%

profile of v2, /device:TPU:32, one launch (start us, length us, event | category | flops | bytes accessed | tf_op | source)
XLA Modules:
  0.0 137.0 jit_solution(6158409356355102034)
XLA Ops:
  0.6 1.1 copy-done
  1.7 1.1 copy-done.3
  2.8 0.9 copy-done.8
  3.7 0.9 copy-done.9
  4.7 2.4 %shard_map.95 = (bf16[8,72,512]{2,1,0:T(8,128)(2,1)}, bf16[576,512]{1,0:T(8,128)(2,1)S(1)}, bf16[576,256]{1,0:T(8,128)(2,1)S(1)}, bf16[576,256]{1,0:T(8,128)(2,1)S(1)}) custom-call(bf16[576,512]{1,0:T(8,128)(2,1)S(1)} %copy-done.3, bf16[576,512]{1,0:T(8,128)(2,1)S(1)} %copy-done, bf16[512,256]{1,0:T(8,128)(2,1)S(1)} %copy-done.8, bf16[256,512]{1,0:T(8,128)(2,1)S(1)} %copy-done.9), custom_call_target="tpu_custom_call" | custom-call | flops 100000000 | bytes 3407872 | tf_op jit(solution)/shard_map/pallas_call | solution.py:47
  7.8 7.4 %all-to-all-start = ((bf16[8,72,512]{2,1,0:T(8,128)(2,1)}), bf16[8,72,512]{2,1,0:T(8,128)(2,1)S(1)}, u32[]{:S(2)}, u32[]{:S(2)}) async-start(bf16[8,72,512]{2,1,0:T(8,128)(2,1)} %get-tuple-element.19), calls=%async_computation | async-start | bytes 1179648 | tf_op jit(solution)/shard_map/all_to_all | solution.py:253
  15.9 13.9 %collective-permute-start.5 = (bf16[72,512]{1,0:T(8,128)(2,1)}, bf16[72,512]{1,0:T(8,128)(2,1)S(1)}, u32[]{:S(2)}, u32[]{:S(2)}) collective-permute-start(bf16[72,512]{1,0:T(8,128)(2,1)} %get-tuple-element.37), channel_id=1, source_target_pairs={{8,0},{16,8},{24,16},{32,24},{40,32},{48,40},{56,48},{64,56},{72,6... | collective-permute-start | bytes 221192 | tf_op jit(solution)/shard_map/ppermute | solution.py:245
  30.7 6.5 %all-to-all-done.parts = bf16[8,72,512]{2,1,0:T(8,128)(2,1)S(1)} async-done(((bf16[8,72,512]{2,1,0:T(8,128)(2,1)}), bf16[8,72,512]{2,1,0:T(8,128)(2,1)S(1)}, u32[]{:S(2)}, u32[]{:S(2)}) %all-to-all-start) | async-done | bytes 589856 | tf_op jit(solution)/shard_map/all_to_all | solution.py:253
  37.2 0.9 shard_map.96
  38.8 14.1 %collective-permute-start = (bf16[72,512]{1,0:T(8,128)(2,1)}, bf16[72,512]{1,0:T(8,128)(2,1)}, u32[]{:S(2)}, u32[]{:S(2)}) collective-permute-start(bf16[72,512]{1,0:T(8,128)(2,1)} %get-tuple-element.20), channel_id=1, source_target_pairs={{0,760},{8,0},{16,8},{24,16},{32,24},{40,32},{48,40},{56,48},{64,5... | collective-permute-start | bytes 221192 | tf_op jit(solution)/shard_map/ppermute | solution.py:227
  53.4 1.0 copy-done.7
  54.4 4.0 %shard_map.97 = (bf16[4,144,512]{2,1,0:T(8,128)(2,1)S(1)}, bf16[4,144,64]{2,1,0:T(8,128)(2,1)S(1)}, bf16[4,144,64]{2,1,0:T(8,128)(2,1)S(1)}, bf16[4,144,64]{2,1,...) custom-call(bf16[576,512]{1,0:T(8,128)(2,1)S(1)} %copy-done.2, ...), custom_call_target="tpu_custom_call" | custom-call | flops 100000000 | bytes 5268480 | tf_op jit(solution)/shard_map/pallas_call | solution.py:47
  61.8 4.3 %all-to-all-start.2 = ((bf16[4,15,32,128]{3,2,1,0:T(8,128)(2,1)}), bf16[4,15,32,128]{3,2,1,0:T(8,128)(2,1)}, u32[]{:S(2)}, u32[]{:S(2)}) async-start(bf16[4,15,32,128]{3,2,1,0:T(8,128)(2,1)} %get-tuple-element.35), calls=%async_computation.2 | async-start | bytes 983040 | tf_op jit(solution)/shard_map/all_to_all | solution.py:208
  66.1 2.1 %collective-permute-start.3 = (bf16[72,512]{1,0:T(8,128)(2,1)}, bf16[72,512]{1,0:T(8,128)(2,1)S(1)}, u32[]{:S(2)}, u32[]{:S(2)}) collective-permute-start(bf16[72,512]{1,0:T(8,128)(2,1)} %get-tuple-element.20), channel_id=1, source_target_pairs={{0,762},{1,3},{2,4},{3,5},{4,6},{5,7},{6,0},{7,1},{8,2},{9,11},{10... | collective-permute-start | bytes 221192 | tf_op jit(solution)/shard_map/ppermute | solution.py:227
  68.2 1.9 %collective-permute-start.2 = (bf16[72,512]{1,0:T(8,128)(2,1)}, bf16[72,512]{1,0:T(8,128)(2,1)S(1)}, u32[]{:S(2)}, u32[]{:S(2)}) collective-permute-start(bf16[72,512]{1,0:T(8,128)(2,1)} %get-tuple-element.20), channel_id=1, source_target_pairs={{0,764},{1,5},{2,6},{3,7},{4,0},{5,1},{6,2},{7,3},{8,4},{9,13},{10... | collective-permute-start | bytes 221192 | tf_op jit(solution)/shard_map/ppermute | solution.py:227
  70.1 4.8 %collective-permute-start.1 = (bf16[72,512]{1,0:T(8,128)(2,1)}, bf16[72,512]{1,0:T(8,128)(2,1)S(1)}, u32[]{:S(2)}, u32[]{:S(2)}) collective-permute-start(bf16[72,512]{1,0:T(8,128)(2,1)} %get-tuple-element.20), channel_id=1, source_target_pairs={{0,766},{1,7},{2,0},{3,1},{4,2},{5,3},{6,4},{7,5},{8,6},{9,15},{10... | collective-permute-start | bytes 221192 | tf_op jit(solution)/shard_map/ppermute | solution.py:227
  75.8 3.1 %collective-permute-done.1 = bf16[72,512]{1,0:T(8,128)(2,1)S(1)} collective-permute-done((bf16[72,512]{1,0:T(8,128)(2,1)}, bf16[72,512]{1,0:T(8,128)(2,1)S(1)}, u32[]{:S(2)}, u32[]{:S(2)}) %collective-permute-start.1) | collective-permute-done | bytes 73760 | tf_op jit(solution)/shard_map/ppermute | solution.py:227
  78.9 2.1 %collective-permute-start.4 = (bf16[4,72,512]{2,1,0:T(8,128)(2,1)S(1)}, bf16[4,72,512]{2,1,0:T(8,128)(2,1)S(1)}, u32[]{:S(2)}, u32[]{:S(2)}) collective-permute-start(bf16[4,72,512]{2,1,0:T(8,128)(2,1)S(1)} %pad_maximum_fusion.mine), channel_id=1, source_target_pairs={{0,1},{1,0},{2,3},{3,2},{4,5},{5,4},{6,7},{7,6},{8,9},{9,8},{10,11... | collective-permute-start | bytes 884744 | tf_op jit(solution)/shard_map/ppermute | solution.py:282
  81.1 1.5 %collective-permute-done.4.theirs = bf16[4,72,512]{2,1,0:T(8,128)(2,1)S(1)} collective-permute-done((bf16[4,72,512]{2,1,0:T(8,128)(2,1)S(1)}, bf16[4,72,512]{2,1,0:T(8,128)(2,1)S(1)}, u32[]{:S(2)}, u32[]{:S(2)}) %collective-permute-start.4) | collective-permute-done | bytes 294944 | tf_op jit(solution)/shard_map/ppermute | solution.py:282
  82.6 6.0 %shard_map.98 = (bf16[4,72,512]{2,1,0:T(8,128)(2,1)S(1)}, bf16[4,72,512]{2,1,0:T(8,128)(2,1)S(1)}, bf16[4,9,32,128]{3,2,1,0:T(8,128)(2,1)}) custom-call(s32[2]{0:T(128)S(1)} %pad_add_fusion.place, bf16[4,72,512]{2,1,0:T(8,128)(2,1)S(1)} %pad_maximum_fusion.mine, bf16[4,72,512]{2,1,0:T(8,128)(2,1)S(1)} %collective-permute-done.4.theirs, ...), custom_call_target="tpu_custom_call" | custom-call | flops 100000000 | bytes 4202512 | tf_op jit(solution)/shard_map/pallas_call | solution.py:47
  88.6 4.7 %all-to-all-start.1 = ((bf16[4,9,32,128]{3,2,1,0:T(8,128)(2,1)}), bf16[4,9,32,128]{3,2,1,0:T(8,128)(2,1)S(1)}, u32[]{:S(2)}, u32[]{:S(2)}) async-start(bf16[4,9,32,128]{3,2,1,0:T(8,128)(2,1)} %get-tuple-element.34), calls=%async_computation.1 | async-start | bytes 589824 | tf_op jit(solution)/shard_map/all_to_all | solution.py:208
  93.3 1.9 %collective-permute-start.6 = (bf16[4,72,512]{2,1,0:T(8,128)(2,1)S(1)}, bf16[4,72,512]{2,1,0:T(8,128)(2,1)S(1)}, u32[]{:S(2)}, u32[]{:S(2)}) collective-permute-start(bf16[4,72,512]{2,1,0:T(8,128)(2,1)S(1)} %get-tuple-element.32), channel_id=1, source_target_pairs={{0,1},{1,0},{2,3},{3,2},{4,5},{5,4},{6,7},{7,6},{8,9},{9,8},{10,11... | collective-permute-start | bytes 884744 | tf_op jit(solution)/shard_map/ppermute | solution.py:294
  95.2 1.1 reduce.1
  96.3 4.3 %all-to-all-done.1 = bf16[4,9,32,128]{3,2,1,0:T(8,128)(2,1)S(1)} async-done(((bf16[4,9,32,128]{3,2,1,0:T(8,128)(2,1)}), bf16[4,9,32,128]{3,2,1,0:T(8,128)(2,1)S(1)}, u32[]{:S(2)}, u32[]{:S(2)}) %all-to-all-start.1) | async-done | bytes 294944 | tf_op jit(solution)/shard_map/all_to_all | solution.py:208
  101.3 8.7 %all-to-all-start.3 = ((bf16[24,32,128]{2,1,0:T(8,128)(2,1)}), bf16[24,32,128]{2,1,0:T(8,128)(2,1)S(1)}, u32[]{:S(2)}, u32[]{:S(2)}) async-start(bf16[24,32,128]{2,1,0:T(8,128)(2,1)} %pad_maximum_fusion.1), calls=%async_computation.3 | async-start | bytes 393216 | tf_op jit(solution)/shard_map/all_to_all | solution.py:208
  110.2 7.4 %collective-permute-start.7 = (bf16[72,512]{1,0:T(8,128)(2,1)S(1)}, bf16[72,512]{1,0:T(8,128)(2,1)S(1)}, u32[]{:S(2)}, u32[]{:S(2)}) collective-permute-start(bf16[72,512]{1,0:T(8,128)(2,1)S(1)} %get-tuple-element.41), channel_id=1, source_target_pairs={{0,8},{8,16},{16,24},{24,32},{32,40},{40,48},{48,56},{56,64},{64,7... | collective-permute-start | bytes 221192 | tf_op jit(solution)/shard_map/ppermute | solution.py:227
  117.6 1.9 %collective-permute-start.10 = (bf16[72,512]{1,0:T(8,128)(2,1)S(1)}, bf16[72,512]{1,0:T(8,128)(2,1)S(1)}, u32[]{:S(2)}, u32[]{:S(2)}) collective-permute-start(bf16[72,512]{1,0:T(8,128)(2,1)S(1)} %get-tuple-element.38), channel_id=1, source_target_pairs={{0,6},{1,7},{2,8},{3,1},{4,2},{5,3},{6,4},{7,5},{8,14},{9,15},{10,... | collective-permute-start | bytes 221192 | tf_op jit(solution)/shard_map/ppermute | solution.py:227
  119.5 1.9 %collective-permute-start.9 = (bf16[72,512]{1,0:T(8,128)(2,1)S(1)}, bf16[72,512]{1,0:T(8,128)(2,1)S(1)}, u32[]{:S(2)}, u32[]{:S(2)}) collective-permute-start(bf16[72,512]{1,0:T(8,128)(2,1)S(1)} %get-tuple-element.39), channel_id=1, source_target_pairs={{0,4},{1,5},{2,6},{3,7},{4,8},{5,1},{6,2},{7,3},{8,12},{9,13},{10,... | collective-permute-start | bytes 221192 | tf_op jit(solution)/shard_map/ppermute | solution.py:227
  121.4 5.4 %collective-permute-start.8 = (bf16[72,512]{1,0:T(8,128)(2,1)S(1)}, bf16[72,512]{1,0:T(8,128)(2,1)S(1)}, u32[]{:S(2)}, u32[]{:S(2)}) collective-permute-start(bf16[72,512]{1,0:T(8,128)(2,1)S(1)} %get-tuple-element.40), channel_id=1, source_target_pairs={{0,2},{1,3},{2,4},{3,5},{4,6},{5,7},{6,8},{7,1},{8,10},{9,11},{10,... | collective-permute-start | bytes 221192 | tf_op jit(solution)/shard_map/ppermute | solution.py:227
  126.9 4.1 %collective-permute-done.10.fourth = bf16[72,512]{1,0:T(8,128)(2,1)S(1)} collective-permute-done((bf16[72,512]{1,0:T(8,128)(2,1)S(1)}, bf16[72,512]{1,0:T(8,128)(2,1)S(1)}, u32[]{:S(2)}, u32[]{:S(2)}) %collective-permute-start.10) | collective-permute-done | bytes 73760 | tf_op jit(solution)/shard_map/ppermute | solution.py:227
  131.0 1.0 collective-permute-done.9.third
  132.1 3.4 %collective-permute-done.8.second = bf16[72,512]{1,0:T(8,128)(2,1)S(1)} collective-permute-done((bf16[72,512]{1,0:T(8,128)(2,1)S(1)}, bf16[72,512]{1,0:T(8,128)(2,1)S(1)}, u32[]{:S(2)}, u32[]{:S(2)}) %collective-permute-start.8) | collective-permute-done | bytes 73760 | tf_op jit(solution)/shard_map/ppermute | solution.py:227
  (64 shorter events, 10.4 us)
Async XLA Ops:
  0.6 1.1 copy-start
  1.7 1.1 copy-start.3
  2.8 0.9 copy-start.8
  3.7 0.9 copy-start.9
  7.8 7.4 %copy-start.2 = (bf16[576,512]{1,0:T(8,128)(2,1)S(1)}, bf16[576,512]{1,0:T(8,128)(2,1)}, u32[]{:S(2)}) copy-start(bf16[576,512]{1,0:T(8,128)(2,1)} %block_input.1) | copy-start | bytes 1769476
  7.8 22.9 %copy-start.1 = (bf16[576,512]{1,0:T(8,128)(2,1)S(1)}, bf16[576,512]{1,0:T(8,128)(2,1)}, u32[]{:S(2)}) copy-start(bf16[576,512]{1,0:T(8,128)(2,1)} %grad_out.3) | copy-start | bytes 1769476
  7.8 29.4 %all-to-all-start = ((bf16[8,72,512]{2,1,0:T(8,128)(2,1)}), bf16[8,72,512]{2,1,0:T(8,128)(2,1)S(1)}, u32[]{:S(2)}, u32[]{:S(2)}) async-start(bf16[8,72,512]{2,1,0:T(8,128)(2,1)} %get-tuple-element.19), calls=%async_computation | async-start | bytes 1179648 | tf_op jit(solution)/shard_map/all_to_all | solution.py:253
  15.9 37.5 %collective-permute-start.5 = (bf16[72,512]{1,0:T(8,128)(2,1)}, bf16[72,512]{1,0:T(8,128)(2,1)S(1)}, u32[]{:S(2)}, u32[]{:S(2)}) collective-permute-start(bf16[72,512]{1,0:T(8,128)(2,1)} %get-tuple-element.37), channel_id=1, source_target_pairs={{8,0},{16,8},{24,16},{32,24},{40,32},{48,40},{56,48},{64,56},{72,6... | collective-permute-start | bytes 221192 | tf_op jit(solution)/shard_map/ppermute | solution.py:245
  37.2 15.7 %copy-start.22 = (s32[576]{0:T(1024)S(1)}, s32[576]{0:T(1024)}, u32[]{:S(2)}) copy-start(s32[576]{0:T(1024)} %param.11) | copy-start | bytes 6916
  38.8 14.4 %copy-start.21 = (bf16[3,512,64]{1,2,0:T(8,128)(2,1)S(1)}, bf16[3,512,64]{1,2,0:T(8,128)(2,1)}, u32[]{:S(2)}) copy-start(bf16[3,512,64]{1,2,0:T(8,128)(2,1)} %param.12) | copy-start | bytes 589828
  38.8 36.1 %collective-permute-start = (bf16[72,512]{1,0:T(8,128)(2,1)}, bf16[72,512]{1,0:T(8,128)(2,1)}, u32[]{:S(2)}, u32[]{:S(2)}) collective-permute-start(bf16[72,512]{1,0:T(8,128)(2,1)} %get-tuple-element.20), channel_id=1, source_target_pairs={{0,760},{8,0},{16,8},{24,16},{32,24},{40,32},{48,40},{56,48},{64,5... | collective-permute-start | bytes 221192 | tf_op jit(solution)/shard_map/ppermute | solution.py:227
  53.4 1.0 copy-start.7
  58.4 0.8 copy-start.4
  61.8 20.7 %copy-start.13 = (bf16[4,144,64]{2,1,0:T(8,128)(2,1)S(1)}, bf16[4,144,64]{2,1,0:T(8,128)(2,1)}, u32[]{:S(2)}) copy-start(bf16[4,144,64]{2,1,0:T(8,128)(2,1)} %copy-done.12) | copy-start | bytes 221188
  61.8 20.7 %copy-start.15 = (bf16[4,144,64]{2,1,0:T(8,128)(2,1)S(1)}, bf16[4,144,64]{2,1,0:T(8,128)(2,1)}, u32[]{:S(2)}) copy-start(bf16[4,144,64]{2,1,0:T(8,128)(2,1)} %copy-done.14) | copy-start | bytes 221188
  61.8 20.7 %copy-start.17 = (bf16[4,144,64]{2,1,0:T(8,128)(2,1)S(1)}, bf16[4,144,64]{2,1,0:T(8,128)(2,1)}, u32[]{:S(2)}) copy-start(bf16[4,144,64]{2,1,0:T(8,128)(2,1)} %copy-done.16) | copy-start | bytes 221188
  61.8 26.7 %all-to-all-start.2 = ((bf16[4,15,32,128]{3,2,1,0:T(8,128)(2,1)}), bf16[4,15,32,128]{3,2,1,0:T(8,128)(2,1)}, u32[]{:S(2)}, u32[]{:S(2)}) async-start(bf16[4,15,32,128]{3,2,1,0:T(8,128)(2,1)} %get-tuple-element.35), calls=%async_computation.2 | async-start | bytes 983040 | tf_op jit(solution)/shard_map/all_to_all | solution.py:208
  66.1 16.5 %copy-start.5 = (f32[4,144,144]{2,1,0:T(8,128)S(1)}, f32[4,144,144]{2,1,0:T(8,128)}, u32[]{:S(2)}) copy-start(f32[4,144,144]{2,1,0:T(8,128)} %copy-done.4) | copy-start | bytes 995332
  66.1 9.7 %collective-permute-start.3 = (bf16[72,512]{1,0:T(8,128)(2,1)}, bf16[72,512]{1,0:T(8,128)(2,1)S(1)}, u32[]{:S(2)}, u32[]{:S(2)}) collective-permute-start(bf16[72,512]{1,0:T(8,128)(2,1)} %get-tuple-element.20), channel_id=1, source_target_pairs={{0,762},{1,3},{2,4},{3,5},{4,6},{5,7},{6,0},{7,1},{8,2},{9,11},{10... | collective-permute-start | bytes 221192 | tf_op jit(solution)/shard_map/ppermute | solution.py:227
  68.2 7.7 %collective-permute-start.2 = (bf16[72,512]{1,0:T(8,128)(2,1)}, bf16[72,512]{1,0:T(8,128)(2,1)S(1)}, u32[]{:S(2)}, u32[]{:S(2)}) collective-permute-start(bf16[72,512]{1,0:T(8,128)(2,1)} %get-tuple-element.20), channel_id=1, source_target_pairs={{0,764},{1,5},{2,6},{3,7},{4,0},{5,1},{6,2},{7,3},{8,4},{9,13},{10... | collective-permute-start | bytes 221192 | tf_op jit(solution)/shard_map/ppermute | solution.py:227
  70.1 8.8 %collective-permute-start.1 = (bf16[72,512]{1,0:T(8,128)(2,1)}, bf16[72,512]{1,0:T(8,128)(2,1)S(1)}, u32[]{:S(2)}, u32[]{:S(2)}) collective-permute-start(bf16[72,512]{1,0:T(8,128)(2,1)} %get-tuple-element.20), channel_id=1, source_target_pairs={{0,766},{1,7},{2,0},{3,1},{4,2},{5,3},{6,4},{7,5},{8,6},{9,15},{10... | collective-permute-start | bytes 221192 | tf_op jit(solution)/shard_map/ppermute | solution.py:227
  78.9 3.7 %copy-start.11 = (bf16[4,144,64]{2,1,0:T(8,128)(2,1)S(1)}, bf16[4,144,64]{2,1,0:T(8,128)(2,1)}, u32[]{:S(2)}) copy-start(bf16[4,144,64]{2,1,0:T(8,128)(2,1)} %copy-done.10) | copy-start | bytes 221188
  78.9 3.7 %copy-start.20 = (bf16[64,512]{1,0:T(8,128)(2,1)S(1)}, bf16[64,512]{1,0:T(8,128)(2,1)}, u32[]{:S(2)}) copy-start(bf16[64,512]{1,0:T(8,128)(2,1)} %out_weight.1) | copy-start | bytes 196612
  78.9 3.6 %collective-permute-start.4 = (bf16[4,72,512]{2,1,0:T(8,128)(2,1)S(1)}, bf16[4,72,512]{2,1,0:T(8,128)(2,1)S(1)}, u32[]{:S(2)}, u32[]{:S(2)}) collective-permute-start(bf16[4,72,512]{2,1,0:T(8,128)(2,1)S(1)} %pad_maximum_fusion.mine), channel_id=1, source_target_pairs={{0,1},{1,0},{2,3},{3,2},{4,5},{5,4},{6,7},{7,6},{8,9},{9,8},{10,11... | collective-permute-start | bytes 884744 | tf_op jit(solution)/shard_map/ppermute | solution.py:282
  88.6 12.0 %all-to-all-start.1 = ((bf16[4,9,32,128]{3,2,1,0:T(8,128)(2,1)}), bf16[4,9,32,128]{3,2,1,0:T(8,128)(2,1)S(1)}, u32[]{:S(2)}, u32[]{:S(2)}) async-start(bf16[4,9,32,128]{3,2,1,0:T(8,128)(2,1)} %get-tuple-element.34), calls=%async_computation.1 | async-start | bytes 589824 | tf_op jit(solution)/shard_map/all_to_all | solution.py:208
  93.3 16.8 %collective-permute-start.6 = (bf16[4,72,512]{2,1,0:T(8,128)(2,1)S(1)}, bf16[4,72,512]{2,1,0:T(8,128)(2,1)S(1)}, u32[]{:S(2)}, u32[]{:S(2)}) collective-permute-start(bf16[4,72,512]{2,1,0:T(8,128)(2,1)S(1)} %get-tuple-element.32), channel_id=1, source_target_pairs={{0,1},{1,0},{2,3},{3,2},{4,5},{5,4},{6,7},{7,6},{8,9},{9,8},{10,11... | collective-permute-start | bytes 884744 | tf_op jit(solution)/shard_map/ppermute | solution.py:294
  101.3 35.0 %all-to-all-start.3 = ((bf16[24,32,128]{2,1,0:T(8,128)(2,1)}), bf16[24,32,128]{2,1,0:T(8,128)(2,1)S(1)}, u32[]{:S(2)}, u32[]{:S(2)}) async-start(bf16[24,32,128]{2,1,0:T(8,128)(2,1)} %pad_maximum_fusion.1), calls=%async_computation.3 | async-start | bytes 393216 | tf_op jit(solution)/shard_map/all_to_all | solution.py:208
  110.1 25.3 %copy-start.19 = (f32[72,512]{1,0:T(8,128)S(1)}, f32[72,512]{1,0:T(8,128)}, u32[]{:S(2)}) copy-start(f32[72,512]{1,0:T(8,128)} %copy-done.18) | copy-start | bytes 442372
  110.2 16.7 %collective-permute-start.7 = (bf16[72,512]{1,0:T(8,128)(2,1)S(1)}, bf16[72,512]{1,0:T(8,128)(2,1)S(1)}, u32[]{:S(2)}, u32[]{:S(2)}) collective-permute-start(bf16[72,512]{1,0:T(8,128)(2,1)S(1)} %get-tuple-element.41), channel_id=1, source_target_pairs={{0,8},{8,16},{16,24},{24,32},{32,40},{40,48},{48,56},{56,64},{64,7... | collective-permute-start | bytes 221192 | tf_op jit(solution)/shard_map/ppermute | solution.py:227
  117.6 13.5 %collective-permute-start.10 = (bf16[72,512]{1,0:T(8,128)(2,1)S(1)}, bf16[72,512]{1,0:T(8,128)(2,1)S(1)}, u32[]{:S(2)}, u32[]{:S(2)}) collective-permute-start(bf16[72,512]{1,0:T(8,128)(2,1)S(1)} %get-tuple-element.38), channel_id=1, source_target_pairs={{0,6},{1,7},{2,8},{3,1},{4,2},{5,3},{6,4},{7,5},{8,14},{9,15},{10,... | collective-permute-start | bytes 221192 | tf_op jit(solution)/shard_map/ppermute | solution.py:227
  119.5 12.6 %collective-permute-start.9 = (bf16[72,512]{1,0:T(8,128)(2,1)S(1)}, bf16[72,512]{1,0:T(8,128)(2,1)S(1)}, u32[]{:S(2)}, u32[]{:S(2)}) collective-permute-start(bf16[72,512]{1,0:T(8,128)(2,1)S(1)} %get-tuple-element.39), channel_id=1, source_target_pairs={{0,4},{1,5},{2,6},{3,7},{4,8},{5,1},{6,2},{7,3},{8,12},{9,13},{10,... | collective-permute-start | bytes 221192 | tf_op jit(solution)/shard_map/ppermute | solution.py:227
  121.4 14.0 %collective-permute-start.8 = (bf16[72,512]{1,0:T(8,128)(2,1)S(1)}, bf16[72,512]{1,0:T(8,128)(2,1)S(1)}, u32[]{:S(2)}, u32[]{:S(2)}) collective-permute-start(bf16[72,512]{1,0:T(8,128)(2,1)S(1)} %get-tuple-element.40), channel_id=1, source_target_pairs={{0,2},{1,3},{2,4},{3,5},{4,6},{5,7},{6,8},{7,1},{8,10},{9,11},{10,... | collective-permute-start | bytes 221192 | tf_op jit(solution)/shard_map/ppermute | solution.py:227
  (6 other events, 4.0 us)

commit v3 on v2

v3 whole, which is shorter than its diff:
```python
import jax
import jax.numpy as jnp
from jax import lax
from jax.experimental import pallas as pl
from jax.experimental.pallas import tpu as pltpu
from jax.sharding import Mesh, PartitionSpec as P

HS = 64
WIN = 144
HALF = 72
WIN_AXES = ("y", "x", "zh")
HEAD_AXES = ("zl", "core")
BLOCK = (32, 128)
EPSILON = 1e-05
BF = jnp.bfloat16
F32 = jnp.float32


def normalize(values):
    data_f = values.astype(F32)
    centred = data_f - jnp.mean(data_f, axis=-1, keepdims=True)
    factor = lax.rsqrt(jnp.mean(centred * centred, axis=-1, keepdims=True) + EPSILON)
    return (centred * factor, factor)


def norm_back(normed, factor, upper):
    inner = upper - jnp.mean(upper, axis=-1, keepdims=True)
    return factor * (inner - normed * jnp.mean(upper * normed, axis=-1, keepdims=True))


def dot(left, right):
    return lax.dot_general(left, right, (((1,), (0,)), ((), ())), preferred_element_type=F32)


def contract_rows(left, right):
    return lax.dot_general(left, right, (((0,), (0,)), ((), ())), preferred_element_type=F32)


def contract_cols(left, right):
    return lax.dot_general(left, right, (((1,), (1,)), ((), ())), preferred_element_type=F32)


def call(kernel, outs, args, scratch=(), flops=10**8, scalars=0, after=()):
    vmem = pl.BlockSpec(memory_space=pltpu.VMEM)
    smem = pl.BlockSpec(memory_space=pltpu.SMEM)
    size = sum(a.size * a.dtype.itemsize for a in args)
    return pl.pallas_call(
        kernel,
        out_shape=[jax.ShapeDtypeStruct(shape, dtype) for shape, dtype in outs],
        in_specs=[smem] * scalars
        + [vmem] * (len(args) - scalars)
        + [pl.BlockSpec(memory_space=pl.ANY)] * len(after),
        out_specs=[vmem] * len(outs),
        scratch_shapes=list(scratch),
        compiler_params=pltpu.CompilerParams(vmem_limit_bytes=40 * 2**20),
        cost_estimate=pl.CostEstimate(flops=flops, bytes_accessed=2 * size, transcendentals=0),
    )(*args, *after)


def mlp_kernel(stream, grad_out, up_weight, down_weight, unit_grad, unit_out, act_out, pre_out):
    unit = normalize(stream[...])[0].astype(BF)
    pre = dot(unit, up_weight[...])
    upper = contract_cols(grad_out[...], down_weight[...])
    scale = 0.7978845608028654
    square = pre * pre
    bent = jnp.tanh(scale * (pre + 0.044715 * (square * pre)))
    slope = 0.5 * (1.0 + bent) + 0.5 * pre * (1.0 - bent * bent) * (
        scale * (1.0 + 3 * 0.044715 * square)
    )
    pre_grad = (upper * slope).astype(BF)
    unit_out[...] = unit
    act_out[...] = (0.5 * pre * (1.0 + bent)).astype(BF)
    pre_out[...] = pre_grad
    grad = contract_cols(pre_grad, up_weight[...])
    unit_grad[0] = grad[:HALF].astype(BF)
    unit_grad[1] = grad[HALF:].astype(BF)


def mlp(stream, grad_out, up_weight, down_weight):
    rows, width = stream.shape
    units = up_weight.shape[1]
    whole = lambda array: pl.BlockSpec(array.shape, lambda i: (0, 0))
    part = lambda columns: pl.BlockSpec((WIN, columns), lambda i: (i, 0))
    return pl.pallas_call(
        mlp_kernel,
        grid=(rows // WIN,),
        out_shape=[
            jax.ShapeDtypeStruct((rows // HALF, HALF, width), BF),
            jax.ShapeDtypeStruct((rows, width), BF),
            jax.ShapeDtypeStruct((rows, units), BF),
            jax.ShapeDtypeStruct((rows, units), BF),
        ],
        in_specs=[part(width), part(width), whole(up_weight), whole(down_weight)],
        out_specs=[
            pl.BlockSpec((2, HALF, width), lambda i: (i, 0, 0)),
            part(width),
            part(units),
            part(units),
        ],
        compiler_params=pltpu.CompilerParams(vmem_limit_bytes=56 * 2**20),
        cost_estimate=pl.CostEstimate(
            flops=6 * rows * width * units, bytes_accessed=3 * 2**20, transcendentals=0
        ),
    )(stream, grad_out, up_weight, down_weight)


def forward_kernel(
    block_input, far_input, labels_col, labels_row, qkv_weight, out_weight, unit, act, pre_grad,
    grad_out,
    turned_in, query_out, key_out, turned_value, probs_out, turned_probs, turned_attended,
    turned_qkv, turned_out, ffn, rows_f32,
):
    near = normalize(block_input[...])[0]
    far = normalize(far_input[...])[0]
    windows = block_input.shape[0] // WIN
    for i in range(3):
        turned_qkv[HS * i : HS * i + HS, :] = qkv_weight[i].astype(F32).T.astype(BF)
    turned_out[...] = out_weight[...].astype(F32).T.astype(BF)
    for index in range(windows):
        start = HALF + WIN * index
        if index < windows - 1:
            piece = near[start : start + WIN]
        else:
            piece = jnp.concatenate([near[start:], far], axis=0)
        inputs = piece.astype(BF)
        turned_in[index] = piece.T.astype(BF)
        query, key, value = [dot(inputs, qkv_weight[i]) for i in range(3)]
        query, key = query.astype(BF), key.astype(BF)
        query_out[index] = query
        key_out[index] = key
        turned_value[index] = value.T.astype(BF)
        scores = contract_cols(query, key) * HS**-0.5
        kept = jnp.where(labels_col[index] == labels_row[index], scores, -jnp.inf)
        raised = jnp.exp(kept - jnp.max(kept, axis=-1, keepdims=True))
        probs = raised / jnp.sum(raised, axis=-1, keepdims=True)
        probs_out[index] = probs
        turned_probs[index] = probs.T.astype(BF)
        turned_attended[index] = dot(probs.astype(BF), value.astype(BF)).T.astype(BF)
    up_grad = contract_rows(unit[...], pre_grad[...])
    ups, wide = up_grad.shape[0], up_grad.shape[1] // 128
    for column in range(wide):
        rows_f32[pl.ds(column, ups, stride=wide), :] = up_grad[:, 128 * column : 128 * column + 128]
    down_grad = contract_rows(act[...], grad_out[...])
    downs, wide = down_grad.shape[0], down_grad.shape[1] // 128
    base = ups * up_grad.shape[1] // 128
    for column in range(wide):
        rows_f32[pl.ds(base + column, downs, stride=wide), :] = down_grad[
            :, 128 * column : 128 * column + 128
        ]
    for owner in range(32, 96):
        block = rows_f32[32 * (owner - 32) : 32 * (owner - 31), :].astype(BF)
        ffn[owner - 32] = block


def middle_kernel(parts, stream, grad_out, _, mid, grad_mid):
    summed = jnp.sum(parts[...].astype(F32), axis=0)
    normed, factor = normalize(stream[...])
    middle = grad_out[...].astype(F32) + norm_back(normed, factor, summed)
    mid[...] = middle
    grad_mid[...] = middle.astype(BF)


def window_back(
    upper, index, query, key, turned_value, probs_in, turned_probs, turned_attended, turned_in,
    turned_qkv, turned_out,
):
    probs = probs_in[index]
    attended_grad = dot(upper, turned_out[...]).astype(BF)
    out_grad = dot(turned_attended[index], upper)
    prob_grad = dot(attended_grad, turned_value[index])
    inner = prob_grad - jnp.sum(prob_grad * probs, axis=-1, keepdims=True)
    score_grad = (probs * inner * HS**-0.5).astype(BF)
    grads = jnp.concatenate(
        [
            dot(score_grad, key[index]),
            contract_rows(score_grad, query[index]),
            dot(turned_probs[index], attended_grad),
        ],
        axis=1,
    ).astype(BF)
    return dot(grads, turned_qkv[...]), dot(turned_in[index], grads), out_grad


def near_kernel(grad_mid, *refs):
    saved, (in_grad, qkv_total, out_total) = refs[:9], refs[9:]
    qkv_sum, out_sum = 0.0, 0.0
    grads = grad_mid[...].astype(F32)
    for index in range(grad_mid.shape[0] // WIN - 1):
        upper = grads[HALF + WIN * index : HALF + WIN * index + WIN].astype(BF)
        rows, qkv_grad, out_grad = window_back(upper, index, *saved)
        qkv_sum, out_sum = qkv_sum + qkv_grad, out_sum + out_grad
        in_grad[2 * index] = rows[:HALF].astype(BF)
        in_grad[2 * index + 1] = rows[HALF:].astype(BF)
    qkv_total[...] = qkv_sum
    out_total[...] = out_sum


def far_kernel(place, own, far, *refs):
    saved, (in_near, qkv_total, out_total, ffn) = refs[:9], refs[9:13]
    in_grad, first, second, third, fourth, grads, outs, pieces = refs[13:]
    upper = jnp.concatenate([own[...].astype(F32), far[...].astype(F32)], axis=0).astype(BF)
    rows, qkv_grad, out_grad = window_back(upper, saved[0].shape[0] - 1, *saved)
    count = in_grad.shape[0]
    in_grad[count - 1] = rows[:HALF].astype(BF)
    in_grad[0] = rows[HALF:].astype(BF)
    for chunk in range(count - 2):
        in_grad[chunk + 1] = in_near[chunk]
    qkv_grad = qkv_total[...] + qkv_grad
    out_grad = out_total[...] + out_grad
    for i in range(3):
        grads[i] = qkv_grad[:, HS * i : HS * i + HS]
    for column in range(out_grad.shape[1] // 128):
        outs[pl.ds(column, HS, stride=4), :] = out_grad[:, 128 * column : 128 * column + 128]
    slots = [lax.rem(x - place[0] + 4, 4) for x in range(4)]
    for owner in range(96):
        if owner < 24:
            kind, start = owner // 8, owner % 8 * 64
            even = grads[kind, pl.ds(start, 32, stride=2), :]
            odd = grads[kind, pl.ds(start + 1, 32, stride=2), :]
            block = jnp.concatenate([even, odd], axis=1).astype(BF)
        elif owner < 32:
            block = outs[32 * (owner - 24) : 32 * (owner - 23), :].astype(BF)
        else:
            block = ffn[owner - 32]
        pieces[slots[owner % 12 // 3], owner // 12 * 3 + owner % 3] = block
    for slot, out in enumerate((first, second, third, fourth)):
        out[...] = pieces[slot]


def sum_kernel(parts, total, total_b):
    total[...] = jnp.sum(parts[...].astype(F32), axis=0)
    total_b[...] = total[...].astype(BF)


def final_kernel(place, summed, arrived, mid, block_input, grad_input):
    total = jnp.where(place[0] == 0, arrived[...].astype(F32), summed[...])
    normed, factor = normalize(block_input[...])
    grad_input[...] = (mid[...] + norm_back(normed, factor, total)).astype(BF)


def exchange(pieces, axis):
    received = lax.all_to_all(pieces, axis, 0, 0)
    return jnp.sum(received.astype(F32), axis=0)


def shards(block_input, stream, grad_out, regions, qkv_weight, out_weight, up_weight, down_weight):
    rows, width = block_input.shape
    windows = rows // WIN
    head_count = lax.axis_size(HEAD_AXES)
    share_rows = rows // head_count
    head = lax.axis_index(HEAD_AXES)
    columns = qkv_weight.shape[2]
    count = lax.axis_size(WIN_AXES)

    def share(values):
        return lax.dynamic_slice_in_dim(values, head * share_rows, share_rows, 0)

    def from_next(values):
        return lax.ppermute(values, WIN_AXES, [((i + 1) % count, i) for i in range(count)])

    far_input = from_next(block_input[:HALF])
    unit_grad, unit, act, pre_grad = mlp(stream, grad_out, up_weight, down_weight)
    parts = lax.all_to_all(unit_grad, HEAD_AXES, 0, 0)
    labels = regions.reshape(windows, WIN)
    per_window = (windows, WIN, columns)
    turned_in, query, key, value, probs, turned_probs, attended, qkv_t, out_t, ffn = call(
        forward_kernel,
        [
            ((windows, width, WIN), BF),
            (per_window, BF),
            (per_window, BF),
            ((windows, columns, WIN), BF),
            ((windows, WIN, WIN), F32),
            ((windows, WIN, WIN), BF),
            ((windows, columns, WIN), BF),
            ((3 * columns, width), BF),
            ((width, columns), BF),
            ((64,) + BLOCK, BF),
        ],
        (
            block_input, far_input, labels[:, :, None], labels[:, None, :], qkv_weight, out_weight,
            unit, act, pre_grad, grad_out,
        ),
        scratch=[pltpu.VMEM((64 * 32, 128), F32)],
    )
    mid, own_grad_mid = call(
        middle_kernel,
        [((share_rows, width), F32), ((share_rows, width), BF)],
        (parts, share(stream), share(grad_out)),
        after=(query,),
    )
    grad_mid = lax.all_gather(own_grad_mid, HEAD_AXES, axis=0, tiled=True)
    far_grad = from_next(grad_mid[:HALF])
    saved = (query, key, value, probs, turned_probs, attended, turned_in, qkv_t, out_t)
    in_near, qkv_total, out_total = call(
        near_kernel,
        [((head_count - 2, HALF, width), BF), ((width, 3 * columns), F32), ((columns, width), F32)],
        (grad_mid, *saved),
    )
    in_grad, *pieces = call(
        far_kernel,
        [((head_count, HALF, width), BF)] + [((24,) + BLOCK, BF)] * 4,
        (
            lax.axis_index("x").astype(jnp.int32).reshape(1), grad_mid[rows - HALF :], far_grad,
            *saved, in_near, qkv_total, out_total, ffn,
        ),
        scratch=[
            pltpu.VMEM((3, width, columns), F32),
            pltpu.VMEM((8 * 32, 128), F32),
            pltpu.VMEM((4, 24) + BLOCK, BF),
        ],
        scalars=1,
    )
    in_parts = lax.all_to_all(in_grad, HEAD_AXES, 0, 0)
    moved = [
        lax.ppermute(pieces[k], "x", [(i, (i + k) % 4) for i in range(4)]) for k in range(1, 4)
    ]
    partial_sum = sum(piece.astype(F32) for piece in [pieces[0]] + moved).astype(BF)
    summed, summed_b = call(
        sum_kernel, [((share_rows, width), F32), ((share_rows, width), BF)], (in_parts,)
    )
    size = lax.axis_size(HEAD_AXES)
    arrived = lax.ppermute(
        summed_b,
        WIN_AXES + HEAD_AXES,
        [(i * size, (i + 1) % count * size) for i in range(count)],
    )
    owned = exchange(partial_sum, ("y", "zh"))
    (grad_input,) = call(
        final_kernel,
        [((share_rows, width), BF)],
        (head.astype(jnp.int32).reshape(1), summed, arrived, mid, share(block_input)),
        scalars=1,
    )
    return (grad_input, owned.reshape(1, -1))


def solution(mesh):
    fine = Mesh(mesh.devices.reshape(8, 4, 3, 4, 2), WIN_AXES + HEAD_AXES)
    return jax.shard_map(
        shards,
        mesh=fine,
        in_specs=(
            P(WIN_AXES, None),
            P(WIN_AXES, None),
            P(WIN_AXES, None),
            P(WIN_AXES),
            P(None, None, HEAD_AXES),
            P(HEAD_AXES, None),
            P(None, HEAD_AXES),
            P(HEAD_AXES, None),
        ),
        out_specs=(P(WIN_AXES + HEAD_AXES, None), P(HEAD_AXES, WIN_AXES)),
        check_vma=False,
    )
```

time: 138 us -> 141 us (1.022)
  the two profiles are of different devices: /device:TPU:32 before, /device:TPU:16 now
where the time goes in v3:
time: 141 us; the launch traced here: 140 us
  starting transfers between devices  59.1 us (42%)
  blocking collectives  25.5 us (18%)
  local copies, waits for them, and re-layouts  21.5 us (15%)
  waiting for transfers between devices  17.5 us (12%)
  Pallas kernels  14.3 us (10%)
  other arithmetic  1.41 us (1%)
    all_gather x1, blocking collectives, shards(): grad_mid = lax.all_gather(own_grad_mid, HEAD_AXES, axis=0, tiled=True)  25.5 us
    ppermute x2, starting transfers between devices, from_next(): lax.ppermute(values, WIN_AXES, [((i + 1) % count, i) for i in range(count)])  18.6 us
    unnamed x65, local copies, waits for them, and re-layouts  16 us
    all_to_all x1, starting transfers between devices, exchange(): received = lax.all_to_all(pieces, axis, 0, 0)  11.1 us
    ppermute x3, starting transfers between devices, shards(): lax.ppermute(pieces[k], 'x', [(i, (i + k) % 4) for i in range(4)])  10.4 us
    pallas_call x6, Pallas kernels, call(): pl.pallas_call(kernel, out_shape=[jax.ShapeDtypeStruct(shape, dtype) for...  9.47 us
    ppermute x1, starting transfers between devices, shards(): lax.ppermute(summed_b, WIN_AXES + HEAD_AXES, [(i * size, (i + 1) % count...  7.41 us
    all_to_all x1, starting transfers between devices, shards(): parts = lax.all_to_all(unit_grad, HEAD_AXES, 0, 0)  7.28 us
  transfers between devices with their start and end apart: 9, of which 5 were waited for; matrix products, arithmetic and copies ran while one was open for 5% of the time, Pallas kernels for 4%

profile of v3, /device:TPU:16, one launch (start us, length us, event | category | flops | bytes accessed | tf_op | source)
XLA Modules:
  0.0 140.2 jit_solution(16613337615845330534)
XLA Ops:
  0.6 4.8 %shard_map.95 = (bf16[8,72,512]{2,1,0:T(8,128)(2,1)}, bf16[576,512]{1,0:T(8,128)(2,1)}, bf16[576,256]{1,0:T(8,128)(2,1)}, bf16[576,256]{1,0:T(8,128)(2,1)}) custom-call(bf16[576,512]{1,0:T(8,128)(2,1)} %stream.1, bf16[576,512]{1,0:T(8,128)(2,1)} %grad_out.3, bf16[512,256]{1,0:T(8,128)(2,1)} %up_weight.1, bf16[256,512]{1,0:T(8,128)(2,1)} %down_weight.1), custom_call_target="tpu_custom_call" | custom-call | flops 452984832 | bytes 3145728 | tf_op jit(solution)/shard_map/pallas_call | solution.py:84
  5.4 7.3 %all-to-all-start = ((bf16[8,72,512]{2,1,0:T(8,128)(2,1)}), bf16[8,72,512]{2,1,0:T(8,128)(2,1)S(1)}, u32[]{:S(2)}, u32[]{:S(2)}) async-start(bf16[8,72,512]{2,1,0:T(8,128)(2,1)} %get-tuple-element.28), calls=%async_computation | async-start | bytes 1179648 | tf_op jit(solution)/shard_map/all_to_all | solution.py:263
  12.7 1.6 %constant_dynamic-slice_fusion = (bf16[72,512]{1,0:T(8,128)(2,1)}, bf16[72,512]{1,0:T(8,128)(2,1)S(1)}) fusion(bf16[576,512]{1,0:T(8,128)(2,1)} %block_input.1, s32[]{:T(128)S(6)} %select_n.2), kind=kLoop, calls=%fused_computation.2 | loop fusion | bytes 294916 | tf_op jit(solution)/shard_map/dynamic_slice | solution.py:256
  14.4 13.9 %collective-permute-start = (bf16[72,512]{1,0:T(8,128)(2,1)S(1)}, bf16[72,512]{1,0:T(8,128)(2,1)S(1)}, u32[]{:S(2)}, u32[]{:S(2)}) collective-permute-start(bf16[72,512]{1,0:T(8,128)(2,1)S(1)} %get-tuple-element.55), channel_id=1, source_target_pairs={{8,0},{16,8},{24,16},{32,24},{40,32},{48,40},{56,48},{64,56},{72,6... | collective-permute-start | bytes 221192 | tf_op jit(solution)/shard_map/ppermute | solution.py:259
  29.0 1.0 broadcast_in_dim_reshape.8.labels_col
  30.2 1.6 %constant_dynamic-slice_fusion.1 = (bf16[72,512]{1,0:T(8,128)(2,1)}, bf16[72,512]{1,0:T(8,128)(2,1)}) fusion(bf16[576,512]{1,0:T(8,128)(2,1)S(1)} %copy-done, s32[]{:T(128)S(6)} %select_n.2, bf16[576,512]{1,0:T(8,128)(2,1)} %stream.1), kind=kLoop, calls=%fused_computation.3 | loop fusion | bytes 294916 | tf_op jit(solution)/shard_map/dynamic_slice | solution.py:256
  32.5 1.1 copy-done.4
  33.6 1.1 copy-done.5
  34.6 1.0 copy-done.16
  35.6 1.0 copy-done.17
  38.3 3.1 %shard_map.96 = (bf16[4,512,144]{2,1,0:T(8,128)(2,1)S(1)}, bf16[4,144,64]{2,1,0:T(8,128)(2,1)S(1)}, bf16[4,144,64]{2,1,0:T(8,128)(2,1)S(1)}, bf16[4,64,144]{2,1,...) custom-call(bf16[576,512]{1,0:T(8,128)(2,1)S(1)} %copy-done.4, ...), custom_call_target="tpu_custom_call" | custom-call | flops 100000000 | bytes 5399552 | tf_op jit(solution)/shard_map/pallas_call | solution.py:47
  45.5 0.9 copy-done.19
  46.4 0.9 copy-done.20
  47.6 25.5 %all_gather.3.grad_mid = bf16[576,512]{1,0:T(8,128)(2,1)S(1)} all-gather(bf16[72,512]{1,0:T(8,128)(2,1)S(1)} %get-tuple-element.33), channel_id=1, replica_groups=mesh['y'=8,'x'=4,'zh'=3,'zl'=4,'core'=2] {'zl','core'}, dimensions={0}, use_global_device_ids=true | all-gather | bytes 663552 | tf_op jit(solution)/shard_map/all_gather | solution.py:292
  73.8 4.7 %collective-permute-start.1 = (bf16[72,512]{1,0:T(8,128)(2,1)S(1)}, bf16[72,512]{1,0:T(8,128)(2,1)}, u32[]{:S(2)}, u32[]{:S(2)}) collective-permute-start(bf16[72,512]{1,0:T(8,128)(2,1)S(1)} %get-tuple-element.56), channel_id=1, source_target_pairs={{8,0},{16,8},{24,16},{32,24},{40,32},{48,40},{56,48},{64,56},{72,6... | collective-permute-start | bytes 221192 | tf_op jit(solution)/shard_map/ppermute | solution.py:259
  78.5 0.9 copy-done.11
  79.4 0.9 copy-done.13
  80.3 0.9 copy-done.15
  81.2 2.3 %shard_map.98 = (bf16[6,72,512]{2,1,0:T(8,128)(2,1)S(1)}, f32[512,192]{1,0:T(8,128)S(1)}, f32[64,512]{1,0:T(8,128)S(1)}) custom-call(bf16[576,512]{1,0:T(8,128)(2,1)S(1)} %all_gather.3.grad_mid, bf16[4,144,64]{2,1,0:T(8,128)(2,1)S(1)} %get-tuple-element.32._.refs_0_, bf16[4,144,64]{2,1,0:T(8,128)(2,1)S(1)} %copy-done.7, bf16[4,64,144]{2,1,0:T(8,128)(2,1)S(1)} %copy-done.11, ...), custom_call_target="tpu_custom_call" | custom-call | flops 100000000 | bytes 4468736 | tf_op jit(solution)/shard_map/pallas_call | solution.py:47
  83.6 2.2 %collective-permute-done.1.far = bf16[72,512]{1,0:T(8,128)(2,1)} collective-permute-done((bf16[72,512]{1,0:T(8,128)(2,1)S(1)}, bf16[72,512]{1,0:T(8,128)(2,1)}, u32[]{:S(2)}, u32[]{:S(2)}) %collective-permute-start.1) | collective-permute-done | bytes 73760 | tf_op jit(solution)/shard_map/ppermute | solution.py:259
  85.8 2.8 %shard_map.99 = (bf16[8,72,512]{2,1,0:T(8,128)(2,1)}, bf16[24,32,128]{2,1,0:T(8,128)(2,1)S(1)}, bf16[24,32,128]{2,1,0:T(8,128)(2,1)S(1)}, bf16[24,32,128]{2,1,0:T(8,128)(2,1)S(1)}, bf16[24,32,128]{2,1,0:T(8,128)(2,1)S(1)}) custom-call(s32[1]{0:T(128)} %bitcast.1.place, bf16[72,512]{1,0:T(8,128)(2,1)S(1)} %copy-done.21, ...), custom_call_target="tpu_custom_call" | custom-call | flops 100000000 | bytes 6565896 | tf_op jit(solution)/shard_map/pallas_call | solution.py:47
  89.3 4.3 %all-to-all-start.1 = ((bf16[8,72,512]{2,1,0:T(8,128)(2,1)}), bf16[8,72,512]{2,1,0:T(8,128)(2,1)S(1)}, u32[]{:S(2)}, u32[]{:S(2)}) async-start(bf16[8,72,512]{2,1,0:T(8,128)(2,1)} %get-tuple-element.46), calls=%async_computation.1 | async-start | bytes 1179648 | tf_op jit(solution)/shard_map/all_to_all | solution.py:314
  93.6 2.4 %collective-permute-start.3 = (bf16[24,32,128]{2,1,0:T(8,128)(2,1)S(1)}, bf16[24,32,128]{2,1,0:T(8,128)(2,1)S(1)}, u32[]{:S(2)}, u32[]{:S(2)}) collective-permute-start(bf16[24,32,128]{2,1,0:T(8,128)(2,1)S(1)} %copy-done.29), channel_id=1, source_target_pairs={{0,24},{24,48},{48,72},{72,0},{1,25},{25,49},{49,73},{73,1},{2,26}... | collective-permute-start | bytes 589832 | tf_op jit(solution)/shard_map/ppermute | solution.py:316
  96.0 4.6 %collective-permute-start.4 = (bf16[24,32,128]{2,1,0:T(8,128)(2,1)S(1)}, bf16[24,32,128]{2,1,0:T(8,128)(2,1)S(1)}, u32[]{:S(2)}, u32[]{:S(2)}) collective-permute-start(bf16[24,32,128]{2,1,0:T(8,128)(2,1)S(1)} %get-tuple-element.52), channel_id=1, source_target_pairs={{0,48},{24,72},{48,0},{72,24},{1,49},{25,73},{49,1},{73,25},{2,50}... | collective-permute-start | bytes 589832 | tf_op jit(solution)/shard_map/ppermute | solution.py:316
  100.7 3.4 %collective-permute-start.5 = (bf16[24,32,128]{2,1,0:T(8,128)(2,1)S(1)}, bf16[24,32,128]{2,1,0:T(8,128)(2,1)S(1)}, u32[]{:S(2)}, u32[]{:S(2)}) collective-permute-start(bf16[24,32,128]{2,1,0:T(8,128)(2,1)S(1)} %get-tuple-element.53), channel_id=1, source_target_pairs={{0,72},{24,0},{48,24},{72,48},{1,73},{25,1},{49,25},{73,49},{2,74}... | collective-permute-start | bytes 589832 | tf_op jit(solution)/shard_map/ppermute | solution.py:316
  104.0 4.2 %collective-permute-done.3 = bf16[24,32,128]{2,1,0:T(8,128)(2,1)S(1)} collective-permute-done((bf16[24,32,128]{2,1,0:T(8,128)(2,1)S(1)}, bf16[24,32,128]{2,1,0:T(8,128)(2,1)S(1)}, u32[]{:S(2)}, u32[]{:S(2)}) %collective-permute-start.3) | collective-permute-done | bytes 196640 | tf_op jit(solution)/shard_map/ppermute | solution.py:316
  108.2 2.5 %collective-permute-done.5 = bf16[24,32,128]{2,1,0:T(8,128)(2,1)S(1)} collective-permute-done((bf16[24,32,128]{2,1,0:T(8,128)(2,1)S(1)}, bf16[24,32,128]{2,1,0:T(8,128)(2,1)S(1)}, u32[]{:S(2)}, u32[]{:S(2)}) %collective-permute-start.5) | collective-permute-done | bytes 196640 | tf_op jit(solution)/shard_map/ppermute | solution.py:316
  111.5 11.1 %all-to-all-start.2 = ((bf16[24,32,128]{2,1,0:T(8,128)(2,1)}), bf16[24,32,128]{2,1,0:T(8,128)(2,1)S(1)}, u32[]{:S(2)}, u32[]{:S(2)}) async-start(bf16[24,32,128]{2,1,0:T(8,128)(2,1)} %add_convert_fusion), calls=%async_computation.2 | async-start | bytes 393216 | tf_op jit(solution)/shard_map/all_to_all | solution.py:242
  122.7 7.4 %collective-permute-start.2 = (bf16[72,512]{1,0:T(8,128)(2,1)S(1)}, bf16[72,512]{1,0:T(8,128)(2,1)S(1)}, u32[]{:S(2)}, u32[]{:S(2)}) collective-permute-start(bf16[72,512]{1,0:T(8,128)(2,1)S(1)} %get-tuple-element.48), channel_id=1, source_target_pairs={{0,8},{8,16},{16,24},{24,32},{32,40},{40,48},{48,56},{56,64},{64,7... | collective-permute-start | bytes 221192 | tf_op jit(solution)/shard_map/ppermute | solution.py:323
  130.1 4.1 %all-to-all-done.2 = bf16[24,32,128]{2,1,0:T(8,128)(2,1)S(1)} async-done(((bf16[24,32,128]{2,1,0:T(8,128)(2,1)}), bf16[24,32,128]{2,1,0:T(8,128)(2,1)S(1)}, u32[]{:S(2)}, u32[]{:S(2)}) %all-to-all-start.2) | async-done | bytes 196640 | tf_op jit(solution)/shard_map/all_to_all | solution.py:242
  134.8 4.5 %collective-permute-done.2.arrived = bf16[72,512]{1,0:T(8,128)(2,1)S(1)} collective-permute-done((bf16[72,512]{1,0:T(8,128)(2,1)S(1)}, bf16[72,512]{1,0:T(8,128)(2,1)S(1)}, u32[]{:S(2)}, u32[]{:S(2)}) %collective-permute-start.2) | collective-permute-done | bytes 73760 | tf_op jit(solution)/shard_map/ppermute | solution.py:323
  139.3 0.9 shard_map.101
  (66 shorter events, 10.6 us)
Async XLA Ops:
  5.4 22.9 %copy-start.31 = (s32[576]{0:T(1024)S(1)}, s32[576]{0:T(1024)}, u32[]{:S(2)}) copy-start(s32[576]{0:T(1024)} %param.11) | copy-start | bytes 6916
  5.4 40.1 %all-to-all-start = ((bf16[8,72,512]{2,1,0:T(8,128)(2,1)}), bf16[8,72,512]{2,1,0:T(8,128)(2,1)S(1)}, u32[]{:S(2)}, u32[]{:S(2)}) async-start(bf16[8,72,512]{2,1,0:T(8,128)(2,1)} %get-tuple-element.28), calls=%async_computation | async-start | bytes 1179648 | tf_op jit(solution)/shard_map/all_to_all | solution.py:263
  12.7 17.2 %copy-start.30 = (bf16[3,512,64]{1,2,0:T(8,128)(2,1)S(1)}, bf16[3,512,64]{1,2,0:T(8,128)(2,1)}, u32[]{:S(2)}) copy-start(bf16[3,512,64]{1,2,0:T(8,128)(2,1)} %param.12) | copy-start | bytes 589828
  12.7 17.5 %copy-start = (bf16[576,512]{1,0:T(8,128)(2,1)S(1)}, bf16[576,512]{1,0:T(8,128)(2,1)}, u32[]{:S(2)}) copy-start(bf16[576,512]{1,0:T(8,128)(2,1)} %grad_out.3) | copy-start | bytes 1769476
  14.4 17.4 %collective-permute-start = (bf16[72,512]{1,0:T(8,128)(2,1)S(1)}, bf16[72,512]{1,0:T(8,128)(2,1)S(1)}, u32[]{:S(2)}, u32[]{:S(2)}) collective-permute-start(bf16[72,512]{1,0:T(8,128)(2,1)S(1)} %get-tuple-element.55), channel_id=1, source_target_pairs={{8,0},{16,8},{24,16},{32,24},{40,32},{48,40},{56,48},{64,56},{72,6... | collective-permute-start | bytes 221192 | tf_op jit(solution)/shard_map/ppermute | solution.py:259
  30.2 2.2 %copy-start.1 = (s32[4,144,1]{2,1,0:T(8,128)S(1)}, s32[4,144,1]{2,1,0:T(8,128)}, u32[]{:S(2)}) copy-start(s32[4,144,1]{2,1,0:T(8,128)} %broadcast_in_dim_reshape.8.labels_col) | copy-start | bytes 6916
  32.5 1.1 copy-start.4
  33.6 1.1 copy-start.5
  34.6 1.0 copy-start.16
  35.6 1.0 copy-start.17
  36.5 0.9 copy-start.25
  37.4 0.8 copy-start.26
  45.5 0.9 copy-start.19
  46.4 0.9 copy-start.20
  47.6 25.6 %copy-start.22 = (f32[72,512]{1,0:T(8,128)}, f32[72,512]{1,0:T(8,128)S(1)}, u32[]{:S(2)}) copy-start(f32[72,512]{1,0:T(8,128)S(1)} %get-tuple-element.49.mid) | copy-start | bytes 442372
  47.6 30.9 %copy-start.7 = (bf16[4,144,64]{2,1,0:T(8,128)(2,1)S(1)}, bf16[4,144,64]{2,1,0:T(8,128)(2,1)}, u32[]{:S(2)}) copy-start(bf16[4,144,64]{2,1,0:T(8,128)(2,1)} %copy-done.6) | copy-start | bytes 221188
  73.1 5.4 %copy-start.3 = (bf16[4,144,144]{2,1,0:T(8,128)(2,1)S(1)}, bf16[4,144,144]{2,1,0:T(8,128)(2,1)}, u32[]{:S(2)}) copy-start(bf16[4,144,144]{2,1,0:T(8,128)(2,1)} %copy-done.2) | copy-start | bytes 497668
  73.8 12.0 %collective-permute-start.1 = (bf16[72,512]{1,0:T(8,128)(2,1)S(1)}, bf16[72,512]{1,0:T(8,128)(2,1)}, u32[]{:S(2)}, u32[]{:S(2)}) collective-permute-start(bf16[72,512]{1,0:T(8,128)(2,1)S(1)} %get-tuple-element.56), channel_id=1, source_target_pairs={{8,0},{16,8},{24,16},{32,24},{40,32},{48,40},{56,48},{64,56},{72,6... | collective-permute-start | bytes 221192 | tf_op jit(solution)/shard_map/ppermute | solution.py:259
  78.5 0.9 copy-start.11
  79.4 0.9 copy-start.13
  80.3 0.9 copy-start.15
  81.2 4.6 %copy-start.9 = (bf16[64,32,128]{2,1,0:T(8,128)(2,1)S(1)}, bf16[64,32,128]{2,1,0:T(8,128)(2,1)}, u32[]{:S(2)}) copy-start(bf16[64,32,128]{2,1,0:T(8,128)(2,1)} %copy-done.8) | copy-start | bytes 1572868
  81.2 4.6 %copy-start.21 = (bf16[72,512]{1,0:T(8,128)(2,1)S(1)}, bf16[72,512]{1,0:T(8,128)(2,1)}, u32[]{:S(2)}) copy-start(bf16[72,512]{1,0:T(8,128)(2,1)} %get-tuple-element.57.own) | copy-start | bytes 221188
  89.3 4.3 %copy-start.29 = (bf16[24,32,128]{2,1,0:T(8,128)(2,1)S(1)}, bf16[24,32,128]{2,1,0:T(8,128)(2,1)}, u32[]{:S(2)}) copy-start(bf16[24,32,128]{2,1,0:T(8,128)(2,1)} %copy-done.28) | copy-start | bytes 589828
  89.3 22.2 %all-to-all-start.1 = ((bf16[8,72,512]{2,1,0:T(8,128)(2,1)}), bf16[8,72,512]{2,1,0:T(8,128)(2,1)S(1)}, u32[]{:S(2)}, u32[]{:S(2)}) async-start(bf16[8,72,512]{2,1,0:T(8,128)(2,1)} %get-tuple-element.46), calls=%async_computation.1 | async-start | bytes 1179648 | tf_op jit(solution)/shard_map/all_to_all | solution.py:314
  93.6 14.6 %collective-permute-start.3 = (bf16[24,32,128]{2,1,0:T(8,128)(2,1)S(1)}, bf16[24,32,128]{2,1,0:T(8,128)(2,1)S(1)}, u32[]{:S(2)}, u32[]{:S(2)}) collective-permute-start(bf16[24,32,128]{2,1,0:T(8,128)(2,1)S(1)} %copy-done.29), channel_id=1, source_target_pairs={{0,24},{24,48},{48,72},{72,0},{1,25},{25,49},{49,73},{73,1},{2,26}... | collective-permute-start | bytes 589832 | tf_op jit(solution)/shard_map/ppermute | solution.py:316
  96.0 12.2 %collective-permute-start.4 = (bf16[24,32,128]{2,1,0:T(8,128)(2,1)S(1)}, bf16[24,32,128]{2,1,0:T(8,128)(2,1)S(1)}, u32[]{:S(2)}, u32[]{:S(2)}) collective-permute-start(bf16[24,32,128]{2,1,0:T(8,128)(2,1)S(1)} %get-tuple-element.52), channel_id=1, source_target_pairs={{0,48},{24,72},{48,0},{72,24},{1,49},{25,73},{49,1},{73,25},{2,50}... | collective-permute-start | bytes 589832 | tf_op jit(solution)/shard_map/ppermute | solution.py:316
  100.7 10.0 %collective-permute-start.5 = (bf16[24,32,128]{2,1,0:T(8,128)(2,1)S(1)}, bf16[24,32,128]{2,1,0:T(8,128)(2,1)S(1)}, u32[]{:S(2)}, u32[]{:S(2)}) collective-permute-start(bf16[24,32,128]{2,1,0:T(8,128)(2,1)S(1)} %get-tuple-element.53), channel_id=1, source_target_pairs={{0,72},{24,0},{48,24},{72,48},{1,73},{25,1},{49,25},{73,49},{2,74}... | collective-permute-start | bytes 589832 | tf_op jit(solution)/shard_map/ppermute | solution.py:316
  111.5 22.7 %all-to-all-start.2 = ((bf16[24,32,128]{2,1,0:T(8,128)(2,1)}), bf16[24,32,128]{2,1,0:T(8,128)(2,1)S(1)}, u32[]{:S(2)}, u32[]{:S(2)}) async-start(bf16[24,32,128]{2,1,0:T(8,128)(2,1)} %add_convert_fusion), calls=%async_computation.2 | async-start | bytes 393216 | tf_op jit(solution)/shard_map/all_to_all | solution.py:242
  122.7 16.7 %copy-start.23 = (f32[72,512]{1,0:T(8,128)S(1)}, f32[72,512]{1,0:T(8,128)}, u32[]{:S(2)}) copy-start(f32[72,512]{1,0:T(8,128)} %copy-done.22) | copy-start | bytes 442372
  122.7 16.6 %copy-start.18 = (bf16[72,512]{1,0:T(8,128)(2,1)S(1)}, bf16[72,512]{1,0:T(8,128)(2,1)}, u32[]{:S(2)}) copy-start(bf16[72,512]{1,0:T(8,128)(2,1)} %get-tuple-element.54.block_input) | copy-start | bytes 221188
  122.7 16.6 %collective-permute-start.2 = (bf16[72,512]{1,0:T(8,128)(2,1)S(1)}, bf16[72,512]{1,0:T(8,128)(2,1)S(1)}, u32[]{:S(2)}, u32[]{:S(2)}) collective-permute-start(bf16[72,512]{1,0:T(8,128)(2,1)S(1)} %get-tuple-element.48), channel_id=1, source_target_pairs={{0,8},{8,16},{16,24},{24,32},{32,40},{40,48},{48,56},{56,64},{64,7... | collective-permute-start | bytes 221192 | tf_op jit(solution)/shard_map/ppermute | solution.py:323
  (9 other events, 6.1 us)

commit v4 on v3

v4 whole, which is shorter than its diff:
```python
import jax
import jax.numpy as jnp
from jax import lax
from jax.experimental import pallas as pl
from jax.experimental.pallas import tpu as pltpu
from jax.sharding import Mesh, PartitionSpec as P

HS = 64
WIN = 144
HALF = 72
WIN_AXES = ("y", "x", "zh")
HEAD_AXES = ("zl", "core")
BLOCK = (32, 128)
EPSILON = 1e-05
BF = jnp.bfloat16
F32 = jnp.float32


def normalize(values):
    data_f = values.astype(F32)
    centred = data_f - jnp.mean(data_f, axis=-1, keepdims=True)
    factor = lax.rsqrt(jnp.mean(centred * centred, axis=-1, keepdims=True) + EPSILON)
    return (centred * factor, factor)


def norm_back(normed, factor, upper):
    inner = upper - jnp.mean(upper, axis=-1, keepdims=True)
    return factor * (inner - normed * jnp.mean(upper * normed, axis=-1, keepdims=True))


def dot(left, right):
    return lax.dot_general(left, right, (((1,), (0,)), ((), ())), preferred_element_type=F32)


def contract_rows(left, right):
    return lax.dot_general(left, right, (((0,), (0,)), ((), ())), preferred_element_type=F32)


def contract_cols(left, right):
    return lax.dot_general(left, right, (((1,), (1,)), ((), ())), preferred_element_type=F32)


VMEM = pl.BlockSpec(memory_space=pltpu.VMEM)
SMEM = pl.BlockSpec(memory_space=pltpu.SMEM)
ANY = pl.BlockSpec(memory_space=pl.ANY)


def call(kernel, grid, ins, outs, args, scratch=(), chosen=None, flops=10**8):
    spec = pltpu.PrefetchScalarGridSpec(
        num_scalar_prefetch=0 if chosen is None else 1,
        grid=grid,
        in_specs=ins,
        out_specs=[out[2] for out in outs],
        scratch_shapes=list(scratch),
    )
    first = () if chosen is None else (chosen,)
    return pl.pallas_call(
        kernel,
        grid_spec=spec,
        out_shape=[jax.ShapeDtypeStruct(out[0], out[1]) for out in outs],
        compiler_params=pltpu.CompilerParams(vmem_limit_bytes=24 * 2**20),
        cost_estimate=pl.CostEstimate(flops=flops, bytes_accessed=2 * 2**20, transcendentals=0),
    )(*first, *args)


def whole(array):
    zeros = (0,) * len(array.shape)
    return pl.BlockSpec(array.shape, lambda *_: zeros)


def mlp_kernel(
    place, stream, grad_out, up_weight, down_weight, unit_grad, first, second, third, fourth, early,
    up_sum, down_sum, rows_f32, pieces,
):
    step = pl.program_id(0)
    unit = normalize(stream[...])[0].astype(BF)
    pre = dot(unit, up_weight[...])
    upper = contract_cols(grad_out[...], down_weight[...])
    scale = 0.7978845608028654
    square = pre * pre
    bent = jnp.tanh(scale * (pre + 0.044715 * (square * pre)))
    slope = 0.5 * (1.0 + bent) + 0.5 * pre * (1.0 - bent * bent) * (
        scale * (1.0 + 3 * 0.044715 * square)
    )
    pre_grad = (upper * slope).astype(BF)
    act = (0.5 * pre * (1.0 + bent)).astype(BF)
    grad = contract_cols(pre_grad, up_weight[...])
    unit_grad[0] = grad[:HALF].astype(BF)
    unit_grad[1] = grad[HALF:].astype(BF)
    up_part = contract_rows(unit, pre_grad)
    down_part = contract_rows(act, grad_out[...])

    @pl.when(step == 0)
    def _():
        up_sum[...] = up_part
        down_sum[...] = down_part

    @pl.when(step > 0)
    def _():
        up_sum[...] += up_part
        down_sum[...] += down_part

    @pl.when(step == pl.num_programs(0) - 1)
    def _():
        base = 0
        for total in (up_sum, down_sum):
            rows, wide = total.shape[0], total.shape[1] // 128
            for column in range(wide):
                rows_f32[pl.ds(base + column, rows, stride=wide), :] = total[
                    :, 128 * column : 128 * column + 128
                ]
            base += rows * wide
        slots = [lax.rem(x - place[0] + 4, 4) for x in range(4)]
        for owner in range(32, 96):
            block = rows_f32[32 * (owner - 32) : 32 * (owner - 31), :].astype(BF)
            if owner < 36:
                early[owner - 32] = block
            else:
                pieces[slots[owner % 12 // 3], owner // 12 * 3 + owner % 3 - 9] = block
        for slot, out in enumerate((first, second, third, fourth)):
            out[...] = pieces[slot]


def mlp(x_place, stream, grad_out, up_weight, down_weight):
    rows, width = stream.shape
    units = up_weight.shape[1]
    part = lambda columns: pl.BlockSpec((WIN, columns), lambda i, s: (i, 0))
    late = jax.ShapeDtypeStruct((15,) + BLOCK, BF)
    early = jax.ShapeDtypeStruct((4,) + BLOCK, BF)
    return call(
        mlp_kernel,
        (rows // WIN,),
        [part(width), part(width), whole(up_weight), whole(down_weight)],
        [((rows // HALF, HALF, width), BF, pl.BlockSpec((2, HALF, width), lambda i, s: (i, 0, 0)))]
        + [(late.shape, BF, whole(late))] * 4
        + [(early.shape, BF, whole(early))],
        (stream, grad_out, up_weight, down_weight),
        scratch=[
            pltpu.VMEM((width, units), F32),
            pltpu.VMEM((units, width), F32),
            pltpu.VMEM((64 * 32, 128), F32),
            pltpu.VMEM((4, 15) + BLOCK, BF),
        ],
        chosen=x_place,
        flops=10 * rows * width * units,
    )


def forward_kernel(lead, trail, far, labels, turned_qkv, hidden, packed, probs_out):
    step = pl.program_id(0)
    tail = jnp.where(step == pl.num_programs(0) - 1, far[...].astype(F32), trail[0].astype(F32))
    piece = jnp.concatenate([normalize(lead[0])[0], normalize(tail)[0]], axis=0)
    inputs = piece.astype(BF)
    hidden[0] = inputs
    query, key, value = [contract_cols(inputs, turned_qkv[i]).astype(BF) for i in range(3)]
    row = labels[pl.ds(step, 1), :].astype(F32)
    column = jnp.broadcast_to(row, (8, WIN)).T[:, :1]
    scores = contract_cols(query, key) * HS**-0.5
    kept = jnp.where(column == row, scores, -jnp.inf)
    raised = jnp.exp(kept - jnp.max(kept, axis=-1, keepdims=True))
    probs = raised / jnp.sum(raised, axis=-1, keepdims=True)
    probs_out[0] = probs
    attended = dot(probs.astype(BF), value).astype(BF)
    packed[0] = jnp.concatenate([query, key, value, attended], axis=1)


def middle_kernel(place, parts, stream, grad_out, _, mid, grad_mid):
    summed = jnp.sum(parts[...].astype(F32), axis=0)
    normed, factor = normalize(stream[0])
    middle = grad_out[0].astype(F32) + norm_back(normed, factor, summed)
    mid[...] = middle
    grad_mid[...] = middle.astype(BF)


def window_back(upper, hidden, packed, probs_in, turned_qkv, out_weight):
    probs = probs_in[0]
    query, key, value, attended = [packed[0][:, HS * i : HS * i + HS] for i in range(4)]
    attended_grad = contract_cols(upper, out_weight[...]).astype(BF)
    out_grad = contract_rows(attended, upper)
    prob_grad = contract_cols(attended_grad, value)
    inner = prob_grad - jnp.sum(prob_grad * probs, axis=-1, keepdims=True)
    score_grad = (probs * inner * HS**-0.5).astype(BF)
    grads = jnp.concatenate(
        [
            dot(score_grad, key),
            contract_rows(score_grad, query),
            contract_rows(probs.astype(BF), attended_grad),
        ],
        axis=1,
    ).astype(BF)
    return dot(grads, turned_qkv[...]), contract_rows(hidden[0], grads), out_grad


def near_kernel(lead, trail, *refs):
    saved, (in_grad, qkv_total, out_total) = refs[:5], refs[5:]
    step = pl.program_id(0)
    upper = jnp.concatenate([lead[0].astype(F32), trail[0].astype(F32)], axis=0).astype(BF)
    rows, qkv_grad, out_grad = window_back(upper, *saved)
    in_grad[2 * step] = rows[:HALF].astype(BF)
    in_grad[2 * step + 1] = rows[HALF:].astype(BF)

    @pl.when(step == 0)
    def _():
        qkv_total[...] = qkv_grad
        out_total[...] = out_grad

    @pl.when(step > 0)
    def _():
        qkv_total[...] += qkv_grad
        out_total[...] += out_grad


def far_kernel(place, own, far, *refs):
    saved, (in_near, qkv_total, out_total, early) = refs[:5], refs[5:9]
    in_grad, first, second, third, fourth, grads, outs, pieces = refs[9:]
    upper = jnp.concatenate([own[0].astype(F32), far[...].astype(F32)], axis=0).astype(BF)
    rows, qkv_grad, out_grad = window_back(upper, *saved)
    in_grad[in_grad.shape[0] - 1] = rows[:HALF].astype(BF)
    in_grad[0] = rows[HALF:].astype(BF)
    for chunk in range(in_near.shape[0]):
        in_grad[chunk + 1] = in_near[chunk]
    qkv_grad = qkv_total[...] + qkv_grad
    out_grad = out_total[...] + out_grad
    for i in range(3):
        grads[i] = qkv_grad[:, HS * i : HS * i + HS]
    for column in range(out_grad.shape[1] // 128):
        outs[pl.ds(column, HS, stride=4), :] = out_grad[:, 128 * column : 128 * column + 128]
    slots = [lax.rem(x - place[0] + 4, 4) for x in range(4)]
    for owner in range(36):
        if owner < 24:
            kind, start = owner // 8, owner % 8 * 64
            even = grads[kind, pl.ds(start, 32, stride=2), :]
            odd = grads[kind, pl.ds(start + 1, 32, stride=2), :]
            block = jnp.concatenate([even, odd], axis=1).astype(BF)
        elif owner < 32:
            block = outs[32 * (owner - 24) : 32 * (owner - 23), :].astype(BF)
        else:
            block = early[owner - 32]
        pieces[slots[owner % 12 // 3], owner // 12 * 3 + owner % 3] = block
    for slot, out in enumerate((first, second, third, fourth)):
        out[...] = pieces[slot]


def sum_kernel(parts, total, total_b):
    total[...] = jnp.sum(parts[...].astype(F32), axis=0)
    total_b[...] = total[...].astype(BF)


def final_kernel(place, summed, arrived, mid, block_input, grad_input):
    total = jnp.where(place[0] == 0, arrived[...].astype(F32), summed[...])
    normed, factor = normalize(block_input[0])
    grad_input[...] = (mid[...] + norm_back(normed, factor, total)).astype(BF)


def exchange(pieces, axis):
    received = lax.all_to_all(pieces, axis, 0, 0)
    return jnp.sum(received.astype(F32), axis=0)


def shards(block_input, stream, grad_out, regions, qkv_weight, out_weight, up_weight, down_weight):
    rows, width = block_input.shape
    windows = rows // WIN
    head_count = lax.axis_size(HEAD_AXES)
    share_rows = rows // head_count
    head = lax.axis_index(HEAD_AXES)
    columns = qkv_weight.shape[2]
    count = lax.axis_size(WIN_AXES)
    head_place = head.astype(jnp.int32).reshape(1)
    x_place = lax.axis_index("x").astype(jnp.int32).reshape(1)
    chunk = (1, HALF, width)
    chunked = [array.reshape(-1, HALF, width) for array in (block_input, stream, grad_out)]
    chunks_in, chunks_mid, chunks_out = chunked
    turned_qkv = jnp.swapaxes(qkv_weight, 1, 2)

    def from_next(values):
        return lax.ppermute(values, WIN_AXES, [((i + 1) % count, i) for i in range(count)])

    def along_x(pieces):
        moved = [
            lax.ppermute(pieces[k], "x", [(i, (i + k) % 4) for i in range(4)]) for k in range(1, 4)
        ]
        return sum(piece.astype(F32) for piece in [pieces[0]] + moved).astype(BF)

    far_input = from_next(block_input[:HALF])
    unit_grad, *late, early = mlp(x_place, stream, grad_out, up_weight, down_weight)
    parts = lax.all_to_all(unit_grad, HEAD_AXES, 0, 0)
    late_sum = along_x(late)
    labels = regions.reshape(windows, WIN)
    window = lambda columns, offset=0: pl.BlockSpec(
        (1, WIN, columns), lambda i, *_: (i + offset, 0, 0)
    )
    hidden, packed, probs = call(
        forward_kernel,
        (windows,),
        [
            pl.BlockSpec(chunk, lambda i: (2 * i + 1, 0, 0)),
            pl.BlockSpec(chunk, lambda i: (jnp.minimum(2 * i + 2, 2 * windows - 1), 0, 0)),
            whole(far_input),
            whole(labels),
            whole(turned_qkv),
        ],
        [
            ((windows, WIN, width), BF, window(width)),
            ((windows, WIN, 4 * columns), BF, window(4 * columns)),
            ((windows, WIN, WIN), F32, window(WIN)),
        ],
        (chunks_in, chunks_in, far_input, labels, turned_qkv),
    )
    mine = pl.BlockSpec(chunk, lambda i, place: (place[0], 0, 0))
    row_part = jax.ShapeDtypeStruct((share_rows, width), BF)
    mid, own_grad_mid = call(
        middle_kernel,
        (1,),
        [whole(parts), mine, mine, ANY],
        [(row_part.shape, F32, whole(row_part)), (row_part.shape, BF, whole(row_part))],
        (parts, chunks_mid, chunks_out, probs),
        chosen=head_place,
    )
    grad_mid = lax.all_gather(own_grad_mid, HEAD_AXES, axis=0)
    far_grad = from_next(grad_mid[0])
    weights = (turned_qkv.reshape(-1, width), out_weight)
    in_near, qkv_total, out_total = call(
        near_kernel,
        (windows - 1,),
        [
            pl.BlockSpec(chunk, lambda i: (2 * i + 1, 0, 0)),
            pl.BlockSpec(chunk, lambda i: (2 * i + 2, 0, 0)),
            window(width),
            window(4 * columns),
            window(WIN),
            *[whole(weight) for weight in weights],
        ],
        [
            ((head_count - 2, HALF, width), BF, VMEM),
            ((width, 3 * columns), F32, VMEM),
            ((columns, width), F32, VMEM),
        ],
        (grad_mid, grad_mid, hidden, packed, probs, *weights),
    )
    last = windows - 1
    piece = jax.ShapeDtypeStruct((9,) + BLOCK, BF)
    in_grad, *pieces = call(
        far_kernel,
        (1,),
        [
            pl.BlockSpec(chunk, lambda i, s: (head_count - 1, 0, 0)),
            whole(far_grad),
            window(width, last),
            window(4 * columns, last),
            window(WIN, last),
            *[whole(weight) for weight in weights],
            VMEM,
            VMEM,
            VMEM,
            whole(early),
        ],
        [((head_count, HALF, width), BF, VMEM)] + [(piece.shape, BF, whole(piece))] * 4,
        (
            grad_mid, far_grad, hidden, packed, probs, *weights, in_near, qkv_total, out_total,
            early,
        ),
        scratch=[
            pltpu.VMEM((3, width, columns), F32),
            pltpu.VMEM((8 * 32, 128), F32),
            pltpu.VMEM((4, 9) + BLOCK, BF),
        ],
        chosen=x_place,
    )
    in_parts = lax.all_to_all(in_grad, HEAD_AXES, 0, 0)
    early_sum = along_x(pieces)
    summed, summed_b = call(
        sum_kernel,
        (1,),
        [whole(in_parts)],
        [(row_part.shape, F32, whole(row_part)), (row_part.shape, BF, whole(row_part))],
        (in_parts,),
    )
    arrived = lax.ppermute(
        summed_b,
        WIN_AXES + HEAD_AXES,
        [(i * head_count, (i + 1) % count * head_count) for i in range(count)],
    )
    owned = exchange(jnp.concatenate([early_sum, late_sum], 0), ("y", "zh"))
    (grad_input,) = call(
        final_kernel,
        (1,),
        [whole(summed), whole(arrived), whole(mid), mine],
        [(row_part.shape, BF, whole(row_part))],
        (summed, arrived, mid, chunks_in),
        chosen=head_place,
    )
    return (grad_input, owned.reshape(1, -1))


def solution(mesh):
    fine = Mesh(mesh.devices.reshape(8, 4, 3, 4, 2), WIN_AXES + HEAD_AXES)
    return jax.shard_map(
        shards,
        mesh=fine,
        in_specs=(
            P(WIN_AXES, None),
            P(WIN_AXES, None),
            P(WIN_AXES, None),
            P(WIN_AXES),
            P(None, None, HEAD_AXES),
            P(HEAD_AXES, None),
            P(None, HEAD_AXES),
            P(HEAD_AXES, None),
        ),
        out_specs=(P(WIN_AXES + HEAD_AXES, None), P(HEAD_AXES, WIN_AXES)),
        check_vma=False,
    )
```

time: 141 us -> 140 us (level)
  the two profiles are of different devices: /device:TPU:16 before, /device:TPU:6 now
where the time goes in v4:
time: 140 us; the launch traced here: 139 us
  starting transfers between devices  65.3 us (47%)
  blocking collectives  26.2 us (19%)
  waiting for transfers between devices  22.2 us (16%)
  Pallas kernels  14.3 us (10%)
  local copies, waits for them, and re-layouts  8.48 us (6%)
  other arithmetic  1.46 us (1%)
    all_gather x1, blocking collectives, shards(): grad_mid = lax.all_gather(own_grad_mid, HEAD_AXES, axis=0)  26.2 us
    ppermute x6, starting transfers between devices, along_x(): lax.ppermute(pieces[k], 'x', [(i, (i + k) % 4) for i in range(4)])  19.1 us
    ppermute x2, starting transfers between devices, from_next(): lax.ppermute(values, WIN_AXES, [((i + 1) % count, i) for i in range(count)])  15.3 us
    pallas_call x7, Pallas kernels, call(): pl.pallas_call(kernel, grid_spec=spec, out_shape=[jax.ShapeDtypeStruct(ou...  14.3 us
    all_to_all x1, starting transfers between devices, exchange(): received = lax.all_to_all(pieces, axis, 0, 0)  12 us
    ppermute x2, waiting for transfers between devices, from_next(): lax.ppermute(values, WIN_AXES, [((i + 1) % count, i) for i in range(count)])  9.99 us
    unnamed x40, local copies, waits for them, and re-layouts  8.39 us
    ppermute x1, starting transfers between devices, shards(): lax.ppermute(summed_b, WIN_AXES + HEAD_AXES, [(i * head_count, (i + 1) %...  7.79 us
  transfers between devices with their start and end apart: 12, of which 6 were waited for; matrix products, arithmetic and copies ran while one was open for 1% of the time, Pallas kernels for 5%

profile of v4, /device:TPU:6, one launch (start us, length us, event | category | flops | bytes accessed | tf_op | source)
XLA Modules:
  0.0 138.8 jit_solution(740592752120629119)
XLA Ops:
  0.6 1.1 copy-done.2
  1.7 1.1 copy-done.4
  2.8 0.9 copy-done.11
  3.7 0.9 copy-done.12
  4.7 4.2 %shard_map.95 = (bf16[8,72,512]{2,1,0:T(8,128)(2,1)}, bf16[15,32,128]{2,1,0:T(8,128)(2,1)S(1)}, bf16[15,32,128]{2,1,0:T(8,128)(2,1)S(1)}, bf16[15,32,128]{2,1,0:...) custom-call(s32[1]{0:T(128)} %bitcast.1.place, bf16[576,512]{1,0:T(8,128)(2,1)S(1)} %copy-done.2, ...), custom_call_target="tpu_custom_call" | custom-call | flops 754974720 | bytes 2097152 | tf_op jit(solution)/shard_map/pallas_call | solution.py:57
  9.5 0.7 copy-done.13
  11.5 7.4 %all-to-all-start = ((bf16[8,72,512]{2,1,0:T(8,128)(2,1)}), bf16[8,72,512]{2,1,0:T(8,128)(2,1)S(1)}, u32[]{:S(2)}, u32[]{:S(2)}) async-start(bf16[8,72,512]{2,1,0:T(8,128)(2,1)} %get-tuple-element.23), calls=%async_computation | async-start | bytes 1179648 | tf_op jit(solution)/shard_map/all_to_all | solution.py:286
  18.9 12.1 %collective-permute-start = (bf16[72,512]{1,0:T(8,128)(2,1)S(1)}, bf16[72,512]{1,0:T(8,128)(2,1)S(1)}, u32[]{:S(2)}, u32[]{:S(2)}) collective-permute-start(bf16[72,512]{1,0:T(8,128)(2,1)S(1)} %slice.6), channel_id=1, source_target_pairs={{8,0},{16,8},{24,16},{32,24},{40,32},{48,40},{56,48},{64,56},{72,6... | collective-permute-start | bytes 221192 | tf_op jit(solution)/shard_map/ppermute | solution.py:276
  31.1 0.7 copy-done.19
  31.8 4.6 %collective-permute-done.far = bf16[72,512]{1,0:T(8,128)(2,1)S(1)} collective-permute-done((bf16[72,512]{1,0:T(8,128)(2,1)S(1)}, bf16[72,512]{1,0:T(8,128)(2,1)S(1)}, u32[]{:S(2)}, u32[]{:S(2)}) %collective-permute-start) | collective-permute-done | bytes 73760 | tf_op jit(solution)/shard_map/ppermute | solution.py:276
  36.5 3.6 %shard_map.96 = (bf16[4,144,512]{2,1,0:T(8,128)(2,1)S(1)}, bf16[4,144,256]{2,1,0:T(8,128)(2,1)S(1)}, f32[4,144,144]{2,1,0:T(8,128)S(1)}) custom-call(bf16[8,72,512]{2,1,0:T(8,128)(2,1)S(1)} %bitcast.13, bf16[8,72,512]{2,1,0:T(8,128)(2,1)S(1)} %bitcast.14, bf16[72,512]{1,0:T(8,128)(2,1)S(1)} %collective-permute-done.far, s32[4,144]{1,0:T(4,128)S(1)} %reshape.33.labels, ...), custom_call_target="tpu_custom_call" | custom-call | flops 100000000 | bytes 2097152 | tf_op jit(solution)/shard_map/pallas_call | solution.py:57
  40.0 0.8 all-to-all-done.parts
  40.9 1.1 copy-done.5
  42.2 26.2 %all-gather = bf16[576,512]{1,0:T(8,128)(2,1)S(1)} all-gather(bf16[72,512]{1,0:T(8,128)(2,1)S(1)} %get-tuple-element.25), channel_id=2, replica_groups=mesh['y'=8,'x'=4,'zh'=3,'zl'=4,'core'=2] {'zl','core'}, dimensions={0}, use_global_device_ids=true | all-gather | bytes 663552 | tf_op jit(solution)/shard_map/all_gather | solution.py:319
  68.4 3.2 %collective-permute-start.1 = (bf16[72,512]{1,0:T(8,128)(2,1)S(1)}, bf16[72,512]{1,0:T(8,128)(2,1)S(1)}, u32[]{:S(2)}, u32[]{:S(2)}) collective-permute-start(bf16[72,512]{1,0:T(8,128)(2,1)S(1)} %slice.9), channel_id=1, source_target_pairs={{8,0},{16,8},{24,16},{32,24},{40,32},{48,40},{56,48},{64,56},{72,6... | collective-permute-start | bytes 221192 | tf_op jit(solution)/shard_map/ppermute | solution.py:276
  71.6 3.2 %shard_map.98 = (bf16[6,72,512]{2,1,0:T(8,128)(2,1)S(1)}, f32[512,192]{1,0:T(8,128)S(1)}, f32[64,512]{1,0:T(8,128)S(1)}) custom-call(bf16[8,72,512]{2,1,0:T(8,128)(2,1)S(1)} %bitcast.10, bf16[8,72,512]{2,1,0:T(8,128)(2,1)S(1)} %bitcast.11, bf16[4,144,512]{2,1,0:T(8,128)(2,1)S(1)} %get-tuple-element.26.refs_0_, ...), custom_call_target="tpu_custom_call" | custom-call | flops 100000000 | bytes 2097152 | tf_op jit(solution)/shard_map/pallas_call | solution.py:57
  74.8 5.4 %collective-permute-done.1.far = bf16[72,512]{1,0:T(8,128)(2,1)S(1)} collective-permute-done((bf16[72,512]{1,0:T(8,128)(2,1)S(1)}, bf16[72,512]{1,0:T(8,128)(2,1)S(1)}, u32[]{:S(2)}, u32[]{:S(2)}) %collective-permute-start.1) | collective-permute-done | bytes 73760 | tf_op jit(solution)/shard_map/ppermute | solution.py:276
  80.2 2.0 %shard_map.99 = (bf16[8,72,512]{2,1,0:T(8,128)(2,1)}, bf16[9,32,128]{2,1,0:T(8,128)(2,1)S(1)}, bf16[9,32,128]{2,1,0:T(8,128)(2,1)S(1)}, bf16[9,32,128]{2,1,0:T(8,128)(2,1)S(1)}, bf16[9,32,128]{2,1,0:T(8,128)(2,1)S(1)}) custom-call(s32[1]{0:T(128)} %bitcast.1.place, bf16[8,72,512]{2,1,0:T(8,128)(2,1)S(1)} %bitcast.12, ...), custom_call_target="tpu_custom_call" | custom-call | flops 100000000 | bytes 2097152 | tf_op jit(solution)/shard_map/pallas_call | solution.py:57
  82.2 3.7 %all-to-all-start.1 = ((bf16[8,72,512]{2,1,0:T(8,128)(2,1)}), bf16[8,72,512]{2,1,0:T(8,128)(2,1)S(1)}, u32[]{:S(2)}, u32[]{:S(2)}) async-start(bf16[8,72,512]{2,1,0:T(8,128)(2,1)} %get-tuple-element.32), calls=%async_computation.1 | async-start | bytes 1179648 | tf_op jit(solution)/shard_map/all_to_all | solution.py:369
  85.9 2.5 %collective-permute-start.6 = (bf16[15,32,128]{2,1,0:T(8,128)(2,1)S(1)}, bf16[15,32,128]{2,1,0:T(8,128)(2,1)S(1)}, u32[]{:S(2)}, u32[]{:S(2)}) collective-permute-start(bf16[15,32,128]{2,1,0:T(8,128)(2,1)S(1)} %copy-done.18), channel_id=1, source_target_pairs={{0,24},{24,48},{48,72},{72,0},{1,25},{25,49},{49,73},{73,1},{2,26}... | collective-permute-start | bytes 368648 | tf_op jit(solution)/shard_map/ppermute | solution.py:280
  88.4 4.5 %collective-permute-start.7 = (bf16[15,32,128]{2,1,0:T(8,128)(2,1)S(1)}, bf16[15,32,128]{2,1,0:T(8,128)(2,1)S(1)}, u32[]{:S(2)}, u32[]{:S(2)}) collective-permute-start(bf16[15,32,128]{2,1,0:T(8,128)(2,1)S(1)} %copy-done.16), channel_id=1, source_target_pairs={{0,48},{24,72},{48,0},{72,24},{1,49},{25,73},{49,1},{73,25},{2,50}... | collective-permute-start | bytes 368648 | tf_op jit(solution)/shard_map/ppermute | solution.py:280
  92.9 1.9 %collective-permute-start.8 = (bf16[15,32,128]{2,1,0:T(8,128)(2,1)S(1)}, bf16[15,32,128]{2,1,0:T(8,128)(2,1)S(1)}, u32[]{:S(2)}, u32[]{:S(2)}) collective-permute-start(bf16[15,32,128]{2,1,0:T(8,128)(2,1)S(1)} %copy-done.14), channel_id=1, source_target_pairs={{0,72},{24,0},{48,24},{72,48},{1,73},{25,1},{49,25},{73,49},{2,74}... | collective-permute-start | bytes 368648 | tf_op jit(solution)/shard_map/ppermute | solution.py:280
  94.8 5.1 %collective-permute-start.3 = (bf16[9,32,128]{2,1,0:T(8,128)(2,1)S(1)}, bf16[9,32,128]{2,1,0:T(8,128)(2,1)S(1)}, u32[]{:S(2)}, u32[]{:S(2)}) collective-permute-start(bf16[9,32,128]{2,1,0:T(8,128)(2,1)S(1)} %get-tuple-element.37), channel_id=1, source_target_pairs={{0,24},{24,48},{48,72},{72,0},{1,25},{25,49},{49,73},{73,1},{2,26}... | collective-permute-start | bytes 221192 | tf_op jit(solution)/shard_map/ppermute | solution.py:280
  99.9 1.9 %collective-permute-start.4 = (bf16[9,32,128]{2,1,0:T(8,128)(2,1)S(1)}, bf16[9,32,128]{2,1,0:T(8,128)(2,1)S(1)}, u32[]{:S(2)}, u32[]{:S(2)}) collective-permute-start(bf16[9,32,128]{2,1,0:T(8,128)(2,1)S(1)} %get-tuple-element.38), channel_id=1, source_target_pairs={{0,48},{24,72},{48,0},{72,24},{1,49},{25,73},{49,1},{73,25},{2,50}... | collective-permute-start | bytes 221192 | tf_op jit(solution)/shard_map/ppermute | solution.py:280
  101.9 3.1 %collective-permute-start.5 = (bf16[9,32,128]{2,1,0:T(8,128)(2,1)S(1)}, bf16[9,32,128]{2,1,0:T(8,128)(2,1)S(1)}, u32[]{:S(2)}, u32[]{:S(2)}) collective-permute-start(bf16[9,32,128]{2,1,0:T(8,128)(2,1)S(1)} %get-tuple-element.39), channel_id=1, source_target_pairs={{0,72},{24,0},{48,24},{72,48},{1,73},{25,1},{49,25},{73,49},{2,74}... | collective-permute-start | bytes 221192 | tf_op jit(solution)/shard_map/ppermute | solution.py:280
  105.1 3.2 %collective-permute-done.4 = bf16[9,32,128]{2,1,0:T(8,128)(2,1)S(1)} collective-permute-done((bf16[9,32,128]{2,1,0:T(8,128)(2,1)S(1)}, bf16[9,32,128]{2,1,0:T(8,128)(2,1)S(1)}, u32[]{:S(2)}, u32[]{:S(2)}) %collective-permute-start.4) | collective-permute-done | bytes 73760 | tf_op jit(solution)/shard_map/ppermute | solution.py:280
  108.3 1.1 collective-permute-done.5
  109.4 0.7 pad_maximum_fusion
  110.1 12.0 %all-to-all-start.2 = ((bf16[24,32,128]{2,1,0:T(8,128)(2,1)}), bf16[24,32,128]{2,1,0:T(8,128)(2,1)S(1)}, u32[]{:S(2)}, u32[]{:S(2)}) async-start(bf16[24,32,128]{2,1,0:T(8,128)(2,1)} %pad_maximum_fusion), calls=%async_computation.2 | async-start | bytes 393216 | tf_op jit(solution)/shard_map/all_to_all | solution.py:256
  122.3 7.8 %collective-permute-start.2 = (bf16[72,512]{1,0:T(8,128)(2,1)S(1)}, bf16[72,512]{1,0:T(8,128)(2,1)S(1)}, u32[]{:S(2)}, u32[]{:S(2)}) collective-permute-start(bf16[72,512]{1,0:T(8,128)(2,1)S(1)} %get-tuple-element.34), channel_id=1, source_target_pairs={{0,8},{8,16},{16,24},{24,32},{32,40},{40,48},{48,56},{56,64},{64,7... | collective-permute-start | bytes 221192 | tf_op jit(solution)/shard_map/ppermute | solution.py:378
  130.1 7.1 %all-to-all-done.2 = bf16[24,32,128]{2,1,0:T(8,128)(2,1)S(1)} async-done(((bf16[24,32,128]{2,1,0:T(8,128)(2,1)}), bf16[24,32,128]{2,1,0:T(8,128)(2,1)S(1)}, u32[]{:S(2)}, u32[]{:S(2)}) %all-to-all-start.2) | async-done | bytes 196640 | tf_op jit(solution)/shard_map/all_to_all | solution.py:256
  137.9 0.9 shard_map.101
  (47 shorter events, 3.2 us)
Async XLA Ops:
  0.6 1.1 copy-start.2
  1.7 1.1 copy-start.4
  2.8 0.9 copy-start.11
  3.7 0.9 copy-start.12
  8.9 0.6 copy-start.9
  9.5 0.7 copy-start.13
  10.2 0.6 copy-start.15
  10.8 0.6 copy-start.17
  11.5 7.4 %copy-start = (bf16[576,512]{1,0:T(8,128)(2,1)S(1)}, bf16[576,512]{1,0:T(8,128)(2,1)}, u32[]{:S(2)}) copy-start(bf16[576,512]{1,0:T(8,128)(2,1)} %param.8) | copy-start | bytes 1769476
  11.5 25.0 %copy-start.1 = (bf16[3,512,64]{1,2,0:T(8,128)(2,1)S(1)}, bf16[3,512,64]{1,2,0:T(8,128)(2,1)}, u32[]{:S(2)}) copy-start(bf16[3,512,64]{1,2,0:T(8,128)(2,1)} %param.12) | copy-start | bytes 589828
  11.5 29.4 %all-to-all-start = ((bf16[8,72,512]{2,1,0:T(8,128)(2,1)}), bf16[8,72,512]{2,1,0:T(8,128)(2,1)S(1)}, u32[]{:S(2)}, u32[]{:S(2)}) async-start(bf16[8,72,512]{2,1,0:T(8,128)(2,1)} %get-tuple-element.23), calls=%async_computation | async-start | bytes 1179648 | tf_op jit(solution)/shard_map/all_to_all | solution.py:286
  18.9 17.5 %collective-permute-start = (bf16[72,512]{1,0:T(8,128)(2,1)S(1)}, bf16[72,512]{1,0:T(8,128)(2,1)S(1)}, u32[]{:S(2)}, u32[]{:S(2)}) collective-permute-start(bf16[72,512]{1,0:T(8,128)(2,1)S(1)} %slice.6), channel_id=1, source_target_pairs={{8,0},{16,8},{24,16},{32,24},{40,32},{48,40},{56,48},{64,56},{72,6... | collective-permute-start | bytes 221192 | tf_op jit(solution)/shard_map/ppermute | solution.py:276
  31.0 0.7 copy-start.19
  36.5 4.4 %copy-start.3 = (bf16[576,512]{1,0:T(8,128)(2,1)S(1)}, bf16[576,512]{1,0:T(8,128)(2,1)}, u32[]{:S(2)}) copy-start(bf16[576,512]{1,0:T(8,128)(2,1)} %stream.1) | copy-start | bytes 1769476
  40.9 1.1 copy-start.5
  42.2 26.2 %copy-start.7 = (f32[72,512]{1,0:T(8,128)}, f32[72,512]{1,0:T(8,128)S(1)}, u32[]{:S(2)}) copy-start(f32[72,512]{1,0:T(8,128)S(1)} %get-tuple-element.35.mid) | copy-start | bytes 442372
  68.4 3.2 %copy-start.6 = (bf16[64,512]{1,0:T(8,128)(2,1)S(1)}, bf16[64,512]{1,0:T(8,128)(2,1)}, u32[]{:S(2)}) copy-start(bf16[64,512]{1,0:T(8,128)(2,1)} %refs_4_.3) | copy-start | bytes 196612
  68.4 11.7 %collective-permute-start.1 = (bf16[72,512]{1,0:T(8,128)(2,1)S(1)}, bf16[72,512]{1,0:T(8,128)(2,1)S(1)}, u32[]{:S(2)}, u32[]{:S(2)}) collective-permute-start(bf16[72,512]{1,0:T(8,128)(2,1)S(1)} %slice.9), channel_id=1, source_target_pairs={{8,0},{16,8},{24,16},{32,24},{40,32},{48,40},{56,48},{64,56},{72,6... | collective-permute-start | bytes 221192 | tf_op jit(solution)/shard_map/ppermute | solution.py:276
  82.2 3.7 %copy-start.18 = (bf16[15,32,128]{2,1,0:T(8,128)(2,1)S(1)}, bf16[15,32,128]{2,1,0:T(8,128)(2,1)}, u32[]{:S(2)}) copy-start(bf16[15,32,128]{2,1,0:T(8,128)(2,1)} %copy-done.17) | copy-start | bytes 368644
  82.2 6.2 %copy-start.16 = (bf16[15,32,128]{2,1,0:T(8,128)(2,1)S(1)}, bf16[15,32,128]{2,1,0:T(8,128)(2,1)}, u32[]{:S(2)}) copy-start(bf16[15,32,128]{2,1,0:T(8,128)(2,1)} %copy-done.15) | copy-start | bytes 368644
  82.2 10.7 %copy-start.14 = (bf16[15,32,128]{2,1,0:T(8,128)(2,1)S(1)}, bf16[15,32,128]{2,1,0:T(8,128)(2,1)}, u32[]{:S(2)}) copy-start(bf16[15,32,128]{2,1,0:T(8,128)(2,1)} %copy-done.13) | copy-start | bytes 368644
  82.2 22.9 %copy-start.10 = (bf16[15,32,128]{2,1,0:T(8,128)(2,1)S(1)}, bf16[15,32,128]{2,1,0:T(8,128)(2,1)}, u32[]{:S(2)}) copy-start(bf16[15,32,128]{2,1,0:T(8,128)(2,1)} %copy-done.9) | copy-start | bytes 368644
  82.2 27.9 %all-to-all-start.1 = ((bf16[8,72,512]{2,1,0:T(8,128)(2,1)}), bf16[8,72,512]{2,1,0:T(8,128)(2,1)S(1)}, u32[]{:S(2)}, u32[]{:S(2)}) async-start(bf16[8,72,512]{2,1,0:T(8,128)(2,1)} %get-tuple-element.32), calls=%async_computation.1 | async-start | bytes 1179648 | tf_op jit(solution)/shard_map/all_to_all | solution.py:369
  85.9 16.0 %collective-permute-start.6 = (bf16[15,32,128]{2,1,0:T(8,128)(2,1)S(1)}, bf16[15,32,128]{2,1,0:T(8,128)(2,1)S(1)}, u32[]{:S(2)}, u32[]{:S(2)}) collective-permute-start(bf16[15,32,128]{2,1,0:T(8,128)(2,1)S(1)} %copy-done.18), channel_id=1, source_target_pairs={{0,24},{24,48},{48,72},{72,0},{1,25},{25,49},{49,73},{73,1},{2,26}... | collective-permute-start | bytes 368648 | tf_op jit(solution)/shard_map/ppermute | solution.py:280
  88.4 16.6 %collective-permute-start.7 = (bf16[15,32,128]{2,1,0:T(8,128)(2,1)S(1)}, bf16[15,32,128]{2,1,0:T(8,128)(2,1)S(1)}, u32[]{:S(2)}, u32[]{:S(2)}) collective-permute-start(bf16[15,32,128]{2,1,0:T(8,128)(2,1)S(1)} %copy-done.16), channel_id=1, source_target_pairs={{0,48},{24,72},{48,0},{72,24},{1,49},{25,73},{49,1},{73,25},{2,50}... | collective-permute-start | bytes 368648 | tf_op jit(solution)/shard_map/ppermute | solution.py:280
  92.9 12.1 %collective-permute-start.8 = (bf16[15,32,128]{2,1,0:T(8,128)(2,1)S(1)}, bf16[15,32,128]{2,1,0:T(8,128)(2,1)S(1)}, u32[]{:S(2)}, u32[]{:S(2)}) collective-permute-start(bf16[15,32,128]{2,1,0:T(8,128)(2,1)S(1)} %copy-done.14), channel_id=1, source_target_pairs={{0,72},{24,0},{48,24},{72,48},{1,73},{25,1},{49,25},{73,49},{2,74}... | collective-permute-start | bytes 368648 | tf_op jit(solution)/shard_map/ppermute | solution.py:280
  94.8 10.3 %collective-permute-start.3 = (bf16[9,32,128]{2,1,0:T(8,128)(2,1)S(1)}, bf16[9,32,128]{2,1,0:T(8,128)(2,1)S(1)}, u32[]{:S(2)}, u32[]{:S(2)}) collective-permute-start(bf16[9,32,128]{2,1,0:T(8,128)(2,1)S(1)} %get-tuple-element.37), channel_id=1, source_target_pairs={{0,24},{24,48},{48,72},{72,0},{1,25},{25,49},{49,73},{73,1},{2,26}... | collective-permute-start | bytes 221192 | tf_op jit(solution)/shard_map/ppermute | solution.py:280
  99.9 8.3 %collective-permute-start.4 = (bf16[9,32,128]{2,1,0:T(8,128)(2,1)S(1)}, bf16[9,32,128]{2,1,0:T(8,128)(2,1)S(1)}, u32[]{:S(2)}, u32[]{:S(2)}) collective-permute-start(bf16[9,32,128]{2,1,0:T(8,128)(2,1)S(1)} %get-tuple-element.38), channel_id=1, source_target_pairs={{0,48},{24,72},{48,0},{72,24},{1,49},{25,73},{49,1},{73,25},{2,50}... | collective-permute-start | bytes 221192 | tf_op jit(solution)/shard_map/ppermute | solution.py:280
  101.9 7.5 %collective-permute-start.5 = (bf16[9,32,128]{2,1,0:T(8,128)(2,1)S(1)}, bf16[9,32,128]{2,1,0:T(8,128)(2,1)S(1)}, u32[]{:S(2)}, u32[]{:S(2)}) collective-permute-start(bf16[9,32,128]{2,1,0:T(8,128)(2,1)S(1)} %get-tuple-element.39), channel_id=1, source_target_pairs={{0,72},{24,0},{48,24},{72,48},{1,73},{25,1},{49,25},{73,49},{2,74}... | collective-permute-start | bytes 221192 | tf_op jit(solution)/shard_map/ppermute | solution.py:280
  110.1 27.1 %all-to-all-start.2 = ((bf16[24,32,128]{2,1,0:T(8,128)(2,1)}), bf16[24,32,128]{2,1,0:T(8,128)(2,1)S(1)}, u32[]{:S(2)}, u32[]{:S(2)}) async-start(bf16[24,32,128]{2,1,0:T(8,128)(2,1)} %pad_maximum_fusion), calls=%async_computation.2 | async-start | bytes 393216 | tf_op jit(solution)/shard_map/all_to_all | solution.py:256
  122.3 15.6 %copy-start.8 = (f32[72,512]{1,0:T(8,128)S(1)}, f32[72,512]{1,0:T(8,128)}, u32[]{:S(2)}) copy-start(f32[72,512]{1,0:T(8,128)} %copy-done.7) | copy-start | bytes 442372
  122.3 15.6 %collective-permute-start.2 = (bf16[72,512]{1,0:T(8,128)(2,1)S(1)}, bf16[72,512]{1,0:T(8,128)(2,1)S(1)}, u32[]{:S(2)}, u32[]{:S(2)}) collective-permute-start(bf16[72,512]{1,0:T(8,128)(2,1)S(1)} %get-tuple-element.34), channel_id=1, source_target_pairs={{0,8},{8,16},{16,24},{24,32},{32,40},{40,48},{48,56},{56,64},{64,7... | collective-permute-start | bytes 221192 | tf_op jit(solution)/shard_map/ppermute | solution.py:378

commit v5 on v4

--- a/solution.py
+++ b/solution.py
@@ -45,7 +45,7 @@
 ANY = pl.BlockSpec(memory_space=pl.ANY)
 
 
-def call(kernel, grid, ins, outs, args, scratch=(), chosen=None, flops=10**8):
+def call(kernel, grid, ins, outs, args, scratch=(), chosen=None, flops=10**8, vmem=60):
     spec = pltpu.PrefetchScalarGridSpec(
         num_scalar_prefetch=0 if chosen is None else 1,
         grid=grid,
@@ -58,7 +58,7 @@
         kernel,
         grid_spec=spec,
         out_shape=[jax.ShapeDtypeStruct(out[0], out[1]) for out in outs],
-        compiler_params=pltpu.CompilerParams(vmem_limit_bytes=24 * 2**20),
+        compiler_params=pltpu.CompilerParams(vmem_limit_bytes=vmem * 2**20),
         cost_estimate=pl.CostEstimate(flops=flops, bytes_accessed=2 * 2**20, transcendentals=0),
     )(*first, *args)
 
@@ -146,25 +146,29 @@
     )
 
 
-def forward_kernel(lead, trail, far, labels, turned_qkv, hidden, packed, probs_out):
-    step = pl.program_id(0)
-    tail = jnp.where(step == pl.num_programs(0) - 1, far[...].astype(F32), trail[0].astype(F32))
-    piece = jnp.concatenate([normalize(lead[0])[0], normalize(tail)[0]], axis=0)
+def window_forward(lead, tail, row, turned_qkv):
+    piece = jnp.concatenate([normalize(lead)[0], normalize(tail)[0]], axis=0)
     inputs = piece.astype(BF)
-    hidden[0] = inputs
-    query, key, value = [contract_cols(inputs, turned_qkv[i]).astype(BF) for i in range(3)]
-    row = labels[pl.ds(step, 1), :].astype(F32)
+    query, key, value = [
+        contract_cols(inputs, turned_qkv[HS * i : HS * i + HS, :]).astype(BF) for i in range(3)
+    ]
+    row = row.astype(F32)
     column = jnp.broadcast_to(row, (8, WIN)).T[:, :1]
     scores = contract_cols(query, key) * HS**-0.5
     kept = jnp.where(column == row, scores, -jnp.inf)
     raised = jnp.exp(kept - jnp.max(kept, axis=-1, keepdims=True))
     probs = raised / jnp.sum(raised, axis=-1, keepdims=True)
-    probs_out[0] = probs
     attended = dot(probs.astype(BF), value).astype(BF)
-    packed[0] = jnp.concatenate([query, key, value, attended], axis=1)
-
-
-def middle_kernel(place, parts, stream, grad_out, _, mid, grad_mid):
+    return inputs, (query, key, value, attended), probs
+
+
+def forward_kernel(lead, tail, labels, turned_qkv, hidden, packed, probs_out):
+    row = labels[pl.ds(pl.program_id(0), 1), :]
+    hidden[0], parts, probs_out[0] = window_forward(lead[0], tail[0], row, turned_qkv)
+    packed[0] = jnp.concatenate(parts, axis=1)
+
+
+def middle_kernel(place, parts, stream, grad_out, _, __, mid, grad_mid):
     summed = jnp.sum(parts[...].astype(F32), axis=0)
     normed, factor = normalize(stream[0])
     middle = grad_out[0].astype(F32) + norm_back(normed, factor, summed)
@@ -172,9 +176,8 @@
     grad_mid[...] = middle.astype(BF)
 
 
-def window_back(upper, hidden, packed, probs_in, turned_qkv, out_weight):
-    probs = probs_in[0]
-    query, key, value, attended = [packed[0][:, HS * i : HS * i + HS] for i in range(4)]
+def window_back(upper, hidden, parts, probs, turned_qkv, out_weight):
+    query, key, value, attended = parts
     attended_grad = contract_cols(upper, out_weight[...]).astype(BF)
     out_grad = contract_rows(attended, upper)
     prob_grad = contract_cols(attended_grad, value)
@@ -188,14 +191,17 @@
         ],
         axis=1,
     ).astype(BF)
-    return dot(grads, turned_qkv[...]), contract_rows(hidden[0], grads), out_grad
+    return dot(grads, turned_qkv[...]), contract_rows(hidden, grads), out_grad
 
 
 def near_kernel(lead, trail, *refs):
-    saved, (in_grad, qkv_total, out_total) = refs[:5], refs[5:]
+    hidden, packed, probs, turned_qkv, out_weight, in_grad, qkv_total, out_total = refs
+    parts = [packed[0][:, HS * i : HS * i + HS] for i in range(4)]
     step = pl.program_id(0)
     upper = jnp.concatenate([lead[0].astype(F32), trail[0].astype(F32)], axis=0).astype(BF)
-    rows, qkv_grad, out_grad = window_back(upper, *saved)
+    rows, qkv_grad, out_grad = window_back(
+        upper, hidden[0], parts, probs[0], turned_qkv, out_weight
+    )
     in_grad[2 * step] = rows[:HALF].astype(BF)
     in_grad[2 * step + 1] = rows[HALF:].astype(BF)
 
@@ -210,11 +216,13 @@
         out_total[...] += out_grad
 
 
-def far_kernel(place, own, far, *refs):
-    saved, (in_near, qkv_total, out_total, early) = refs[:5], refs[5:9]
-    in_grad, first, second, third, fourth, grads, outs, pieces = refs[9:]
+def far_kernel(
+    place, own, far, lead, tail, labels, turned_qkv, out_weight, in_near, qkv_total, out_total,
+    early, in_grad, first, second, third, fourth, grads, outs, pieces,
+):
+    saved = window_forward(lead[0], tail[...], labels[labels.shape[0] - 1 :, :], turned_qkv)
     upper = jnp.concatenate([own[0].astype(F32), far[...].astype(F32)], axis=0).astype(BF)
-    rows, qkv_grad, out_grad = window_back(upper, *saved)
+    rows, qkv_grad, out_grad = window_back(upper, *saved, turned_qkv, out_weight)
     in_grad[in_grad.shape[0] - 1] = rows[:HALF].astype(BF)
     in_grad[0] = rows[HALF:].astype(BF)
     for chunk in range(in_near.shape[0]):
@@ -286,42 +294,41 @@
     parts = lax.all_to_all(unit_grad, HEAD_AXES, 0, 0)
     late_sum = along_x(late)
     labels = regions.reshape(windows, WIN)
-    window = lambda columns, offset=0: pl.BlockSpec(
-        (1, WIN, columns), lambda i, *_: (i + offset, 0, 0)
-    )
+    window = lambda columns: pl.BlockSpec((1, WIN, columns), lambda i: (i, 0, 0))
+    weights = (turned_qkv.reshape(-1, width), out_weight)
+    near = windows - 1
     hidden, packed, probs = call(
         forward_kernel,
-        (windows,),
+        (near,),
         [
             pl.BlockSpec(chunk, lambda i: (2 * i + 1, 0, 0)),
-            pl.BlockSpec(chunk, lambda i: (jnp.minimum(2 * i + 2, 2 * windows - 1), 0, 0)),
-            whole(far_input),
+            pl.BlockSpec(chunk, lambda i: (2 * i + 2, 0, 0)),
             whole(labels),
-            whole(turned_qkv),
-        ],
-        [
-            ((windows, WIN, width), BF, window(width)),
-            ((windows, WIN, 4 * columns), BF, window(4 * columns)),
-            ((windows, WIN, WIN), F32, window(WIN)),
-        ],
-        (chunks_in, chunks_in, far_input, labels, turned_qkv),
+            whole(weights[0]),
+        ],
+        [
+            ((near, WIN, width), BF, window(width)),
+            ((near, WIN, 4 * columns), BF, window(4 * columns)),
+            ((near, WIN, WIN), F32, window(WIN)),
+        ],
+        (chunks_in, chunks_in, labels, weights[0]),
     )
     mine = pl.BlockSpec(chunk, lambda i, place: (place[0], 0, 0))
     row_part = jax.ShapeDtypeStruct((share_rows, width), BF)
     mid, own_grad_mid = call(
         middle_kernel,
         (1,),
-        [whole(parts), mine, mine, ANY],
+        [whole(parts), mine, mine, ANY, ANY],
         [(row_part.shape, F32, whole(row_part)), (row_part.shape, BF, whole(row_part))],
-        (parts, chunks_mid, chunks_out, probs),
+        (parts, chunks_mid, chunks_out, probs, late_sum),
         chosen=head_place,
+        vmem=16,
     )
     grad_mid = lax.all_gather(own_grad_mid, HEAD_AXES, axis=0)
     far_grad = from_next(grad_mid[0])
-    weights = (turned_qkv.reshape(-1, width), out_weight)
     in_near, qkv_total, out_total = call(
         near_kernel,
-        (windows - 1,),
+        (near,),
         [
             pl.BlockSpec(chunk, lambda i: (2 * i + 1, 0, 0)),
             pl.BlockSpec(chunk, lambda i: (2 * i + 2, 0, 0)),
@@ -336,8 +343,8 @@
             ((columns, width), F32, VMEM),
         ],
         (grad_mid, grad_mid, hidden, packed, probs, *weights),
-    )
-    last = windows - 1
+        vmem=56,
+    )
     piece = jax.ShapeDtypeStruct((9,) + BLOCK, BF)
     in_grad, *pieces = call(
         far_kernel,
@@ -345,9 +352,9 @@
         [
             pl.BlockSpec(chunk, lambda i, s: (head_count - 1, 0, 0)),
             whole(far_grad),
-            window(width, last),
-            window(4 * columns, last),
-            window(WIN, last),
+            pl.BlockSpec(chunk, lambda i, s: (head_count - 1, 0, 0)),
+            whole(far_input),
+            whole(labels),
             *[whole(weight) for weight in weights],
             VMEM,
             VMEM,
@@ -356,8 +363,8 @@
         ],
         [((head_count, HALF, width), BF, VMEM)] + [(piece.shape, BF, whole(piece))] * 4,
         (
-            grad_mid, far_grad, hidden, packed, probs, *weights, in_near, qkv_total, out_total,
-            early,
+            grad_mid, far_grad, chunks_in, far_input, labels, *weights, in_near, qkv_total,
+            out_total, early,
         ),
         scratch=[
             pltpu.VMEM((3, width, columns), F32),
@@ -365,6 +372,7 @@
             pltpu.VMEM((4, 9) + BLOCK, BF),
         ],
         chosen=x_place,
+        vmem=56,
     )
     in_parts = lax.all_to_all(in_grad, HEAD_AXES, 0, 0)
     early_sum = along_x(pieces)
@@ -374,6 +382,7 @@
         [whole(in_parts)],
         [(row_part.shape, F32, whole(row_part)), (row_part.shape, BF, whole(row_part))],
         (in_parts,),
+        vmem=16,
     )
     arrived = lax.ppermute(
         summed_b,
@@ -388,6 +397,7 @@
         [(row_part.shape, BF, whole(row_part))],
         (summed, arrived, mid, chunks_in),
         chosen=head_place,
+        vmem=16,
     )
     return (grad_input, owned.reshape(1, -1))
 

time: 140 us -> 128 us (0.914)
  blocking collectives: 26.2 us -> 15.4 us
  Pallas kernels: 14.3 us -> 21.4 us
  local copies, waits for them, and re-layouts: 8.48 us -> 3.13 us
  waiting for transfers between devices: 22.2 us -> 17.3 us
  starting transfers between devices: 65.3 us -> 66.9 us
    all_gather x1, blocking collectives: 26.2 us -> 15.4 us  [shards(): grad_mid = lax.all_gather(own_grad_mid, HEAD_AXES, axis=0)]
    pallas_call x7, Pallas kernels: 14.3 us -> 21.4 us  [call(): pl.pallas_call(kernel, grid_spec=spec, out_shape=[jax.ShapeDtypeStruct(ou...]
    unnamed x40 -> x32, local copies, waits for them, and re-layouts: 8.39 us -> 1.55 us
    ppermute x2, waiting for transfers between devices: 9.99 us -> 4.76 us  [from_next(): lax.ppermute(values, WIN_AXES, [((i + 1) % count, i) for i in range(count)])]
    ppermute x6, starting transfers between devices: 19.1 us -> 23.4 us  [along_x(): lax.ppermute(pieces[k], 'x', [(i, (i + k) % 4) for i in range(4)])]
    ppermute x2, starting transfers between devices: 15.3 us -> 12.4 us  [from_next(): lax.ppermute(values, WIN_AXES, [((i + 1) % count, i) for i in range(count)])]
  transfers between devices with their start and end apart: 12 -> 12, of which waited for: 6 -> 5; matrix products, arithmetic and copies ran while one was open for 1% -> 2% of each run, Pallas kernels for 5% -> 8%
where the time goes in v5:
time: 128 us; the launch traced here: 127 us
  starting transfers between devices  66.9 us (52%)
  Pallas kernels  21.4 us (17%)
  waiting for transfers between devices  17.3 us (14%)
  blocking collectives  15.4 us (12%)
  local copies, waits for them, and re-layouts  3.13 us (2%)
  other arithmetic  1.45 us (1%)
    ppermute x6, starting transfers between devices, along_x(): lax.ppermute(pieces[k], 'x', [(i, (i + k) % 4) for i in range(4)])  23.4 us
    pallas_call x7, Pallas kernels, call(): pl.pallas_call(kernel, grid_spec=spec, out_shape=[jax.ShapeDtypeStruct(ou...  21.4 us
    all_gather x1, blocking collectives, shards(): grad_mid = lax.all_gather(own_grad_mid, HEAD_AXES, axis=0)  15.4 us
    ppermute x2, starting transfers between devices, from_next(): lax.ppermute(values, WIN_AXES, [((i + 1) % count, i) for i in range(count)])  12.4 us
    all_to_all x1, starting transfers between devices, exchange(): received = lax.all_to_all(pieces, axis, 0, 0)  12.3 us
    ppermute x1, starting transfers between devices, shards(): lax.ppermute(summed_b, WIN_AXES + HEAD_AXES, [(i * head_count, (i + 1) %...  7.66 us
    all_to_all x1, waiting for transfers between devices, exchange(): received = lax.all_to_all(pieces, axis, 0, 0)  7.62 us
    all_to_all x1, starting transfers between devices, shards(): parts = lax.all_to_all(unit_grad, HEAD_AXES, 0, 0)  7.41 us
  transfers between devices with their start and end apart: 12, of which 5 were waited for; matrix products, arithmetic and copies ran while one was open for 2% of the time, Pallas kernels for 8%

profile of v5, /device:TPU:6, one launch (start us, length us, event | category | flops | bytes accessed | tf_op | source)
XLA Modules:
  0.0 126.5 jit_solution(4464571460996329728)
XLA Ops:
  0.6 5.9 %shard_map.95 = (bf16[8,72,512]{2,1,0:T(8,128)(2,1)}, bf16[15,32,128]{2,1,0:T(8,128)(2,1)}, bf16[15,32,128]{2,1,0:T(8,128)(2,1)}, bf16[15,32,128]{2,1,0:T(8,128)...) custom-call(s32[1]{0:T(128)} %bitcast.1.place, bf16[576,512]{1,0:T(8,128)(2,1)} %stream.1, ...), custom_call_target="tpu_custom_call" | custom-call | flops 754974720 | bytes 2097152 | tf_op jit(solution)/shard_map/pallas_call | solution.py:57
  6.5 7.4 %all-to-all-start = ((bf16[8,72,512]{2,1,0:T(8,128)(2,1)}), bf16[8,72,512]{2,1,0:T(8,128)(2,1)S(1)}, u32[]{:S(2)}, u32[]{:S(2)}) async-start(bf16[8,72,512]{2,1,0:T(8,128)(2,1)} %get-tuple-element.23), calls=%async_computation | async-start | bytes 1179648 | tf_op jit(solution)/shard_map/all_to_all | solution.py:294
  14.0 7.7 %collective-permute-start = (bf16[15,32,128]{2,1,0:T(8,128)(2,1)S(1)}, bf16[15,32,128]{2,1,0:T(8,128)(2,1)S(1)}, u32[]{:S(2)}, u32[]{:S(2)}) collective-permute-start(bf16[15,32,128]{2,1,0:T(8,128)(2,1)S(1)} %copy-done.12), channel_id=1, source_target_pairs={{0,24},{24,48},{48,72},{72,0},{1,25},{25,49},{49,73},{73,1},{2,26}... | collective-permute-start | bytes 368648 | tf_op jit(solution)/shard_map/ppermute | solution.py:288
  21.7 1.9 %collective-permute-start.1 = (bf16[15,32,128]{2,1,0:T(8,128)(2,1)S(1)}, bf16[15,32,128]{2,1,0:T(8,128)(2,1)S(1)}, u32[]{:S(2)}, u32[]{:S(2)}) collective-permute-start(bf16[15,32,128]{2,1,0:T(8,128)(2,1)S(1)} %copy-done.11), channel_id=1, source_target_pairs={{0,48},{24,72},{48,0},{72,24},{1,49},{25,73},{49,1},{73,25},{2,50}... | collective-permute-start | bytes 368648 | tf_op jit(solution)/shard_map/ppermute | solution.py:288
  23.6 2.8 %collective-permute-start.2 = (bf16[15,32,128]{2,1,0:T(8,128)(2,1)S(1)}, bf16[15,32,128]{2,1,0:T(8,128)(2,1)S(1)}, u32[]{:S(2)}, u32[]{:S(2)}) collective-permute-start(bf16[15,32,128]{2,1,0:T(8,128)(2,1)S(1)} %copy-done.10), channel_id=1, source_target_pairs={{0,72},{24,0},{48,24},{72,48},{1,73},{25,1},{49,25},{73,49},{2,74}... | collective-permute-start | bytes 368648 | tf_op jit(solution)/shard_map/ppermute | solution.py:288
  26.4 0.9 slice.7
  27.3 8.6 %collective-permute-start.4 = (bf16[72,512]{1,0:T(8,128)(2,1)S(1)}, bf16[72,512]{1,0:T(8,128)(2,1)S(1)}, u32[]{:S(2)}, u32[]{:S(2)}) collective-permute-start(bf16[72,512]{1,0:T(8,128)(2,1)S(1)} %slice.7), channel_id=1, source_target_pairs={{8,0},{16,8},{24,16},{32,24},{40,32},{48,40},{56,48},{64,56},{72,6... | collective-permute-start | bytes 221192 | tf_op jit(solution)/shard_map/ppermute | solution.py:284
  35.9 0.7 reshape.33.labels
  36.6 4.7 %shard_map.96 = (bf16[3,144,512]{2,1,0:T(8,128)(2,1)}, bf16[3,144,256]{2,1,0:T(8,128)(2,1)}, f32[3,144,144]{2,1,0:T(8,128)}) custom-call(bf16[8,72,512]{2,1,0:T(8,128)(2,1)} %bitcast.10, bf16[8,72,512]{2,1,0:T(8,128)(2,1)} %bitcast.11, s32[4,144]{1,0:T(4,128)} %reshape.33.labels, bf16[192,512]{1,0:T(8,128)(2,1)} %bitcast.19), custom_call_target="tpu_custom_call" | custom-call | flops 100000000 | bytes 2097152 | tf_op jit(solution)/shard_map/pallas_call | solution.py:57
  41.3 0.1 add_convert_fusion.__
  41.4 0.9 copy-done.1
  42.2 0.3 shard_map.97
  42.5 15.4 %all-gather = bf16[576,512]{1,0:T(8,128)(2,1)S(1)} all-gather(bf16[72,512]{1,0:T(8,128)(2,1)S(1)} %get-tuple-element.29), channel_id=2, replica_groups=mesh['y'=8,'x'=4,'zh'=3,'zl'=4,'core'=2] {'zl','core'}, dimensions={0}, use_global_device_ids=true | all-gather | bytes 663552 | tf_op jit(solution)/shard_map/all_gather | solution.py:327
  57.9 3.8 %collective-permute-start.3 = (bf16[72,512]{1,0:T(8,128)(2,1)S(1)}, bf16[72,512]{1,0:T(8,128)(2,1)S(1)}, u32[]{:S(2)}, u32[]{:S(2)}) collective-permute-start(bf16[72,512]{1,0:T(8,128)(2,1)S(1)} %slice.9), channel_id=1, source_target_pairs={{8,0},{16,8},{24,16},{32,24},{40,32},{48,40},{56,48},{64,56},{72,6... | collective-permute-start | bytes 221192 | tf_op jit(solution)/shard_map/ppermute | solution.py:284
  61.8 5.5 %shard_map.98 = (bf16[6,72,512]{2,1,0:T(8,128)(2,1)}, f32[512,192]{1,0:T(8,128)}, f32[64,512]{1,0:T(8,128)}) custom-call(bf16[8,72,512]{2,1,0:T(8,128)(2,1)} %bitcast.16, bf16[8,72,512]{2,1,0:T(8,128)(2,1)} %bitcast.17, bf16[3,144,512]{2,1,0:T(8,128)(2,1)} %get-tuple-element.30.refs_0_, bf16[3,144,256]{2,1,0:T(8,128)(2,1)} %get-tuple-element.31.refs_1_, ...), custom_call_target="tpu_custom_call" | custom-call | flops 100000000 | bytes 2097152 | tf_op jit(solution)/shard_map/pallas_call | solution.py:57
  67.3 4.8 %collective-permute-done.3.far = bf16[72,512]{1,0:T(8,128)(2,1)S(1)} collective-permute-done((bf16[72,512]{1,0:T(8,128)(2,1)S(1)}, bf16[72,512]{1,0:T(8,128)(2,1)S(1)}, u32[]{:S(2)}, u32[]{:S(2)}) %collective-permute-start.3) | collective-permute-done | bytes 73760 | tf_op jit(solution)/shard_map/ppermute | solution.py:284
  72.1 0.6 copy-done.7
  72.7 4.0 %shard_map.99 = (bf16[8,72,512]{2,1,0:T(8,128)(2,1)}, bf16[9,32,128]{2,1,0:T(8,128)(2,1)}, bf16[9,32,128]{2,1,0:T(8,128)(2,1)}, bf16[9,32,128]{2,1,0:T(8,128)(2,1)}, bf16[9,32,128]{2,1,0:T(8,128)(2,1)}) custom-call(s32[1]{0:T(128)} %bitcast.1.place, bf16[8,72,512]{2,1,0:T(8,128)(2,1)} %bitcast.18, bf16[72,512]{1,0:T(8,128)(2,1)} %copy-done.7, ...), custom_call_target="tpu_custom_call" | custom-call | flops 100000000 | bytes 2097152 | tf_op jit(solution)/shard_map/pallas_call | solution.py:57
  76.7 3.8 %all-to-all-start.1 = ((bf16[8,72,512]{2,1,0:T(8,128)(2,1)}), bf16[8,72,512]{2,1,0:T(8,128)(2,1)S(1)}, u32[]{:S(2)}, u32[]{:S(2)}) async-start(bf16[8,72,512]{2,1,0:T(8,128)(2,1)} %get-tuple-element.36), calls=%async_computation.1 | async-start | bytes 1179648 | tf_op jit(solution)/shard_map/all_to_all | solution.py:377
  80.5 6.3 %collective-permute-start.6 = (bf16[9,32,128]{2,1,0:T(8,128)(2,1)S(1)}, bf16[9,32,128]{2,1,0:T(8,128)(2,1)S(1)}, u32[]{:S(2)}, u32[]{:S(2)}) collective-permute-start(bf16[9,32,128]{2,1,0:T(8,128)(2,1)S(1)} %copy-done.15), channel_id=1, source_target_pairs={{0,24},{24,48},{48,72},{72,0},{1,25},{25,49},{49,73},{73,1},{2,26}... | collective-permute-start | bytes 221192 | tf_op jit(solution)/shard_map/ppermute | solution.py:288
  86.8 1.9 %collective-permute-start.7 = (bf16[9,32,128]{2,1,0:T(8,128)(2,1)S(1)}, bf16[9,32,128]{2,1,0:T(8,128)(2,1)S(1)}, u32[]{:S(2)}, u32[]{:S(2)}) collective-permute-start(bf16[9,32,128]{2,1,0:T(8,128)(2,1)S(1)} %copy-done.14), channel_id=1, source_target_pairs={{0,48},{24,72},{48,0},{72,24},{1,49},{25,73},{49,1},{73,25},{2,50}... | collective-permute-start | bytes 221192 | tf_op jit(solution)/shard_map/ppermute | solution.py:288
  88.8 2.8 %collective-permute-start.8 = (bf16[9,32,128]{2,1,0:T(8,128)(2,1)S(1)}, bf16[9,32,128]{2,1,0:T(8,128)(2,1)S(1)}, u32[]{:S(2)}, u32[]{:S(2)}) collective-permute-start(bf16[9,32,128]{2,1,0:T(8,128)(2,1)S(1)} %copy-done.13), channel_id=1, source_target_pairs={{0,72},{24,0},{48,24},{72,48},{1,73},{25,1},{49,25},{73,49},{2,74}... | collective-permute-start | bytes 221192 | tf_op jit(solution)/shard_map/ppermute | solution.py:288
  91.6 3.1 %collective-permute-done.7 = bf16[9,32,128]{2,1,0:T(8,128)(2,1)S(1)} collective-permute-done((bf16[9,32,128]{2,1,0:T(8,128)(2,1)S(1)}, bf16[9,32,128]{2,1,0:T(8,128)(2,1)S(1)}, u32[]{:S(2)}, u32[]{:S(2)}) %collective-permute-start.7) | collective-permute-done | bytes 73760 | tf_op jit(solution)/shard_map/ppermute | solution.py:288
  94.6 1.6 %collective-permute-done.8 = bf16[9,32,128]{2,1,0:T(8,128)(2,1)S(1)} collective-permute-done((bf16[9,32,128]{2,1,0:T(8,128)(2,1)S(1)}, bf16[9,32,128]{2,1,0:T(8,128)(2,1)S(1)}, u32[]{:S(2)}, u32[]{:S(2)}) %collective-permute-start.8) | collective-permute-done | bytes 73760 | tf_op jit(solution)/shard_map/ppermute | solution.py:288
  96.3 0.7 pad_maximum_fusion
  97.0 0.2 all-to-all-done.1.parts
  97.3 12.3 %all-to-all-start.2 = ((bf16[24,32,128]{2,1,0:T(8,128)(2,1)}), bf16[24,32,128]{2,1,0:T(8,128)(2,1)S(1)}, u32[]{:S(2)}, u32[]{:S(2)}) async-start(bf16[24,32,128]{2,1,0:T(8,128)(2,1)} %pad_maximum_fusion), calls=%async_computation.2 | async-start | bytes 393216 | tf_op jit(solution)/shard_map/all_to_all | solution.py:264
  109.6 0.1 shard_map.100
  109.7 7.7 %collective-permute-start.5 = (bf16[72,512]{1,0:T(8,128)(2,1)S(1)}, bf16[72,512]{1,0:T(8,128)(2,1)S(1)}, u32[]{:S(2)}, u32[]{:S(2)}) collective-permute-start(bf16[72,512]{1,0:T(8,128)(2,1)S(1)} %get-tuple-element.38), channel_id=1, source_target_pairs={{0,8},{8,16},{16,24},{24,32},{32,40},{40,48},{48,56},{56,64},{64,7... | collective-permute-start | bytes 221192 | tf_op jit(solution)/shard_map/ppermute | solution.py:387
  117.3 7.6 %all-to-all-done.2 = bf16[24,32,128]{2,1,0:T(8,128)(2,1)S(1)} async-done(((bf16[24,32,128]{2,1,0:T(8,128)(2,1)}), bf16[24,32,128]{2,1,0:T(8,128)(2,1)S(1)}, u32[]{:S(2)}, u32[]{:S(2)}) %all-to-all-start.2) | async-done | bytes 196640 | tf_op jit(solution)/shard_map/all_to_all | solution.py:264
  125.0 0.6 convert_reduce_fusion
  125.6 0.9 shard_map.101
  (39 shorter events, 0.1 us)
Async XLA Ops:
  6.5 7.4 %copy-start.12 = (bf16[15,32,128]{2,1,0:T(8,128)(2,1)S(1)}, bf16[15,32,128]{2,1,0:T(8,128)(2,1)}, u32[]{:S(2)}) copy-start(bf16[15,32,128]{2,1,0:T(8,128)(2,1)} %get-tuple-element.26) | copy-start | bytes 368644
  6.5 15.2 %copy-start.11 = (bf16[15,32,128]{2,1,0:T(8,128)(2,1)S(1)}, bf16[15,32,128]{2,1,0:T(8,128)(2,1)}, u32[]{:S(2)}) copy-start(bf16[15,32,128]{2,1,0:T(8,128)(2,1)} %get-tuple-element.27) | copy-start | bytes 368644
  6.5 17.1 %copy-start.10 = (bf16[15,32,128]{2,1,0:T(8,128)(2,1)S(1)}, bf16[15,32,128]{2,1,0:T(8,128)(2,1)}, u32[]{:S(2)}) copy-start(bf16[15,32,128]{2,1,0:T(8,128)(2,1)} %get-tuple-element.28) | copy-start | bytes 368644
  6.5 34.8 %all-to-all-start = ((bf16[8,72,512]{2,1,0:T(8,128)(2,1)}), bf16[8,72,512]{2,1,0:T(8,128)(2,1)S(1)}, u32[]{:S(2)}, u32[]{:S(2)}) async-start(bf16[8,72,512]{2,1,0:T(8,128)(2,1)} %get-tuple-element.23), calls=%async_computation | async-start | bytes 1179648 | tf_op jit(solution)/shard_map/all_to_all | solution.py:294
  14.0 27.3 %collective-permute-start = (bf16[15,32,128]{2,1,0:T(8,128)(2,1)S(1)}, bf16[15,32,128]{2,1,0:T(8,128)(2,1)S(1)}, u32[]{:S(2)}, u32[]{:S(2)}) collective-permute-start(bf16[15,32,128]{2,1,0:T(8,128)(2,1)S(1)} %copy-done.12), channel_id=1, source_target_pairs={{0,24},{24,48},{48,72},{72,0},{1,25},{25,49},{49,73},{73,1},{2,26}... | collective-permute-start | bytes 368648 | tf_op jit(solution)/shard_map/ppermute | solution.py:288
  21.7 19.6 %collective-permute-start.1 = (bf16[15,32,128]{2,1,0:T(8,128)(2,1)S(1)}, bf16[15,32,128]{2,1,0:T(8,128)(2,1)S(1)}, u32[]{:S(2)}, u32[]{:S(2)}) collective-permute-start(bf16[15,32,128]{2,1,0:T(8,128)(2,1)S(1)} %copy-done.11), channel_id=1, source_target_pairs={{0,48},{24,72},{48,0},{72,24},{1,49},{25,73},{49,1},{73,25},{2,50}... | collective-permute-start | bytes 368648 | tf_op jit(solution)/shard_map/ppermute | solution.py:288
  23.6 17.6 %collective-permute-start.2 = (bf16[15,32,128]{2,1,0:T(8,128)(2,1)S(1)}, bf16[15,32,128]{2,1,0:T(8,128)(2,1)S(1)}, u32[]{:S(2)}, u32[]{:S(2)}) collective-permute-start(bf16[15,32,128]{2,1,0:T(8,128)(2,1)S(1)} %copy-done.10), channel_id=1, source_target_pairs={{0,72},{24,0},{48,24},{72,48},{1,73},{25,1},{49,25},{73,49},{2,74}... | collective-permute-start | bytes 368648 | tf_op jit(solution)/shard_map/ppermute | solution.py:288
  26.4 9.5 %copy-start.9 = (s32[576]{0:T(1024)S(1)}, s32[576]{0:T(1024)}, u32[]{:S(2)}) copy-start(s32[576]{0:T(1024)} %param.11) | copy-start | bytes 6916
  27.3 40.0 %collective-permute-start.4 = (bf16[72,512]{1,0:T(8,128)(2,1)S(1)}, bf16[72,512]{1,0:T(8,128)(2,1)S(1)}, u32[]{:S(2)}, u32[]{:S(2)}) collective-permute-start(bf16[72,512]{1,0:T(8,128)(2,1)S(1)} %slice.7), channel_id=1, source_target_pairs={{8,0},{16,8},{24,16},{32,24},{40,32},{48,40},{56,48},{64,56},{72,6... | collective-permute-start | bytes 221192 | tf_op jit(solution)/shard_map/ppermute | solution.py:284
  36.6 4.7 %copy-start.5 = (bf16[15,32,128]{2,1,0:T(8,128)(2,1)S(1)}, bf16[15,32,128]{2,1,0:T(8,128)(2,1)}, u32[]{:S(2)}) copy-start(bf16[15,32,128]{2,1,0:T(8,128)(2,1)} %get-tuple-element.25) | copy-start | bytes 368644
  36.6 4.8 %copy-start.2 = (bf16[576,512]{1,0:T(8,128)(2,1)S(1)}, bf16[576,512]{1,0:T(8,128)(2,1)}, u32[]{:S(2)}) copy-start(bf16[576,512]{1,0:T(8,128)(2,1)} %stream.1) | copy-start | bytes 1769476
  36.6 4.8 %copy-start.3 = (bf16[576,512]{1,0:T(8,128)(2,1)S(1)}, bf16[576,512]{1,0:T(8,128)(2,1)}, u32[]{:S(2)}) copy-start(bf16[576,512]{1,0:T(8,128)(2,1)} %grad_out.1) | copy-start | bytes 1769476
  41.2 1.0 copy-start.1
  57.9 3.8 %copy-start.4 = (bf16[576,512]{1,0:T(8,128)(2,1)}, bf16[576,512]{1,0:T(8,128)(2,1)S(1)}, u32[]{:S(2)}) copy-start(bf16[576,512]{1,0:T(8,128)(2,1)S(1)} %all-gather) | copy-start | bytes 1769476
  57.9 14.1 %collective-permute-start.3 = (bf16[72,512]{1,0:T(8,128)(2,1)S(1)}, bf16[72,512]{1,0:T(8,128)(2,1)S(1)}, u32[]{:S(2)}, u32[]{:S(2)}) collective-permute-start(bf16[72,512]{1,0:T(8,128)(2,1)S(1)} %slice.9), channel_id=1, source_target_pairs={{8,0},{16,8},{24,16},{32,24},{40,32},{48,40},{56,48},{64,56},{72,6... | collective-permute-start | bytes 221192 | tf_op jit(solution)/shard_map/ppermute | solution.py:284
  67.3 4.8 %copy-start.6 = (bf16[72,512]{1,0:T(8,128)(2,1)}, bf16[72,512]{1,0:T(8,128)(2,1)S(1)}, u32[]{:S(2)}) copy-start(bf16[72,512]{1,0:T(8,128)(2,1)S(1)} %collective-permute-done.4.tail) | copy-start | bytes 221188
  72.0 0.6 copy-start.7
  76.7 3.8 %copy-start.15 = (bf16[9,32,128]{2,1,0:T(8,128)(2,1)S(1)}, bf16[9,32,128]{2,1,0:T(8,128)(2,1)}, u32[]{:S(2)}) copy-start(bf16[9,32,128]{2,1,0:T(8,128)(2,1)} %get-tuple-element.41) | copy-start | bytes 221188
  76.7 10.1 %copy-start.14 = (bf16[9,32,128]{2,1,0:T(8,128)(2,1)S(1)}, bf16[9,32,128]{2,1,0:T(8,128)(2,1)}, u32[]{:S(2)}) copy-start(bf16[9,32,128]{2,1,0:T(8,128)(2,1)} %get-tuple-element.42) | copy-start | bytes 221188
  76.7 12.1 %copy-start.13 = (bf16[9,32,128]{2,1,0:T(8,128)(2,1)S(1)}, bf16[9,32,128]{2,1,0:T(8,128)(2,1)}, u32[]{:S(2)}) copy-start(bf16[9,32,128]{2,1,0:T(8,128)(2,1)} %get-tuple-element.43) | copy-start | bytes 221188
  76.7 19.5 %copy-start.8 = (bf16[9,32,128]{2,1,0:T(8,128)(2,1)S(1)}, bf16[9,32,128]{2,1,0:T(8,128)(2,1)}, u32[]{:S(2)}) copy-start(bf16[9,32,128]{2,1,0:T(8,128)(2,1)} %get-tuple-element.40) | copy-start | bytes 221188
  76.7 20.5 %all-to-all-start.1 = ((bf16[8,72,512]{2,1,0:T(8,128)(2,1)}), bf16[8,72,512]{2,1,0:T(8,128)(2,1)S(1)}, u32[]{:S(2)}, u32[]{:S(2)}) async-start(bf16[8,72,512]{2,1,0:T(8,128)(2,1)} %get-tuple-element.36), calls=%async_computation.1 | async-start | bytes 1179648 | tf_op jit(solution)/shard_map/all_to_all | solution.py:377
  80.5 11.1 %collective-permute-start.6 = (bf16[9,32,128]{2,1,0:T(8,128)(2,1)S(1)}, bf16[9,32,128]{2,1,0:T(8,128)(2,1)S(1)}, u32[]{:S(2)}, u32[]{:S(2)}) collective-permute-start(bf16[9,32,128]{2,1,0:T(8,128)(2,1)S(1)} %copy-done.15), channel_id=1, source_target_pairs={{0,24},{24,48},{48,72},{72,0},{1,25},{25,49},{49,73},{73,1},{2,26}... | collective-permute-start | bytes 221192 | tf_op jit(solution)/shard_map/ppermute | solution.py:288
  86.8 7.8 %collective-permute-start.7 = (bf16[9,32,128]{2,1,0:T(8,128)(2,1)S(1)}, bf16[9,32,128]{2,1,0:T(8,128)(2,1)S(1)}, u32[]{:S(2)}, u32[]{:S(2)}) collective-permute-start(bf16[9,32,128]{2,1,0:T(8,128)(2,1)S(1)} %copy-done.14), channel_id=1, source_target_pairs={{0,48},{24,72},{48,0},{72,24},{1,49},{25,73},{49,1},{73,25},{2,50}... | collective-permute-start | bytes 221192 | tf_op jit(solution)/shard_map/ppermute | solution.py:288
  88.8 7.5 %collective-permute-start.8 = (bf16[9,32,128]{2,1,0:T(8,128)(2,1)S(1)}, bf16[9,32,128]{2,1,0:T(8,128)(2,1)S(1)}, u32[]{:S(2)}, u32[]{:S(2)}) collective-permute-start(bf16[9,32,128]{2,1,0:T(8,128)(2,1)S(1)} %copy-done.13), channel_id=1, source_target_pairs={{0,72},{24,0},{48,24},{72,48},{1,73},{25,1},{49,25},{73,49},{2,74}... | collective-permute-start | bytes 221192 | tf_op jit(solution)/shard_map/ppermute | solution.py:288
  97.0 28.6 %copy-start = (bf16[576,512]{1,0:T(8,128)(2,1)S(1)}, bf16[576,512]{1,0:T(8,128)(2,1)}, u32[]{:S(2)}) copy-start(bf16[576,512]{1,0:T(8,128)(2,1)} %param.8) | copy-start | bytes 1769476
  97.3 27.7 %all-to-all-start.2 = ((bf16[24,32,128]{2,1,0:T(8,128)(2,1)}), bf16[24,32,128]{2,1,0:T(8,128)(2,1)S(1)}, u32[]{:S(2)}, u32[]{:S(2)}) async-start(bf16[24,32,128]{2,1,0:T(8,128)(2,1)} %pad_maximum_fusion), calls=%async_computation.2 | async-start | bytes 393216 | tf_op jit(solution)/shard_map/all_to_all | solution.py:264
  109.7 15.9 %collective-permute-start.5 = (bf16[72,512]{1,0:T(8,128)(2,1)S(1)}, bf16[72,512]{1,0:T(8,128)(2,1)S(1)}, u32[]{:S(2)}, u32[]{:S(2)}) collective-permute-start(bf16[72,512]{1,0:T(8,128)(2,1)S(1)} %get-tuple-element.38), channel_id=1, source_target_pairs={{0,8},{8,16},{16,24},{24,32},{32,40},{40,48},{48,56},{56,64},{64,7... | collective-permute-start | bytes 221192 | tf_op jit(solution)/shard_map/ppermute | solution.py:387

commit v6 on v5

--- a/solution.py
+++ b/solution.py
@@ -45,7 +45,7 @@
 ANY = pl.BlockSpec(memory_space=pl.ANY)
 
 
-def call(kernel, grid, ins, outs, args, scratch=(), chosen=None, flops=10**8, vmem=60):
+def call(kernel, grid, ins, outs, args, scratch=(), chosen=None, flops=10**8, vmem=60, aliases=None):
     spec = pltpu.PrefetchScalarGridSpec(
         num_scalar_prefetch=0 if chosen is None else 1,
         grid=grid,
@@ -58,7 +58,8 @@
         kernel,
         grid_spec=spec,
         out_shape=[jax.ShapeDtypeStruct(out[0], out[1]) for out in outs],
-        compiler_params=pltpu.CompilerParams(vmem_limit_bytes=vmem * 2**20),
+        input_output_aliases=aliases or {},
+        compiler_params=pltpu.CompilerParams(vmem_limit_bytes=int(vmem * 2**20)),
         cost_estimate=pl.CostEstimate(flops=flops, bytes_accessed=2 * 2**20, transcendentals=0),
     )(*first, *args)
 
@@ -69,8 +70,7 @@
 
 
 def mlp_kernel(
-    place, stream, grad_out, up_weight, down_weight, unit_grad, first, second, third, fourth, early,
-    up_sum, down_sum, rows_f32, pieces,
+    stream, grad_out, up_weight, down_weight, unit_grad, late, early, up_sum, down_sum, rows_f32
 ):
     step = pl.program_id(0)
     unit = normalize(stream[...])[0].astype(BF)
@@ -110,39 +110,33 @@
                     :, 128 * column : 128 * column + 128
                 ]
             base += rows * wide
-        slots = [lax.rem(x - place[0] + 4, 4) for x in range(4)]
         for owner in range(32, 96):
             block = rows_f32[32 * (owner - 32) : 32 * (owner - 31), :].astype(BF)
             if owner < 36:
                 early[owner - 32] = block
             else:
-                pieces[slots[owner % 12 // 3], owner // 12 * 3 + owner % 3 - 9] = block
-        for slot, out in enumerate((first, second, third, fourth)):
-            out[...] = pieces[slot]
-
-
-def mlp(x_place, stream, grad_out, up_weight, down_weight):
+                late[owner % 12 // 3, owner // 12 * 3 + owner % 3 - 9] = block
+
+
+def mlp(stream, grad_out, up_weight, down_weight):
     rows, width = stream.shape
     units = up_weight.shape[1]
-    part = lambda columns: pl.BlockSpec((WIN, columns), lambda i, s: (i, 0))
-    late = jax.ShapeDtypeStruct((15,) + BLOCK, BF)
+    part = lambda columns: pl.BlockSpec((WIN, columns), lambda i: (i, 0))
+    late = jax.ShapeDtypeStruct((4, 15) + BLOCK, BF)
     early = jax.ShapeDtypeStruct((4,) + BLOCK, BF)
     return call(
         mlp_kernel,
         (rows // WIN,),
         [part(width), part(width), whole(up_weight), whole(down_weight)],
-        [((rows // HALF, HALF, width), BF, pl.BlockSpec((2, HALF, width), lambda i, s: (i, 0, 0)))]
-        + [(late.shape, BF, whole(late))] * 4
-        + [(early.shape, BF, whole(early))],
+        [((rows // HALF, HALF, width), BF, pl.BlockSpec((2, HALF, width), lambda i: (i, 0, 0)))]
+        + [(late.shape, BF, whole(late)), (early.shape, BF, whole(early))],
         (stream, grad_out, up_weight, down_weight),
         scratch=[
             pltpu.VMEM((width, units), F32),
             pltpu.VMEM((units, width), F32),
             pltpu.VMEM((64 * 32, 128), F32),
-            pltpu.VMEM((4, 15) + BLOCK, BF),
-        ],
-        chosen=x_place,
-        flops=10 * rows * width * units,
+        ],
+        flops=69 * 10**8,
     )
 
 
@@ -162,16 +156,20 @@
     return inputs, (query, key, value, attended), probs
 
 
-def forward_kernel(lead, tail, labels, turned_qkv, hidden, packed, probs_out):
+def forward_kernel(
+    place, lead, tail, labels, turned_qkv, stream, grad_out, hidden, packed, probs_out, own
+):
     row = labels[pl.ds(pl.program_id(0), 1), :]
     hidden[0], parts, probs_out[0] = window_forward(lead[0], tail[0], row, turned_qkv)
     packed[0] = jnp.concatenate(parts, axis=1)
-
-
-def middle_kernel(place, parts, stream, grad_out, _, __, mid, grad_mid):
+    own[0] = stream[0]
+    own[1] = grad_out[0]
+
+
+def middle_kernel(parts, own, _, mid, grad_mid, __):
     summed = jnp.sum(parts[...].astype(F32), axis=0)
-    normed, factor = normalize(stream[0])
-    middle = grad_out[0].astype(F32) + norm_back(normed, factor, summed)
+    normed, factor = normalize(own[0])
+    middle = own[1].astype(F32) + norm_back(normed, factor, summed)
     mid[...] = middle
     grad_mid[...] = middle.astype(BF)
 
@@ -254,15 +252,24 @@
     total_b[...] = total[...].astype(BF)
 
 
-def final_kernel(place, summed, arrived, mid, block_input, grad_input):
+def final_kernel(place, summed, arrived, mid, block_input, grad_input, token):
     total = jnp.where(place[0] == 0, arrived[...].astype(F32), summed[...])
     normed, factor = normalize(block_input[0])
     grad_input[...] = (mid[...] + norm_back(normed, factor, total)).astype(BF)
-
-
-def exchange(pieces, axis):
-    received = lax.all_to_all(pieces, axis, 0, 0)
-    return jnp.sum(received.astype(F32), axis=0)
+    token[...] = jnp.zeros_like(token)
+
+
+def join_kernel(first, second, third, fourth, late, joined):
+    count = first.shape[0]
+    near = (first[...].astype(F32) + second[...].astype(F32)) + (
+        third[...].astype(F32) + fourth[...].astype(F32)
+    )
+    joined[:count] = near.astype(BF)
+    joined[count:] = jnp.sum(late[...].astype(F32), axis=0).astype(BF)
+
+
+def total_kernel(received, _, owned):
+    owned[...] = jnp.sum(received[...].astype(F32), axis=0)
 
 
 def shards(block_input, stream, grad_out, regions, qkv_weight, out_weight, up_weight, down_weight):
@@ -283,45 +290,49 @@
     def from_next(values):
         return lax.ppermute(values, WIN_AXES, [((i + 1) % count, i) for i in range(count)])
 
-    def along_x(pieces):
-        moved = [
-            lax.ppermute(pieces[k], "x", [(i, (i + k) % 4) for i in range(4)]) for k in range(1, 4)
-        ]
-        return sum(piece.astype(F32) for piece in [pieces[0]] + moved).astype(BF)
-
     far_input = from_next(block_input[:HALF])
-    unit_grad, *late, early = mlp(x_place, stream, grad_out, up_weight, down_weight)
+    unit_grad, late, early = mlp(stream, grad_out, up_weight, down_weight)
     parts = lax.all_to_all(unit_grad, HEAD_AXES, 0, 0)
-    late_sum = along_x(late)
     labels = regions.reshape(windows, WIN)
-    window = lambda columns: pl.BlockSpec((1, WIN, columns), lambda i: (i, 0, 0))
+    window = lambda columns: pl.BlockSpec((1, WIN, columns), lambda i, *_: (i, 0, 0))
     weights = (turned_qkv.reshape(-1, width), out_weight)
     near = windows - 1
-    hidden, packed, probs = call(
+    token = jax.ShapeDtypeStruct((8, 128), F32)
+    row_part = jax.ShapeDtypeStruct((share_rows, width), BF)
+    mine = pl.BlockSpec(chunk, lambda i, place: (place[0], 0, 0))
+    own_rows = jax.ShapeDtypeStruct((2, share_rows, width), BF)
+    hidden, packed, probs, own = call(
         forward_kernel,
         (near,),
         [
-            pl.BlockSpec(chunk, lambda i: (2 * i + 1, 0, 0)),
-            pl.BlockSpec(chunk, lambda i: (2 * i + 2, 0, 0)),
+            pl.BlockSpec(chunk, lambda i, _: (2 * i + 1, 0, 0)),
+            pl.BlockSpec(chunk, lambda i, _: (2 * i + 2, 0, 0)),
             whole(labels),
             whole(weights[0]),
+            mine,
+            mine,
         ],
         [
             ((near, WIN, width), BF, window(width)),
             ((near, WIN, 4 * columns), BF, window(4 * columns)),
             ((near, WIN, WIN), F32, window(WIN)),
-        ],
-        (chunks_in, chunks_in, labels, weights[0]),
-    )
-    mine = pl.BlockSpec(chunk, lambda i, place: (place[0], 0, 0))
-    row_part = jax.ShapeDtypeStruct((share_rows, width), BF)
-    mid, own_grad_mid = call(
+            (own_rows.shape, BF, whole(own_rows)),
+        ],
+        (chunks_in, chunks_in, labels, weights[0], chunks_mid, chunks_out),
+        chosen=head_place,
+        flops=53 * 10**8,
+    )
+    mid, own_grad_mid, late = call(
         middle_kernel,
         (1,),
-        [whole(parts), mine, mine, ANY, ANY],
-        [(row_part.shape, F32, whole(row_part)), (row_part.shape, BF, whole(row_part))],
-        (parts, chunks_mid, chunks_out, probs, late_sum),
-        chosen=head_place,
+        [whole(parts), whole(own), ANY],
+        [
+            (row_part.shape, F32, whole(row_part)),
+            (row_part.shape, BF, whole(row_part)),
+            (late.shape, BF, ANY),
+        ],
+        (parts, own, late),
+        aliases={2: 2},
         vmem=16,
     )
     grad_mid = lax.all_gather(own_grad_mid, HEAD_AXES, axis=0)
@@ -343,8 +354,10 @@
             ((columns, width), F32, VMEM),
         ],
         (grad_mid, grad_mid, hidden, packed, probs, *weights),
-        vmem=56,
-    )
+        flops=37 * 10**8,
+        vmem=24,
+    )
+    late_parts = lax.all_to_all(late, "x", 0, 0)
     piece = jax.ShapeDtypeStruct((9,) + BLOCK, BF)
     in_grad, *pieces = call(
         far_kernel,
@@ -373,9 +386,21 @@
         ],
         chosen=x_place,
         vmem=56,
+        flops=46 * 10**8,
     )
     in_parts = lax.all_to_all(in_grad, HEAD_AXES, 0, 0)
-    early_sum = along_x(pieces)
+    moved = [
+        lax.ppermute(pieces[k], "x", [(i, (i + k) % 4) for i in range(4)]) for k in range(1, 4)
+    ]
+    joined = jax.ShapeDtypeStruct((24,) + BLOCK, BF)
+    (partial_sum,) = call(
+        join_kernel,
+        (1,),
+        [whole(piece)] * 4 + [whole(late_parts)],
+        [(joined.shape, BF, whole(joined))],
+        (pieces[0], *moved, late_parts),
+        vmem=16,
+    )
     summed, summed_b = call(
         sum_kernel,
         (1,),
@@ -389,14 +414,23 @@
         WIN_AXES + HEAD_AXES,
         [(i * head_count, (i + 1) % count * head_count) for i in range(count)],
     )
-    owned = exchange(jnp.concatenate([early_sum, late_sum], 0), ("y", "zh"))
-    (grad_input,) = call(
+    received = lax.all_to_all(partial_sum, ("y", "zh"), 0, 0)
+    grad_input, ready = call(
         final_kernel,
         (1,),
         [whole(summed), whole(arrived), whole(mid), mine],
-        [(row_part.shape, BF, whole(row_part))],
+        [(row_part.shape, BF, whole(row_part)), (token.shape, F32, whole(token))],
         (summed, arrived, mid, chunks_in),
         chosen=head_place,
+        vmem=16,
+    )
+    owner_block = jax.ShapeDtypeStruct(BLOCK, F32)
+    (owned,) = call(
+        total_kernel,
+        (1,),
+        [whole(received), ANY],
+        [(BLOCK, F32, whole(owner_block))],
+        (received, ready),
         vmem=16,
     )
     return (grad_input, owned.reshape(1, -1))

time: 128 us -> 130 us (1.016)
  local copies, waits for them, and re-layouts: 3.13 us -> 6.07 us
  other arithmetic: 1.45 us -> 0 us
  blocking collectives: 15.4 us -> 16.8 us
    ppermute x6 -> x3, starting transfers between devices: 23.4 us -> 8.68 us  [shards(): lax.ppermute(pieces[k], 'x', [(i, (i + k) % 4) for i in range(4)])]
    ppermute x2, starting transfers between devices: 12.4 us -> 22.7 us  [from_next(): lax.ppermute(values, WIN_AXES, [((i + 1) % count, i) for i in range(count)])]
    all_to_all x1 -> x2, starting transfers between devices: 12.3 us -> 17.5 us  [the longest x1 8.9 us: shards(): late_parts = lax.all_to_all(late, 'x', 0, 0)]
    ppermute x2, waiting for transfers between devices: 4.76 us -> 0.01 us  [from_next(): lax.ppermute(values, WIN_AXES, [((i + 1) % count, i) for i in range(count)])]
    all_to_all x1 -> x2, waiting for transfers between devices: 7.62 us -> 4.1 us  [the longest x1 4.1 us: shards(): received = lax.all_to_all(partial_sum, ('y', 'zh'), 0, 0)]
    ppermute x1, waiting for transfers between devices: 0.01 us -> 3.39 us  [shards(): lax.ppermute(summed_b, WIN_AXES + HEAD_AXES, [(i * head_count, (i + 1) %...]
    all_to_all x1, waiting for transfers between devices: 0.01 us -> 2.98 us  [shards(): parts = lax.all_to_all(unit_grad, HEAD_AXES, 0, 0)]
    unnamed x32 -> x36, local copies, waits for them, and re-layouts: 1.55 us -> 4.5 us
  transfers between devices with their start and end apart: 12 -> 10, of which waited for: 5 -> 6; matrix products, arithmetic and copies ran while one was open for 2% -> 1% of each run, Pallas kernels for 8% -> 11%
where the time goes in v6:
time: 130 us; the launch traced here: 129 us
  starting transfers between devices  67.5 us (52%)
  Pallas kernels  20.3 us (16%)
  waiting for transfers between devices  17.6 us (14%)
  blocking collectives  16.8 us (13%)
  local copies, waits for them, and re-layouts  6.07 us (5%)
    ppermute x2, starting transfers between devices, from_next(): lax.ppermute(values, WIN_AXES, [((i + 1) % count, i) for i in range(count)])  22.7 us
    pallas_call x9, Pallas kernels, call(): pl.pallas_call(kernel, grid_spec=spec, out_shape=[jax.ShapeDtypeStruct(ou...  20.3 us
    all_gather x1, blocking collectives, shards(): grad_mid = lax.all_gather(own_grad_mid, HEAD_AXES, axis=0)  16.8 us
    all_to_all x1, starting transfers between devices, shards(): late_parts = lax.all_to_all(late, 'x', 0, 0)  8.9 us
    ppermute x3, starting transfers between devices, shards(): lax.ppermute(pieces[k], 'x', [(i, (i + k) % 4) for i in range(4)])  8.68 us
    all_to_all x1, starting transfers between devices, shards(): received = lax.all_to_all(partial_sum, ('y', 'zh'), 0, 0)  8.61 us
    ppermute x1, starting transfers between devices, shards(): lax.ppermute(summed_b, WIN_AXES + HEAD_AXES, [(i * head_count, (i + 1) %...  7.66 us
    all_to_all x1, starting transfers between devices, shards(): parts = lax.all_to_all(unit_grad, HEAD_AXES, 0, 0)  7.27 us
  transfers between devices with their start and end apart: 10, of which 6 were waited for; matrix products, arithmetic and copies ran while one was open for 1% of the time, Pallas kernels for 11%

profile of v6, /device:TPU:6, one launch (start us, length us, event | category | flops | bytes accessed | tf_op | source)
XLA Modules:
  0.0 129.3 jit_solution(10323325803981078396)
XLA Ops:
  0.6 5.8 %shard_map.95 = (bf16[8,72,512]{2,1,0:T(8,128)(2,1)}, bf16[4,15,32,128]{3,2,1,0:T(8,128)(2,1)}, bf16[4,32,128]{2,1,0:T(8,128)(2,1)}) custom-call(bf16[576,512]{1,0:T(8,128)(2,1)} %stream.1, bf16[576,512]{1,0:T(8,128)(2,1)} %grad_out.1, bf16[512,256]{1,0:T(8,128)(2,1)} %up_weight.1, bf16[256,512]{1,0:T(8,128)(2,1)} %down_weight.1), custom_call_target="tpu_custom_call" | custom-call | flops 6899999744 | bytes 2097152 | tf_op jit(solution)/shard_map/pallas_call | solution.py:57
  6.5 7.3 %all-to-all-start = ((bf16[8,72,512]{2,1,0:T(8,128)(2,1)}), bf16[8,72,512]{2,1,0:T(8,128)(2,1)S(1)}, u32[]{:S(2)}, u32[]{:S(2)}) async-start(bf16[8,72,512]{2,1,0:T(8,128)(2,1)} %get-tuple-element.24), calls=%async_computation | async-start | bytes 1179648 | tf_op jit(solution)/shard_map/all_to_all | solution.py:295
  13.7 0.9 slice.7
  14.6 12.1 %collective-permute-start.1 = (bf16[72,512]{1,0:T(8,128)(2,1)S(1)}, bf16[72,512]{1,0:T(8,128)(2,1)S(1)}, u32[]{:S(2)}, u32[]{:S(2)}) collective-permute-start(bf16[72,512]{1,0:T(8,128)(2,1)S(1)} %slice.7), channel_id=1, source_target_pairs={{8,0},{16,8},{24,16},{32,24},{40,32},{48,40},{56,48},{64,56},{72,6... | collective-permute-start | bytes 221192 | tf_op jit(solution)/shard_map/ppermute | solution.py:291
  26.8 0.7 copy-done.12
  27.4 0.7 reshape.31.labels
  28.1 4.6 %shard_map.96 = (bf16[3,144,512]{2,1,0:T(8,128)(2,1)}, bf16[3,144,256]{2,1,0:T(8,128)(2,1)}, f32[3,144,144]{2,1,0:T(8,128)}, bf16[2,72,512]{2,1,0:T(8,128)(2,1)}) custom-call(s32[1]{0:T(128)} %bitcast.place, bf16[8,72,512]{2,1,0:T(8,128)(2,1)} %bitcast.10, bf16[8,72,512]{2,1,0:T(8,128)(2,1)} %bitcast.11, s32[4,144]{1,0:T(4,128)} %reshape.31.labels, ...), custom_call_target="tpu_custom_call" | custom-call | flops 5299999744 | bytes 2097152 | tf_op jit(solution)/shard_map/pallas_call | solution.py:57
  32.7 3.0 %all-to-all-done.parts = bf16[8,72,512]{2,1,0:T(8,128)(2,1)S(1)} async-done(((bf16[8,72,512]{2,1,0:T(8,128)(2,1)}), bf16[8,72,512]{2,1,0:T(8,128)(2,1)S(1)}, u32[]{:S(2)}, u32[]{:S(2)}) %all-to-all-start) | async-done | bytes 589856 | tf_op jit(solution)/shard_map/all_to_all | solution.py:295
  35.7 0.9 copy-done.2
  36.9 16.8 %all-gather = bf16[576,512]{1,0:T(8,128)(2,1)S(1)} all-gather(bf16[72,512]{1,0:T(8,128)(2,1)S(1)} %get-tuple-element.27), channel_id=2, replica_groups=mesh['y'=8,'x'=4,'zh'=3,'zl'=4,'core'=2] {'zl','core'}, dimensions={0}, use_global_device_ids=true | all-gather | bytes 663552 | tf_op jit(solution)/shard_map/all_gather | solution.py:338
  53.7 10.6 %collective-permute-start = (bf16[72,512]{1,0:T(8,128)(2,1)S(1)}, bf16[72,512]{1,0:T(8,128)(2,1)S(1)}, u32[]{:S(2)}, u32[]{:S(2)}) collective-permute-start(bf16[72,512]{1,0:T(8,128)(2,1)S(1)} %slice.9), channel_id=1, source_target_pairs={{8,0},{16,8},{24,16},{32,24},{40,32},{48,40},{56,48},{64,56},{72,6... | collective-permute-start | bytes 221192 | tf_op jit(solution)/shard_map/ppermute | solution.py:291
  64.4 8.9 %all-to-all-start.2 = ((bf16[4,15,32,128]{3,2,1,0:T(8,128)(2,1)}), bf16[4,15,32,128]{3,2,1,0:T(8,128)(2,1)S(1)}, u32[]{:S(2)}, u32[]{:S(2)}) async-start(bf16[4,15,32,128]{3,2,1,0:T(8,128)(2,1)} %get-tuple-element.44), calls=%async_computation.2 | async-start | bytes 983040 | tf_op jit(solution)/shard_map/all_to_all | solution.py:360
  73.4 3.1 %shard_map.98 = (bf16[6,72,512]{2,1,0:T(8,128)(2,1)S(1)}, f32[512,192]{1,0:T(8,128)S(1)}, f32[64,512]{1,0:T(8,128)S(1)}) custom-call(bf16[8,72,512]{2,1,0:T(8,128)(2,1)S(1)} %bitcast.14, bf16[8,72,512]{2,1,0:T(8,128)(2,1)S(1)} %bitcast.15, bf16[3,144,512]{2,1,0:T(8,128)(2,1)S(1)} %copy-done.7, bf16[3,144,256]{2,1,0:T(8,128)(2,1)S(1)} %copy-done.10, ...), custom_call_target="tpu_custom_call" | custom-call | flops 3700000000 | bytes 2097152 | tf_op jit(solution)/shard_map/pallas_call | solution.py:57
  76.5 0.8 copy-done.6
  77.3 0.8 copy-done.9
  78.1 0.6 copy-done.11
  78.8 0.6 copy-done.13
  79.4 4.0 %shard_map.99 = (bf16[8,72,512]{2,1,0:T(8,128)(2,1)}, bf16[9,32,128]{2,1,0:T(8,128)(2,1)}, bf16[9,32,128]{2,1,0:T(8,128)(2,1)}, bf16[9,32,128]{2,1,0:T(8,128)(2,1)}, bf16[9,32,128]{2,1,0:T(8,128)(2,1)}) custom-call(s32[1]{0:T(128)} %bitcast.1.place, bf16[8,72,512]{2,1,0:T(8,128)(2,1)} %bitcast.16, bf16[72,512]{1,0:T(8,128)(2,1)} %copy-done.17, ...), custom_call_target="tpu_custom_call" | custom-call | flops 4600000000 | bytes 2097152 | tf_op jit(solution)/shard_map/pallas_call | solution.py:57
  83.5 3.7 %all-to-all-start.1 = ((bf16[8,72,512]{2,1,0:T(8,128)(2,1)}), bf16[8,72,512]{2,1,0:T(8,128)(2,1)S(1)}, u32[]{:S(2)}, u32[]{:S(2)}) async-start(bf16[8,72,512]{2,1,0:T(8,128)(2,1)} %get-tuple-element.35), calls=%async_computation.1 | async-start | bytes 1179648 | tf_op jit(solution)/shard_map/all_to_all | solution.py:391
  87.2 2.0 %collective-permute-start.3 = (bf16[9,32,128]{2,1,0:T(8,128)(2,1)S(1)}, bf16[9,32,128]{2,1,0:T(8,128)(2,1)S(1)}, u32[]{:S(2)}, u32[]{:S(2)}) collective-permute-start(bf16[9,32,128]{2,1,0:T(8,128)(2,1)S(1)} %copy-done.16), channel_id=1, source_target_pairs={{0,24},{24,48},{48,72},{72,0},{1,25},{25,49},{49,73},{73,1},{2,26}... | collective-permute-start | bytes 221192 | tf_op jit(solution)/shard_map/ppermute | solution.py:393
  89.2 4.8 %collective-permute-start.4 = (bf16[9,32,128]{2,1,0:T(8,128)(2,1)S(1)}, bf16[9,32,128]{2,1,0:T(8,128)(2,1)S(1)}, u32[]{:S(2)}, u32[]{:S(2)}) collective-permute-start(bf16[9,32,128]{2,1,0:T(8,128)(2,1)S(1)} %copy-done.15), channel_id=1, source_target_pairs={{0,48},{24,72},{48,0},{72,24},{1,49},{25,73},{49,1},{73,25},{2,50}... | collective-permute-start | bytes 221192 | tf_op jit(solution)/shard_map/ppermute | solution.py:393
  94.0 1.9 %collective-permute-start.5 = (bf16[9,32,128]{2,1,0:T(8,128)(2,1)S(1)}, bf16[9,32,128]{2,1,0:T(8,128)(2,1)S(1)}, u32[]{:S(2)}, u32[]{:S(2)}) collective-permute-start(bf16[9,32,128]{2,1,0:T(8,128)(2,1)S(1)} %copy-done.14), channel_id=1, source_target_pairs={{0,72},{24,0},{48,24},{72,48},{1,73},{25,1},{49,25},{73,49},{2,74}... | collective-permute-start | bytes 221192 | tf_op jit(solution)/shard_map/ppermute | solution.py:393
  95.9 1.2 collective-permute-done.4.third
  97.1 4.4 %collective-permute-done.5.fourth = bf16[9,32,128]{2,1,0:T(8,128)(2,1)S(1)} collective-permute-done((bf16[9,32,128]{2,1,0:T(8,128)(2,1)S(1)}, bf16[9,32,128]{2,1,0:T(8,128)(2,1)S(1)}, u32[]{:S(2)}, u32[]{:S(2)}) %collective-permute-start.5) | collective-permute-done | bytes 73760 | tf_op jit(solution)/shard_map/ppermute | solution.py:393
  101.4 0.8 shard_map.102
  102.2 1.6 %all-to-all-done.1.parts = bf16[8,72,512]{2,1,0:T(8,128)(2,1)S(1)} async-done(((bf16[8,72,512]{2,1,0:T(8,128)(2,1)}), bf16[8,72,512]{2,1,0:T(8,128)(2,1)S(1)}, u32[]{:S(2)}, u32[]{:S(2)}) %all-to-all-start.1) | async-done | bytes 589856 | tf_op jit(solution)/shard_map/all_to_all | solution.py:391
  103.9 8.6 %all-to-all-start.3 = ((bf16[24,32,128]{2,1,0:T(8,128)(2,1)}), bf16[24,32,128]{2,1,0:T(8,128)(2,1)S(1)}, u32[]{:S(2)}, u32[]{:S(2)}) async-start(bf16[24,32,128]{2,1,0:T(8,128)(2,1)} %shard_map.102), calls=%async_computation.3 | async-start | bytes 393216 | tf_op jit(solution)/shard_map/all_to_all | solution.py:417
  112.6 7.7 %collective-permute-start.2 = (bf16[72,512]{1,0:T(8,128)(2,1)S(1)}, bf16[72,512]{1,0:T(8,128)(2,1)S(1)}, u32[]{:S(2)}, u32[]{:S(2)}) collective-permute-start(bf16[72,512]{1,0:T(8,128)(2,1)S(1)} %get-tuple-element.37), channel_id=1, source_target_pairs={{0,8},{8,16},{16,24},{24,32},{32,40},{40,48},{48,56},{56,64},{64,7... | collective-permute-start | bytes 221192 | tf_op jit(solution)/shard_map/ppermute | solution.py:412
  120.3 3.4 %collective-permute-done.2.arrived = bf16[72,512]{1,0:T(8,128)(2,1)S(1)} collective-permute-done((bf16[72,512]{1,0:T(8,128)(2,1)S(1)}, bf16[72,512]{1,0:T(8,128)(2,1)S(1)}, u32[]{:S(2)}, u32[]{:S(2)}) %collective-permute-start.2) | collective-permute-done | bytes 73760 | tf_op jit(solution)/shard_map/ppermute | solution.py:412
  123.7 0.9 shard_map.101
  124.6 4.1 %all-to-all-done.3.received = bf16[24,32,128]{2,1,0:T(8,128)(2,1)S(1)} async-done(((bf16[24,32,128]{2,1,0:T(8,128)(2,1)}), bf16[24,32,128]{2,1,0:T(8,128)(2,1)S(1)}, u32[]{:S(2)}, u32[]{:S(2)}) %all-to-all-start.3) | async-done | bytes 196640 | tf_op jit(solution)/shard_map/all_to_all | solution.py:417
  128.7 0.6 shard_map.103
  (37 shorter events, 0.5 us)
Async XLA Ops:
  6.5 29.2 %all-to-all-start = ((bf16[8,72,512]{2,1,0:T(8,128)(2,1)}), bf16[8,72,512]{2,1,0:T(8,128)(2,1)S(1)}, u32[]{:S(2)}, u32[]{:S(2)}) async-start(bf16[8,72,512]{2,1,0:T(8,128)(2,1)} %get-tuple-element.24), calls=%async_computation | async-start | bytes 1179648 | tf_op jit(solution)/shard_map/all_to_all | solution.py:295
  14.6 64.1 %collective-permute-start.1 = (bf16[72,512]{1,0:T(8,128)(2,1)S(1)}, bf16[72,512]{1,0:T(8,128)(2,1)S(1)}, u32[]{:S(2)}, u32[]{:S(2)}) collective-permute-start(bf16[72,512]{1,0:T(8,128)(2,1)S(1)} %slice.7), channel_id=1, source_target_pairs={{8,0},{16,8},{24,16},{32,24},{40,32},{48,40},{56,48},{64,56},{72,6... | collective-permute-start | bytes 221192 | tf_op jit(solution)/shard_map/ppermute | solution.py:291
  26.7 0.7 copy-start.12
  35.7 0.9 copy-start.2
  36.9 36.4 %copy-start.8 = (f32[3,144,144]{2,1,0:T(8,128)S(1)}, f32[3,144,144]{2,1,0:T(8,128)}, u32[]{:S(2)}) copy-start(f32[3,144,144]{2,1,0:T(8,128)} %get-tuple-element.30.refs_2_) | copy-start | bytes 746500
  53.7 22.8 %copy-start.1 = (bf16[576,512]{1,0:T(8,128)(2,1)}, bf16[576,512]{1,0:T(8,128)(2,1)S(1)}, u32[]{:S(2)}) copy-start(bf16[576,512]{1,0:T(8,128)(2,1)S(1)} %all-gather) | copy-start | bytes 1769476
  53.7 25.0 %collective-permute-start = (bf16[72,512]{1,0:T(8,128)(2,1)S(1)}, bf16[72,512]{1,0:T(8,128)(2,1)S(1)}, u32[]{:S(2)}, u32[]{:S(2)}) collective-permute-start(bf16[72,512]{1,0:T(8,128)(2,1)S(1)} %slice.9), channel_id=1, source_target_pairs={{8,0},{16,8},{24,16},{32,24},{40,32},{48,40},{56,48},{64,56},{72,6... | collective-permute-start | bytes 221192 | tf_op jit(solution)/shard_map/ppermute | solution.py:291
  64.4 8.9 %copy-start.4 = (bf16[3,512,64]{1,2,0:T(8,128)(2,1)S(1)}, bf16[3,512,64]{1,2,0:T(8,128)(2,1)}, u32[]{:S(2)}) copy-start(bf16[3,512,64]{1,2,0:T(8,128)(2,1)} %param.12) | copy-start | bytes 589828
  64.4 8.9 %copy-start.5 = (bf16[64,512]{1,0:T(8,128)(2,1)S(1)}, bf16[64,512]{1,0:T(8,128)(2,1)}, u32[]{:S(2)}) copy-start(bf16[64,512]{1,0:T(8,128)(2,1)} %out_weight.1) | copy-start | bytes 196612
  64.4 8.9 %copy-start.7 = (bf16[3,144,512]{2,1,0:T(8,128)(2,1)S(1)}, bf16[3,144,512]{2,1,0:T(8,128)(2,1)}, u32[]{:S(2)}) copy-start(bf16[3,144,512]{2,1,0:T(8,128)(2,1)} %get-tuple-element.28.refs_0_) | copy-start | bytes 1327108
  64.4 8.9 %copy-start.10 = (bf16[3,144,256]{2,1,0:T(8,128)(2,1)S(1)}, bf16[3,144,256]{2,1,0:T(8,128)(2,1)}, u32[]{:S(2)}) copy-start(bf16[3,144,256]{2,1,0:T(8,128)(2,1)} %get-tuple-element.29.refs_1_) | copy-start | bytes 663556
  64.4 19.0 %all-to-all-start.2 = ((bf16[4,15,32,128]{3,2,1,0:T(8,128)(2,1)}), bf16[4,15,32,128]{3,2,1,0:T(8,128)(2,1)S(1)}, u32[]{:S(2)}, u32[]{:S(2)}) async-start(bf16[4,15,32,128]{3,2,1,0:T(8,128)(2,1)} %get-tuple-element.44), calls=%async_computation.2 | async-start | bytes 983040 | tf_op jit(solution)/shard_map/all_to_all | solution.py:360
  76.5 0.8 copy-start.6
  77.3 0.8 copy-start.9
  78.1 0.6 copy-start.11
  78.8 0.6 copy-start.13
  78.8 0.6 copy-start.17
  83.5 3.7 %copy-start.16 = (bf16[9,32,128]{2,1,0:T(8,128)(2,1)S(1)}, bf16[9,32,128]{2,1,0:T(8,128)(2,1)}, u32[]{:S(2)}) copy-start(bf16[9,32,128]{2,1,0:T(8,128)(2,1)} %get-tuple-element.41) | copy-start | bytes 221188
  83.5 5.7 %copy-start.15 = (bf16[9,32,128]{2,1,0:T(8,128)(2,1)S(1)}, bf16[9,32,128]{2,1,0:T(8,128)(2,1)}, u32[]{:S(2)}) copy-start(bf16[9,32,128]{2,1,0:T(8,128)(2,1)} %get-tuple-element.42) | copy-start | bytes 221188
  83.5 10.5 %copy-start.14 = (bf16[9,32,128]{2,1,0:T(8,128)(2,1)S(1)}, bf16[9,32,128]{2,1,0:T(8,128)(2,1)}, u32[]{:S(2)}) copy-start(bf16[9,32,128]{2,1,0:T(8,128)(2,1)} %get-tuple-element.43) | copy-start | bytes 221188
  83.5 18.0 %copy-start.3 = (bf16[9,32,128]{2,1,0:T(8,128)(2,1)S(1)}, bf16[9,32,128]{2,1,0:T(8,128)(2,1)}, u32[]{:S(2)}) copy-start(bf16[9,32,128]{2,1,0:T(8,128)(2,1)} %get-tuple-element.40.first) | copy-start | bytes 221188
  83.5 20.4 %all-to-all-start.1 = ((bf16[8,72,512]{2,1,0:T(8,128)(2,1)}), bf16[8,72,512]{2,1,0:T(8,128)(2,1)S(1)}, u32[]{:S(2)}, u32[]{:S(2)}) async-start(bf16[8,72,512]{2,1,0:T(8,128)(2,1)} %get-tuple-element.35), calls=%async_computation.1 | async-start | bytes 1179648 | tf_op jit(solution)/shard_map/all_to_all | solution.py:391
  87.2 8.7 %collective-permute-start.3 = (bf16[9,32,128]{2,1,0:T(8,128)(2,1)S(1)}, bf16[9,32,128]{2,1,0:T(8,128)(2,1)S(1)}, u32[]{:S(2)}, u32[]{:S(2)}) collective-permute-start(bf16[9,32,128]{2,1,0:T(8,128)(2,1)S(1)} %copy-done.16), channel_id=1, source_target_pairs={{0,24},{24,48},{48,72},{72,0},{1,25},{25,49},{49,73},{73,1},{2,26}... | collective-permute-start | bytes 221192 | tf_op jit(solution)/shard_map/ppermute | solution.py:393
  89.2 7.9 %collective-permute-start.4 = (bf16[9,32,128]{2,1,0:T(8,128)(2,1)S(1)}, bf16[9,32,128]{2,1,0:T(8,128)(2,1)S(1)}, u32[]{:S(2)}, u32[]{:S(2)}) collective-permute-start(bf16[9,32,128]{2,1,0:T(8,128)(2,1)S(1)} %copy-done.15), channel_id=1, source_target_pairs={{0,48},{24,72},{48,0},{72,24},{1,49},{25,73},{49,1},{73,25},{2,50}... | collective-permute-start | bytes 221192 | tf_op jit(solution)/shard_map/ppermute | solution.py:393
  94.0 7.5 %collective-permute-start.5 = (bf16[9,32,128]{2,1,0:T(8,128)(2,1)S(1)}, bf16[9,32,128]{2,1,0:T(8,128)(2,1)S(1)}, u32[]{:S(2)}, u32[]{:S(2)}) collective-permute-start(bf16[9,32,128]{2,1,0:T(8,128)(2,1)S(1)} %copy-done.14), channel_id=1, source_target_pairs={{0,72},{24,0},{48,24},{72,48},{1,73},{25,1},{49,25},{73,49},{2,74}... | collective-permute-start | bytes 221192 | tf_op jit(solution)/shard_map/ppermute | solution.py:393
  102.2 21.4 %copy-start = (bf16[576,512]{1,0:T(8,128)(2,1)S(1)}, bf16[576,512]{1,0:T(8,128)(2,1)}, u32[]{:S(2)}) copy-start(bf16[576,512]{1,0:T(8,128)(2,1)} %param.8) | copy-start | bytes 1769476
  103.9 24.8 %all-to-all-start.3 = ((bf16[24,32,128]{2,1,0:T(8,128)(2,1)}), bf16[24,32,128]{2,1,0:T(8,128)(2,1)S(1)}, u32[]{:S(2)}, u32[]{:S(2)}) async-start(bf16[24,32,128]{2,1,0:T(8,128)(2,1)} %shard_map.102), calls=%async_computation.3 | async-start | bytes 393216 | tf_op jit(solution)/shard_map/all_to_all | solution.py:417
  112.6 11.1 %collective-permute-start.2 = (bf16[72,512]{1,0:T(8,128)(2,1)S(1)}, bf16[72,512]{1,0:T(8,128)(2,1)S(1)}, u32[]{:S(2)}, u32[]{:S(2)}) collective-permute-start(bf16[72,512]{1,0:T(8,128)(2,1)S(1)} %get-tuple-element.37), channel_id=1, source_target_pairs={{0,8},{8,16},{16,24},{24,32},{32,40},{40,48},{48,56},{56,64},{64,7... | collective-permute-start | bytes 221192 | tf_op jit(solution)/shard_map/ppermute | solution.py:412

commit v7 on v6

--- a/solution.py
+++ b/solution.py
@@ -166,6 +166,19 @@
     own[1] = grad_out[0]
 
 
+def last_forward_kernel(
+    lead, tail, labels, turned_qkv, _, __, ___, hidden, packed, probs_out, token
+):
+    row = labels[labels.shape[0] - 1 :, :]
+    hidden[0], parts, probs_out[0] = window_forward(lead[0], tail[...], row, turned_qkv)
+    packed[0] = jnp.concatenate(parts, axis=1)
+    token[...] = jnp.zeros_like(token)
+
+
+def give_kernel(place, own, far, _, given):
+    given[...] = jnp.where(place[0] == 0, far[...].astype(F32), own[...].astype(F32)).astype(BF)
+
+
 def middle_kernel(parts, own, _, mid, grad_mid, __):
     summed = jnp.sum(parts[...].astype(F32), axis=0)
     normed, factor = normalize(own[0])
@@ -192,59 +205,49 @@
     return dot(grads, turned_qkv[...]), contract_rows(hidden, grads), out_grad
 
 
-def near_kernel(lead, trail, *refs):
-    hidden, packed, probs, turned_qkv, out_weight, in_grad, qkv_total, out_total = refs
+def backward_kernel(
+    place, lead, trail, hidden, packed, probs, turned_qkv, out_weight, early, in_grad, first, second,
+    third, fourth, qkv_sum, out_sum, grads, outs, pieces,
+):
+    step = pl.program_id(0)
     parts = [packed[0][:, HS * i : HS * i + HS] for i in range(4)]
-    step = pl.program_id(0)
     upper = jnp.concatenate([lead[0].astype(F32), trail[0].astype(F32)], axis=0).astype(BF)
-    rows, qkv_grad, out_grad = window_back(
+    rows, qkv_part, out_part = window_back(
         upper, hidden[0], parts, probs[0], turned_qkv, out_weight
     )
-    in_grad[2 * step] = rows[:HALF].astype(BF)
-    in_grad[2 * step + 1] = rows[HALF:].astype(BF)
+    in_grad[2 * step + 1] = rows[:HALF].astype(BF)
+    in_grad[lax.rem(2 * step + 2, in_grad.shape[0])] = rows[HALF:].astype(BF)
 
     @pl.when(step == 0)
     def _():
-        qkv_total[...] = qkv_grad
-        out_total[...] = out_grad
+        qkv_sum[...] = qkv_part
+        out_sum[...] = out_part
 
     @pl.when(step > 0)
     def _():
-        qkv_total[...] += qkv_grad
-        out_total[...] += out_grad
-
-
-def far_kernel(
-    place, own, far, lead, tail, labels, turned_qkv, out_weight, in_near, qkv_total, out_total,
-    early, in_grad, first, second, third, fourth, grads, outs, pieces,
-):
-    saved = window_forward(lead[0], tail[...], labels[labels.shape[0] - 1 :, :], turned_qkv)
-    upper = jnp.concatenate([own[0].astype(F32), far[...].astype(F32)], axis=0).astype(BF)
-    rows, qkv_grad, out_grad = window_back(upper, *saved, turned_qkv, out_weight)
-    in_grad[in_grad.shape[0] - 1] = rows[:HALF].astype(BF)
-    in_grad[0] = rows[HALF:].astype(BF)
-    for chunk in range(in_near.shape[0]):
-        in_grad[chunk + 1] = in_near[chunk]
-    qkv_grad = qkv_total[...] + qkv_grad
-    out_grad = out_total[...] + out_grad
-    for i in range(3):
-        grads[i] = qkv_grad[:, HS * i : HS * i + HS]
-    for column in range(out_grad.shape[1] // 128):
-        outs[pl.ds(column, HS, stride=4), :] = out_grad[:, 128 * column : 128 * column + 128]
-    slots = [lax.rem(x - place[0] + 4, 4) for x in range(4)]
-    for owner in range(36):
-        if owner < 24:
-            kind, start = owner // 8, owner % 8 * 64
-            even = grads[kind, pl.ds(start, 32, stride=2), :]
-            odd = grads[kind, pl.ds(start + 1, 32, stride=2), :]
-            block = jnp.concatenate([even, odd], axis=1).astype(BF)
-        elif owner < 32:
-            block = outs[32 * (owner - 24) : 32 * (owner - 23), :].astype(BF)
-        else:
-            block = early[owner - 32]
-        pieces[slots[owner % 12 // 3], owner // 12 * 3 + owner % 3] = block
-    for slot, out in enumerate((first, second, third, fourth)):
-        out[...] = pieces[slot]
+        qkv_sum[...] += qkv_part
+        out_sum[...] += out_part
+
+    @pl.when(step == pl.num_programs(0) - 1)
+    def _():
+        for i in range(3):
+            grads[i] = qkv_sum[:, HS * i : HS * i + HS]
+        for column in range(out_sum.shape[1] // 128):
+            outs[pl.ds(column, HS, stride=4), :] = out_sum[:, 128 * column : 128 * column + 128]
+        slots = [lax.rem(x - place[0] + 4, 4) for x in range(4)]
+        for owner in range(36):
+            if owner < 24:
+                kind, start = owner // 8, owner % 8 * 64
+                even = grads[kind, pl.ds(start, 32, stride=2), :]
+                odd = grads[kind, pl.ds(start + 1, 32, stride=2), :]
+                block = jnp.concatenate([even, odd], axis=1).astype(BF)
+            elif owner < 32:
+                block = outs[32 * (owner - 24) : 32 * (owner - 23), :].astype(BF)
+            else:
+                block = early[owner - 32]
+            pieces[slots[owner % 12 // 3], owner // 12 * 3 + owner % 3] = block
+        for slot, out in enumerate((first, second, third, fourth)):
+            out[...] = pieces[slot]
 
 
 def sum_kernel(parts, total, total_b):
@@ -296,14 +299,13 @@
     labels = regions.reshape(windows, WIN)
     window = lambda columns: pl.BlockSpec((1, WIN, columns), lambda i, *_: (i, 0, 0))
     weights = (turned_qkv.reshape(-1, width), out_weight)
-    near = windows - 1
     token = jax.ShapeDtypeStruct((8, 128), F32)
     row_part = jax.ShapeDtypeStruct((share_rows, width), BF)
     mine = pl.BlockSpec(chunk, lambda i, place: (place[0], 0, 0))
     own_rows = jax.ShapeDtypeStruct((2, share_rows, width), BF)
     hidden, packed, probs, own = call(
         forward_kernel,
-        (near,),
+        (windows - 1,),
         [
             pl.BlockSpec(chunk, lambda i, _: (2 * i + 1, 0, 0)),
             pl.BlockSpec(chunk, lambda i, _: (2 * i + 2, 0, 0)),
@@ -313,9 +315,9 @@
             mine,
         ],
         [
-            ((near, WIN, width), BF, window(width)),
-            ((near, WIN, 4 * columns), BF, window(4 * columns)),
-            ((near, WIN, WIN), F32, window(WIN)),
+            ((windows, WIN, width), BF, window(width)),
+            ((windows, WIN, 4 * columns), BF, window(4 * columns)),
+            ((windows, WIN, WIN), F32, window(WIN)),
             (own_rows.shape, BF, whole(own_rows)),
         ],
         (chunks_in, chunks_in, labels, weights[0], chunks_mid, chunks_out),
@@ -335,58 +337,71 @@
         aliases={2: 2},
         vmem=16,
     )
-    grad_mid = lax.all_gather(own_grad_mid, HEAD_AXES, axis=0)
-    far_grad = from_next(grad_mid[0])
-    in_near, qkv_total, out_total = call(
-        near_kernel,
-        (near,),
-        [
-            pl.BlockSpec(chunk, lambda i: (2 * i + 1, 0, 0)),
-            pl.BlockSpec(chunk, lambda i: (2 * i + 2, 0, 0)),
+    far_grad = lax.ppermute(
+        own_grad_mid,
+        WIN_AXES + HEAD_AXES,
+        [((i + 1) % count * head_count, i * head_count) for i in range(count)],
+    )
+    late_parts = lax.all_to_all(late, "x", 0, 0)
+    final = lambda columns: pl.BlockSpec((1, WIN, columns), lambda i: (windows - 1, 0, 0))
+    hidden, packed, probs, done = call(
+        last_forward_kernel,
+        (1,),
+        [
+            pl.BlockSpec(chunk, lambda i: (head_count - 1, 0, 0)),
+            whole(far_input),
+            whole(labels),
+            whole(weights[0]),
+            ANY,
+            ANY,
+            ANY,
+        ],
+        [
+            (hidden.shape, BF, final(width)),
+            (packed.shape, BF, final(4 * columns)),
+            (probs.shape, F32, final(WIN)),
+            (token.shape, F32, whole(token)),
+        ],
+        (chunks_in, far_input, labels, weights[0], hidden, packed, probs),
+        aliases={4: 0, 5: 1, 6: 2},
+        flops=20 * 10**8,
+    )
+    (given,) = call(
+        give_kernel,
+        (1,),
+        [whole(own_grad_mid), whole(far_grad), ANY],
+        [(row_part.shape, BF, whole(row_part))],
+        (own_grad_mid, far_grad, done),
+        chosen=head_place,
+        vmem=16,
+    )
+    grad_mid = lax.all_gather(given, HEAD_AXES, axis=0)
+    piece = jax.ShapeDtypeStruct((9,) + BLOCK, BF)
+    in_rows = jax.ShapeDtypeStruct((head_count, HALF, width), BF)
+    in_grad, *pieces = call(
+        backward_kernel,
+        (windows,),
+        [
+            pl.BlockSpec(chunk, lambda i, _: (2 * i + 1, 0, 0)),
+            pl.BlockSpec(chunk, lambda i, _: (lax.rem(2 * i + 2, head_count), 0, 0)),
             window(width),
             window(4 * columns),
             window(WIN),
             *[whole(weight) for weight in weights],
-        ],
-        [
-            ((head_count - 2, HALF, width), BF, VMEM),
-            ((width, 3 * columns), F32, VMEM),
-            ((columns, width), F32, VMEM),
-        ],
-        (grad_mid, grad_mid, hidden, packed, probs, *weights),
-        flops=37 * 10**8,
-        vmem=24,
-    )
-    late_parts = lax.all_to_all(late, "x", 0, 0)
-    piece = jax.ShapeDtypeStruct((9,) + BLOCK, BF)
-    in_grad, *pieces = call(
-        far_kernel,
-        (1,),
-        [
-            pl.BlockSpec(chunk, lambda i, s: (head_count - 1, 0, 0)),
-            whole(far_grad),
-            pl.BlockSpec(chunk, lambda i, s: (head_count - 1, 0, 0)),
-            whole(far_input),
-            whole(labels),
-            *[whole(weight) for weight in weights],
-            VMEM,
-            VMEM,
-            VMEM,
             whole(early),
         ],
-        [((head_count, HALF, width), BF, VMEM)] + [(piece.shape, BF, whole(piece))] * 4,
-        (
-            grad_mid, far_grad, chunks_in, far_input, labels, *weights, in_near, qkv_total,
-            out_total, early,
-        ),
+        [(in_rows.shape, BF, whole(in_rows))] + [(piece.shape, BF, whole(piece))] * 4,
+        (grad_mid, grad_mid, hidden, packed, probs, *weights, early),
         scratch=[
+            pltpu.VMEM((width, 3 * columns), F32),
+            pltpu.VMEM((columns, width), F32),
             pltpu.VMEM((3, width, columns), F32),
             pltpu.VMEM((8 * 32, 128), F32),
             pltpu.VMEM((4, 9) + BLOCK, BF),
         ],
         chosen=x_place,
-        vmem=56,
-        flops=46 * 10**8,
+        vmem=24,
+        flops=70 * 10**8,
     )
     in_parts = lax.all_to_all(in_grad, HEAD_AXES, 0, 0)
     moved = [

time: 130 us -> 126 us (0.969)
  local copies, waits for them, and re-layouts: 6.07 us -> 3.81 us
  blocking collectives: 16.8 us -> 15.3 us
    ppermute x0 -> x1, starting transfers between devices: none -> 12.1 us  [shards(): lax.ppermute(own_grad_mid, WIN_AXES + HEAD_AXES, [((i + 1) % count * head...]
    ppermute x2 -> x1, starting transfers between devices: 22.7 us -> 12.1 us  [from_next(): lax.ppermute(values, WIN_AXES, [((i + 1) % count, i) for i in range(count)])]
    unnamed x36 -> x22, local copies, waits for them, and re-layouts: 4.5 us -> 2.25 us
    all_to_all x1, starting transfers between devices: 8.61 us -> 6.47 us  [shards(): received = lax.all_to_all(partial_sum, ('y', 'zh'), 0, 0)]
    all_gather x1, blocking collectives: 16.8 us -> 15.3 us  [shards(): grad_mid = lax.all_gather(given, HEAD_AXES, axis=0)]
    pallas_call x9 -> x10, Pallas kernels: 20.3 us -> 21.1 us  [call(): pl.pallas_call(kernel, grid_spec=spec, out_shape=[jax.ShapeDtypeStruct(ou...]
  transfers between devices with their start and end apart: 10 -> 10, of which waited for: 6 -> 6; matrix products, arithmetic and copies ran while one was open for 1% -> 1% of each run, Pallas kernels for 11% -> 12%
where the time goes in v7:
time: 126 us; the launch traced here: 125 us
  starting transfers between devices  66.7 us (53%)
  Pallas kernels  21.1 us (17%)
  waiting for transfers between devices  17.7 us (14%)
  blocking collectives  15.3 us (12%)
  local copies, waits for them, and re-layouts  3.81 us (3%)
    pallas_call x10, Pallas kernels, call(): pl.pallas_call(kernel, grid_spec=spec, out_shape=[jax.ShapeDtypeStruct(ou...  21.1 us
    all_gather x1, blocking collectives, shards(): grad_mid = lax.all_gather(given, HEAD_AXES, axis=0)  15.3 us
    ppermute x1, starting transfers between devices, shards(): lax.ppermute(own_grad_mid, WIN_AXES + HEAD_AXES, [((i + 1) % count * head...  12.1 us
    ppermute x1, starting transfers between devices, from_next(): lax.ppermute(values, WIN_AXES, [((i + 1) % count, i) for i in range(count)])  12.1 us
    all_to_all x1, starting transfers between devices, shards(): late_parts = lax.all_to_all(late, 'x', 0, 0)  8.9 us
    ppermute x3, starting transfers between devices, shards(): lax.ppermute(pieces[k], 'x', [(i, (i + k) % 4) for i in range(4)])  8.68 us
    ppermute x1, starting transfers between devices, shards(): lax.ppermute(summed_b, WIN_AXES + HEAD_AXES, [(i * head_count, (i + 1) %...  7.66 us
    all_to_all x1, starting transfers between devices, shards(): parts = lax.all_to_all(unit_grad, HEAD_AXES, 0, 0)  7.27 us
  transfers between devices with their start and end apart: 10, of which 6 were waited for; matrix products, arithmetic and copies ran while one was open for 1% of the time, Pallas kernels for 12%

profile of v7, /device:TPU:6, one launch (start us, length us, event | category | flops | bytes accessed | tf_op | source)
XLA Modules:
  0.0 125.4 jit_solution(3309914842427231250)
XLA Ops:
  0.6 5.8 %shard_map.95 = (bf16[8,72,512]{2,1,0:T(8,128)(2,1)}, bf16[4,15,32,128]{3,2,1,0:T(8,128)(2,1)}, bf16[4,32,128]{2,1,0:T(8,128)(2,1)}) custom-call(bf16[576,512]{1,0:T(8,128)(2,1)} %stream.1, bf16[576,512]{1,0:T(8,128)(2,1)} %grad_out.1, bf16[512,256]{1,0:T(8,128)(2,1)} %up_weight.1, bf16[256,512]{1,0:T(8,128)(2,1)} %down_weight.1), custom_call_target="tpu_custom_call" | custom-call | flops 6899999744 | bytes 2097152 | tf_op jit(solution)/shard_map/pallas_call | solution.py:57
  6.4 7.3 %all-to-all-start = ((bf16[8,72,512]{2,1,0:T(8,128)(2,1)}), bf16[8,72,512]{2,1,0:T(8,128)(2,1)S(1)}, u32[]{:S(2)}, u32[]{:S(2)}) async-start(bf16[8,72,512]{2,1,0:T(8,128)(2,1)} %get-tuple-element.25), calls=%async_computation | async-start | bytes 1179648 | tf_op jit(solution)/shard_map/all_to_all | solution.py:298
  13.7 0.9 slice.3
  14.6 12.1 %collective-permute-start.1 = (bf16[72,512]{1,0:T(8,128)(2,1)S(1)}, bf16[72,512]{1,0:T(8,128)(2,1)S(1)}, u32[]{:S(2)}, u32[]{:S(2)}) collective-permute-start(bf16[72,512]{1,0:T(8,128)(2,1)S(1)} %slice.3), channel_id=1, source_target_pairs={{8,0},{16,8},{24,16},{32,24},{40,32},{48,40},{56,48},{64,56},{72,6... | collective-permute-start | bytes 221192 | tf_op jit(solution)/shard_map/ppermute | solution.py:294
  26.7 0.7 copy-done.9
  27.4 0.7 reshape.31.labels
  28.1 4.6 %shard_map.96 = (bf16[4,144,512]{2,1,0:T(8,128)(2,1)}, bf16[4,144,256]{2,1,0:T(8,128)(2,1)}, f32[4,144,144]{2,1,0:T(8,128)}, bf16[2,72,512]{2,1,0:T(8,128)(2,1)}) custom-call(s32[1]{0:T(128)} %bitcast.place, bf16[8,72,512]{2,1,0:T(8,128)(2,1)} %bitcast.10, bf16[8,72,512]{2,1,0:T(8,128)(2,1)} %bitcast.11, s32[4,144]{1,0:T(4,128)} %reshape.31.labels, ...), custom_call_target="tpu_custom_call" | custom-call | flops 5299999744 | bytes 2097152 | tf_op jit(solution)/shard_map/pallas_call | solution.py:57
  32.7 3.0 %all-to-all-done.parts = bf16[8,72,512]{2,1,0:T(8,128)(2,1)S(1)} async-done(((bf16[8,72,512]{2,1,0:T(8,128)(2,1)}), bf16[8,72,512]{2,1,0:T(8,128)(2,1)S(1)}, u32[]{:S(2)}, u32[]{:S(2)}) %all-to-all-start) | async-done | bytes 589856 | tf_op jit(solution)/shard_map/all_to_all | solution.py:298
  35.7 0.9 copy-done.1
  36.6 0.3 shard_map.97
  36.9 12.1 %collective-permute-start = (bf16[72,512]{1,0:T(8,128)(2,1)S(1)}, bf16[72,512]{1,0:T(8,128)(2,1)S(1)}, u32[]{:S(2)}, u32[]{:S(2)}) collective-permute-start(bf16[72,512]{1,0:T(8,128)(2,1)S(1)} %get-tuple-element.28.own), channel_id=1, source_target_pairs={{8,0},{16,8},{24,16},{32,24},{40,32},{48,40},{56,48},{64,56},{72,6... | collective-permute-start | bytes 221192 | tf_op jit(solution)/shard_map/ppermute | solution.py:340
  49.0 0.0 copy-start.10
  49.0 0.6 copy-done.10
  49.7 2.6 %shard_map.98 = (bf16[4,144,512]{2,1,0:T(8,128)(2,1)}, bf16[4,144,256]{2,1,0:T(8,128)(2,1)}, f32[4,144,144]{2,1,0:T(8,128)}, f32[8,128]{1,0:T(8,128)}) custom-call(bf16[8,72,512]{2,1,0:T(8,128)(2,1)} %bitcast.12, bf16[72,512]{1,0:T(8,128)(2,1)} %copy-done.10, s32[4,144]{1,0:T(4,128)} %reshape.31.labels, ...), custom_call_target="tpu_custom_call", output_to_operand_aliasing={{0}: (4, {}), {1}: (5, {}), {2}: (6, {})} | custom-call | flops 2000000000 | bytes 2097152 | tf_op jit(solution)/shard_map/pallas_call | solution.py:57
  52.3 8.9 %all-to-all-start.2 = ((bf16[4,15,32,128]{3,2,1,0:T(8,128)(2,1)}), bf16[4,15,32,128]{3,2,1,0:T(8,128)(2,1)S(1)}, u32[]{:S(2)}, u32[]{:S(2)}) async-start(bf16[4,15,32,128]{3,2,1,0:T(8,128)(2,1)} %get-tuple-element.46), calls=%async_computation.2 | async-start | bytes 983040 | tf_op jit(solution)/shard_map/all_to_all | solution.py:345
  61.2 15.3 %all-gather = bf16[576,512]{1,0:T(8,128)(2,1)S(1)} all-gather(bf16[72,512]{1,0:T(8,128)(2,1)S(1)} %shard_map.99), channel_id=2, replica_groups=mesh['y'=8,'x'=4,'zh'=3,'zl'=4,'core'=2] {'zl','core'}, dimensions={0}, use_global_device_ids=true | all-gather | bytes 663552 | tf_op jit(solution)/shard_map/all_gather | solution.py:378
  76.6 5.3 %shard_map.100 = (bf16[8,72,512]{2,1,0:T(8,128)(2,1)}, bf16[9,32,128]{2,1,0:T(8,128)(2,1)S(1)}, bf16[9,32,128]{2,1,0:T(8,128)(2,1)S(1)}, bf16[9,32,128]{2,1,0:T(8,128)(2,1)S(1)}, bf16[9,32,128]{2,1,0:T(8,128)(2,1)S(1)}) custom-call(s32[1]{0:T(128)} %bitcast.1.place, bf16[8,72,512]{2,1,0:T(8,128)(2,1)S(1)} %bitcast.14, bf16[8,72,512]{2,1,0:T(8,128)(2,1)S(1)} %bitcast.15, ...), custom_call_target="tpu_custom_call" | custom-call | flops 7000000000 | bytes 2097152 | tf_op jit(solution)/shard_map/pallas_call | solution.py:57
  81.9 3.5 %all-to-all-start.1 = ((bf16[8,72,512]{2,1,0:T(8,128)(2,1)}), bf16[8,72,512]{2,1,0:T(8,128)(2,1)S(1)}, u32[]{:S(2)}, u32[]{:S(2)}) async-start(bf16[8,72,512]{2,1,0:T(8,128)(2,1)} %get-tuple-element.37), calls=%async_computation.1 | async-start | bytes 1179648 | tf_op jit(solution)/shard_map/all_to_all | solution.py:406
  85.5 2.0 %collective-permute-start.3 = (bf16[9,32,128]{2,1,0:T(8,128)(2,1)S(1)}, bf16[9,32,128]{2,1,0:T(8,128)(2,1)S(1)}, u32[]{:S(2)}, u32[]{:S(2)}) collective-permute-start(bf16[9,32,128]{2,1,0:T(8,128)(2,1)S(1)} %get-tuple-element.43), channel_id=1, source_target_pairs={{0,24},{24,48},{48,72},{72,0},{1,25},{25,49},{49,73},{73,1},{2,26}... | collective-permute-start | bytes 221192 | tf_op jit(solution)/shard_map/ppermute | solution.py:408
  87.4 4.8 %collective-permute-start.4 = (bf16[9,32,128]{2,1,0:T(8,128)(2,1)S(1)}, bf16[9,32,128]{2,1,0:T(8,128)(2,1)S(1)}, u32[]{:S(2)}, u32[]{:S(2)}) collective-permute-start(bf16[9,32,128]{2,1,0:T(8,128)(2,1)S(1)} %get-tuple-element.44), channel_id=1, source_target_pairs={{0,48},{24,72},{48,0},{72,24},{1,49},{25,73},{49,1},{73,25},{2,50}... | collective-permute-start | bytes 221192 | tf_op jit(solution)/shard_map/ppermute | solution.py:408
  92.2 1.9 %collective-permute-start.5 = (bf16[9,32,128]{2,1,0:T(8,128)(2,1)S(1)}, bf16[9,32,128]{2,1,0:T(8,128)(2,1)S(1)}, u32[]{:S(2)}, u32[]{:S(2)}) collective-permute-start(bf16[9,32,128]{2,1,0:T(8,128)(2,1)S(1)} %get-tuple-element.45), channel_id=1, source_target_pairs={{0,72},{24,0},{48,24},{72,48},{1,73},{25,1},{49,25},{73,49},{2,74}... | collective-permute-start | bytes 221192 | tf_op jit(solution)/shard_map/ppermute | solution.py:408
  94.2 1.2 collective-permute-done.4.third
  95.3 4.3 %collective-permute-done.5.fourth = bf16[9,32,128]{2,1,0:T(8,128)(2,1)S(1)} collective-permute-done((bf16[9,32,128]{2,1,0:T(8,128)(2,1)S(1)}, bf16[9,32,128]{2,1,0:T(8,128)(2,1)S(1)}, u32[]{:S(2)}, u32[]{:S(2)}) %collective-permute-start.5) | collective-permute-done | bytes 73760 | tf_op jit(solution)/shard_map/ppermute | solution.py:408
  99.7 0.8 shard_map.103
  100.5 1.7 %all-to-all-done.1.parts = bf16[8,72,512]{2,1,0:T(8,128)(2,1)S(1)} async-done(((bf16[8,72,512]{2,1,0:T(8,128)(2,1)}), bf16[8,72,512]{2,1,0:T(8,128)(2,1)S(1)}, u32[]{:S(2)}, u32[]{:S(2)}) %all-to-all-start.1) | async-done | bytes 589856 | tf_op jit(solution)/shard_map/all_to_all | solution.py:406
  102.1 6.5 %all-to-all-start.3 = ((bf16[24,32,128]{2,1,0:T(8,128)(2,1)}), bf16[24,32,128]{2,1,0:T(8,128)(2,1)S(1)}, u32[]{:S(2)}, u32[]{:S(2)}) async-start(bf16[24,32,128]{2,1,0:T(8,128)(2,1)} %shard_map.103), calls=%async_computation.3 | async-start | bytes 393216 | tf_op jit(solution)/shard_map/all_to_all | solution.py:432
  108.6 0.1 shard_map.101
  108.7 7.7 %collective-permute-start.2 = (bf16[72,512]{1,0:T(8,128)(2,1)S(1)}, bf16[72,512]{1,0:T(8,128)(2,1)S(1)}, u32[]{:S(2)}, u32[]{:S(2)}) collective-permute-start(bf16[72,512]{1,0:T(8,128)(2,1)S(1)} %get-tuple-element.39), channel_id=1, source_target_pairs={{0,8},{8,16},{16,24},{24,32},{32,40},{40,48},{48,56},{56,64},{64,7... | collective-permute-start | bytes 221192 | tf_op jit(solution)/shard_map/ppermute | solution.py:427
  116.4 3.4 %collective-permute-done.2.arrived = bf16[72,512]{1,0:T(8,128)(2,1)S(1)} collective-permute-done((bf16[72,512]{1,0:T(8,128)(2,1)S(1)}, bf16[72,512]{1,0:T(8,128)(2,1)S(1)}, u32[]{:S(2)}, u32[]{:S(2)}) %collective-permute-start.2) | collective-permute-done | bytes 73760 | tf_op jit(solution)/shard_map/ppermute | solution.py:427
  119.8 0.9 shard_map.102
  120.7 4.1 %all-to-all-done.3.received = bf16[24,32,128]{2,1,0:T(8,128)(2,1)S(1)} async-done(((bf16[24,32,128]{2,1,0:T(8,128)(2,1)}), bf16[24,32,128]{2,1,0:T(8,128)(2,1)S(1)}, u32[]{:S(2)}, u32[]{:S(2)}) %all-to-all-start.3) | async-done | bytes 196640 | tf_op jit(solution)/shard_map/all_to_all | solution.py:432
  124.8 0.6 shard_map.104
  (23 shorter events, 0.1 us)
Async XLA Ops:
  6.4 29.2 %all-to-all-start = ((bf16[8,72,512]{2,1,0:T(8,128)(2,1)}), bf16[8,72,512]{2,1,0:T(8,128)(2,1)S(1)}, u32[]{:S(2)}, u32[]{:S(2)}) async-start(bf16[8,72,512]{2,1,0:T(8,128)(2,1)} %get-tuple-element.25), calls=%async_computation | async-start | bytes 1179648 | tf_op jit(solution)/shard_map/all_to_all | solution.py:298
  14.6 34.4 %collective-permute-start.1 = (bf16[72,512]{1,0:T(8,128)(2,1)S(1)}, bf16[72,512]{1,0:T(8,128)(2,1)S(1)}, u32[]{:S(2)}, u32[]{:S(2)}) collective-permute-start(bf16[72,512]{1,0:T(8,128)(2,1)S(1)} %slice.3), channel_id=1, source_target_pairs={{8,0},{16,8},{24,16},{32,24},{40,32},{48,40},{56,48},{64,56},{72,6... | collective-permute-start | bytes 221192 | tf_op jit(solution)/shard_map/ppermute | solution.py:294
  26.7 0.7 copy-start.9
  35.7 0.9 copy-start.1
  36.9 24.3 %collective-permute-start = (bf16[72,512]{1,0:T(8,128)(2,1)S(1)}, bf16[72,512]{1,0:T(8,128)(2,1)S(1)}, u32[]{:S(2)}, u32[]{:S(2)}) collective-permute-start(bf16[72,512]{1,0:T(8,128)(2,1)S(1)} %get-tuple-element.28.own), channel_id=1, source_target_pairs={{8,0},{16,8},{24,16},{32,24},{40,32},{48,40},{56,48},{64,56},{72,6... | collective-permute-start | bytes 221192 | tf_op jit(solution)/shard_map/ppermute | solution.py:340
  49.0 0.6 copy-start.10
  52.3 8.9 %copy-start.4 = (f32[8,128]{1,0:T(8,128)S(1)}, f32[8,128]{1,0:T(8,128)}, u32[]{:S(2)}) copy-start(f32[8,128]{1,0:T(8,128)} %get-tuple-element.32._) | copy-start | bytes 12292
  52.3 24.3 %copy-start.6 = (f32[4,144,144]{2,1,0:T(8,128)S(1)}, f32[4,144,144]{2,1,0:T(8,128)}, u32[]{:S(2)}) copy-start(f32[4,144,144]{2,1,0:T(8,128)} %get-tuple-element.35.probs) | copy-start | bytes 995332
  52.3 24.3 %copy-start.7 = (bf16[4,144,256]{2,1,0:T(8,128)(2,1)S(1)}, bf16[4,144,256]{2,1,0:T(8,128)(2,1)}, u32[]{:S(2)}) copy-start(bf16[4,144,256]{2,1,0:T(8,128)(2,1)} %get-tuple-element.34.packed) | copy-start | bytes 884740
  52.3 29.6 %all-to-all-start.2 = ((bf16[4,15,32,128]{3,2,1,0:T(8,128)(2,1)}), bf16[4,15,32,128]{3,2,1,0:T(8,128)(2,1)S(1)}, u32[]{:S(2)}, u32[]{:S(2)}) async-start(bf16[4,15,32,128]{3,2,1,0:T(8,128)(2,1)} %get-tuple-element.46), calls=%async_computation.2 | async-start | bytes 983040 | tf_op jit(solution)/shard_map/all_to_all | solution.py:345
  61.2 15.4 %copy-start.5 = (bf16[4,144,512]{2,1,0:T(8,128)(2,1)S(1)}, bf16[4,144,512]{2,1,0:T(8,128)(2,1)}, u32[]{:S(2)}) copy-start(bf16[4,144,512]{2,1,0:T(8,128)(2,1)} %get-tuple-element.33.hidden) | copy-start | bytes 1769476
  61.2 15.4 %copy-start.2 = (bf16[3,512,64]{1,2,0:T(8,128)(2,1)S(1)}, bf16[3,512,64]{1,2,0:T(8,128)(2,1)}, u32[]{:S(2)}) copy-start(bf16[3,512,64]{1,2,0:T(8,128)(2,1)} %param.12) | copy-start | bytes 589828
  61.2 15.4 %copy-start.3 = (bf16[64,512]{1,0:T(8,128)(2,1)S(1)}, bf16[64,512]{1,0:T(8,128)(2,1)}, u32[]{:S(2)}) copy-start(bf16[64,512]{1,0:T(8,128)(2,1)} %out_weight.1) | copy-start | bytes 196612
  61.2 15.4 %copy-start.8 = (bf16[4,32,128]{2,1,0:T(8,128)(2,1)S(1)}, bf16[4,32,128]{2,1,0:T(8,128)(2,1)}, u32[]{:S(2)}) copy-start(bf16[4,32,128]{2,1,0:T(8,128)(2,1)} %get-tuple-element.36.early) | copy-start | bytes 98308
  81.9 20.2 %all-to-all-start.1 = ((bf16[8,72,512]{2,1,0:T(8,128)(2,1)}), bf16[8,72,512]{2,1,0:T(8,128)(2,1)S(1)}, u32[]{:S(2)}, u32[]{:S(2)}) async-start(bf16[8,72,512]{2,1,0:T(8,128)(2,1)} %get-tuple-element.37), calls=%async_computation.1 | async-start | bytes 1179648 | tf_op jit(solution)/shard_map/all_to_all | solution.py:406
  85.5 8.7 %collective-permute-start.3 = (bf16[9,32,128]{2,1,0:T(8,128)(2,1)S(1)}, bf16[9,32,128]{2,1,0:T(8,128)(2,1)S(1)}, u32[]{:S(2)}, u32[]{:S(2)}) collective-permute-start(bf16[9,32,128]{2,1,0:T(8,128)(2,1)S(1)} %get-tuple-element.43), channel_id=1, source_target_pairs={{0,24},{24,48},{48,72},{72,0},{1,25},{25,49},{49,73},{73,1},{2,26}... | collective-permute-start | bytes 221192 | tf_op jit(solution)/shard_map/ppermute | solution.py:408
  87.4 7.9 %collective-permute-start.4 = (bf16[9,32,128]{2,1,0:T(8,128)(2,1)S(1)}, bf16[9,32,128]{2,1,0:T(8,128)(2,1)S(1)}, u32[]{:S(2)}, u32[]{:S(2)}) collective-permute-start(bf16[9,32,128]{2,1,0:T(8,128)(2,1)S(1)} %get-tuple-element.44), channel_id=1, source_target_pairs={{0,48},{24,72},{48,0},{72,24},{1,49},{25,73},{49,1},{73,25},{2,50}... | collective-permute-start | bytes 221192 | tf_op jit(solution)/shard_map/ppermute | solution.py:408
  92.2 7.5 %collective-permute-start.5 = (bf16[9,32,128]{2,1,0:T(8,128)(2,1)S(1)}, bf16[9,32,128]{2,1,0:T(8,128)(2,1)S(1)}, u32[]{:S(2)}, u32[]{:S(2)}) collective-permute-start(bf16[9,32,128]{2,1,0:T(8,128)(2,1)S(1)} %get-tuple-element.45), channel_id=1, source_target_pairs={{0,72},{24,0},{48,24},{72,48},{1,73},{25,1},{49,25},{73,49},{2,74}... | collective-permute-start | bytes 221192 | tf_op jit(solution)/shard_map/ppermute | solution.py:408
  100.5 19.3 %copy-start = (bf16[576,512]{1,0:T(8,128)(2,1)S(1)}, bf16[576,512]{1,0:T(8,128)(2,1)}, u32[]{:S(2)}) copy-start(bf16[576,512]{1,0:T(8,128)(2,1)} %param.8) | copy-start | bytes 1769476
  102.1 22.7 %all-to-all-start.3 = ((bf16[24,32,128]{2,1,0:T(8,128)(2,1)}), bf16[24,32,128]{2,1,0:T(8,128)(2,1)S(1)}, u32[]{:S(2)}, u32[]{:S(2)}) async-start(bf16[24,32,128]{2,1,0:T(8,128)(2,1)} %shard_map.103), calls=%async_computation.3 | async-start | bytes 393216 | tf_op jit(solution)/shard_map/all_to_all | solution.py:432
  108.7 11.1 %collective-permute-start.2 = (bf16[72,512]{1,0:T(8,128)(2,1)S(1)}, bf16[72,512]{1,0:T(8,128)(2,1)S(1)}, u32[]{:S(2)}, u32[]{:S(2)}) collective-permute-start(bf16[72,512]{1,0:T(8,128)(2,1)S(1)} %get-tuple-element.39), channel_id=1, source_target_pairs={{0,8},{8,16},{16,24},{24,32},{32,40},{40,48},{48,56},{56,64},{64,7... | collective-permute-start | bytes 221192 | tf_op jit(solution)/shard_map/ppermute | solution.py:427

commit v8 on v7

--- a/solution.py
+++ b/solution.py
@@ -157,29 +157,26 @@
 
 
 def forward_kernel(
-    place, lead, tail, labels, turned_qkv, stream, grad_out, hidden, packed, probs_out, own
+    place, lead, trail, far, labels, turned_qkv, stream, grad_out, hidden, packed, probs_out, own
 ):
-    row = labels[pl.ds(pl.program_id(0), 1), :]
-    hidden[0], parts, probs_out[0] = window_forward(lead[0], tail[0], row, turned_qkv)
+    step = pl.program_id(0)
+    tail = jnp.where(step == pl.num_programs(0) - 1, far[...].astype(F32), trail[0].astype(F32))
+    row = labels[pl.ds(step, 1), :]
+    hidden[0], parts, probs_out[0] = window_forward(lead[0], tail, row, turned_qkv)
     packed[0] = jnp.concatenate(parts, axis=1)
     own[0] = stream[0]
     own[1] = grad_out[0]
 
 
-def last_forward_kernel(
-    lead, tail, labels, turned_qkv, _, __, ___, hidden, packed, probs_out, token
-):
-    row = labels[labels.shape[0] - 1 :, :]
-    hidden[0], parts, probs_out[0] = window_forward(lead[0], tail[...], row, turned_qkv)
-    packed[0] = jnp.concatenate(parts, axis=1)
-    token[...] = jnp.zeros_like(token)
-
-
-def give_kernel(place, own, far, _, given):
+def give_kernel(place, own, far, given):
     given[...] = jnp.where(place[0] == 0, far[...].astype(F32), own[...].astype(F32)).astype(BF)
 
 
-def middle_kernel(parts, own, _, mid, grad_mid, __):
+def gate_kernel(_, __, ___):
+    pass
+
+
+def middle_kernel(parts, own, mid, grad_mid):
     summed = jnp.sum(parts[...].astype(F32), axis=0)
     normed, factor = normalize(own[0])
     middle = own[1].astype(F32) + norm_back(normed, factor, summed)
@@ -206,8 +203,8 @@
 
 
 def backward_kernel(
-    place, lead, trail, hidden, packed, probs, turned_qkv, out_weight, early, in_grad, first, second,
-    third, fourth, qkv_sum, out_sum, grads, outs, pieces,
+    place, lead, trail, hidden, packed, probs, turned_qkv, out_weight, early, late, in_grad, first,
+    second, third, fourth, qkv_sum, out_sum, grads, outs, pieces,
 ):
     step = pl.program_id(0)
     parts = [packed[0][:, HS * i : HS * i + HS] for i in range(4)]
@@ -246,6 +243,9 @@
             else:
                 block = early[owner - 32]
             pieces[slots[owner % 12 // 3], owner // 12 * 3 + owner % 3] = block
+        for x in range(4):
+            for index in range(late.shape[1]):
+                pieces[slots[x], 9 + index] = late[x, index]
         for slot, out in enumerate((first, second, third, fourth)):
             out[...] = pieces[slot]
 
@@ -262,13 +262,11 @@
     token[...] = jnp.zeros_like(token)
 
 
-def join_kernel(first, second, third, fourth, late, joined):
-    count = first.shape[0]
-    near = (first[...].astype(F32) + second[...].astype(F32)) + (
+def join_kernel(first, second, third, fourth, joined):
+    total = (first[...].astype(F32) + second[...].astype(F32)) + (
         third[...].astype(F32) + fourth[...].astype(F32)
     )
-    joined[:count] = near.astype(BF)
-    joined[count:] = jnp.sum(late[...].astype(F32), axis=0).astype(BF)
+    joined[...] = total.astype(BF)
 
 
 def total_kernel(received, _, owned):
@@ -295,6 +293,15 @@
 
     far_input = from_next(block_input[:HALF])
     unit_grad, late, early = mlp(stream, grad_out, up_weight, down_weight)
+    (unit_grad,) = call(
+        gate_kernel,
+        (1,),
+        [ANY, ANY],
+        [(unit_grad.shape, BF, ANY)],
+        (unit_grad, far_input),
+        aliases={0: 0},
+        vmem=60,
+    )
     parts = lax.all_to_all(unit_grad, HEAD_AXES, 0, 0)
     labels = regions.reshape(windows, WIN)
     window = lambda columns: pl.BlockSpec((1, WIN, columns), lambda i, *_: (i, 0, 0))
@@ -305,10 +312,11 @@
     own_rows = jax.ShapeDtypeStruct((2, share_rows, width), BF)
     hidden, packed, probs, own = call(
         forward_kernel,
-        (windows - 1,),
+        (windows,),
         [
             pl.BlockSpec(chunk, lambda i, _: (2 * i + 1, 0, 0)),
-            pl.BlockSpec(chunk, lambda i, _: (2 * i + 2, 0, 0)),
+            pl.BlockSpec(chunk, lambda i, _: (jnp.minimum(2 * i + 2, head_count - 1), 0, 0)),
+            whole(far_input),
             whole(labels),
             whole(weights[0]),
             mine,
@@ -320,21 +328,16 @@
             ((windows, WIN, WIN), F32, window(WIN)),
             (own_rows.shape, BF, whole(own_rows)),
         ],
-        (chunks_in, chunks_in, labels, weights[0], chunks_mid, chunks_out),
+        (chunks_in, chunks_in, far_input, labels, weights[0], chunks_mid, chunks_out),
         chosen=head_place,
         flops=53 * 10**8,
     )
-    mid, own_grad_mid, late = call(
+    mid, own_grad_mid = call(
         middle_kernel,
         (1,),
-        [whole(parts), whole(own), ANY],
-        [
-            (row_part.shape, F32, whole(row_part)),
-            (row_part.shape, BF, whole(row_part)),
-            (late.shape, BF, ANY),
-        ],
-        (parts, own, late),
-        aliases={2: 2},
+        [whole(parts), whole(own)],
+        [(row_part.shape, F32, whole(row_part)), (row_part.shape, BF, whole(row_part))],
+        (parts, own),
         vmem=16,
     )
     far_grad = lax.ppermute(
@@ -342,41 +345,17 @@
         WIN_AXES + HEAD_AXES,
         [((i + 1) % count * head_count, i * head_count) for i in range(count)],
     )
-    late_parts = lax.all_to_all(late, "x", 0, 0)
-    final = lambda columns: pl.BlockSpec((1, WIN, columns), lambda i: (windows - 1, 0, 0))
-    hidden, packed, probs, done = call(
-        last_forward_kernel,
-        (1,),
-        [
-            pl.BlockSpec(chunk, lambda i: (head_count - 1, 0, 0)),
-            whole(far_input),
-            whole(labels),
-            whole(weights[0]),
-            ANY,
-            ANY,
-            ANY,
-        ],
-        [
-            (hidden.shape, BF, final(width)),
-            (packed.shape, BF, final(4 * columns)),
-            (probs.shape, F32, final(WIN)),
-            (token.shape, F32, whole(token)),
-        ],
-        (chunks_in, far_input, labels, weights[0], hidden, packed, probs),
-        aliases={4: 0, 5: 1, 6: 2},
-        flops=20 * 10**8,
-    )
     (given,) = call(
         give_kernel,
         (1,),
-        [whole(own_grad_mid), whole(far_grad), ANY],
+        [whole(own_grad_mid), whole(far_grad)],
         [(row_part.shape, BF, whole(row_part))],
-        (own_grad_mid, far_grad, done),
+        (own_grad_mid, far_grad),
         chosen=head_place,
         vmem=16,
     )
     grad_mid = lax.all_gather(given, HEAD_AXES, axis=0)
-    piece = jax.ShapeDtypeStruct((9,) + BLOCK, BF)
+    piece = jax.ShapeDtypeStruct((24,) + BLOCK, BF)
     in_rows = jax.ShapeDtypeStruct((head_count, HALF, width), BF)
     in_grad, *pieces = call(
         backward_kernel,
@@ -389,15 +368,16 @@
             window(WIN),
             *[whole(weight) for weight in weights],
             whole(early),
+            whole(late),
         ],
         [(in_rows.shape, BF, whole(in_rows))] + [(piece.shape, BF, whole(piece))] * 4,
-        (grad_mid, grad_mid, hidden, packed, probs, *weights, early),
+        (grad_mid, grad_mid, hidden, packed, probs, *weights, early, late),
         scratch=[
             pltpu.VMEM((width, 3 * columns), F32),
             pltpu.VMEM((columns, width), F32),
             pltpu.VMEM((3, width, columns), F32),
             pltpu.VMEM((8 * 32, 128), F32),
-            pltpu.VMEM((4, 9) + BLOCK, BF),
+            pltpu.VMEM((4, 24) + BLOCK, BF),
         ],
         chosen=x_place,
         vmem=24,
@@ -407,13 +387,12 @@
     moved = [
         lax.ppermute(pieces[k], "x", [(i, (i + k) % 4) for i in range(4)]) for k in range(1, 4)
     ]
-    joined = jax.ShapeDtypeStruct((24,) + BLOCK, BF)
     (partial_sum,) = call(
         join_kernel,
         (1,),
-        [whole(piece)] * 4 + [whole(late_parts)],
-        [(joined.shape, BF, whole(joined))],
-        (pieces[0], *moved, late_parts),
+        [whole(piece)] * 4,
+        [(piece.shape, BF, whole(piece))],
+        (pieces[0], *moved),
         vmem=16,
     )
     summed, summed_b = call(

time: 126 us -> 136 us (1.079)
  the two profiles are of different devices: /device:TPU:6 before, /device:TPU:8 now
where the time goes in v8:
time: 136 us; the launch traced here: 135 us
  starting transfers between devices  65.7 us (48%)
  waiting for transfers between devices  29.5 us (22%)
  Pallas kernels  19.6 us (14%)
  blocking collectives  15.3 us (11%)
  local copies, waits for them, and re-layouts  3.82 us (3%)
    pallas_call x10, Pallas kernels, call(): pl.pallas_call(kernel, grid_spec=spec, out_shape=[jax.ShapeDtypeStruct(ou...  19.6 us
    ppermute x1, starting transfers between devices, from_next(): lax.ppermute(values, WIN_AXES, [((i + 1) % count, i) for i in range(count)])  16.6 us
    all_gather x1, blocking collectives, shards(): grad_mid = lax.all_gather(given, HEAD_AXES, axis=0)  15.3 us
    all_to_all x1, starting transfers between devices, shards(): received = lax.all_to_all(partial_sum, ('y', 'zh'), 0, 0)  14.4 us
    ppermute x1, starting transfers between devices, shards(): lax.ppermute(own_grad_mid, WIN_AXES + HEAD_AXES, [((i + 1) % count * head...  10.9 us
    all_to_all x1, waiting for transfers between devices, shards(): parts = lax.all_to_all(unit_grad, HEAD_AXES, 0, 0)  9.72 us
    ppermute x1, waiting for transfers between devices, shards(): lax.ppermute(summed_b, WIN_AXES + HEAD_AXES, [(i * head_count, (i + 1) %...  9.21 us
    ppermute x3, starting transfers between devices, shards(): lax.ppermute(pieces[k], 'x', [(i, (i + k) % 4) for i in range(4)])  9 us
  transfers between devices with their start and end apart: 9, of which 6 were waited for; matrix products, arithmetic and copies ran while one was open for 0% of the time, Pallas kernels for 10%

profile of v8, /device:TPU:8, one launch (start us, length us, event | category | flops | bytes accessed | tf_op | source)
XLA Modules:
  0.0 134.8 jit_solution(8565968173735176322)
XLA Ops:
  0.6 0.9 slice.3
  1.5 16.6 %collective-permute-start = (bf16[72,512]{1,0:T(8,128)(2,1)S(1)}, bf16[72,512]{1,0:T(8,128)(2,1)S(1)}, u32[]{:S(2)}, u32[]{:S(2)}) collective-permute-start(bf16[72,512]{1,0:T(8,128)(2,1)S(1)} %slice.3), channel_id=1, source_target_pairs={{8,0},{16,8},{24,16},{32,24},{40,32},{48,40},{56,48},{64,56},{72,6... | collective-permute-start | bytes 221192 | tf_op jit(solution)/shard_map/ppermute | solution.py:292
  18.2 5.8 %shard_map.95 = (bf16[8,72,512]{2,1,0:T(8,128)(2,1)}, bf16[4,15,32,128]{3,2,1,0:T(8,128)(2,1)}, bf16[4,32,128]{2,1,0:T(8,128)(2,1)}) custom-call(bf16[576,512]{1,0:T(8,128)(2,1)} %stream.1, bf16[576,512]{1,0:T(8,128)(2,1)} %grad_out.1, bf16[512,256]{1,0:T(8,128)(2,1)} %up_weight.1, bf16[256,512]{1,0:T(8,128)(2,1)} %down_weight.1), custom_call_target="tpu_custom_call" | custom-call | flops 6899999744 | bytes 2097152 | tf_op jit(solution)/shard_map/pallas_call | solution.py:57
  24.0 0.6 collective-permute-done.__.far
  24.6 0.6 copy-done.9
  25.2 4.0 %all-to-all-start = ((bf16[8,72,512]{2,1,0:T(8,128)(2,1)}), bf16[8,72,512]{2,1,0:T(8,128)(2,1)S(1)}, u32[]{:S(2)}, u32[]{:S(2)}) async-start(bf16[8,72,512]{2,1,0:T(8,128)(2,1)} %shard_map.96), calls=%async_computation | async-start | bytes 1179648 | tf_op jit(solution)/shard_map/all_to_all | solution.py:305
  29.2 0.7 copy-done.10
  29.9 0.7 reshape.31.labels
  30.5 5.7 %shard_map.97 = (bf16[4,144,512]{2,1,0:T(8,128)(2,1)}, bf16[4,144,256]{2,1,0:T(8,128)(2,1)}, f32[4,144,144]{2,1,0:T(8,128)}, bf16[2,72,512]{2,1,0:T(8,128)(2,1)}) custom-call(s32[1]{0:T(128)} %bitcast.place, bf16[8,72,512]{2,1,0:T(8,128)(2,1)} %bitcast.10, bf16[8,72,512]{2,1,0:T(8,128)(2,1)} %bitcast.11, bf16[72,512]{1,0:T(8,128)(2,1)} %copy-done.9, ...), custom_call_target="tpu_custom_call" | custom-call | flops 5299999744 | bytes 2097152 | tf_op jit(solution)/shard_map/pallas_call | solution.py:57
  36.2 9.7 %all-to-all-done.parts = bf16[8,72,512]{2,1,0:T(8,128)(2,1)S(1)} async-done(((bf16[8,72,512]{2,1,0:T(8,128)(2,1)}), bf16[8,72,512]{2,1,0:T(8,128)(2,1)S(1)}, u32[]{:S(2)}, u32[]{:S(2)}) %all-to-all-start) | async-done | bytes 589856 | tf_op jit(solution)/shard_map/all_to_all | solution.py:305
  45.9 0.9 copy-done.1
  46.9 0.3 shard_map.98
  47.2 10.9 %collective-permute-start.1 = (bf16[72,512]{1,0:T(8,128)(2,1)S(1)}, bf16[72,512]{1,0:T(8,128)(2,1)S(1)}, u32[]{:S(2)}, u32[]{:S(2)}) collective-permute-start(bf16[72,512]{1,0:T(8,128)(2,1)S(1)} %get-tuple-element.22.own), channel_id=1, source_target_pairs={{8,0},{16,8},{24,16},{32,24},{40,32},{48,40},{56,48},{64,56},{72,6... | collective-permute-start | bytes 221192 | tf_op jit(solution)/shard_map/ppermute | solution.py:343
  58.0 2.0 %collective-permute-done.1.far = bf16[72,512]{1,0:T(8,128)(2,1)S(1)} collective-permute-done((bf16[72,512]{1,0:T(8,128)(2,1)S(1)}, bf16[72,512]{1,0:T(8,128)(2,1)S(1)}, u32[]{:S(2)}, u32[]{:S(2)}) %collective-permute-start.1) | collective-permute-done | bytes 73760 | tf_op jit(solution)/shard_map/ppermute | solution.py:343
  60.0 0.0 copy-start.2
  60.0 0.0 copy-start.3
  60.1 15.3 %all-gather = bf16[576,512]{1,0:T(8,128)(2,1)S(1)} all-gather(bf16[72,512]{1,0:T(8,128)(2,1)S(1)} %shard_map.99), channel_id=2, replica_groups=mesh['y'=8,'x'=4,'zh'=3,'zl'=4,'core'=2] {'zl','core'}, dimensions={0}, use_global_device_ids=true | all-gather | bytes 663552 | tf_op jit(solution)/shard_map/all_gather | solution.py:357
  75.4 5.4 %shard_map.100 = (bf16[8,72,512]{2,1,0:T(8,128)(2,1)}, bf16[24,32,128]{2,1,0:T(8,128)(2,1)S(1)}, bf16[24,32,128]{2,1,0:T(8,128)(2,1)S(1)}, bf16[24,32,128]{2,1,0:T(8,128)(2,1)S(1)}, bf16[24,32,128]{2,1,0:T(8,128)(2,1)S(1)}) custom-call(s32[1]{0:T(128)} %bitcast.1.place, bf16[8,72,512]{2,1,0:T(8,128)(2,1)S(1)} %bitcast.13, bf16[8,72,512]{2,1,0:T(8,128)(2,1)S(1)} %bitcast.14, ...), custom_call_target="tpu_custom_call" | custom-call | flops 7000000000 | bytes 2097152 | tf_op jit(solution)/shard_map/pallas_call | solution.py:57
  80.8 3.5 %all-to-all-start.1 = ((bf16[8,72,512]{2,1,0:T(8,128)(2,1)}), bf16[8,72,512]{2,1,0:T(8,128)(2,1)S(1)}, u32[]{:S(2)}, u32[]{:S(2)}) async-start(bf16[8,72,512]{2,1,0:T(8,128)(2,1)} %get-tuple-element.28), calls=%async_computation.1 | async-start | bytes 1179648 | tf_op jit(solution)/shard_map/all_to_all | solution.py:386
  84.3 1.9 %collective-permute-start.3 = (bf16[24,32,128]{2,1,0:T(8,128)(2,1)S(1)}, bf16[24,32,128]{2,1,0:T(8,128)(2,1)S(1)}, u32[]{:S(2)}, u32[]{:S(2)}) collective-permute-start(bf16[24,32,128]{2,1,0:T(8,128)(2,1)S(1)} %get-tuple-element.34), channel_id=1, source_target_pairs={{0,24},{24,48},{48,72},{72,0},{1,25},{25,49},{49,73},{73,1},{2,26}... | collective-permute-start | bytes 589832 | tf_op jit(solution)/shard_map/ppermute | solution.py:388
  86.3 2.2 %collective-permute-start.4 = (bf16[24,32,128]{2,1,0:T(8,128)(2,1)S(1)}, bf16[24,32,128]{2,1,0:T(8,128)(2,1)S(1)}, u32[]{:S(2)}, u32[]{:S(2)}) collective-permute-start(bf16[24,32,128]{2,1,0:T(8,128)(2,1)S(1)} %get-tuple-element.35), channel_id=1, source_target_pairs={{0,48},{24,72},{48,0},{72,24},{1,49},{25,73},{49,1},{73,25},{2,50}... | collective-permute-start | bytes 589832 | tf_op jit(solution)/shard_map/ppermute | solution.py:388
  88.5 4.9 %collective-permute-start.5 = (bf16[24,32,128]{2,1,0:T(8,128)(2,1)S(1)}, bf16[24,32,128]{2,1,0:T(8,128)(2,1)S(1)}, u32[]{:S(2)}, u32[]{:S(2)}) collective-permute-start(bf16[24,32,128]{2,1,0:T(8,128)(2,1)S(1)} %get-tuple-element.36), channel_id=1, source_target_pairs={{0,72},{24,0},{48,24},{72,48},{1,73},{25,1},{49,25},{73,49},{2,74}... | collective-permute-start | bytes 589832 | tf_op jit(solution)/shard_map/ppermute | solution.py:388
  93.4 5.5 %collective-permute-done.3.second = bf16[24,32,128]{2,1,0:T(8,128)(2,1)S(1)} collective-permute-done((bf16[24,32,128]{2,1,0:T(8,128)(2,1)S(1)}, bf16[24,32,128]{2,1,0:T(8,128)(2,1)S(1)}, u32[]{:S(2)}, u32[]{:S(2)}) %collective-permute-start.3) | collective-permute-done | bytes 196640 | tf_op jit(solution)/shard_map/ppermute | solution.py:388
  98.9 0.0 collective-permute-done.4.third
  98.9 2.5 %collective-permute-done.5.fourth = bf16[24,32,128]{2,1,0:T(8,128)(2,1)S(1)} collective-permute-done((bf16[24,32,128]{2,1,0:T(8,128)(2,1)S(1)}, bf16[24,32,128]{2,1,0:T(8,128)(2,1)S(1)}, u32[]{:S(2)}, u32[]{:S(2)}) %collective-permute-start.5) | collective-permute-done | bytes 196640 | tf_op jit(solution)/shard_map/ppermute | solution.py:388
  101.4 0.8 shard_map.103
  102.2 14.4 %all-to-all-start.2 = ((bf16[24,32,128]{2,1,0:T(8,128)(2,1)}), bf16[24,32,128]{2,1,0:T(8,128)(2,1)S(1)}, u32[]{:S(2)}, u32[]{:S(2)}) async-start(bf16[24,32,128]{2,1,0:T(8,128)(2,1)} %shard_map.103), calls=%async_computation.2 | async-start | bytes 393216 | tf_op jit(solution)/shard_map/all_to_all | solution.py:411
  116.6 0.1 shard_map.101
  116.7 7.3 %collective-permute-start.2 = (bf16[72,512]{1,0:T(8,128)(2,1)S(1)}, bf16[72,512]{1,0:T(8,128)(2,1)S(1)}, u32[]{:S(2)}, u32[]{:S(2)}) collective-permute-start(bf16[72,512]{1,0:T(8,128)(2,1)S(1)} %get-tuple-element.30), channel_id=1, source_target_pairs={{0,8},{8,16},{16,24},{24,32},{32,40},{40,48},{48,56},{56,64},{64,7... | collective-permute-start | bytes 221192 | tf_op jit(solution)/shard_map/ppermute | solution.py:406
  124.0 9.2 %collective-permute-done.2.arrived = bf16[72,512]{1,0:T(8,128)(2,1)S(1)} collective-permute-done((bf16[72,512]{1,0:T(8,128)(2,1)S(1)}, bf16[72,512]{1,0:T(8,128)(2,1)S(1)}, u32[]{:S(2)}, u32[]{:S(2)}) %collective-permute-start.2) | collective-permute-done | bytes 73760 | tf_op jit(solution)/shard_map/ppermute | solution.py:406
  133.2 0.9 shard_map.102
  134.1 0.6 shard_map.104
  (21 shorter events, 0.1 us)
Async XLA Ops:
  1.5 23.0 %collective-permute-start = (bf16[72,512]{1,0:T(8,128)(2,1)S(1)}, bf16[72,512]{1,0:T(8,128)(2,1)S(1)}, u32[]{:S(2)}, u32[]{:S(2)}) collective-permute-start(bf16[72,512]{1,0:T(8,128)(2,1)S(1)} %slice.3), channel_id=1, source_target_pairs={{8,0},{16,8},{24,16},{32,24},{40,32},{48,40},{56,48},{64,56},{72,6... | collective-permute-start | bytes 221192 | tf_op jit(solution)/shard_map/ppermute | solution.py:292
  24.5 0.6 copy-start.9
  25.2 20.8 %all-to-all-start = ((bf16[8,72,512]{2,1,0:T(8,128)(2,1)}), bf16[8,72,512]{2,1,0:T(8,128)(2,1)S(1)}, u32[]{:S(2)}, u32[]{:S(2)}) async-start(bf16[8,72,512]{2,1,0:T(8,128)(2,1)} %shard_map.96), calls=%async_computation | async-start | bytes 1179648 | tf_op jit(solution)/shard_map/all_to_all | solution.py:305
  29.2 0.7 copy-start.10
  30.5 44.8 %copy-start.7 = (bf16[4,15,32,128]{3,2,1,0:T(8,128)(2,1)S(1)}, bf16[4,15,32,128]{3,2,1,0:T(8,128)(2,1)}, u32[]{:S(2)}) copy-start(bf16[4,15,32,128]{3,2,1,0:T(8,128)(2,1)} %get-tuple-element.27.late) | copy-start | bytes 1474564
  45.9 0.9 copy-start.1
  46.9 28.5 %copy-start.5 = (f32[4,144,144]{2,1,0:T(8,128)S(1)}, f32[4,144,144]{2,1,0:T(8,128)}, u32[]{:S(2)}) copy-start(f32[4,144,144]{2,1,0:T(8,128)} %get-tuple-element.25.probs) | copy-start | bytes 995332
  46.9 28.5 %copy-start.6 = (bf16[4,144,256]{2,1,0:T(8,128)(2,1)S(1)}, bf16[4,144,256]{2,1,0:T(8,128)(2,1)}, u32[]{:S(2)}) copy-start(bf16[4,144,256]{2,1,0:T(8,128)(2,1)} %get-tuple-element.24.packed) | copy-start | bytes 884740
  47.1 28.2 %copy-start.4 = (bf16[4,144,512]{2,1,0:T(8,128)(2,1)S(1)}, bf16[4,144,512]{2,1,0:T(8,128)(2,1)}, u32[]{:S(2)}) copy-start(bf16[4,144,512]{2,1,0:T(8,128)(2,1)} %get-tuple-element.23.hidden) | copy-start | bytes 1769476
  47.2 12.8 %collective-permute-start.1 = (bf16[72,512]{1,0:T(8,128)(2,1)S(1)}, bf16[72,512]{1,0:T(8,128)(2,1)S(1)}, u32[]{:S(2)}, u32[]{:S(2)}) collective-permute-start(bf16[72,512]{1,0:T(8,128)(2,1)S(1)} %get-tuple-element.22.own), channel_id=1, source_target_pairs={{8,0},{16,8},{24,16},{32,24},{40,32},{48,40},{56,48},{64,56},{72,6... | collective-permute-start | bytes 221192 | tf_op jit(solution)/shard_map/ppermute | solution.py:343
  60.0 15.4 %copy-start.2 = (bf16[3,512,64]{1,2,0:T(8,128)(2,1)S(1)}, bf16[3,512,64]{1,2,0:T(8,128)(2,1)}, u32[]{:S(2)}) copy-start(bf16[3,512,64]{1,2,0:T(8,128)(2,1)} %param.12) | copy-start | bytes 589828
  60.0 15.4 %copy-start.3 = (bf16[64,512]{1,0:T(8,128)(2,1)S(1)}, bf16[64,512]{1,0:T(8,128)(2,1)}, u32[]{:S(2)}) copy-start(bf16[64,512]{1,0:T(8,128)(2,1)} %out_weight.1) | copy-start | bytes 196612
  60.0 15.4 %copy-start.8 = (bf16[4,32,128]{2,1,0:T(8,128)(2,1)S(1)}, bf16[4,32,128]{2,1,0:T(8,128)(2,1)}, u32[]{:S(2)}) copy-start(bf16[4,32,128]{2,1,0:T(8,128)(2,1)} %get-tuple-element.26.early) | copy-start | bytes 98308
  80.8 21.4 %all-to-all-start.1 = ((bf16[8,72,512]{2,1,0:T(8,128)(2,1)}), bf16[8,72,512]{2,1,0:T(8,128)(2,1)S(1)}, u32[]{:S(2)}, u32[]{:S(2)}) async-start(bf16[8,72,512]{2,1,0:T(8,128)(2,1)} %get-tuple-element.28), calls=%async_computation.1 | async-start | bytes 1179648 | tf_op jit(solution)/shard_map/all_to_all | solution.py:386
  84.3 14.5 %collective-permute-start.3 = (bf16[24,32,128]{2,1,0:T(8,128)(2,1)S(1)}, bf16[24,32,128]{2,1,0:T(8,128)(2,1)S(1)}, u32[]{:S(2)}, u32[]{:S(2)}) collective-permute-start(bf16[24,32,128]{2,1,0:T(8,128)(2,1)S(1)} %get-tuple-element.34), channel_id=1, source_target_pairs={{0,24},{24,48},{48,72},{72,0},{1,25},{25,49},{49,73},{73,1},{2,26}... | collective-permute-start | bytes 589832 | tf_op jit(solution)/shard_map/ppermute | solution.py:388
  86.3 12.6 %collective-permute-start.4 = (bf16[24,32,128]{2,1,0:T(8,128)(2,1)S(1)}, bf16[24,32,128]{2,1,0:T(8,128)(2,1)S(1)}, u32[]{:S(2)}, u32[]{:S(2)}) collective-permute-start(bf16[24,32,128]{2,1,0:T(8,128)(2,1)S(1)} %get-tuple-element.35), channel_id=1, source_target_pairs={{0,48},{24,72},{48,0},{72,24},{1,49},{25,73},{49,1},{73,25},{2,50}... | collective-permute-start | bytes 589832 | tf_op jit(solution)/shard_map/ppermute | solution.py:388
  88.5 12.9 %collective-permute-start.5 = (bf16[24,32,128]{2,1,0:T(8,128)(2,1)S(1)}, bf16[24,32,128]{2,1,0:T(8,128)(2,1)S(1)}, u32[]{:S(2)}, u32[]{:S(2)}) collective-permute-start(bf16[24,32,128]{2,1,0:T(8,128)(2,1)S(1)} %get-tuple-element.36), channel_id=1, source_target_pairs={{0,72},{24,0},{48,24},{72,48},{1,73},{25,1},{49,25},{73,49},{2,74}... | collective-permute-start | bytes 589832 | tf_op jit(solution)/shard_map/ppermute | solution.py:388
  102.2 31.0 %copy-start = (bf16[576,512]{1,0:T(8,128)(2,1)S(1)}, bf16[576,512]{1,0:T(8,128)(2,1)}, u32[]{:S(2)}) copy-start(bf16[576,512]{1,0:T(8,128)(2,1)} %param.8) | copy-start | bytes 1769476
  102.2 31.9 %all-to-all-start.2 = ((bf16[24,32,128]{2,1,0:T(8,128)(2,1)}), bf16[24,32,128]{2,1,0:T(8,128)(2,1)S(1)}, u32[]{:S(2)}, u32[]{:S(2)}) async-start(bf16[24,32,128]{2,1,0:T(8,128)(2,1)} %shard_map.103), calls=%async_computation.2 | async-start | bytes 393216 | tf_op jit(solution)/shard_map/all_to_all | solution.py:411
  116.7 16.5 %collective-permute-start.2 = (bf16[72,512]{1,0:T(8,128)(2,1)S(1)}, bf16[72,512]{1,0:T(8,128)(2,1)S(1)}, u32[]{:S(2)}, u32[]{:S(2)}) collective-permute-start(bf16[72,512]{1,0:T(8,128)(2,1)S(1)} %get-tuple-element.30), channel_id=1, source_target_pairs={{0,8},{8,16},{16,24},{24,32},{32,40},{40,48},{48,56},{56,64},{64,7... | collective-permute-start | bytes 221192 | tf_op jit(solution)/shard_map/ppermute | solution.py:406

commit v9 on v7

--- a/solution.py
+++ b/solution.py
@@ -70,7 +70,8 @@
 
 
 def mlp_kernel(
-    stream, grad_out, up_weight, down_weight, unit_grad, late, early, up_sum, down_sum, rows_f32
+    place, stream, grad_out, up_weight, down_weight, keep, give, late, early, up_sum, down_sum,
+    rows_f32,
 ):
     step = pl.program_id(0)
     unit = normalize(stream[...])[0].astype(BF)
@@ -85,8 +86,9 @@
     pre_grad = (upper * slope).astype(BF)
     act = (0.5 * pre * (1.0 + bent)).astype(BF)
     grad = contract_cols(pre_grad, up_weight[...])
-    unit_grad[0] = grad[:HALF].astype(BF)
-    unit_grad[1] = grad[HALF:].astype(BF)
+    even = place[0] == 0
+    keep[0] = jnp.where(even, grad[:HALF], grad[HALF:]).astype(BF)
+    give[0] = jnp.where(even, grad[HALF:], grad[:HALF]).astype(BF)
     up_part = contract_rows(unit, pre_grad)
     down_part = contract_rows(act, grad_out[...])
 
@@ -115,20 +117,20 @@
             if owner < 36:
                 early[owner - 32] = block
             else:
-                late[owner % 12 // 3, owner // 12 * 3 + owner % 3 - 9] = block
-
-
-def mlp(stream, grad_out, up_weight, down_weight):
+                late[owner % 12 // 3 * 15 + owner // 12 * 3 + owner % 3 - 9] = block
+
+
+def mlp(place, stream, grad_out, up_weight, down_weight):
     rows, width = stream.shape
     units = up_weight.shape[1]
-    part = lambda columns: pl.BlockSpec((WIN, columns), lambda i: (i, 0))
-    late = jax.ShapeDtypeStruct((4, 15) + BLOCK, BF)
+    part = lambda columns: pl.BlockSpec((WIN, columns), lambda i, _: (i, 0))
+    late = jax.ShapeDtypeStruct((60,) + BLOCK, BF)
     early = jax.ShapeDtypeStruct((4,) + BLOCK, BF)
     return call(
         mlp_kernel,
         (rows // WIN,),
         [part(width), part(width), whole(up_weight), whole(down_weight)],
-        [((rows // HALF, HALF, width), BF, pl.BlockSpec((2, HALF, width), lambda i: (i, 0, 0)))]
+        [((rows // WIN, HALF, width), BF, pl.BlockSpec((1, HALF, width), lambda i, _: (i, 0, 0)))] * 2
         + [(late.shape, BF, whole(late)), (early.shape, BF, whole(early))],
         (stream, grad_out, up_weight, down_weight),
         scratch=[
@@ -136,6 +138,7 @@
             pltpu.VMEM((units, width), F32),
             pltpu.VMEM((64 * 32, 128), F32),
         ],
+        chosen=place,
         flops=69 * 10**8,
     )
 
@@ -167,7 +170,7 @@
 
 
 def last_forward_kernel(
-    lead, tail, labels, turned_qkv, _, __, ___, hidden, packed, probs_out, token
+    lead, tail, labels, turned_qkv, hidden, packed, probs_out, token
 ):
     row = labels[labels.shape[0] - 1 :, :]
     hidden[0], parts, probs_out[0] = window_forward(lead[0], tail[...], row, turned_qkv)
@@ -179,7 +182,11 @@
     given[...] = jnp.where(place[0] == 0, far[...].astype(F32), own[...].astype(F32)).astype(BF)
 
 
-def middle_kernel(parts, own, _, mid, grad_mid, __):
+def pair_kernel(keep, taken, pair):
+    pair[...] = (keep[...].astype(F32) + taken[...].astype(F32)).astype(BF)
+
+
+def middle_kernel(parts, own, mid, grad_mid):
     summed = jnp.sum(parts[...].astype(F32), axis=0)
     normed, factor = normalize(own[0])
     middle = own[1].astype(F32) + norm_back(normed, factor, summed)
@@ -206,14 +213,17 @@
 
 
 def backward_kernel(
-    place, lead, trail, hidden, packed, probs, turned_qkv, out_weight, early, in_grad, first, second,
-    third, fourth, qkv_sum, out_sum, grads, outs, pieces,
+    place, lead, trail, hidden, packed, probs, last_hidden, last_packed, last_probs, turned_qkv,
+    out_weight, early, _, in_grad, first, second, third, fourth, qkv_sum, out_sum, grads, outs, pieces,
 ):
     step = pl.program_id(0)
-    parts = [packed[0][:, HS * i : HS * i + HS] for i in range(4)]
+    last = step == pl.num_programs(0) - 1
+    saved = jnp.where(last, last_packed[0].astype(F32), packed[0].astype(F32)).astype(BF)
+    parts = [saved[:, HS * i : HS * i + HS] for i in range(4)]
+    inputs = jnp.where(last, last_hidden[0].astype(F32), hidden[0].astype(F32)).astype(BF)
     upper = jnp.concatenate([lead[0].astype(F32), trail[0].astype(F32)], axis=0).astype(BF)
     rows, qkv_part, out_part = window_back(
-        upper, hidden[0], parts, probs[0], turned_qkv, out_weight
+        upper, inputs, parts, jnp.where(last, last_probs[0], probs[0]), turned_qkv, out_weight
     )
     in_grad[2 * step + 1] = rows[:HALF].astype(BF)
     in_grad[lax.rem(2 * step + 2, in_grad.shape[0])] = rows[HALF:].astype(BF)
@@ -268,7 +278,7 @@
         third[...].astype(F32) + fourth[...].astype(F32)
     )
     joined[:count] = near.astype(BF)
-    joined[count:] = jnp.sum(late[...].astype(F32), axis=0).astype(BF)
+    joined[count:] = late[...]
 
 
 def total_kernel(received, _, owned):
@@ -294,8 +304,19 @@
         return lax.ppermute(values, WIN_AXES, [((i + 1) % count, i) for i in range(count)])
 
     far_input = from_next(block_input[:HALF])
-    unit_grad, late, early = mlp(stream, grad_out, up_weight, down_weight)
-    parts = lax.all_to_all(unit_grad, HEAD_AXES, 0, 0)
+    core_place = lax.axis_index("core").astype(jnp.int32).reshape(1)
+    keep, give, late, early = mlp(core_place, stream, grad_out, up_weight, down_weight)
+    late_sum = lax.psum_scatter(late, "x", scatter_dimension=0, tiled=True)
+    taken = lax.ppermute(give, "core", [(0, 1), (1, 0)])
+    (pair,) = call(
+        pair_kernel,
+        (1,),
+        [whole(keep), whole(taken)],
+        [(keep.shape, BF, whole(keep))],
+        (keep, taken),
+        vmem=16,
+    )
+    parts = lax.all_to_all(pair, "zl", 0, 0)
     labels = regions.reshape(windows, WIN)
     window = lambda columns: pl.BlockSpec((1, WIN, columns), lambda i, *_: (i, 0, 0))
     weights = (turned_qkv.reshape(-1, width), out_weight)
@@ -315,26 +336,21 @@
             mine,
         ],
         [
-            ((windows, WIN, width), BF, window(width)),
-            ((windows, WIN, 4 * columns), BF, window(4 * columns)),
-            ((windows, WIN, WIN), F32, window(WIN)),
+            ((windows - 1, WIN, width), BF, window(width)),
+            ((windows - 1, WIN, 4 * columns), BF, window(4 * columns)),
+            ((windows - 1, WIN, WIN), F32, window(WIN)),
             (own_rows.shape, BF, whole(own_rows)),
         ],
         (chunks_in, chunks_in, labels, weights[0], chunks_mid, chunks_out),
         chosen=head_place,
         flops=53 * 10**8,
     )
-    mid, own_grad_mid, late = call(
+    mid, own_grad_mid = call(
         middle_kernel,
         (1,),
-        [whole(parts), whole(own), ANY],
-        [
-            (row_part.shape, F32, whole(row_part)),
-            (row_part.shape, BF, whole(row_part)),
-            (late.shape, BF, ANY),
-        ],
-        (parts, own, late),
-        aliases={2: 2},
+        [whole(parts), whole(own)],
+        [(row_part.shape, F32, whole(row_part)), (row_part.shape, BF, whole(row_part))],
+        (parts, own),
         vmem=16,
     )
     far_grad = lax.ppermute(
@@ -342,9 +358,8 @@
         WIN_AXES + HEAD_AXES,
         [((i + 1) % count * head_count, i * head_count) for i in range(count)],
     )
-    late_parts = lax.all_to_all(late, "x", 0, 0)
-    final = lambda columns: pl.BlockSpec((1, WIN, columns), lambda i: (windows - 1, 0, 0))
-    hidden, packed, probs, done = call(
+    one = lambda columns: pl.BlockSpec((1, WIN, columns), lambda *_: (0, 0, 0))
+    *last, done = call(
         last_forward_kernel,
         (1,),
         [
@@ -352,18 +367,14 @@
             whole(far_input),
             whole(labels),
             whole(weights[0]),
-            ANY,
-            ANY,
-            ANY,
-        ],
-        [
-            (hidden.shape, BF, final(width)),
-            (packed.shape, BF, final(4 * columns)),
-            (probs.shape, F32, final(WIN)),
+        ],
+        [
+            ((1, WIN, width), BF, one(width)),
+            ((1, WIN, 4 * columns), BF, one(4 * columns)),
+            ((1, WIN, WIN), F32, one(WIN)),
             (token.shape, F32, whole(token)),
         ],
-        (chunks_in, far_input, labels, weights[0], hidden, packed, probs),
-        aliases={4: 0, 5: 1, 6: 2},
+        (chunks_in, far_input, labels, weights[0]),
         flops=20 * 10**8,
     )
     (given,) = call(
@@ -384,14 +395,19 @@
         [
             pl.BlockSpec(chunk, lambda i, _: (2 * i + 1, 0, 0)),
             pl.BlockSpec(chunk, lambda i, _: (lax.rem(2 * i + 2, head_count), 0, 0)),
-            window(width),
-            window(4 * columns),
-            window(WIN),
+            *[
+                pl.BlockSpec((1, WIN, size), lambda i, _: (jnp.minimum(i, windows - 2), 0, 0))
+                for size in (width, 4 * columns, WIN)
+            ],
+            one(width),
+            one(4 * columns),
+            one(WIN),
             *[whole(weight) for weight in weights],
             whole(early),
+            ANY,
         ],
         [(in_rows.shape, BF, whole(in_rows))] + [(piece.shape, BF, whole(piece))] * 4,
-        (grad_mid, grad_mid, hidden, packed, probs, *weights, early),
+        (grad_mid, grad_mid, hidden, packed, probs, *last, *weights, early, late_sum),
         scratch=[
             pltpu.VMEM((width, 3 * columns), F32),
             pltpu.VMEM((columns, width), F32),
@@ -411,9 +427,9 @@
     (partial_sum,) = call(
         join_kernel,
         (1,),
-        [whole(piece)] * 4 + [whole(late_parts)],
+        [whole(piece)] * 4 + [whole(late_sum)],
         [(joined.shape, BF, whole(joined))],
-        (pieces[0], *moved, late_parts),
+        (pieces[0], *moved, late_sum),
         vmem=16,
     )
     summed, summed_b = call(

time: 126 us -> 139 us (1.10)
  between operations: 0.82 us -> 14.3 us
  waiting for transfers between devices: 17.7 us -> 14.6 us
  local copies, waits for them, and re-layouts: 3.81 us -> 6.36 us
  starting transfers between devices: 66.7 us -> 65.3 us
    all_to_all x2 -> x1, starting transfers between devices: 16.2 us -> 7.26 us  [shards(): parts = lax.all_to_all(pair, 'zl', 0, 0)]
    all_to_all x1, starting transfers between devices: 6.47 us -> 13.8 us  [shards(): received = lax.all_to_all(partial_sum, ('y', 'zh'), 0, 0)]
    ppermute x1, starting transfers between devices: 12.1 us -> 6.92 us  [shards(): lax.ppermute(own_grad_mid, WIN_AXES + HEAD_AXES, [((i + 1) % count * head...]
    ppermute x3, starting transfers between devices: 8.68 us -> 11.9 us  [shards(): lax.ppermute(pieces[k], 'x', [(i, (i + k) % 4) for i in range(4)])]
    all_to_all x2 -> x1, waiting for transfers between devices: 2.98 us -> 0.01 us  [shards(): parts = lax.all_to_all(pair, 'zl', 0, 0)]
    unnamed x22 -> x34, local copies, waits for them, and re-layouts: 2.25 us -> 4.79 us
    ppermute x0 -> x1, starting transfers between devices: none -> 1.92 us  [shards(): taken = lax.ppermute(give, 'core', [(0, 1), (1, 0)])]
    ppermute x0 -> x1, waiting for transfers between devices: none -> 1.76 us  [shards(): taken = lax.ppermute(give, 'core', [(0, 1), (1, 0)])]
  transfers between devices with their start and end apart: 10 -> 11, of which waited for: 6 -> 5; matrix products, arithmetic and copies ran while one was open for 1% -> 1% of each run, Pallas kernels for 12% -> 7%
where the time goes in v9:
time: 139 us; the launch traced here: 138 us
  starting transfers between devices  65.3 us (47%)
  Pallas kernels  21.9 us (16%)
  blocking collectives  15.3 us (11%)
  waiting for transfers between devices  14.6 us (11%)
  between operations  14.3 us (10%)
  local copies, waits for them, and re-layouts  6.36 us (5%)
    pallas_call x11, Pallas kernels, call(): pl.pallas_call(kernel, grid_spec=spec, out_shape=[jax.ShapeDtypeStruct(ou...  21.9 us
    all_gather x1, blocking collectives, shards(): grad_mid = lax.all_gather(given, HEAD_AXES, axis=0)  15.3 us
    all_to_all x1, starting transfers between devices, shards(): received = lax.all_to_all(partial_sum, ('y', 'zh'), 0, 0)  13.8 us
    ppermute x1, starting transfers between devices, from_next(): lax.ppermute(values, WIN_AXES, [((i + 1) % count, i) for i in range(count)])  12.1 us
    ppermute x3, starting transfers between devices, shards(): lax.ppermute(pieces[k], 'x', [(i, (i + k) % 4) for i in range(4)])  11.9 us
    ppermute x1, starting transfers between devices, shards(): lax.ppermute(summed_b, WIN_AXES + HEAD_AXES, [(i * head_count, (i + 1) %...  7.66 us
    all_to_all x1, starting transfers between devices, shards(): parts = lax.all_to_all(pair, 'zl', 0, 0)  7.26 us
    ppermute x1, starting transfers between devices, shards(): lax.ppermute(own_grad_mid, WIN_AXES + HEAD_AXES, [((i + 1) % count * head...  6.92 us
  transfers between devices with their start and end apart: 11, of which 5 were waited for; matrix products, arithmetic and copies ran while one was open for 1% of the time, Pallas kernels for 7%

profile of v9, /device:TPU:6, one launch (start us, length us, event | category | flops | bytes accessed | tf_op | source)
XLA Modules:
  0.0 137.8 jit_solution(10606429523813848978)
XLA Ops:
  7.2 5.8 %shard_map.95 = (bf16[4,72,512]{2,1,0:T(8,128)(2,1)}, bf16[4,72,512]{2,1,0:T(8,128)(2,1)}, bf16[60,32,128]{2,1,0:T(8,128)(2,1)}, bf16[4,32,128]{2,1,0:T(8,128)(2,1)}) custom-call(s32[1]{0:T(128)} %bitcast.2.place, bf16[576,512]{1,0:T(8,128)(2,1)} %stream.1, bf16[576,512]{1,0:T(8,128)(2,1)} %grad_out.1, bf16[512,256]{1,0:T(8,128)(2,1)} %up_weight.1, ...), custom_call_target="tpu_custom_call" | custom-call | flops 6899999744 | bytes 2097152 | tf_op jit(solution)/shard_map/pallas_call | solution.py:57
  13.0 1.9 %collective-permute-start = (bf16[4,72,512]{2,1,0:T(8,128)(2,1)}, bf16[4,72,512]{2,1,0:T(8,128)(2,1)S(1)}, u32[]{:S(2)}, u32[]{:S(2)}) collective-permute-start(bf16[4,72,512]{2,1,0:T(8,128)(2,1)} %get-tuple-element.26), channel_id=1, source_target_pairs={{0,1},{1,0},{2,3},{3,2},{4,5},{5,4},{6,7},{7,6},{8,9},{9,8},{10,11... | collective-permute-start | bytes 884744 | tf_op jit(solution)/shard_map/ppermute | solution.py:310
  14.9 1.8 %collective-permute-done.taken = bf16[4,72,512]{2,1,0:T(8,128)(2,1)S(1)} collective-permute-done((bf16[4,72,512]{2,1,0:T(8,128)(2,1)}, bf16[4,72,512]{2,1,0:T(8,128)(2,1)S(1)}, u32[]{:S(2)}, u32[]{:S(2)}) %collective-permute-start) | collective-permute-done | bytes 294944 | tf_op jit(solution)/shard_map/ppermute | solution.py:310
  16.7 1.0 copy-done.1
  17.6 0.8 shard_map.96
  18.4 7.3 %all-to-all-start = ((bf16[4,72,512]{2,1,0:T(8,128)(2,1)}), bf16[4,72,512]{2,1,0:T(8,128)(2,1)S(1)}, u32[]{:S(2)}, u32[]{:S(2)}) async-start(bf16[4,72,512]{2,1,0:T(8,128)(2,1)} %shard_map.96), calls=%async_computation | async-start | bytes 589824 | tf_op jit(solution)/shard_map/all_to_all | solution.py:319
  25.7 0.7 reduce-scatter.2.cloned.1.call-update
  26.4 0.9 slice.3
  27.3 12.1 %collective-permute-start.2 = (bf16[72,512]{1,0:T(8,128)(2,1)S(1)}, bf16[72,512]{1,0:T(8,128)(2,1)S(1)}, u32[]{:S(2)}, u32[]{:S(2)}) collective-permute-start(bf16[72,512]{1,0:T(8,128)(2,1)S(1)} %slice.3), channel_id=1, source_target_pairs={{8,0},{16,8},{24,16},{32,24},{40,32},{48,40},{56,48},{64,56},{72,6... | collective-permute-start | bytes 221192 | tf_op jit(solution)/shard_map/ppermute | solution.py:304
  39.4 0.7 copy-done.15
  40.1 0.7 reshape.35.labels
  40.8 4.6 %shard_map.97 = (bf16[3,144,512]{2,1,0:T(8,128)(2,1)}, bf16[3,144,256]{2,1,0:T(8,128)(2,1)}, f32[3,144,144]{2,1,0:T(8,128)}, bf16[2,72,512]{2,1,0:T(8,128)(2,1)}) custom-call(s32[1]{0:T(128)} %bitcast.place, bf16[8,72,512]{2,1,0:T(8,128)(2,1)} %bitcast.11, bf16[8,72,512]{2,1,0:T(8,128)(2,1)} %bitcast.12, s32[4,144]{1,0:T(4,128)} %reshape.35.labels, ...), custom_call_target="tpu_custom_call" | custom-call | flops 5299999744 | bytes 2097152 | tf_op jit(solution)/shard_map/pallas_call | solution.py:57
  45.4 0.9 copy-done.2
  46.6 6.9 %collective-permute-start.1 = (bf16[72,512]{1,0:T(8,128)(2,1)S(1)}, bf16[72,512]{1,0:T(8,128)(2,1)S(1)}, u32[]{:S(2)}, u32[]{:S(2)}) collective-permute-start(bf16[72,512]{1,0:T(8,128)(2,1)S(1)} %get-tuple-element.28.own), channel_id=1, source_target_pairs={{8,0},{16,8},{24,16},{32,24},{40,32},{48,40},{56,48},{64,56},{72,6... | collective-permute-start | bytes 221192 | tf_op jit(solution)/shard_map/ppermute | solution.py:356
  54.2 2.7 %shard_map.99 = (bf16[1,144,512]{2,1,0:T(8,128)(2,1)}, bf16[1,144,256]{2,1,0:T(8,128)(2,1)}, f32[1,144,144]{2,1,0:T(8,128)}, f32[8,128]{1,0:T(8,128)}) custom-call(bf16[8,72,512]{2,1,0:T(8,128)(2,1)} %bitcast.13, bf16[72,512]{1,0:T(8,128)(2,1)} %copy-done.16, s32[4,144]{1,0:T(4,128)} %reshape.35.labels, bf16[192,512]{1,0:T(8,128)(2,1)} %bitcast.18), custom_call_target="tpu_custom_call" | custom-call | flops 2000000000 | bytes 2097152 | tf_op jit(solution)/shard_map/pallas_call | solution.py:57
  56.9 0.7 copy-done.7
  57.7 15.3 %all-gather = bf16[576,512]{1,0:T(8,128)(2,1)S(1)} all-gather(bf16[72,512]{1,0:T(8,128)(2,1)S(1)} %shard_map.100), channel_id=2, replica_groups=mesh['y'=8,'x'=4,'zh'=3,'zl'=4,'core'=2] {'zl','core'}, dimensions={0}, use_global_device_ids=true | all-gather | bytes 663552 | tf_op jit(solution)/shard_map/all_gather | solution.py:389
  73.1 0.9 copy-done.3
  73.9 5.3 %shard_map.101 = (bf16[8,72,512]{2,1,0:T(8,128)(2,1)}, bf16[9,32,128]{2,1,0:T(8,128)(2,1)S(1)}, bf16[9,32,128]{2,1,0:T(8,128)(2,1)S(1)}, bf16[9,32,128]{2,1,0:T(8,128)(2,1)S(1)}, bf16[9,32,128]{2,1,0:T(8,128)(2,1)S(1)}) custom-call(s32[1]{0:T(128)} %bitcast.1.place, bf16[8,72,512]{2,1,0:T(8,128)(2,1)S(1)} %bitcast.15, bf16[8,72,512]{2,1,0:T(8,128)(2,1)S(1)} %bitcast.16, ...), custom_call_target="tpu_custom_call" | custom-call | flops 7000000000 | bytes 2097152 | tf_op jit(solution)/shard_map/pallas_call | solution.py:57
  79.3 3.7 %all-to-all-start.1 = ((bf16[8,72,512]{2,1,0:T(8,128)(2,1)}), bf16[8,72,512]{2,1,0:T(8,128)(2,1)S(1)}, u32[]{:S(2)}, u32[]{:S(2)}) async-start(bf16[8,72,512]{2,1,0:T(8,128)(2,1)} %get-tuple-element.38), calls=%async_computation.2 | async-start | bytes 1179648 | tf_op jit(solution)/shard_map/all_to_all | solution.py:422
  82.9 7.2 %collective-permute-start.4 = (bf16[9,32,128]{2,1,0:T(8,128)(2,1)S(1)}, bf16[9,32,128]{2,1,0:T(8,128)(2,1)S(1)}, u32[]{:S(2)}, u32[]{:S(2)}) collective-permute-start(bf16[9,32,128]{2,1,0:T(8,128)(2,1)S(1)} %get-tuple-element.44), channel_id=1, source_target_pairs={{0,24},{24,48},{48,72},{72,0},{1,25},{25,49},{49,73},{73,1},{2,26}... | collective-permute-start | bytes 221192 | tf_op jit(solution)/shard_map/ppermute | solution.py:424
  90.1 1.9 %collective-permute-start.5 = (bf16[9,32,128]{2,1,0:T(8,128)(2,1)S(1)}, bf16[9,32,128]{2,1,0:T(8,128)(2,1)S(1)}, u32[]{:S(2)}, u32[]{:S(2)}) collective-permute-start(bf16[9,32,128]{2,1,0:T(8,128)(2,1)S(1)} %get-tuple-element.45), channel_id=1, source_target_pairs={{0,48},{24,72},{48,0},{72,24},{1,49},{25,73},{49,1},{73,25},{2,50}... | collective-permute-start | bytes 221192 | tf_op jit(solution)/shard_map/ppermute | solution.py:424
  92.1 2.8 %collective-permute-start.6 = (bf16[9,32,128]{2,1,0:T(8,128)(2,1)S(1)}, bf16[9,32,128]{2,1,0:T(8,128)(2,1)S(1)}, u32[]{:S(2)}, u32[]{:S(2)}) collective-permute-start(bf16[9,32,128]{2,1,0:T(8,128)(2,1)S(1)} %get-tuple-element.46), channel_id=1, source_target_pairs={{0,72},{24,0},{48,24},{72,48},{1,73},{25,1},{49,25},{73,49},{2,74}... | collective-permute-start | bytes 221192 | tf_op jit(solution)/shard_map/ppermute | solution.py:424
  94.9 3.0 %collective-permute-done.5.third = bf16[9,32,128]{2,1,0:T(8,128)(2,1)S(1)} collective-permute-done((bf16[9,32,128]{2,1,0:T(8,128)(2,1)S(1)}, bf16[9,32,128]{2,1,0:T(8,128)(2,1)S(1)}, u32[]{:S(2)}, u32[]{:S(2)}) %collective-permute-start.5) | collective-permute-done | bytes 73760 | tf_op jit(solution)/shard_map/ppermute | solution.py:424
  97.9 1.6 %collective-permute-done.6.fourth = bf16[9,32,128]{2,1,0:T(8,128)(2,1)S(1)} collective-permute-done((bf16[9,32,128]{2,1,0:T(8,128)(2,1)S(1)}, bf16[9,32,128]{2,1,0:T(8,128)(2,1)S(1)}, u32[]{:S(2)}, u32[]{:S(2)}) %collective-permute-start.6) | collective-permute-done | bytes 73760 | tf_op jit(solution)/shard_map/ppermute | solution.py:424
  99.5 0.7 shard_map.104
  100.3 13.8 %all-to-all-start.2 = ((bf16[24,32,128]{2,1,0:T(8,128)(2,1)}), bf16[24,32,128]{2,1,0:T(8,128)(2,1)S(1)}, u32[]{:S(2)}, u32[]{:S(2)}) async-start(bf16[24,32,128]{2,1,0:T(8,128)(2,1)} %shard_map.104), calls=%async_computation.3 | async-start | bytes 393216 | tf_op jit(solution)/shard_map/all_to_all | solution.py:448
  114.2 7.7 %collective-permute-start.3 = (bf16[72,512]{1,0:T(8,128)(2,1)S(1)}, bf16[72,512]{1,0:T(8,128)(2,1)S(1)}, u32[]{:S(2)}, u32[]{:S(2)}) collective-permute-start(bf16[72,512]{1,0:T(8,128)(2,1)S(1)} %get-tuple-element.40), channel_id=1, source_target_pairs={{0,8},{8,16},{16,24},{24,32},{32,40},{40,48},{48,56},{56,64},{64,7... | collective-permute-start | bytes 221192 | tf_op jit(solution)/shard_map/ppermute | solution.py:443
  121.9 3.4 %collective-permute-done.3.arrived = bf16[72,512]{1,0:T(8,128)(2,1)S(1)} collective-permute-done((bf16[72,512]{1,0:T(8,128)(2,1)S(1)}, bf16[72,512]{1,0:T(8,128)(2,1)S(1)}, u32[]{:S(2)}, u32[]{:S(2)}) %collective-permute-start.3) | collective-permute-done | bytes 73760 | tf_op jit(solution)/shard_map/ppermute | solution.py:443
  125.3 0.9 shard_map.103
  126.2 4.1 %all-to-all-done.2.received = bf16[24,32,128]{2,1,0:T(8,128)(2,1)S(1)} async-done(((bf16[24,32,128]{2,1,0:T(8,128)(2,1)}), bf16[24,32,128]{2,1,0:T(8,128)(2,1)S(1)}, u32[]{:S(2)}, u32[]{:S(2)}) %all-to-all-start.2) | async-done | bytes 196640 | tf_op jit(solution)/shard_map/all_to_all | solution.py:448
  130.3 0.6 shard_map.105
  (39 shorter events, 1.1 us)
Async XLA Ops:
  13.0 3.7 %collective-permute-start = (bf16[4,72,512]{2,1,0:T(8,128)(2,1)}, bf16[4,72,512]{2,1,0:T(8,128)(2,1)S(1)}, u32[]{:S(2)}, u32[]{:S(2)}) collective-permute-start(bf16[4,72,512]{2,1,0:T(8,128)(2,1)} %get-tuple-element.26), channel_id=1, source_target_pairs={{0,1},{1,0},{2,3},{3,2},{4,5},{5,4},{6,7},{7,6},{8,9},{9,8},{10,11... | collective-permute-start | bytes 884744 | tf_op jit(solution)/shard_map/ppermute | solution.py:310
  16.7 1.0 copy-start.1
  18.4 27.0 %all-to-all-start = ((bf16[4,72,512]{2,1,0:T(8,128)(2,1)}), bf16[4,72,512]{2,1,0:T(8,128)(2,1)S(1)}, u32[]{:S(2)}, u32[]{:S(2)}) async-start(bf16[4,72,512]{2,1,0:T(8,128)(2,1)} %shard_map.96), calls=%async_computation | async-start | bytes 589824 | tf_op jit(solution)/shard_map/all_to_all | solution.py:319
  25.7 47.3 %reduce-scatter.2.cloned.1.call-start = ((), (), s32[]{:S(2)}) async-start(), calls=%async_computation.4 | async-start | bytes 614400 | tf_op jit(solution)/shard_map/reduce_scatter | solution.py:309
  27.3 26.2 %collective-permute-start.2 = (bf16[72,512]{1,0:T(8,128)(2,1)S(1)}, bf16[72,512]{1,0:T(8,128)(2,1)S(1)}, u32[]{:S(2)}, u32[]{:S(2)}) collective-permute-start(bf16[72,512]{1,0:T(8,128)(2,1)S(1)} %slice.3), channel_id=1, source_target_pairs={{8,0},{16,8},{24,16},{32,24},{40,32},{48,40},{56,48},{64,56},{72,6... | collective-permute-start | bytes 221192 | tf_op jit(solution)/shard_map/ppermute | solution.py:304
  39.4 0.7 copy-start.15
  45.4 0.9 copy-start.2
  46.6 10.3 %collective-permute-start.1 = (bf16[72,512]{1,0:T(8,128)(2,1)S(1)}, bf16[72,512]{1,0:T(8,128)(2,1)S(1)}, u32[]{:S(2)}, u32[]{:S(2)}) collective-permute-start(bf16[72,512]{1,0:T(8,128)(2,1)S(1)} %get-tuple-element.28.own), channel_id=1, source_target_pairs={{8,0},{16,8},{24,16},{32,24},{40,32},{48,40},{56,48},{64,56},{72,6... | collective-permute-start | bytes 221192 | tf_op jit(solution)/shard_map/ppermute | solution.py:356
  53.5 0.6 copy-start.16
  54.2 18.8 %copy-start.11 = (bf16[3,144,512]{2,1,0:T(8,128)(2,1)S(1)}, bf16[3,144,512]{2,1,0:T(8,128)(2,1)}, u32[]{:S(2)}) copy-start(bf16[3,144,512]{2,1,0:T(8,128)(2,1)} %get-tuple-element.30.hidden) | copy-start | bytes 1327108
  54.2 18.8 %copy-start.12 = (f32[3,144,144]{2,1,0:T(8,128)S(1)}, f32[3,144,144]{2,1,0:T(8,128)}, u32[]{:S(2)}) copy-start(f32[3,144,144]{2,1,0:T(8,128)} %get-tuple-element.32.probs) | copy-start | bytes 746500
  56.9 0.7 copy-start.7
  57.6 15.4 %copy-start.13 = (bf16[3,144,256]{2,1,0:T(8,128)(2,1)S(1)}, bf16[3,144,256]{2,1,0:T(8,128)(2,1)}, u32[]{:S(2)}) copy-start(bf16[3,144,256]{2,1,0:T(8,128)(2,1)} %get-tuple-element.31.packed) | copy-start | bytes 663556
  57.6 15.4 %copy-start.5 = (bf16[3,512,64]{1,2,0:T(8,128)(2,1)S(1)}, bf16[3,512,64]{1,2,0:T(8,128)(2,1)}, u32[]{:S(2)}) copy-start(bf16[3,512,64]{1,2,0:T(8,128)(2,1)} %param.12) | copy-start | bytes 589828
  57.6 15.4 %copy-start.6 = (bf16[64,512]{1,0:T(8,128)(2,1)S(1)}, bf16[64,512]{1,0:T(8,128)(2,1)}, u32[]{:S(2)}) copy-start(bf16[64,512]{1,0:T(8,128)(2,1)} %out_weight.1) | copy-start | bytes 196612
  57.6 15.4 %copy-start.8 = (bf16[1,144,512]{2,1,0:T(8,128)(2,1)S(1)}, bf16[1,144,512]{2,1,0:T(8,128)(2,1)}, u32[]{:S(2)}) copy-start(bf16[1,144,512]{2,1,0:T(8,128)(2,1)} %get-tuple-element.33.last_hidden) | copy-start | bytes 442372
  57.6 15.4 %copy-start.9 = (f32[1,144,144]{2,1,0:T(8,128)S(1)}, f32[1,144,144]{2,1,0:T(8,128)}, u32[]{:S(2)}) copy-start(f32[1,144,144]{2,1,0:T(8,128)} %get-tuple-element.35.last_probs) | copy-start | bytes 248836
  57.6 15.4 %copy-start.10 = (bf16[1,144,256]{2,1,0:T(8,128)(2,1)S(1)}, bf16[1,144,256]{2,1,0:T(8,128)(2,1)}, u32[]{:S(2)}) copy-start(bf16[1,144,256]{2,1,0:T(8,128)(2,1)} %get-tuple-element.34.last_packed) | copy-start | bytes 221188
  57.6 15.4 %copy-start.14 = (bf16[4,32,128]{2,1,0:T(8,128)(2,1)S(1)}, bf16[4,32,128]{2,1,0:T(8,128)(2,1)}, u32[]{:S(2)}) copy-start(bf16[4,32,128]{2,1,0:T(8,128)(2,1)} %get-tuple-element.36.early) | copy-start | bytes 98308
  73.0 0.9 copy-start.3
  79.3 20.3 %copy-start.4 = (bf16[15,32,128]{2,1,0:T(8,128)(2,1)S(1)}, bf16[15,32,128]{2,1,0:T(8,128)(2,1)}, u32[]{:S(2)}) copy-start(bf16[15,32,128]{2,1,0:T(8,128)(2,1)} %reduce-scatter.2.cloned.1.call-done._.late) | copy-start | bytes 368644
  79.3 21.0 %all-to-all-start.1 = ((bf16[8,72,512]{2,1,0:T(8,128)(2,1)}), bf16[8,72,512]{2,1,0:T(8,128)(2,1)S(1)}, u32[]{:S(2)}, u32[]{:S(2)}) async-start(bf16[8,72,512]{2,1,0:T(8,128)(2,1)} %get-tuple-element.38), calls=%async_computation.2 | async-start | bytes 1179648 | tf_op jit(solution)/shard_map/all_to_all | solution.py:422
  82.9 11.9 %collective-permute-start.4 = (bf16[9,32,128]{2,1,0:T(8,128)(2,1)S(1)}, bf16[9,32,128]{2,1,0:T(8,128)(2,1)S(1)}, u32[]{:S(2)}, u32[]{:S(2)}) collective-permute-start(bf16[9,32,128]{2,1,0:T(8,128)(2,1)S(1)} %get-tuple-element.44), channel_id=1, source_target_pairs={{0,24},{24,48},{48,72},{72,0},{1,25},{25,49},{49,73},{73,1},{2,26}... | collective-permute-start | bytes 221192 | tf_op jit(solution)/shard_map/ppermute | solution.py:424
  90.1 7.8 %collective-permute-start.5 = (bf16[9,32,128]{2,1,0:T(8,128)(2,1)S(1)}, bf16[9,32,128]{2,1,0:T(8,128)(2,1)S(1)}, u32[]{:S(2)}, u32[]{:S(2)}) collective-permute-start(bf16[9,32,128]{2,1,0:T(8,128)(2,1)S(1)} %get-tuple-element.45), channel_id=1, source_target_pairs={{0,48},{24,72},{48,0},{72,24},{1,49},{25,73},{49,1},{73,25},{2,50}... | collective-permute-start | bytes 221192 | tf_op jit(solution)/shard_map/ppermute | solution.py:424
  92.1 7.5 %collective-permute-start.6 = (bf16[9,32,128]{2,1,0:T(8,128)(2,1)S(1)}, bf16[9,32,128]{2,1,0:T(8,128)(2,1)S(1)}, u32[]{:S(2)}, u32[]{:S(2)}) collective-permute-start(bf16[9,32,128]{2,1,0:T(8,128)(2,1)S(1)} %get-tuple-element.46), channel_id=1, source_target_pairs={{0,72},{24,0},{48,24},{72,48},{1,73},{25,1},{49,25},{73,49},{2,74}... | collective-permute-start | bytes 221192 | tf_op jit(solution)/shard_map/ppermute | solution.py:424
  100.2 25.0 %copy-start = (bf16[576,512]{1,0:T(8,128)(2,1)S(1)}, bf16[576,512]{1,0:T(8,128)(2,1)}, u32[]{:S(2)}) copy-start(bf16[576,512]{1,0:T(8,128)(2,1)} %param.8) | copy-start | bytes 1769476
  100.3 30.0 %all-to-all-start.2 = ((bf16[24,32,128]{2,1,0:T(8,128)(2,1)}), bf16[24,32,128]{2,1,0:T(8,128)(2,1)S(1)}, u32[]{:S(2)}, u32[]{:S(2)}) async-start(bf16[24,32,128]{2,1,0:T(8,128)(2,1)} %shard_map.104), calls=%async_computation.3 | async-start | bytes 393216 | tf_op jit(solution)/shard_map/all_to_all | solution.py:448
  114.2 11.1 %collective-permute-start.3 = (bf16[72,512]{1,0:T(8,128)(2,1)S(1)}, bf16[72,512]{1,0:T(8,128)(2,1)S(1)}, u32[]{:S(2)}, u32[]{:S(2)}) collective-permute-start(bf16[72,512]{1,0:T(8,128)(2,1)S(1)} %get-tuple-element.40), channel_id=1, source_target_pairs={{0,8},{8,16},{16,24},{24,32},{32,40},{40,48},{48,56},{56,64},{64,7... | collective-permute-start | bytes 221192 | tf_op jit(solution)/shard_map/ppermute | solution.py:443
Sparse Core Ops, SparseCore 0:
  29.6 33.1 reduce-scatter.1

commit v10 on v9

--- a/solution.py
+++ b/solution.py
@@ -117,14 +117,14 @@
             if owner < 36:
                 early[owner - 32] = block
             else:
-                late[owner % 12 // 3 * 15 + owner // 12 * 3 + owner % 3 - 9] = block
+                late[owner % 12 // 3, owner // 12 * 3 + owner % 3 - 9] = block
 
 
 def mlp(place, stream, grad_out, up_weight, down_weight):
     rows, width = stream.shape
     units = up_weight.shape[1]
     part = lambda columns: pl.BlockSpec((WIN, columns), lambda i, _: (i, 0))
-    late = jax.ShapeDtypeStruct((60,) + BLOCK, BF)
+    late = jax.ShapeDtypeStruct((4, 15) + BLOCK, BF)
     early = jax.ShapeDtypeStruct((4,) + BLOCK, BF)
     return call(
         mlp_kernel,
@@ -182,11 +182,11 @@
     given[...] = jnp.where(place[0] == 0, far[...].astype(F32), own[...].astype(F32)).astype(BF)
 
 
-def pair_kernel(keep, taken, pair):
+def pair_kernel(keep, taken, _, __, pair, ___, ____):
     pair[...] = (keep[...].astype(F32) + taken[...].astype(F32)).astype(BF)
 
 
-def middle_kernel(parts, own, mid, grad_mid):
+def middle_kernel(parts, own, _, mid, grad_mid, __):
     summed = jnp.sum(parts[...].astype(F32), axis=0)
     normed, factor = normalize(own[0])
     middle = own[1].astype(F32) + norm_back(normed, factor, summed)
@@ -214,7 +214,7 @@
 
 def backward_kernel(
     place, lead, trail, hidden, packed, probs, last_hidden, last_packed, last_probs, turned_qkv,
-    out_weight, early, _, in_grad, first, second, third, fourth, qkv_sum, out_sum, grads, outs, pieces,
+    out_weight, early, in_grad, first, second, third, fourth, qkv_sum, out_sum, grads, outs, pieces,
 ):
     step = pl.program_id(0)
     last = step == pl.num_programs(0) - 1
@@ -278,7 +278,7 @@
         third[...].astype(F32) + fourth[...].astype(F32)
     )
     joined[:count] = near.astype(BF)
-    joined[count:] = late[...]
+    joined[count:] = jnp.sum(late[...].astype(F32), axis=0).astype(BF)
 
 
 def total_kernel(received, _, owned):
@@ -303,21 +303,26 @@
     def from_next(values):
         return lax.ppermute(values, WIN_AXES, [((i + 1) % count, i) for i in range(count)])
 
-    far_input = from_next(block_input[:HALF])
+    first_rows = chunks_in[0]
+    labels = regions.reshape(windows, WIN)
     core_place = lax.axis_index("core").astype(jnp.int32).reshape(1)
     keep, give, late, early = mlp(core_place, stream, grad_out, up_weight, down_weight)
-    late_sum = lax.psum_scatter(late, "x", scatter_dimension=0, tiled=True)
     taken = lax.ppermute(give, "core", [(0, 1), (1, 0)])
-    (pair,) = call(
+    pair, first_rows, labels = call(
         pair_kernel,
         (1,),
-        [whole(keep), whole(taken)],
-        [(keep.shape, BF, whole(keep))],
-        (keep, taken),
-        vmem=16,
-    )
+        [whole(keep), whole(taken), ANY, ANY],
+        [
+            (keep.shape, BF, whole(keep)),
+            (first_rows.shape, BF, ANY),
+            (labels.shape, labels.dtype, ANY),
+        ],
+        (keep, taken, first_rows, labels),
+        aliases={2: 1, 3: 2},
+        vmem=16,
+    )
+    far_input = from_next(first_rows)
     parts = lax.all_to_all(pair, "zl", 0, 0)
-    labels = regions.reshape(windows, WIN)
     window = lambda columns: pl.BlockSpec((1, WIN, columns), lambda i, *_: (i, 0, 0))
     weights = (turned_qkv.reshape(-1, width), out_weight)
     token = jax.ShapeDtypeStruct((8, 128), F32)
@@ -345,12 +350,17 @@
         chosen=head_place,
         flops=53 * 10**8,
     )
-    mid, own_grad_mid = call(
+    mid, own_grad_mid, late = call(
         middle_kernel,
         (1,),
-        [whole(parts), whole(own)],
-        [(row_part.shape, F32, whole(row_part)), (row_part.shape, BF, whole(row_part))],
-        (parts, own),
+        [whole(parts), whole(own), ANY],
+        [
+            (row_part.shape, F32, whole(row_part)),
+            (row_part.shape, BF, whole(row_part)),
+            (late.shape, BF, ANY),
+        ],
+        (parts, own, late),
+        aliases={2: 2},
         vmem=16,
     )
     far_grad = lax.ppermute(
@@ -358,6 +368,7 @@
         WIN_AXES + HEAD_AXES,
         [((i + 1) % count * head_count, i * head_count) for i in range(count)],
     )
+    late_parts = lax.all_to_all(late, "x", 0, 0)
     one = lambda columns: pl.BlockSpec((1, WIN, columns), lambda *_: (0, 0, 0))
     *last, done = call(
         last_forward_kernel,
@@ -404,10 +415,9 @@
             one(WIN),
             *[whole(weight) for weight in weights],
             whole(early),
-            ANY,
         ],
         [(in_rows.shape, BF, whole(in_rows))] + [(piece.shape, BF, whole(piece))] * 4,
-        (grad_mid, grad_mid, hidden, packed, probs, *last, *weights, early, late_sum),
+        (grad_mid, grad_mid, hidden, packed, probs, *last, *weights, early),
         scratch=[
             pltpu.VMEM((width, 3 * columns), F32),
             pltpu.VMEM((columns, width), F32),
@@ -427,9 +437,9 @@
     (partial_sum,) = call(
         join_kernel,
         (1,),
-        [whole(piece)] * 4 + [whole(late_sum)],
+        [whole(piece)] * 4 + [whole(late_parts)],
         [(joined.shape, BF, whole(joined))],
-        (pieces[0], *moved, late_sum),
+        (pieces[0], *moved, late_parts),
         vmem=16,
     )
     summed, summed_b = call(

time: 139 us -> 124 us (0.89)
  between operations: 14.3 us -> 0.89 us
  local copies, waits for them, and re-layouts: 6.36 us -> 4.11 us
    all_to_all x0 -> x1, starting transfers between devices: none -> 9.07 us  [shards(): late_parts = lax.all_to_all(late, 'x', 0, 0)]
    all_to_all x1, starting transfers between devices: 13.8 us -> 5.57 us  [shards(): received = lax.all_to_all(partial_sum, ('y', 'zh'), 0, 0)]
    ppermute x3, starting transfers between devices: 11.9 us -> 8.69 us  [shards(): lax.ppermute(pieces[k], 'x', [(i, (i + k) % 4) for i in range(4)])]
    ppermute x1, starting transfers between devices: 6.92 us -> 10 us  [shards(): lax.ppermute(own_grad_mid, WIN_AXES + HEAD_AXES, [((i + 1) % count * head...]
    unnamed x34 -> x32, local copies, waits for them, and re-layouts: 4.79 us -> 3.14 us
    all_to_all x1, waiting for transfers between devices: 0.01 us -> 1.65 us  [shards(): in_parts = lax.all_to_all(in_grad, HEAD_AXES, 0, 0)]
  transfers between devices with their start and end apart: 11 -> 11, of which waited for: 5 -> 6; matrix products, arithmetic and copies ran while one was open for 1% -> 1% of each run, Pallas kernels for 7% -> 12%
where the time goes in v10:
time: 124 us; the launch traced here: 123 us
  starting transfers between devices  65.9 us (53%)
  Pallas kernels  22 us (18%)
  blocking collectives  15.3 us (12%)
  waiting for transfers between devices  14.3 us (12%)
  local copies, waits for them, and re-layouts  4.11 us (3%)
    pallas_call x11, Pallas kernels, call(): pl.pallas_call(kernel, grid_spec=spec, out_shape=[jax.ShapeDtypeStruct(ou...  22 us
    all_gather x1, blocking collectives, shards(): grad_mid = lax.all_gather(given, HEAD_AXES, axis=0)  15.3 us
    ppermute x1, starting transfers between devices, from_next(): lax.ppermute(values, WIN_AXES, [((i + 1) % count, i) for i in range(count)])  12.1 us
    ppermute x1, starting transfers between devices, shards(): lax.ppermute(own_grad_mid, WIN_AXES + HEAD_AXES, [((i + 1) % count * head...  10 us
    all_to_all x1, starting transfers between devices, shards(): late_parts = lax.all_to_all(late, 'x', 0, 0)  9.07 us
    ppermute x3, starting transfers between devices, shards(): lax.ppermute(pieces[k], 'x', [(i, (i + k) % 4) for i in range(4)])  8.69 us
    ppermute x1, starting transfers between devices, shards(): lax.ppermute(summed_b, WIN_AXES + HEAD_AXES, [(i * head_count, (i + 1) %...  7.66 us
    all_to_all x1, starting transfers between devices, shards(): parts = lax.all_to_all(pair, 'zl', 0, 0)  7.26 us
  transfers between devices with their start and end apart: 11, of which 6 were waited for; matrix products, arithmetic and copies ran while one was open for 1% of the time, Pallas kernels for 12%

profile of v10, /device:TPU:6, one launch (start us, length us, event | category | flops | bytes accessed | tf_op | source)
XLA Modules:
  0.0 122.5 jit_solution(18167408516946104409)
XLA Ops:
  0.6 5.8 %shard_map.95 = (bf16[4,72,512]{2,1,0:T(8,128)(2,1)}, bf16[4,72,512]{2,1,0:T(8,128)(2,1)}, bf16[4,15,32,128]{3,2,1,0:T(8,128)(2,1)}, bf16[4,32,128]{2,1,0:T(8,128)(2,1)}) custom-call(s32[1]{0:T(128)} %bitcast.2.place, bf16[576,512]{1,0:T(8,128)(2,1)} %stream.1, bf16[576,512]{1,0:T(8,128)(2,1)} %grad_out.1, bf16[512,256]{1,0:T(8,128)(2,1)} %up_weight.1, ...), custom_call_target="tpu_custom_call" | custom-call | flops 6899999744 | bytes 2097152 | tf_op jit(solution)/shard_map/pallas_call | solution.py:57
  6.5 1.9 %collective-permute-start = (bf16[4,72,512]{2,1,0:T(8,128)(2,1)}, bf16[4,72,512]{2,1,0:T(8,128)(2,1)S(1)}, u32[]{:S(2)}, u32[]{:S(2)}) collective-permute-start(bf16[4,72,512]{2,1,0:T(8,128)(2,1)} %get-tuple-element.30), channel_id=1, source_target_pairs={{0,1},{1,0},{2,3},{3,2},{4,5},{5,4},{6,7},{7,6},{8,9},{9,8},{10,11... | collective-permute-start | bytes 884744 | tf_op jit(solution)/shard_map/ppermute | solution.py:310
  8.5 0.9 slice.4._
  9.4 0.8 collective-permute-done.taken
  10.2 1.0 copy-done.1
  11.1 0.8 shard_map.96
  11.9 0.6 copy-done.3
  12.5 7.3 %all-to-all-start = ((bf16[4,72,512]{2,1,0:T(8,128)(2,1)}), bf16[4,72,512]{2,1,0:T(8,128)(2,1)S(1)}, u32[]{:S(2)}, u32[]{:S(2)}) async-start(bf16[4,72,512]{2,1,0:T(8,128)(2,1)} %get-tuple-element.31), calls=%async_computation | async-start | bytes 589824 | tf_op jit(solution)/shard_map/all_to_all | solution.py:325
  19.8 12.1 %collective-permute-start.2 = (bf16[72,512]{1,0:T(8,128)(2,1)S(1)}, bf16[72,512]{1,0:T(8,128)(2,1)S(1)}, u32[]{:S(2)}, u32[]{:S(2)}) collective-permute-start(bf16[72,512]{1,0:T(8,128)(2,1)S(1)} %get-tuple-element.36), channel_id=1, source_target_pairs={{8,0},{16,8},{24,16},{32,24},{40,32},{48,40},{56,48},{64,56},{72,6... | collective-permute-start | bytes 221192 | tf_op jit(solution)/shard_map/ppermute | solution.py:304
  31.9 4.7 %shard_map.97 = (bf16[3,144,512]{2,1,0:T(8,128)(2,1)}, bf16[3,144,256]{2,1,0:T(8,128)(2,1)}, f32[3,144,144]{2,1,0:T(8,128)}, bf16[2,72,512]{2,1,0:T(8,128)(2,1)}) custom-call(s32[1]{0:T(128)} %bitcast.place, bf16[8,72,512]{2,1,0:T(8,128)(2,1)} %bitcast.11, bf16[8,72,512]{2,1,0:T(8,128)(2,1)} %bitcast.12, s32[4,144]{1,0:T(4,128)} %copy-done.3, ...), custom_call_target="tpu_custom_call" | custom-call | flops 5299999744 | bytes 2097152 | tf_op jit(solution)/shard_map/pallas_call | solution.py:57
  36.6 0.9 copy-done.2
  37.5 0.3 shard_map.98
  37.7 10.0 %collective-permute-start.1 = (bf16[72,512]{1,0:T(8,128)(2,1)S(1)}, bf16[72,512]{1,0:T(8,128)(2,1)S(1)}, u32[]{:S(2)}, u32[]{:S(2)}) collective-permute-start(bf16[72,512]{1,0:T(8,128)(2,1)S(1)} %get-tuple-element.35.own), channel_id=1, source_target_pairs={{8,0},{16,8},{24,16},{32,24},{40,32},{48,40},{56,48},{64,56},{72,6... | collective-permute-start | bytes 221192 | tf_op jit(solution)/shard_map/ppermute | solution.py:366
  47.8 0.6 copy-done.15
  48.4 2.6 %shard_map.99 = (bf16[1,144,512]{2,1,0:T(8,128)(2,1)}, bf16[1,144,256]{2,1,0:T(8,128)(2,1)}, f32[1,144,144]{2,1,0:T(8,128)}, f32[8,128]{1,0:T(8,128)}) custom-call(bf16[8,72,512]{2,1,0:T(8,128)(2,1)} %bitcast.13, bf16[72,512]{1,0:T(8,128)(2,1)} %copy-done.15, s32[4,144]{1,0:T(4,128)} %copy-done.3, bf16[192,512]{1,0:T(8,128)(2,1)} %bitcast.18), custom_call_target="tpu_custom_call" | custom-call | flops 2000000000 | bytes 2097152 | tf_op jit(solution)/shard_map/pallas_call | solution.py:57
  51.1 9.1 %all-to-all-start.2 = ((bf16[4,15,32,128]{3,2,1,0:T(8,128)(2,1)}), bf16[4,15,32,128]{3,2,1,0:T(8,128)(2,1)S(1)}, u32[]{:S(2)}, u32[]{:S(2)}) async-start(bf16[4,15,32,128]{3,2,1,0:T(8,128)(2,1)} %get-tuple-element.54), calls=%async_computation.2 | async-start | bytes 983040 | tf_op jit(solution)/shard_map/all_to_all | solution.py:371
  60.2 15.3 %all-gather = bf16[576,512]{1,0:T(8,128)(2,1)S(1)} all-gather(bf16[72,512]{1,0:T(8,128)(2,1)S(1)} %shard_map.100), channel_id=2, replica_groups=mesh['y'=8,'x'=4,'zh'=3,'zl'=4,'core'=2] {'zl','core'}, dimensions={0}, use_global_device_ids=true | all-gather | bytes 663552 | tf_op jit(solution)/shard_map/all_gather | solution.py:400
  75.6 5.4 %shard_map.101 = (bf16[8,72,512]{2,1,0:T(8,128)(2,1)}, bf16[9,32,128]{2,1,0:T(8,128)(2,1)S(1)}, bf16[9,32,128]{2,1,0:T(8,128)(2,1)S(1)}, bf16[9,32,128]{2,1,0:T(8,128)(2,1)S(1)}, bf16[9,32,128]{2,1,0:T(8,128)(2,1)S(1)}) custom-call(s32[1]{0:T(128)} %bitcast.1.place, bf16[8,72,512]{2,1,0:T(8,128)(2,1)S(1)} %bitcast.15, bf16[8,72,512]{2,1,0:T(8,128)(2,1)S(1)} %bitcast.16, ...), custom_call_target="tpu_custom_call" | custom-call | flops 7000000000 | bytes 2097152 | tf_op jit(solution)/shard_map/pallas_call | solution.py:57
  81.0 3.5 %all-to-all-start.1 = ((bf16[8,72,512]{2,1,0:T(8,128)(2,1)}), bf16[8,72,512]{2,1,0:T(8,128)(2,1)S(1)}, u32[]{:S(2)}, u32[]{:S(2)}) async-start(bf16[8,72,512]{2,1,0:T(8,128)(2,1)} %get-tuple-element.45), calls=%async_computation.1 | async-start | bytes 1179648 | tf_op jit(solution)/shard_map/all_to_all | solution.py:432
  84.5 2.0 %collective-permute-start.4 = (bf16[9,32,128]{2,1,0:T(8,128)(2,1)S(1)}, bf16[9,32,128]{2,1,0:T(8,128)(2,1)S(1)}, u32[]{:S(2)}, u32[]{:S(2)}) collective-permute-start(bf16[9,32,128]{2,1,0:T(8,128)(2,1)S(1)} %get-tuple-element.51), channel_id=1, source_target_pairs={{0,24},{24,48},{48,72},{72,0},{1,25},{25,49},{49,73},{73,1},{2,26}... | collective-permute-start | bytes 221192 | tf_op jit(solution)/shard_map/ppermute | solution.py:434
  86.5 4.8 %collective-permute-start.5 = (bf16[9,32,128]{2,1,0:T(8,128)(2,1)S(1)}, bf16[9,32,128]{2,1,0:T(8,128)(2,1)S(1)}, u32[]{:S(2)}, u32[]{:S(2)}) collective-permute-start(bf16[9,32,128]{2,1,0:T(8,128)(2,1)S(1)} %get-tuple-element.52), channel_id=1, source_target_pairs={{0,48},{24,72},{48,0},{72,24},{1,49},{25,73},{49,1},{73,25},{2,50}... | collective-permute-start | bytes 221192 | tf_op jit(solution)/shard_map/ppermute | solution.py:434
  91.3 1.9 %collective-permute-start.6 = (bf16[9,32,128]{2,1,0:T(8,128)(2,1)S(1)}, bf16[9,32,128]{2,1,0:T(8,128)(2,1)S(1)}, u32[]{:S(2)}, u32[]{:S(2)}) collective-permute-start(bf16[9,32,128]{2,1,0:T(8,128)(2,1)S(1)} %get-tuple-element.53), channel_id=1, source_target_pairs={{0,72},{24,0},{48,24},{72,48},{1,73},{25,1},{49,25},{73,49},{2,74}... | collective-permute-start | bytes 221192 | tf_op jit(solution)/shard_map/ppermute | solution.py:434
  93.3 1.2 collective-permute-done.5.third
  94.4 4.3 %collective-permute-done.6.fourth = bf16[9,32,128]{2,1,0:T(8,128)(2,1)S(1)} collective-permute-done((bf16[9,32,128]{2,1,0:T(8,128)(2,1)S(1)}, bf16[9,32,128]{2,1,0:T(8,128)(2,1)S(1)}, u32[]{:S(2)}, u32[]{:S(2)}) %collective-permute-start.6) | collective-permute-done | bytes 73760 | tf_op jit(solution)/shard_map/ppermute | solution.py:434
  98.8 0.8 shard_map.104
  99.6 1.7 %all-to-all-done.1.parts = bf16[8,72,512]{2,1,0:T(8,128)(2,1)S(1)} async-done(((bf16[8,72,512]{2,1,0:T(8,128)(2,1)}), bf16[8,72,512]{2,1,0:T(8,128)(2,1)S(1)}, u32[]{:S(2)}, u32[]{:S(2)}) %all-to-all-start.1) | async-done | bytes 589856 | tf_op jit(solution)/shard_map/all_to_all | solution.py:432
  101.2 5.6 %all-to-all-start.3 = ((bf16[24,32,128]{2,1,0:T(8,128)(2,1)}), bf16[24,32,128]{2,1,0:T(8,128)(2,1)S(1)}, u32[]{:S(2)}, u32[]{:S(2)}) async-start(bf16[24,32,128]{2,1,0:T(8,128)(2,1)} %shard_map.104), calls=%async_computation.3 | async-start | bytes 393216 | tf_op jit(solution)/shard_map/all_to_all | solution.py:458
  106.9 7.7 %collective-permute-start.3 = (bf16[72,512]{1,0:T(8,128)(2,1)S(1)}, bf16[72,512]{1,0:T(8,128)(2,1)S(1)}, u32[]{:S(2)}, u32[]{:S(2)}) collective-permute-start(bf16[72,512]{1,0:T(8,128)(2,1)S(1)} %get-tuple-element.47), channel_id=1, source_target_pairs={{0,8},{8,16},{16,24},{24,32},{32,40},{40,48},{48,56},{56,64},{64,7... | collective-permute-start | bytes 221192 | tf_op jit(solution)/shard_map/ppermute | solution.py:453
  114.6 3.7 %collective-permute-done.3.arrived = bf16[72,512]{1,0:T(8,128)(2,1)S(1)} collective-permute-done((bf16[72,512]{1,0:T(8,128)(2,1)S(1)}, bf16[72,512]{1,0:T(8,128)(2,1)S(1)}, u32[]{:S(2)}, u32[]{:S(2)}) %collective-permute-start.3) | collective-permute-done | bytes 73760 | tf_op jit(solution)/shard_map/ppermute | solution.py:453
  118.3 0.9 shard_map.103
  119.2 2.7 %all-to-all-done.3.received = bf16[24,32,128]{2,1,0:T(8,128)(2,1)S(1)} async-done(((bf16[24,32,128]{2,1,0:T(8,128)(2,1)}), bf16[24,32,128]{2,1,0:T(8,128)(2,1)S(1)}, u32[]{:S(2)}, u32[]{:S(2)}) %all-to-all-start.3) | async-done | bytes 196640 | tf_op jit(solution)/shard_map/all_to_all | solution.py:458
  121.9 0.6 shard_map.105
  (36 shorter events, 0.3 us)
Async XLA Ops:
  0.6 7.8 %copy-start.14 = (s32[576]{0:T(1024)S(1)}, s32[576]{0:T(1024)}, u32[]{:S(2)}) copy-start(s32[576]{0:T(1024)} %param.11) | copy-start | bytes 6916
  6.5 3.7 %collective-permute-start = (bf16[4,72,512]{2,1,0:T(8,128)(2,1)}, bf16[4,72,512]{2,1,0:T(8,128)(2,1)S(1)}, u32[]{:S(2)}, u32[]{:S(2)}) collective-permute-start(bf16[4,72,512]{2,1,0:T(8,128)(2,1)} %get-tuple-element.30), channel_id=1, source_target_pairs={{0,1},{1,0},{2,3},{3,2},{4,5},{5,4},{6,7},{7,6},{8,9},{9,8},{10,11... | collective-permute-start | bytes 884744 | tf_op jit(solution)/shard_map/ppermute | solution.py:310
  10.2 1.0 copy-start.1
  11.9 0.6 copy-start.3
  12.5 24.0 %all-to-all-start = ((bf16[4,72,512]{2,1,0:T(8,128)(2,1)}), bf16[4,72,512]{2,1,0:T(8,128)(2,1)S(1)}, u32[]{:S(2)}, u32[]{:S(2)}) async-start(bf16[4,72,512]{2,1,0:T(8,128)(2,1)} %get-tuple-element.31), calls=%async_computation | async-start | bytes 589824 | tf_op jit(solution)/shard_map/all_to_all | solution.py:325
  19.8 28.0 %collective-permute-start.2 = (bf16[72,512]{1,0:T(8,128)(2,1)S(1)}, bf16[72,512]{1,0:T(8,128)(2,1)S(1)}, u32[]{:S(2)}, u32[]{:S(2)}) collective-permute-start(bf16[72,512]{1,0:T(8,128)(2,1)S(1)} %get-tuple-element.36), channel_id=1, source_target_pairs={{8,0},{16,8},{24,16},{32,24},{40,32},{48,40},{56,48},{64,56},{72,6... | collective-permute-start | bytes 221192 | tf_op jit(solution)/shard_map/ppermute | solution.py:304
  36.6 0.9 copy-start.2
  37.7 22.4 %collective-permute-start.1 = (bf16[72,512]{1,0:T(8,128)(2,1)S(1)}, bf16[72,512]{1,0:T(8,128)(2,1)S(1)}, u32[]{:S(2)}, u32[]{:S(2)}) collective-permute-start(bf16[72,512]{1,0:T(8,128)(2,1)S(1)} %get-tuple-element.35.own), channel_id=1, source_target_pairs={{8,0},{16,8},{24,16},{32,24},{40,32},{48,40},{56,48},{64,56},{72,6... | collective-permute-start | bytes 221192 | tf_op jit(solution)/shard_map/ppermute | solution.py:366
  47.8 0.6 copy-start.15
  51.1 9.1 %copy-start.6 = (f32[8,128]{1,0:T(8,128)S(1)}, f32[8,128]{1,0:T(8,128)}, u32[]{:S(2)}) copy-start(f32[8,128]{1,0:T(8,128)} %get-tuple-element.37._) | copy-start | bytes 12292
  51.1 24.5 %copy-start.10 = (bf16[3,144,512]{2,1,0:T(8,128)(2,1)S(1)}, bf16[3,144,512]{2,1,0:T(8,128)(2,1)}, u32[]{:S(2)}) copy-start(bf16[3,144,512]{2,1,0:T(8,128)(2,1)} %get-tuple-element.38.hidden) | copy-start | bytes 1327108
  51.1 24.5 %copy-start.11 = (f32[3,144,144]{2,1,0:T(8,128)S(1)}, f32[3,144,144]{2,1,0:T(8,128)}, u32[]{:S(2)}) copy-start(f32[3,144,144]{2,1,0:T(8,128)} %get-tuple-element.40.probs) | copy-start | bytes 746500
  51.1 29.9 %all-to-all-start.2 = ((bf16[4,15,32,128]{3,2,1,0:T(8,128)(2,1)}), bf16[4,15,32,128]{3,2,1,0:T(8,128)(2,1)S(1)}, u32[]{:S(2)}, u32[]{:S(2)}) async-start(bf16[4,15,32,128]{3,2,1,0:T(8,128)(2,1)} %get-tuple-element.54), calls=%async_computation.2 | async-start | bytes 983040 | tf_op jit(solution)/shard_map/all_to_all | solution.py:371
  60.1 15.4 %copy-start.12 = (bf16[3,144,256]{2,1,0:T(8,128)(2,1)S(1)}, bf16[3,144,256]{2,1,0:T(8,128)(2,1)}, u32[]{:S(2)}) copy-start(bf16[3,144,256]{2,1,0:T(8,128)(2,1)} %get-tuple-element.39.packed) | copy-start | bytes 663556
  60.2 15.4 %copy-start.4 = (bf16[3,512,64]{1,2,0:T(8,128)(2,1)S(1)}, bf16[3,512,64]{1,2,0:T(8,128)(2,1)}, u32[]{:S(2)}) copy-start(bf16[3,512,64]{1,2,0:T(8,128)(2,1)} %param.12) | copy-start | bytes 589828
  60.2 15.4 %copy-start.5 = (bf16[64,512]{1,0:T(8,128)(2,1)S(1)}, bf16[64,512]{1,0:T(8,128)(2,1)}, u32[]{:S(2)}) copy-start(bf16[64,512]{1,0:T(8,128)(2,1)} %out_weight.1) | copy-start | bytes 196612
  60.2 15.4 %copy-start.7 = (bf16[1,144,512]{2,1,0:T(8,128)(2,1)S(1)}, bf16[1,144,512]{2,1,0:T(8,128)(2,1)}, u32[]{:S(2)}) copy-start(bf16[1,144,512]{2,1,0:T(8,128)(2,1)} %get-tuple-element.41.last_hidden) | copy-start | bytes 442372
  60.2 15.4 %copy-start.8 = (f32[1,144,144]{2,1,0:T(8,128)S(1)}, f32[1,144,144]{2,1,0:T(8,128)}, u32[]{:S(2)}) copy-start(f32[1,144,144]{2,1,0:T(8,128)} %get-tuple-element.43.last_probs) | copy-start | bytes 248836
  60.2 15.4 %copy-start.9 = (bf16[1,144,256]{2,1,0:T(8,128)(2,1)S(1)}, bf16[1,144,256]{2,1,0:T(8,128)(2,1)}, u32[]{:S(2)}) copy-start(bf16[1,144,256]{2,1,0:T(8,128)(2,1)} %get-tuple-element.42.last_packed) | copy-start | bytes 221188
  60.2 15.4 %copy-start.13 = (bf16[4,32,128]{2,1,0:T(8,128)(2,1)S(1)}, bf16[4,32,128]{2,1,0:T(8,128)(2,1)}, u32[]{:S(2)}) copy-start(bf16[4,32,128]{2,1,0:T(8,128)(2,1)} %get-tuple-element.44.early) | copy-start | bytes 98308
  81.0 20.2 %all-to-all-start.1 = ((bf16[8,72,512]{2,1,0:T(8,128)(2,1)}), bf16[8,72,512]{2,1,0:T(8,128)(2,1)S(1)}, u32[]{:S(2)}, u32[]{:S(2)}) async-start(bf16[8,72,512]{2,1,0:T(8,128)(2,1)} %get-tuple-element.45), calls=%async_computation.1 | async-start | bytes 1179648 | tf_op jit(solution)/shard_map/all_to_all | solution.py:432
  84.5 8.7 %collective-permute-start.4 = (bf16[9,32,128]{2,1,0:T(8,128)(2,1)S(1)}, bf16[9,32,128]{2,1,0:T(8,128)(2,1)S(1)}, u32[]{:S(2)}, u32[]{:S(2)}) collective-permute-start(bf16[9,32,128]{2,1,0:T(8,128)(2,1)S(1)} %get-tuple-element.51), channel_id=1, source_target_pairs={{0,24},{24,48},{48,72},{72,0},{1,25},{25,49},{49,73},{73,1},{2,26}... | collective-permute-start | bytes 221192 | tf_op jit(solution)/shard_map/ppermute | solution.py:434
  86.5 7.9 %collective-permute-start.5 = (bf16[9,32,128]{2,1,0:T(8,128)(2,1)S(1)}, bf16[9,32,128]{2,1,0:T(8,128)(2,1)S(1)}, u32[]{:S(2)}, u32[]{:S(2)}) collective-permute-start(bf16[9,32,128]{2,1,0:T(8,128)(2,1)S(1)} %get-tuple-element.52), channel_id=1, source_target_pairs={{0,48},{24,72},{48,0},{72,24},{1,49},{25,73},{49,1},{73,25},{2,50}... | collective-permute-start | bytes 221192 | tf_op jit(solution)/shard_map/ppermute | solution.py:434
  91.3 7.5 %collective-permute-start.6 = (bf16[9,32,128]{2,1,0:T(8,128)(2,1)S(1)}, bf16[9,32,128]{2,1,0:T(8,128)(2,1)S(1)}, u32[]{:S(2)}, u32[]{:S(2)}) collective-permute-start(bf16[9,32,128]{2,1,0:T(8,128)(2,1)S(1)} %get-tuple-element.53), channel_id=1, source_target_pairs={{0,72},{24,0},{48,24},{72,48},{1,73},{25,1},{49,25},{73,49},{2,74}... | collective-permute-start | bytes 221192 | tf_op jit(solution)/shard_map/ppermute | solution.py:434
  99.6 18.7 %copy-start = (bf16[576,512]{1,0:T(8,128)(2,1)S(1)}, bf16[576,512]{1,0:T(8,128)(2,1)}, u32[]{:S(2)}) copy-start(bf16[576,512]{1,0:T(8,128)(2,1)} %param.8) | copy-start | bytes 1769476
  101.2 20.7 %all-to-all-start.3 = ((bf16[24,32,128]{2,1,0:T(8,128)(2,1)}), bf16[24,32,128]{2,1,0:T(8,128)(2,1)S(1)}, u32[]{:S(2)}, u32[]{:S(2)}) async-start(bf16[24,32,128]{2,1,0:T(8,128)(2,1)} %shard_map.104), calls=%async_computation.3 | async-start | bytes 393216 | tf_op jit(solution)/shard_map/all_to_all | solution.py:458
  106.9 11.3 %collective-permute-start.3 = (bf16[72,512]{1,0:T(8,128)(2,1)S(1)}, bf16[72,512]{1,0:T(8,128)(2,1)S(1)}, u32[]{:S(2)}, u32[]{:S(2)}) collective-permute-start(bf16[72,512]{1,0:T(8,128)(2,1)S(1)} %get-tuple-element.47), channel_id=1, source_target_pairs={{0,8},{8,16},{16,24},{24,32},{32,40},{40,48},{48,56},{56,64},{64,7... | collective-permute-start | bytes 221192 | tf_op jit(solution)/shard_map/ppermute | solution.py:453

commit v11 on v10

--- a/solution.py
+++ b/solution.py
@@ -169,24 +169,15 @@
     own[1] = grad_out[0]
 
 
-def last_forward_kernel(
-    lead, tail, labels, turned_qkv, hidden, packed, probs_out, token
-):
-    row = labels[labels.shape[0] - 1 :, :]
-    hidden[0], parts, probs_out[0] = window_forward(lead[0], tail[...], row, turned_qkv)
-    packed[0] = jnp.concatenate(parts, axis=1)
-    token[...] = jnp.zeros_like(token)
-
-
-def give_kernel(place, own, far, _, given):
+def give_kernel(place, own, far, given):
     given[...] = jnp.where(place[0] == 0, far[...].astype(F32), own[...].astype(F32)).astype(BF)
 
 
-def pair_kernel(keep, taken, _, __, pair, ___, ____):
+def pair_kernel(keep, taken, _, pair, __):
     pair[...] = (keep[...].astype(F32) + taken[...].astype(F32)).astype(BF)
 
 
-def middle_kernel(parts, own, _, mid, grad_mid, __):
+def middle_kernel(parts, own, _, __, mid, grad_mid, ___):
     summed = jnp.sum(parts[...].astype(F32), axis=0)
     normed, factor = normalize(own[0])
     middle = own[1].astype(F32) + norm_back(normed, factor, summed)
@@ -213,17 +204,26 @@
 
 
 def backward_kernel(
-    place, lead, trail, hidden, packed, probs, last_hidden, last_packed, last_probs, turned_qkv,
-    out_weight, early, in_grad, first, second, third, fourth, qkv_sum, out_sum, grads, outs, pieces,
+    place, lead, trail, hidden, packed, probs, last_lead, last_tail, labels, turned_qkv, out_weight,
+    early, in_grad, first, second, third, fourth, last_hidden, last_packed, last_probs, qkv_sum, out_sum, grads, outs, pieces,
 ):
     step = pl.program_id(0)
     last = step == pl.num_programs(0) - 1
-    saved = jnp.where(last, last_packed[0].astype(F32), packed[0].astype(F32)).astype(BF)
+
+    @pl.when(step == 0)
+    def _():
+        row = labels[labels.shape[0] - 1 :, :]
+        last_hidden[...], kept, last_probs[...] = window_forward(
+            last_lead[0], last_tail[...], row, turned_qkv
+        )
+        last_packed[...] = jnp.concatenate(kept, axis=1)
+
+    saved = jnp.where(last, last_packed[...].astype(F32), packed[0].astype(F32)).astype(BF)
     parts = [saved[:, HS * i : HS * i + HS] for i in range(4)]
-    inputs = jnp.where(last, last_hidden[0].astype(F32), hidden[0].astype(F32)).astype(BF)
+    inputs = jnp.where(last, last_hidden[...].astype(F32), hidden[0].astype(F32)).astype(BF)
     upper = jnp.concatenate([lead[0].astype(F32), trail[0].astype(F32)], axis=0).astype(BF)
     rows, qkv_part, out_part = window_back(
-        upper, inputs, parts, jnp.where(last, last_probs[0], probs[0]), turned_qkv, out_weight
+        upper, inputs, parts, jnp.where(last, last_probs[...], probs[0]), turned_qkv, out_weight
     )
     in_grad[2 * step + 1] = rows[:HALF].astype(BF)
     in_grad[lax.rem(2 * step + 2, in_grad.shape[0])] = rows[HALF:].astype(BF)
@@ -265,11 +265,10 @@
     total_b[...] = total[...].astype(BF)
 
 
-def final_kernel(place, summed, arrived, mid, block_input, grad_input, token):
+def final_kernel(place, summed, arrived, mid, block_input, grad_input):
     total = jnp.where(place[0] == 0, arrived[...].astype(F32), summed[...])
     normed, factor = normalize(block_input[0])
     grad_input[...] = (mid[...] + norm_back(normed, factor, total)).astype(BF)
-    token[...] = jnp.zeros_like(token)
 
 
 def join_kernel(first, second, third, fourth, late, joined):
@@ -281,7 +280,7 @@
     joined[count:] = jnp.sum(late[...].astype(F32), axis=0).astype(BF)
 
 
-def total_kernel(received, _, owned):
+def total_kernel(received, owned):
     owned[...] = jnp.sum(received[...].astype(F32), axis=0)
 
 
@@ -308,24 +307,19 @@
     core_place = lax.axis_index("core").astype(jnp.int32).reshape(1)
     keep, give, late, early = mlp(core_place, stream, grad_out, up_weight, down_weight)
     taken = lax.ppermute(give, "core", [(0, 1), (1, 0)])
-    pair, first_rows, labels = call(
+    pair, first_rows = call(
         pair_kernel,
         (1,),
-        [whole(keep), whole(taken), ANY, ANY],
-        [
-            (keep.shape, BF, whole(keep)),
-            (first_rows.shape, BF, ANY),
-            (labels.shape, labels.dtype, ANY),
-        ],
-        (keep, taken, first_rows, labels),
-        aliases={2: 1, 3: 2},
+        [whole(keep), whole(taken), ANY],
+        [(keep.shape, BF, whole(keep)), (first_rows.shape, BF, ANY)],
+        (keep, taken, first_rows),
+        aliases={2: 1},
         vmem=16,
     )
     far_input = from_next(first_rows)
     parts = lax.all_to_all(pair, "zl", 0, 0)
     window = lambda columns: pl.BlockSpec((1, WIN, columns), lambda i, *_: (i, 0, 0))
     weights = (turned_qkv.reshape(-1, width), out_weight)
-    token = jax.ShapeDtypeStruct((8, 128), F32)
     row_part = jax.ShapeDtypeStruct((share_rows, width), BF)
     mine = pl.BlockSpec(chunk, lambda i, place: (place[0], 0, 0))
     own_rows = jax.ShapeDtypeStruct((2, share_rows, width), BF)
@@ -353,13 +347,13 @@
     mid, own_grad_mid, late = call(
         middle_kernel,
         (1,),
-        [whole(parts), whole(own), ANY],
+        [whole(parts), whole(own), ANY, ANY],
         [
             (row_part.shape, F32, whole(row_part)),
             (row_part.shape, BF, whole(row_part)),
             (late.shape, BF, ANY),
         ],
-        (parts, own, late),
+        (parts, own, late, far_input),
         aliases={2: 2},
         vmem=16,
     )
@@ -369,31 +363,12 @@
         [((i + 1) % count * head_count, i * head_count) for i in range(count)],
     )
     late_parts = lax.all_to_all(late, "x", 0, 0)
-    one = lambda columns: pl.BlockSpec((1, WIN, columns), lambda *_: (0, 0, 0))
-    *last, done = call(
-        last_forward_kernel,
-        (1,),
-        [
-            pl.BlockSpec(chunk, lambda i: (head_count - 1, 0, 0)),
-            whole(far_input),
-            whole(labels),
-            whole(weights[0]),
-        ],
-        [
-            ((1, WIN, width), BF, one(width)),
-            ((1, WIN, 4 * columns), BF, one(4 * columns)),
-            ((1, WIN, WIN), F32, one(WIN)),
-            (token.shape, F32, whole(token)),
-        ],
-        (chunks_in, far_input, labels, weights[0]),
-        flops=20 * 10**8,
-    )
     (given,) = call(
         give_kernel,
         (1,),
-        [whole(own_grad_mid), whole(far_grad), ANY],
+        [whole(own_grad_mid), whole(far_grad)],
         [(row_part.shape, BF, whole(row_part))],
-        (own_grad_mid, far_grad, done),
+        (own_grad_mid, far_grad),
         chosen=head_place,
         vmem=16,
     )
@@ -410,15 +385,18 @@
                 pl.BlockSpec((1, WIN, size), lambda i, _: (jnp.minimum(i, windows - 2), 0, 0))
                 for size in (width, 4 * columns, WIN)
             ],
-            one(width),
-            one(4 * columns),
-            one(WIN),
+            pl.BlockSpec(chunk, lambda i, _: (head_count - 1, 0, 0)),
+            whole(far_input),
+            whole(labels),
             *[whole(weight) for weight in weights],
             whole(early),
         ],
         [(in_rows.shape, BF, whole(in_rows))] + [(piece.shape, BF, whole(piece))] * 4,
-        (grad_mid, grad_mid, hidden, packed, probs, *last, *weights, early),
+        (grad_mid, grad_mid, hidden, packed, probs, chunks_in, far_input, labels, *weights, early),
         scratch=[
+            pltpu.VMEM((WIN, width), BF),
+            pltpu.VMEM((WIN, 4 * columns), BF),
+            pltpu.VMEM((WIN, WIN), F32),
             pltpu.VMEM((width, 3 * columns), F32),
             pltpu.VMEM((columns, width), F32),
             pltpu.VMEM((3, width, columns), F32),
@@ -456,11 +434,11 @@
         [(i * head_count, (i + 1) % count * head_count) for i in range(count)],
     )
     received = lax.all_to_all(partial_sum, ("y", "zh"), 0, 0)
-    grad_input, ready = call(
+    (grad_input,) = call(
         final_kernel,
         (1,),
         [whole(summed), whole(arrived), whole(mid), mine],
-        [(row_part.shape, BF, whole(row_part)), (token.shape, F32, whole(token))],
+        [(row_part.shape, BF, whole(row_part))],
         (summed, arrived, mid, chunks_in),
         chosen=head_place,
         vmem=16,
@@ -469,9 +447,9 @@
     (owned,) = call(
         total_kernel,
         (1,),
-        [whole(received), ANY],
+        [whole(received)],
         [(BLOCK, F32, whole(owner_block))],
-        (received, ready),
+        (received,),
         vmem=16,
     )
     return (grad_input, owned.reshape(1, -1))

time: 124 us -> 131 us (1.056)
  starting transfers between devices: 65.9 us -> 70.4 us
  waiting for transfers between devices: 14.3 us -> 18.4 us
  Pallas kernels: 22 us -> 20.3 us
    all_to_all x1, waiting for transfers between devices: 2.71 us -> 8.39 us  [shards(): received = lax.all_to_all(partial_sum, ('y', 'zh'), 0, 0)]
    ppermute x1, waiting for transfers between devices: 3.68 us -> 0.01 us  [shards(): lax.ppermute(summed_b, WIN_AXES + HEAD_AXES, [(i * head_count, (i + 1) %...]
    all_to_all x1, starting transfers between devices: 9.07 us -> 12.2 us  [shards(): late_parts = lax.all_to_all(late, 'x', 0, 0)]
    all_to_all x1, starting transfers between devices: 5.57 us -> 7.84 us  [shards(): received = lax.all_to_all(partial_sum, ('y', 'zh'), 0, 0)]
    ppermute x1, waiting for transfers between devices: 0.01 us -> 1.94 us  [from_next(): lax.ppermute(values, WIN_AXES, [((i + 1) % count, i) for i in range(count)])]
    pallas_call x11 -> x10, Pallas kernels: 22 us -> 20.3 us  [call(): pl.pallas_call(kernel, grid_spec=spec, out_shape=[jax.ShapeDtypeStruct(ou...]
    unnamed x32 -> x22, local copies, waits for them, and re-layouts: 3.14 us -> 3.23 us
  transfers between devices with their start and end apart: 11 -> 11, of which waited for: 6 -> 6; matrix products, arithmetic and copies ran while one was open for 1% -> 1% of each run, Pallas kernels for 12% -> 10%
where the time goes in v11:
time: 131 us; the launch traced here: 130 us
  starting transfers between devices  70.4 us (54%)
  Pallas kernels  20.3 us (15%)
  waiting for transfers between devices  18.4 us (14%)
  blocking collectives  15.3 us (12%)
  local copies, waits for them, and re-layouts  4.79 us (4%)
    pallas_call x10, Pallas kernels, call(): pl.pallas_call(kernel, grid_spec=spec, out_shape=[jax.ShapeDtypeStruct(ou...  20.3 us
    all_gather x1, blocking collectives, shards(): grad_mid = lax.all_gather(given, HEAD_AXES, axis=0)  15.3 us
    all_to_all x1, starting transfers between devices, shards(): late_parts = lax.all_to_all(late, 'x', 0, 0)  12.2 us
    ppermute x1, starting transfers between devices, from_next(): lax.ppermute(values, WIN_AXES, [((i + 1) % count, i) for i in range(count)])  12.1 us
    ppermute x1, starting transfers between devices, shards(): lax.ppermute(own_grad_mid, WIN_AXES + HEAD_AXES, [((i + 1) % count * head...  9.16 us
    ppermute x3, starting transfers between devices, shards(): lax.ppermute(pieces[k], 'x', [(i, (i + k) % 4) for i in range(4)])  8.68 us
    all_to_all x1, waiting for transfers between devices, shards(): received = lax.all_to_all(partial_sum, ('y', 'zh'), 0, 0)  8.39 us
    all_to_all x1, starting transfers between devices, shards(): received = lax.all_to_all(partial_sum, ('y', 'zh'), 0, 0)  7.84 us
  transfers between devices with their start and end apart: 11, of which 6 were waited for; matrix products, arithmetic and copies ran while one was open for 1% of the time, Pallas kernels for 10%

profile of v11, /device:TPU:6, one launch (start us, length us, event | category | flops | bytes accessed | tf_op | source)
XLA Modules:
  0.0 130.0 jit_solution(15426211138968980091)
XLA Ops:
  0.6 5.8 %shard_map.95 = (bf16[4,72,512]{2,1,0:T(8,128)(2,1)}, bf16[4,72,512]{2,1,0:T(8,128)(2,1)}, bf16[4,15,32,128]{3,2,1,0:T(8,128)(2,1)}, bf16[4,32,128]{2,1,0:T(8,128)(2,1)}) custom-call(s32[1]{0:T(128)} %bitcast.2.place, bf16[576,512]{1,0:T(8,128)(2,1)} %stream.1, bf16[576,512]{1,0:T(8,128)(2,1)} %grad_out.1, bf16[512,256]{1,0:T(8,128)(2,1)} %up_weight.1, ...), custom_call_target="tpu_custom_call" | custom-call | flops 6899999744 | bytes 2097152 | tf_op jit(solution)/shard_map/pallas_call | solution.py:57
  6.4 1.9 %collective-permute-start = (bf16[4,72,512]{2,1,0:T(8,128)(2,1)}, bf16[4,72,512]{2,1,0:T(8,128)(2,1)S(1)}, u32[]{:S(2)}, u32[]{:S(2)}) collective-permute-start(bf16[4,72,512]{2,1,0:T(8,128)(2,1)} %get-tuple-element.23), channel_id=1, source_target_pairs={{0,1},{1,0},{2,3},{3,2},{4,5},{5,4},{6,7},{7,6},{8,9},{9,8},{10,11... | collective-permute-start | bytes 884744 | tf_op jit(solution)/shard_map/ppermute | solution.py:309
  8.4 0.9 slice.4._
  9.3 0.9 collective-permute-done.taken
  10.1 1.0 copy-done.1
  11.1 0.8 shard_map.96
  11.9 7.3 %all-to-all-start = ((bf16[4,72,512]{2,1,0:T(8,128)(2,1)}), bf16[4,72,512]{2,1,0:T(8,128)(2,1)S(1)}, u32[]{:S(2)}, u32[]{:S(2)}) async-start(bf16[4,72,512]{2,1,0:T(8,128)(2,1)} %get-tuple-element.24), calls=%async_computation | async-start | bytes 589824 | tf_op jit(solution)/shard_map/all_to_all | solution.py:320
  19.2 0.7 copy-done.10
  19.8 0.7 reshape.37.labels
  20.5 12.1 %collective-permute-start.1 = (bf16[72,512]{1,0:T(8,128)(2,1)S(1)}, bf16[72,512]{1,0:T(8,128)(2,1)S(1)}, u32[]{:S(2)}, u32[]{:S(2)}) collective-permute-start(bf16[72,512]{1,0:T(8,128)(2,1)S(1)} %get-tuple-element.27), channel_id=1, source_target_pairs={{8,0},{16,8},{24,16},{32,24},{40,32},{48,40},{56,48},{64,56},{72,6... | collective-permute-start | bytes 221192 | tf_op jit(solution)/shard_map/ppermute | solution.py:303
  32.6 4.7 %shard_map.97 = (bf16[3,144,512]{2,1,0:T(8,128)(2,1)}, bf16[3,144,256]{2,1,0:T(8,128)(2,1)}, f32[3,144,144]{2,1,0:T(8,128)}, bf16[2,72,512]{2,1,0:T(8,128)(2,1)}) custom-call(s32[1]{0:T(128)} %bitcast.place, bf16[8,72,512]{2,1,0:T(8,128)(2,1)} %bitcast.11, bf16[8,72,512]{2,1,0:T(8,128)(2,1)} %bitcast.12, s32[4,144]{1,0:T(4,128)} %reshape.37.labels, ...), custom_call_target="tpu_custom_call" | custom-call | flops 5299999744 | bytes 2097152 | tf_op jit(solution)/shard_map/pallas_call | solution.py:57
  37.3 1.9 %collective-permute-done.1.__.last_tail = bf16[72,512]{1,0:T(8,128)(2,1)S(1)} collective-permute-done((bf16[72,512]{1,0:T(8,128)(2,1)S(1)}, bf16[72,512]{1,0:T(8,128)(2,1)S(1)}, u32[]{:S(2)}, u32[]{:S(2)}) %collective-permute-start.1) | collective-permute-done | bytes 73760 | tf_op jit(solution)/shard_map/ppermute | solution.py:303
  39.3 0.9 copy-done.2
  40.2 0.3 shard_map.98
  40.5 9.2 %collective-permute-start.2 = (bf16[72,512]{1,0:T(8,128)(2,1)S(1)}, bf16[72,512]{1,0:T(8,128)(2,1)S(1)}, u32[]{:S(2)}, u32[]{:S(2)}) collective-permute-start(bf16[72,512]{1,0:T(8,128)(2,1)S(1)} %get-tuple-element.28.own), channel_id=1, source_target_pairs={{8,0},{16,8},{24,16},{32,24},{40,32},{48,40},{56,48},{64,56},{72,6... | collective-permute-start | bytes 221192 | tf_op jit(solution)/shard_map/ppermute | solution.py:360
  49.7 12.2 %all-to-all-start.2 = ((bf16[4,15,32,128]{3,2,1,0:T(8,128)(2,1)}), bf16[4,15,32,128]{3,2,1,0:T(8,128)(2,1)S(1)}, u32[]{:S(2)}, u32[]{:S(2)}) async-start(bf16[4,15,32,128]{3,2,1,0:T(8,128)(2,1)} %get-tuple-element.41), calls=%async_computation.2 | async-start | bytes 983040 | tf_op jit(solution)/shard_map/all_to_all | solution.py:365
  61.9 15.3 %all-gather = bf16[576,512]{1,0:T(8,128)(2,1)S(1)} all-gather(bf16[72,512]{1,0:T(8,128)(2,1)S(1)} %shard_map.99), channel_id=2, replica_groups=mesh['y'=8,'x'=4,'zh'=3,'zl'=4,'core'=2] {'zl','core'}, dimensions={0}, use_global_device_ids=true | all-gather | bytes 663552 | tf_op jit(solution)/shard_map/all_gather | solution.py:375
  77.3 0.6 copy-done.3
  78.0 6.3 %shard_map.100 = (bf16[8,72,512]{2,1,0:T(8,128)(2,1)}, bf16[9,32,128]{2,1,0:T(8,128)(2,1)S(1)}, bf16[9,32,128]{2,1,0:T(8,128)(2,1)S(1)}, bf16[9,32,128]{2,1,0:T(8,128)(2,1)S(1)}, bf16[9,32,128]{2,1,0:T(8,128)(2,1)S(1)}) custom-call(s32[1]{0:T(128)} %bitcast.1.place, bf16[8,72,512]{2,1,0:T(8,128)(2,1)S(1)} %bitcast.15, bf16[8,72,512]{2,1,0:T(8,128)(2,1)S(1)} %bitcast.16, ...), custom_call_target="tpu_custom_call" | custom-call | flops 7000000000 | bytes 2097152 | tf_op jit(solution)/shard_map/pallas_call | solution.py:57
  84.2 3.5 %all-to-all-start.1 = ((bf16[8,72,512]{2,1,0:T(8,128)(2,1)}), bf16[8,72,512]{2,1,0:T(8,128)(2,1)S(1)}, u32[]{:S(2)}, u32[]{:S(2)}) async-start(bf16[8,72,512]{2,1,0:T(8,128)(2,1)} %get-tuple-element.33), calls=%async_computation.1 | async-start | bytes 1179648 | tf_op jit(solution)/shard_map/all_to_all | solution.py:410
  87.8 2.0 %collective-permute-start.4 = (bf16[9,32,128]{2,1,0:T(8,128)(2,1)S(1)}, bf16[9,32,128]{2,1,0:T(8,128)(2,1)S(1)}, u32[]{:S(2)}, u32[]{:S(2)}) collective-permute-start(bf16[9,32,128]{2,1,0:T(8,128)(2,1)S(1)} %get-tuple-element.38), channel_id=1, source_target_pairs={{0,24},{24,48},{48,72},{72,0},{1,25},{25,49},{49,73},{73,1},{2,26}... | collective-permute-start | bytes 221192 | tf_op jit(solution)/shard_map/ppermute | solution.py:412
  89.8 4.8 %collective-permute-start.5 = (bf16[9,32,128]{2,1,0:T(8,128)(2,1)S(1)}, bf16[9,32,128]{2,1,0:T(8,128)(2,1)S(1)}, u32[]{:S(2)}, u32[]{:S(2)}) collective-permute-start(bf16[9,32,128]{2,1,0:T(8,128)(2,1)S(1)} %get-tuple-element.39), channel_id=1, source_target_pairs={{0,48},{24,72},{48,0},{72,24},{1,49},{25,73},{49,1},{73,25},{2,50}... | collective-permute-start | bytes 221192 | tf_op jit(solution)/shard_map/ppermute | solution.py:412
  94.5 1.9 %collective-permute-start.6 = (bf16[9,32,128]{2,1,0:T(8,128)(2,1)S(1)}, bf16[9,32,128]{2,1,0:T(8,128)(2,1)S(1)}, u32[]{:S(2)}, u32[]{:S(2)}) collective-permute-start(bf16[9,32,128]{2,1,0:T(8,128)(2,1)S(1)} %get-tuple-element.40), channel_id=1, source_target_pairs={{0,72},{24,0},{48,24},{72,48},{1,73},{25,1},{49,25},{73,49},{2,74}... | collective-permute-start | bytes 221192 | tf_op jit(solution)/shard_map/ppermute | solution.py:412
  96.5 1.2 collective-permute-done.5.third
  97.7 4.3 %collective-permute-done.6.fourth = bf16[9,32,128]{2,1,0:T(8,128)(2,1)S(1)} collective-permute-done((bf16[9,32,128]{2,1,0:T(8,128)(2,1)S(1)}, bf16[9,32,128]{2,1,0:T(8,128)(2,1)S(1)}, u32[]{:S(2)}, u32[]{:S(2)}) %collective-permute-start.6) | collective-permute-done | bytes 73760 | tf_op jit(solution)/shard_map/ppermute | solution.py:412
  102.0 0.8 shard_map.103
  102.8 1.7 %all-to-all-done.1.parts = bf16[8,72,512]{2,1,0:T(8,128)(2,1)S(1)} async-done(((bf16[8,72,512]{2,1,0:T(8,128)(2,1)}), bf16[8,72,512]{2,1,0:T(8,128)(2,1)S(1)}, u32[]{:S(2)}, u32[]{:S(2)}) %all-to-all-start.1) | async-done | bytes 589856 | tf_op jit(solution)/shard_map/all_to_all | solution.py:410
  104.4 7.8 %all-to-all-start.3 = ((bf16[24,32,128]{2,1,0:T(8,128)(2,1)}), bf16[24,32,128]{2,1,0:T(8,128)(2,1)S(1)}, u32[]{:S(2)}, u32[]{:S(2)}) async-start(bf16[24,32,128]{2,1,0:T(8,128)(2,1)} %shard_map.103), calls=%async_computation.3 | async-start | bytes 393216 | tf_op jit(solution)/shard_map/all_to_all | solution.py:436
  112.4 7.7 %collective-permute-start.3 = (bf16[72,512]{1,0:T(8,128)(2,1)S(1)}, bf16[72,512]{1,0:T(8,128)(2,1)S(1)}, u32[]{:S(2)}, u32[]{:S(2)}) collective-permute-start(bf16[72,512]{1,0:T(8,128)(2,1)S(1)} %get-tuple-element.35), channel_id=1, source_target_pairs={{0,8},{8,16},{16,24},{24,32},{32,40},{40,48},{48,56},{56,64},{64,7... | collective-permute-start | bytes 221192 | tf_op jit(solution)/shard_map/ppermute | solution.py:431
  120.1 8.4 %all-to-all-done.3.received = bf16[24,32,128]{2,1,0:T(8,128)(2,1)S(1)} async-done(((bf16[24,32,128]{2,1,0:T(8,128)(2,1)}), bf16[24,32,128]{2,1,0:T(8,128)(2,1)S(1)}, u32[]{:S(2)}, u32[]{:S(2)}) %all-to-all-start.3) | async-done | bytes 196640 | tf_op jit(solution)/shard_map/all_to_all | solution.py:436
  128.5 0.6 shard_map.104
  129.1 0.9 shard_map.102
  (25 shorter events, 0.2 us)
Async XLA Ops:
  6.4 3.7 %collective-permute-start = (bf16[4,72,512]{2,1,0:T(8,128)(2,1)}, bf16[4,72,512]{2,1,0:T(8,128)(2,1)S(1)}, u32[]{:S(2)}, u32[]{:S(2)}) collective-permute-start(bf16[4,72,512]{2,1,0:T(8,128)(2,1)} %get-tuple-element.23), channel_id=1, source_target_pairs={{0,1},{1,0},{2,3},{3,2},{4,5},{5,4},{6,7},{7,6},{8,9},{9,8},{10,11... | collective-permute-start | bytes 884744 | tf_op jit(solution)/shard_map/ppermute | solution.py:309
  10.1 1.0 copy-start.1
  11.9 27.4 %all-to-all-start = ((bf16[4,72,512]{2,1,0:T(8,128)(2,1)}), bf16[4,72,512]{2,1,0:T(8,128)(2,1)S(1)}, u32[]{:S(2)}, u32[]{:S(2)}) async-start(bf16[4,72,512]{2,1,0:T(8,128)(2,1)} %get-tuple-element.24), calls=%async_computation | async-start | bytes 589824 | tf_op jit(solution)/shard_map/all_to_all | solution.py:320
  19.2 0.7 copy-start.10
  20.5 18.7 %collective-permute-start.1 = (bf16[72,512]{1,0:T(8,128)(2,1)S(1)}, bf16[72,512]{1,0:T(8,128)(2,1)S(1)}, u32[]{:S(2)}, u32[]{:S(2)}) collective-permute-start(bf16[72,512]{1,0:T(8,128)(2,1)S(1)} %get-tuple-element.27), channel_id=1, source_target_pairs={{8,0},{16,8},{24,16},{32,24},{40,32},{48,40},{56,48},{64,56},{72,6... | collective-permute-start | bytes 221192 | tf_op jit(solution)/shard_map/ppermute | solution.py:303
  39.3 0.9 copy-start.2
  40.5 21.4 %collective-permute-start.2 = (bf16[72,512]{1,0:T(8,128)(2,1)S(1)}, bf16[72,512]{1,0:T(8,128)(2,1)S(1)}, u32[]{:S(2)}, u32[]{:S(2)}) collective-permute-start(bf16[72,512]{1,0:T(8,128)(2,1)S(1)} %get-tuple-element.28.own), channel_id=1, source_target_pairs={{8,0},{16,8},{24,16},{32,24},{40,32},{48,40},{56,48},{64,56},{72,6... | collective-permute-start | bytes 221192 | tf_op jit(solution)/shard_map/ppermute | solution.py:360
  49.6 27.6 %copy-start.6 = (bf16[3,144,512]{2,1,0:T(8,128)(2,1)S(1)}, bf16[3,144,512]{2,1,0:T(8,128)(2,1)}, u32[]{:S(2)}) copy-start(bf16[3,144,512]{2,1,0:T(8,128)(2,1)} %get-tuple-element.29.hidden) | copy-start | bytes 1327108
  49.6 27.6 %copy-start.7 = (f32[3,144,144]{2,1,0:T(8,128)S(1)}, f32[3,144,144]{2,1,0:T(8,128)}, u32[]{:S(2)}) copy-start(f32[3,144,144]{2,1,0:T(8,128)} %get-tuple-element.31.probs) | copy-start | bytes 746500
  49.7 27.6 %copy-start.8 = (bf16[3,144,256]{2,1,0:T(8,128)(2,1)S(1)}, bf16[3,144,256]{2,1,0:T(8,128)(2,1)}, u32[]{:S(2)}) copy-start(bf16[3,144,256]{2,1,0:T(8,128)(2,1)} %get-tuple-element.30.packed) | copy-start | bytes 663556
  49.7 34.5 %all-to-all-start.2 = ((bf16[4,15,32,128]{3,2,1,0:T(8,128)(2,1)}), bf16[4,15,32,128]{3,2,1,0:T(8,128)(2,1)S(1)}, u32[]{:S(2)}, u32[]{:S(2)}) async-start(bf16[4,15,32,128]{3,2,1,0:T(8,128)(2,1)} %get-tuple-element.41), calls=%async_computation.2 | async-start | bytes 983040 | tf_op jit(solution)/shard_map/all_to_all | solution.py:365
  61.9 15.4 %copy-start = (bf16[576,512]{1,0:T(8,128)(2,1)S(1)}, bf16[576,512]{1,0:T(8,128)(2,1)}, u32[]{:S(2)}) copy-start(bf16[576,512]{1,0:T(8,128)(2,1)} %param.8) | copy-start | bytes 1769476
  61.9 15.4 %copy-start.4 = (bf16[3,512,64]{1,2,0:T(8,128)(2,1)S(1)}, bf16[3,512,64]{1,2,0:T(8,128)(2,1)}, u32[]{:S(2)}) copy-start(bf16[3,512,64]{1,2,0:T(8,128)(2,1)} %param.12) | copy-start | bytes 589828
  61.9 15.4 %copy-start.5 = (bf16[64,512]{1,0:T(8,128)(2,1)S(1)}, bf16[64,512]{1,0:T(8,128)(2,1)}, u32[]{:S(2)}) copy-start(bf16[64,512]{1,0:T(8,128)(2,1)} %out_weight.1) | copy-start | bytes 196612
  61.9 15.4 %copy-start.9 = (bf16[4,32,128]{2,1,0:T(8,128)(2,1)S(1)}, bf16[4,32,128]{2,1,0:T(8,128)(2,1)}, u32[]{:S(2)}) copy-start(bf16[4,32,128]{2,1,0:T(8,128)(2,1)} %get-tuple-element.32.early) | copy-start | bytes 98308
  77.3 0.7 copy-start.3
  84.2 20.2 %all-to-all-start.1 = ((bf16[8,72,512]{2,1,0:T(8,128)(2,1)}), bf16[8,72,512]{2,1,0:T(8,128)(2,1)S(1)}, u32[]{:S(2)}, u32[]{:S(2)}) async-start(bf16[8,72,512]{2,1,0:T(8,128)(2,1)} %get-tuple-element.33), calls=%async_computation.1 | async-start | bytes 1179648 | tf_op jit(solution)/shard_map/all_to_all | solution.py:410
  87.8 8.7 %collective-permute-start.4 = (bf16[9,32,128]{2,1,0:T(8,128)(2,1)S(1)}, bf16[9,32,128]{2,1,0:T(8,128)(2,1)S(1)}, u32[]{:S(2)}, u32[]{:S(2)}) collective-permute-start(bf16[9,32,128]{2,1,0:T(8,128)(2,1)S(1)} %get-tuple-element.38), channel_id=1, source_target_pairs={{0,24},{24,48},{48,72},{72,0},{1,25},{25,49},{49,73},{73,1},{2,26}... | collective-permute-start | bytes 221192 | tf_op jit(solution)/shard_map/ppermute | solution.py:412
  89.8 7.9 %collective-permute-start.5 = (bf16[9,32,128]{2,1,0:T(8,128)(2,1)S(1)}, bf16[9,32,128]{2,1,0:T(8,128)(2,1)S(1)}, u32[]{:S(2)}, u32[]{:S(2)}) collective-permute-start(bf16[9,32,128]{2,1,0:T(8,128)(2,1)S(1)} %get-tuple-element.39), channel_id=1, source_target_pairs={{0,48},{24,72},{48,0},{72,24},{1,49},{25,73},{49,1},{73,25},{2,50}... | collective-permute-start | bytes 221192 | tf_op jit(solution)/shard_map/ppermute | solution.py:412
  94.5 7.5 %collective-permute-start.6 = (bf16[9,32,128]{2,1,0:T(8,128)(2,1)S(1)}, bf16[9,32,128]{2,1,0:T(8,128)(2,1)S(1)}, u32[]{:S(2)}, u32[]{:S(2)}) collective-permute-start(bf16[9,32,128]{2,1,0:T(8,128)(2,1)S(1)} %get-tuple-element.40), channel_id=1, source_target_pairs={{0,72},{24,0},{48,24},{72,48},{1,73},{25,1},{49,25},{73,49},{2,74}... | collective-permute-start | bytes 221192 | tf_op jit(solution)/shard_map/ppermute | solution.py:412
  104.4 24.0 %all-to-all-start.3 = ((bf16[24,32,128]{2,1,0:T(8,128)(2,1)}), bf16[24,32,128]{2,1,0:T(8,128)(2,1)S(1)}, u32[]{:S(2)}, u32[]{:S(2)}) async-start(bf16[24,32,128]{2,1,0:T(8,128)(2,1)} %shard_map.103), calls=%async_computation.3 | async-start | bytes 393216 | tf_op jit(solution)/shard_map/all_to_all | solution.py:436
  112.4 16.7 %collective-permute-start.3 = (bf16[72,512]{1,0:T(8,128)(2,1)S(1)}, bf16[72,512]{1,0:T(8,128)(2,1)S(1)}, u32[]{:S(2)}, u32[]{:S(2)}) collective-permute-start(bf16[72,512]{1,0:T(8,128)(2,1)S(1)} %get-tuple-element.35), channel_id=1, source_target_pairs={{0,8},{8,16},{16,24},{24,32},{32,40},{40,48},{48,56},{56,64},{64,7... | collective-permute-start | bytes 221192 | tf_op jit(solution)/shard_map/ppermute | solution.py:431

commit v12 on v10

--- a/solution.py
+++ b/solution.py
@@ -182,7 +182,7 @@
     given[...] = jnp.where(place[0] == 0, far[...].astype(F32), own[...].astype(F32)).astype(BF)
 
 
-def pair_kernel(keep, taken, _, __, pair, ___, ____):
+def pair_kernel(keep, taken, _, pair, __):
     pair[...] = (keep[...].astype(F32) + taken[...].astype(F32)).astype(BF)
 
 
@@ -265,11 +265,10 @@
     total_b[...] = total[...].astype(BF)
 
 
-def final_kernel(place, summed, arrived, mid, block_input, grad_input, token):
+def final_kernel(place, summed, arrived, mid, block_input, grad_input):
     total = jnp.where(place[0] == 0, arrived[...].astype(F32), summed[...])
     normed, factor = normalize(block_input[0])
     grad_input[...] = (mid[...] + norm_back(normed, factor, total)).astype(BF)
-    token[...] = jnp.zeros_like(token)
 
 
 def join_kernel(first, second, third, fourth, late, joined):
@@ -281,7 +280,7 @@
     joined[count:] = jnp.sum(late[...].astype(F32), axis=0).astype(BF)
 
 
-def total_kernel(received, _, owned):
+def total_kernel(received, owned):
     owned[...] = jnp.sum(received[...].astype(F32), axis=0)
 
 
@@ -308,17 +307,13 @@
     core_place = lax.axis_index("core").astype(jnp.int32).reshape(1)
     keep, give, late, early = mlp(core_place, stream, grad_out, up_weight, down_weight)
     taken = lax.ppermute(give, "core", [(0, 1), (1, 0)])
-    pair, first_rows, labels = call(
+    pair, first_rows = call(
         pair_kernel,
         (1,),
-        [whole(keep), whole(taken), ANY, ANY],
-        [
-            (keep.shape, BF, whole(keep)),
-            (first_rows.shape, BF, ANY),
-            (labels.shape, labels.dtype, ANY),
-        ],
-        (keep, taken, first_rows, labels),
-        aliases={2: 1, 3: 2},
+        [whole(keep), whole(taken), ANY],
+        [(keep.shape, BF, whole(keep)), (first_rows.shape, BF, ANY)],
+        (keep, taken, first_rows),
+        aliases={2: 1},
         vmem=16,
     )
     far_input = from_next(first_rows)
@@ -456,11 +451,11 @@
         [(i * head_count, (i + 1) % count * head_count) for i in range(count)],
     )
     received = lax.all_to_all(partial_sum, ("y", "zh"), 0, 0)
-    grad_input, ready = call(
+    (grad_input,) = call(
         final_kernel,
         (1,),
         [whole(summed), whole(arrived), whole(mid), mine],
-        [(row_part.shape, BF, whole(row_part)), (token.shape, F32, whole(token))],
+        [(row_part.shape, BF, whole(row_part))],
         (summed, arrived, mid, chunks_in),
         chosen=head_place,
         vmem=16,
@@ -469,9 +464,9 @@
     (owned,) = call(
         total_kernel,
         (1,),
-        [whole(received), ANY],
+        [whole(received)],
         [(BLOCK, F32, whole(owner_block))],
-        (received, ready),
+        (received,),
         vmem=16,
     )
     return (grad_input, owned.reshape(1, -1))

time: 124 us -> 124 us (level)
  starting transfers between devices: 65.9 us -> 64.3 us
    all_to_all x1, waiting for transfers between devices: 2.71 us -> 7.16 us  [shards(): received = lax.all_to_all(partial_sum, ('y', 'zh'), 0, 0)]
    ppermute x1, waiting for transfers between devices: 3.68 us -> 0.01 us  [shards(): lax.ppermute(summed_b, WIN_AXES + HEAD_AXES, [(i * head_count, (i + 1) %...]
    ppermute x1, starting transfers between devices: 10 us -> 8.49 us  [shards(): lax.ppermute(own_grad_mid, WIN_AXES + HEAD_AXES, [((i + 1) % count * head...]
    unnamed x32 -> x30, local copies, waits for them, and re-layouts: 3.14 us -> 3.23 us
  transfers between devices with their start and end apart: 11 -> 11, of which waited for: 6 -> 5; matrix products, arithmetic and copies ran while one was open for 1% -> 1% of each run, Pallas kernels for 12% -> 12%
where the time goes in v12:
time: 124 us; the launch traced here: 123 us
  starting transfers between devices  64.3 us (52%)
  Pallas kernels  22.1 us (18%)
  blocking collectives  15.3 us (12%)
  waiting for transfers between devices  15.2 us (12%)
  local copies, waits for them, and re-layouts  4.79 us (4%)
    pallas_call x11, Pallas kernels, call(): pl.pallas_call(kernel, grid_spec=spec, out_shape=[jax.ShapeDtypeStruct(ou...  22.1 us
    all_gather x1, blocking collectives, shards(): grad_mid = lax.all_gather(given, HEAD_AXES, axis=0)  15.3 us
    ppermute x1, starting transfers between devices, from_next(): lax.ppermute(values, WIN_AXES, [((i + 1) % count, i) for i in range(count)])  12.1 us
    all_to_all x1, starting transfers between devices, shards(): late_parts = lax.all_to_all(late, 'x', 0, 0)  8.92 us
    ppermute x3, starting transfers between devices, shards(): lax.ppermute(pieces[k], 'x', [(i, (i + k) % 4) for i in range(4)])  8.68 us
    ppermute x1, starting transfers between devices, shards(): lax.ppermute(own_grad_mid, WIN_AXES + HEAD_AXES, [((i + 1) % count * head...  8.49 us
    ppermute x1, starting transfers between devices, shards(): lax.ppermute(summed_b, WIN_AXES + HEAD_AXES, [(i * head_count, (i + 1) %...  7.66 us
    all_to_all x1, starting transfers between devices, shards(): parts = lax.all_to_all(pair, 'zl', 0, 0)  7.26 us
  transfers between devices with their start and end apart: 11, of which 5 were waited for; matrix products, arithmetic and copies ran while one was open for 1% of the time, Pallas kernels for 12%

profile of v12, /device:TPU:6, one launch (start us, length us, event | category | flops | bytes accessed | tf_op | source)
XLA Modules:
  0.0 122.6 jit_solution(9731985857212747055)
XLA Ops:
  0.6 5.8 %shard_map.95 = (bf16[4,72,512]{2,1,0:T(8,128)(2,1)}, bf16[4,72,512]{2,1,0:T(8,128)(2,1)}, bf16[4,15,32,128]{3,2,1,0:T(8,128)(2,1)}, bf16[4,32,128]{2,1,0:T(8,128)(2,1)}) custom-call(s32[1]{0:T(128)} %bitcast.2.place, bf16[576,512]{1,0:T(8,128)(2,1)} %stream.1, bf16[576,512]{1,0:T(8,128)(2,1)} %grad_out.1, bf16[512,256]{1,0:T(8,128)(2,1)} %up_weight.1, ...), custom_call_target="tpu_custom_call" | custom-call | flops 6899999744 | bytes 2097152 | tf_op jit(solution)/shard_map/pallas_call | solution.py:57
  6.5 1.9 %collective-permute-start = (bf16[4,72,512]{2,1,0:T(8,128)(2,1)}, bf16[4,72,512]{2,1,0:T(8,128)(2,1)S(1)}, u32[]{:S(2)}, u32[]{:S(2)}) collective-permute-start(bf16[4,72,512]{2,1,0:T(8,128)(2,1)} %get-tuple-element.27), channel_id=1, source_target_pairs={{0,1},{1,0},{2,3},{3,2},{4,5},{5,4},{6,7},{7,6},{8,9},{9,8},{10,11... | collective-permute-start | bytes 884744 | tf_op jit(solution)/shard_map/ppermute | solution.py:309
  8.4 0.9 slice.4._
  9.3 0.9 collective-permute-done.taken
  10.2 1.0 copy-done.1
  11.1 0.8 shard_map.96
  11.9 7.3 %all-to-all-start = ((bf16[4,72,512]{2,1,0:T(8,128)(2,1)}), bf16[4,72,512]{2,1,0:T(8,128)(2,1)S(1)}, u32[]{:S(2)}, u32[]{:S(2)}) async-start(bf16[4,72,512]{2,1,0:T(8,128)(2,1)} %get-tuple-element.28), calls=%async_computation | async-start | bytes 589824 | tf_op jit(solution)/shard_map/all_to_all | solution.py:320
  19.2 0.7 copy-done.13
  19.9 0.7 reshape.37.labels
  20.6 12.1 %collective-permute-start.2 = (bf16[72,512]{1,0:T(8,128)(2,1)S(1)}, bf16[72,512]{1,0:T(8,128)(2,1)S(1)}, u32[]{:S(2)}, u32[]{:S(2)}) collective-permute-start(bf16[72,512]{1,0:T(8,128)(2,1)S(1)} %get-tuple-element.32), channel_id=1, source_target_pairs={{8,0},{16,8},{24,16},{32,24},{40,32},{48,40},{56,48},{64,56},{72,6... | collective-permute-start | bytes 221192 | tf_op jit(solution)/shard_map/ppermute | solution.py:303
  32.7 4.7 %shard_map.97 = (bf16[3,144,512]{2,1,0:T(8,128)(2,1)}, bf16[3,144,256]{2,1,0:T(8,128)(2,1)}, f32[3,144,144]{2,1,0:T(8,128)}, bf16[2,72,512]{2,1,0:T(8,128)(2,1)}) custom-call(s32[1]{0:T(128)} %bitcast.place, bf16[8,72,512]{2,1,0:T(8,128)(2,1)} %bitcast.11, bf16[8,72,512]{2,1,0:T(8,128)(2,1)} %bitcast.12, s32[4,144]{1,0:T(4,128)} %reshape.37.labels, ...), custom_call_target="tpu_custom_call" | custom-call | flops 5299999744 | bytes 2097152 | tf_op jit(solution)/shard_map/pallas_call | solution.py:57
  37.4 0.9 copy-done.2
  38.3 0.3 shard_map.98
  38.6 8.5 %collective-permute-start.1 = (bf16[72,512]{1,0:T(8,128)(2,1)S(1)}, bf16[72,512]{1,0:T(8,128)(2,1)S(1)}, u32[]{:S(2)}, u32[]{:S(2)}) collective-permute-start(bf16[72,512]{1,0:T(8,128)(2,1)S(1)} %get-tuple-element.31.own), channel_id=1, source_target_pairs={{8,0},{16,8},{24,16},{32,24},{40,32},{48,40},{56,48},{64,56},{72,6... | collective-permute-start | bytes 221192 | tf_op jit(solution)/shard_map/ppermute | solution.py:361
  47.1 0.6 copy-done.14
  47.7 2.6 %shard_map.99 = (bf16[1,144,512]{2,1,0:T(8,128)(2,1)}, bf16[1,144,256]{2,1,0:T(8,128)(2,1)}, f32[1,144,144]{2,1,0:T(8,128)}, f32[8,128]{1,0:T(8,128)}) custom-call(bf16[8,72,512]{2,1,0:T(8,128)(2,1)} %bitcast.13, bf16[72,512]{1,0:T(8,128)(2,1)} %copy-done.14, s32[4,144]{1,0:T(4,128)} %reshape.37.labels, bf16[192,512]{1,0:T(8,128)(2,1)} %bitcast.18), custom_call_target="tpu_custom_call" | custom-call | flops 2000000000 | bytes 2097152 | tf_op jit(solution)/shard_map/pallas_call | solution.py:57
  50.3 8.9 %all-to-all-start.2 = ((bf16[4,15,32,128]{3,2,1,0:T(8,128)(2,1)}), bf16[4,15,32,128]{3,2,1,0:T(8,128)(2,1)S(1)}, u32[]{:S(2)}, u32[]{:S(2)}) async-start(bf16[4,15,32,128]{3,2,1,0:T(8,128)(2,1)} %get-tuple-element.49), calls=%async_computation.2 | async-start | bytes 983040 | tf_op jit(solution)/shard_map/all_to_all | solution.py:366
  59.4 15.3 %all-gather = bf16[576,512]{1,0:T(8,128)(2,1)S(1)} all-gather(bf16[72,512]{1,0:T(8,128)(2,1)S(1)} %shard_map.100), channel_id=2, replica_groups=mesh['y'=8,'x'=4,'zh'=3,'zl'=4,'core'=2] {'zl','core'}, dimensions={0}, use_global_device_ids=true | all-gather | bytes 663552 | tf_op jit(solution)/shard_map/all_gather | solution.py:395
  74.7 5.4 %shard_map.101 = (bf16[8,72,512]{2,1,0:T(8,128)(2,1)}, bf16[9,32,128]{2,1,0:T(8,128)(2,1)S(1)}, bf16[9,32,128]{2,1,0:T(8,128)(2,1)S(1)}, bf16[9,32,128]{2,1,0:T(8,128)(2,1)S(1)}, bf16[9,32,128]{2,1,0:T(8,128)(2,1)S(1)}) custom-call(s32[1]{0:T(128)} %bitcast.1.place, bf16[8,72,512]{2,1,0:T(8,128)(2,1)S(1)} %bitcast.15, bf16[8,72,512]{2,1,0:T(8,128)(2,1)S(1)} %bitcast.16, ...), custom_call_target="tpu_custom_call" | custom-call | flops 7000000000 | bytes 2097152 | tf_op jit(solution)/shard_map/pallas_call | solution.py:57
  80.1 3.5 %all-to-all-start.1 = ((bf16[8,72,512]{2,1,0:T(8,128)(2,1)}), bf16[8,72,512]{2,1,0:T(8,128)(2,1)S(1)}, u32[]{:S(2)}, u32[]{:S(2)}) async-start(bf16[8,72,512]{2,1,0:T(8,128)(2,1)} %get-tuple-element.41), calls=%async_computation.1 | async-start | bytes 1179648 | tf_op jit(solution)/shard_map/all_to_all | solution.py:427
  83.7 2.0 %collective-permute-start.4 = (bf16[9,32,128]{2,1,0:T(8,128)(2,1)S(1)}, bf16[9,32,128]{2,1,0:T(8,128)(2,1)S(1)}, u32[]{:S(2)}, u32[]{:S(2)}) collective-permute-start(bf16[9,32,128]{2,1,0:T(8,128)(2,1)S(1)} %get-tuple-element.46), channel_id=1, source_target_pairs={{0,24},{24,48},{48,72},{72,0},{1,25},{25,49},{49,73},{73,1},{2,26}... | collective-permute-start | bytes 221192 | tf_op jit(solution)/shard_map/ppermute | solution.py:429
  85.7 4.8 %collective-permute-start.5 = (bf16[9,32,128]{2,1,0:T(8,128)(2,1)S(1)}, bf16[9,32,128]{2,1,0:T(8,128)(2,1)S(1)}, u32[]{:S(2)}, u32[]{:S(2)}) collective-permute-start(bf16[9,32,128]{2,1,0:T(8,128)(2,1)S(1)} %get-tuple-element.47), channel_id=1, source_target_pairs={{0,48},{24,72},{48,0},{72,24},{1,49},{25,73},{49,1},{73,25},{2,50}... | collective-permute-start | bytes 221192 | tf_op jit(solution)/shard_map/ppermute | solution.py:429
  90.4 1.9 %collective-permute-start.6 = (bf16[9,32,128]{2,1,0:T(8,128)(2,1)S(1)}, bf16[9,32,128]{2,1,0:T(8,128)(2,1)S(1)}, u32[]{:S(2)}, u32[]{:S(2)}) collective-permute-start(bf16[9,32,128]{2,1,0:T(8,128)(2,1)S(1)} %get-tuple-element.48), channel_id=1, source_target_pairs={{0,72},{24,0},{48,24},{72,48},{1,73},{25,1},{49,25},{73,49},{2,74}... | collective-permute-start | bytes 221192 | tf_op jit(solution)/shard_map/ppermute | solution.py:429
  92.4 1.2 collective-permute-done.5.third
  93.6 4.3 %collective-permute-done.6.fourth = bf16[9,32,128]{2,1,0:T(8,128)(2,1)S(1)} collective-permute-done((bf16[9,32,128]{2,1,0:T(8,128)(2,1)S(1)}, bf16[9,32,128]{2,1,0:T(8,128)(2,1)S(1)}, u32[]{:S(2)}, u32[]{:S(2)}) %collective-permute-start.6) | collective-permute-done | bytes 73760 | tf_op jit(solution)/shard_map/ppermute | solution.py:429
  97.9 0.8 shard_map.104
  98.7 1.7 %all-to-all-done.1.parts = bf16[8,72,512]{2,1,0:T(8,128)(2,1)S(1)} async-done(((bf16[8,72,512]{2,1,0:T(8,128)(2,1)}), bf16[8,72,512]{2,1,0:T(8,128)(2,1)S(1)}, u32[]{:S(2)}, u32[]{:S(2)}) %all-to-all-start.1) | async-done | bytes 589856 | tf_op jit(solution)/shard_map/all_to_all | solution.py:427
  100.3 5.7 %all-to-all-start.3 = ((bf16[24,32,128]{2,1,0:T(8,128)(2,1)}), bf16[24,32,128]{2,1,0:T(8,128)(2,1)S(1)}, u32[]{:S(2)}, u32[]{:S(2)}) async-start(bf16[24,32,128]{2,1,0:T(8,128)(2,1)} %shard_map.104), calls=%async_computation.3 | async-start | bytes 393216 | tf_op jit(solution)/shard_map/all_to_all | solution.py:453
  106.2 7.7 %collective-permute-start.3 = (bf16[72,512]{1,0:T(8,128)(2,1)S(1)}, bf16[72,512]{1,0:T(8,128)(2,1)S(1)}, u32[]{:S(2)}, u32[]{:S(2)}) collective-permute-start(bf16[72,512]{1,0:T(8,128)(2,1)S(1)} %get-tuple-element.43), channel_id=1, source_target_pairs={{0,8},{8,16},{16,24},{24,32},{32,40},{40,48},{48,56},{56,64},{64,7... | collective-permute-start | bytes 221192 | tf_op jit(solution)/shard_map/ppermute | solution.py:448
  113.9 7.2 %all-to-all-done.3.received = bf16[24,32,128]{2,1,0:T(8,128)(2,1)S(1)} async-done(((bf16[24,32,128]{2,1,0:T(8,128)(2,1)}), bf16[24,32,128]{2,1,0:T(8,128)(2,1)S(1)}, u32[]{:S(2)}, u32[]{:S(2)}) %all-to-all-start.3) | async-done | bytes 196640 | tf_op jit(solution)/shard_map/all_to_all | solution.py:453
  121.0 0.6 shard_map.105
  121.7 0.9 shard_map.103
  (34 shorter events, 0.2 us)
Async XLA Ops:
  6.5 3.7 %collective-permute-start = (bf16[4,72,512]{2,1,0:T(8,128)(2,1)}, bf16[4,72,512]{2,1,0:T(8,128)(2,1)S(1)}, u32[]{:S(2)}, u32[]{:S(2)}) collective-permute-start(bf16[4,72,512]{2,1,0:T(8,128)(2,1)} %get-tuple-element.27), channel_id=1, source_target_pairs={{0,1},{1,0},{2,3},{3,2},{4,5},{5,4},{6,7},{7,6},{8,9},{9,8},{10,11... | collective-permute-start | bytes 884744 | tf_op jit(solution)/shard_map/ppermute | solution.py:309
  10.2 1.0 copy-start.1
  11.9 25.4 %all-to-all-start = ((bf16[4,72,512]{2,1,0:T(8,128)(2,1)}), bf16[4,72,512]{2,1,0:T(8,128)(2,1)S(1)}, u32[]{:S(2)}, u32[]{:S(2)}) async-start(bf16[4,72,512]{2,1,0:T(8,128)(2,1)} %get-tuple-element.28), calls=%async_computation | async-start | bytes 589824 | tf_op jit(solution)/shard_map/all_to_all | solution.py:320
  19.2 0.7 copy-start.13
  20.6 26.5 %collective-permute-start.2 = (bf16[72,512]{1,0:T(8,128)(2,1)S(1)}, bf16[72,512]{1,0:T(8,128)(2,1)S(1)}, u32[]{:S(2)}, u32[]{:S(2)}) collective-permute-start(bf16[72,512]{1,0:T(8,128)(2,1)S(1)} %get-tuple-element.32), channel_id=1, source_target_pairs={{8,0},{16,8},{24,16},{32,24},{40,32},{48,40},{56,48},{64,56},{72,6... | collective-permute-start | bytes 221192 | tf_op jit(solution)/shard_map/ppermute | solution.py:303
  37.4 0.9 copy-start.2
  38.6 20.7 %collective-permute-start.1 = (bf16[72,512]{1,0:T(8,128)(2,1)S(1)}, bf16[72,512]{1,0:T(8,128)(2,1)S(1)}, u32[]{:S(2)}, u32[]{:S(2)}) collective-permute-start(bf16[72,512]{1,0:T(8,128)(2,1)S(1)} %get-tuple-element.31.own), channel_id=1, source_target_pairs={{8,0},{16,8},{24,16},{32,24},{40,32},{48,40},{56,48},{64,56},{72,6... | collective-permute-start | bytes 221192 | tf_op jit(solution)/shard_map/ppermute | solution.py:361
  47.1 0.6 copy-start.14
  50.3 8.9 %copy-start.5 = (f32[8,128]{1,0:T(8,128)S(1)}, f32[8,128]{1,0:T(8,128)}, u32[]{:S(2)}) copy-start(f32[8,128]{1,0:T(8,128)} %get-tuple-element.33._) | copy-start | bytes 12292
  50.3 24.4 %copy-start.9 = (bf16[3,144,512]{2,1,0:T(8,128)(2,1)S(1)}, bf16[3,144,512]{2,1,0:T(8,128)(2,1)}, u32[]{:S(2)}) copy-start(bf16[3,144,512]{2,1,0:T(8,128)(2,1)} %get-tuple-element.34.hidden) | copy-start | bytes 1327108
  50.3 24.4 %copy-start.10 = (f32[3,144,144]{2,1,0:T(8,128)S(1)}, f32[3,144,144]{2,1,0:T(8,128)}, u32[]{:S(2)}) copy-start(f32[3,144,144]{2,1,0:T(8,128)} %get-tuple-element.36.probs) | copy-start | bytes 746500
  50.3 29.8 %all-to-all-start.2 = ((bf16[4,15,32,128]{3,2,1,0:T(8,128)(2,1)}), bf16[4,15,32,128]{3,2,1,0:T(8,128)(2,1)S(1)}, u32[]{:S(2)}, u32[]{:S(2)}) async-start(bf16[4,15,32,128]{3,2,1,0:T(8,128)(2,1)} %get-tuple-element.49), calls=%async_computation.2 | async-start | bytes 983040 | tf_op jit(solution)/shard_map/all_to_all | solution.py:366
  59.3 15.4 %copy-start.11 = (bf16[3,144,256]{2,1,0:T(8,128)(2,1)S(1)}, bf16[3,144,256]{2,1,0:T(8,128)(2,1)}, u32[]{:S(2)}) copy-start(bf16[3,144,256]{2,1,0:T(8,128)(2,1)} %get-tuple-element.35.packed) | copy-start | bytes 663556
  59.3 15.4 %copy-start.3 = (bf16[3,512,64]{1,2,0:T(8,128)(2,1)S(1)}, bf16[3,512,64]{1,2,0:T(8,128)(2,1)}, u32[]{:S(2)}) copy-start(bf16[3,512,64]{1,2,0:T(8,128)(2,1)} %param.12) | copy-start | bytes 589828
  59.3 15.4 %copy-start.4 = (bf16[64,512]{1,0:T(8,128)(2,1)S(1)}, bf16[64,512]{1,0:T(8,128)(2,1)}, u32[]{:S(2)}) copy-start(bf16[64,512]{1,0:T(8,128)(2,1)} %out_weight.1) | copy-start | bytes 196612
  59.3 15.4 %copy-start.6 = (bf16[1,144,512]{2,1,0:T(8,128)(2,1)S(1)}, bf16[1,144,512]{2,1,0:T(8,128)(2,1)}, u32[]{:S(2)}) copy-start(bf16[1,144,512]{2,1,0:T(8,128)(2,1)} %get-tuple-element.37.last_hidden) | copy-start | bytes 442372
  59.3 15.4 %copy-start.7 = (f32[1,144,144]{2,1,0:T(8,128)S(1)}, f32[1,144,144]{2,1,0:T(8,128)}, u32[]{:S(2)}) copy-start(f32[1,144,144]{2,1,0:T(8,128)} %get-tuple-element.39.last_probs) | copy-start | bytes 248836
  59.3 15.4 %copy-start.8 = (bf16[1,144,256]{2,1,0:T(8,128)(2,1)S(1)}, bf16[1,144,256]{2,1,0:T(8,128)(2,1)}, u32[]{:S(2)}) copy-start(bf16[1,144,256]{2,1,0:T(8,128)(2,1)} %get-tuple-element.38.last_packed) | copy-start | bytes 221188
  59.3 15.4 %copy-start.12 = (bf16[4,32,128]{2,1,0:T(8,128)(2,1)S(1)}, bf16[4,32,128]{2,1,0:T(8,128)(2,1)}, u32[]{:S(2)}) copy-start(bf16[4,32,128]{2,1,0:T(8,128)(2,1)} %get-tuple-element.40.early) | copy-start | bytes 98308
  80.1 20.2 %all-to-all-start.1 = ((bf16[8,72,512]{2,1,0:T(8,128)(2,1)}), bf16[8,72,512]{2,1,0:T(8,128)(2,1)S(1)}, u32[]{:S(2)}, u32[]{:S(2)}) async-start(bf16[8,72,512]{2,1,0:T(8,128)(2,1)} %get-tuple-element.41), calls=%async_computation.1 | async-start | bytes 1179648 | tf_op jit(solution)/shard_map/all_to_all | solution.py:427
  83.7 8.7 %collective-permute-start.4 = (bf16[9,32,128]{2,1,0:T(8,128)(2,1)S(1)}, bf16[9,32,128]{2,1,0:T(8,128)(2,1)S(1)}, u32[]{:S(2)}, u32[]{:S(2)}) collective-permute-start(bf16[9,32,128]{2,1,0:T(8,128)(2,1)S(1)} %get-tuple-element.46), channel_id=1, source_target_pairs={{0,24},{24,48},{48,72},{72,0},{1,25},{25,49},{49,73},{73,1},{2,26}... | collective-permute-start | bytes 221192 | tf_op jit(solution)/shard_map/ppermute | solution.py:429
  85.7 7.9 %collective-permute-start.5 = (bf16[9,32,128]{2,1,0:T(8,128)(2,1)S(1)}, bf16[9,32,128]{2,1,0:T(8,128)(2,1)S(1)}, u32[]{:S(2)}, u32[]{:S(2)}) collective-permute-start(bf16[9,32,128]{2,1,0:T(8,128)(2,1)S(1)} %get-tuple-element.47), channel_id=1, source_target_pairs={{0,48},{24,72},{48,0},{72,24},{1,49},{25,73},{49,1},{73,25},{2,50}... | collective-permute-start | bytes 221192 | tf_op jit(solution)/shard_map/ppermute | solution.py:429
  90.4 7.5 %collective-permute-start.6 = (bf16[9,32,128]{2,1,0:T(8,128)(2,1)S(1)}, bf16[9,32,128]{2,1,0:T(8,128)(2,1)S(1)}, u32[]{:S(2)}, u32[]{:S(2)}) collective-permute-start(bf16[9,32,128]{2,1,0:T(8,128)(2,1)S(1)} %get-tuple-element.48), channel_id=1, source_target_pairs={{0,72},{24,0},{48,24},{72,48},{1,73},{25,1},{49,25},{73,49},{2,74}... | collective-permute-start | bytes 221192 | tf_op jit(solution)/shard_map/ppermute | solution.py:429
  98.7 23.0 %copy-start = (bf16[576,512]{1,0:T(8,128)(2,1)S(1)}, bf16[576,512]{1,0:T(8,128)(2,1)}, u32[]{:S(2)}) copy-start(bf16[576,512]{1,0:T(8,128)(2,1)} %param.8) | copy-start | bytes 1769476
  100.3 20.7 %all-to-all-start.3 = ((bf16[24,32,128]{2,1,0:T(8,128)(2,1)}), bf16[24,32,128]{2,1,0:T(8,128)(2,1)S(1)}, u32[]{:S(2)}, u32[]{:S(2)}) async-start(bf16[24,32,128]{2,1,0:T(8,128)(2,1)} %shard_map.104), calls=%async_computation.3 | async-start | bytes 393216 | tf_op jit(solution)/shard_map/all_to_all | solution.py:453
  106.2 15.5 %collective-permute-start.3 = (bf16[72,512]{1,0:T(8,128)(2,1)S(1)}, bf16[72,512]{1,0:T(8,128)(2,1)S(1)}, u32[]{:S(2)}, u32[]{:S(2)}) collective-permute-start(bf16[72,512]{1,0:T(8,128)(2,1)S(1)} %get-tuple-element.43), channel_id=1, source_target_pairs={{0,8},{8,16},{16,24},{24,32},{32,40},{40,48},{48,56},{56,64},{64,7... | collective-permute-start | bytes 221192 | tf_op jit(solution)/shard_map/ppermute | solution.py:448
